TPU v7x, 256 devices: a whole 4x4x8 slice. The times are simulated.
256 devices in a mesh: node: 16 (over x, y), feat: 16 (over z, core).
Axes of the slice: x: 4, y: 4, z: 8, core: 2. Of those that a mesh axis runs over, the one named last changes fastest.
Arguments:
- features: bfloat16 [1024, 131072], P('feat', 'node'), may hold values from -6 to 6
- tile_values: bfloat16 [1024, 2, 128, 128], P('node'), may hold values from -0.375 to 0.375
- tile_cols: int32 [1024, 2], P('node'), may hold values from 0 to 1023, as said below
- tile_count: int32 [1024], P('node'), may hold values from 1 to 2, as said below
- w_self: bfloat16 [1024, 1024], replicated, may hold values from -0.1875 to 0.1875
- w_neigh: bfloat16 [1024, 1024], replicated, may hold values from -0.1875 to 0.1875
- cotangent: bfloat16 [1024, 131072], P(None, ('node', 'feat')), may hold values from -6 to 6
Outputs:
- hidden: bfloat16 [1024, 131072], P(None, ('node', 'feat'))
- grad_features: bfloat16 [1024, 131072], P('feat', 'node')
- grad_w_neigh: float32 [1024, 1024], P(('node', 'feat'))
Inputs may be any that keep to these rules, and one draw needn't show every extreme that they name: `tile_cols`: slot 0 of row block r names block r itself; every other slot names a block of the row block's own partition of 64 blocks or of the partition just before or after it. `tile_count`: the first row block of every partition has all 2 slots live.
All inputs are finite; a program needn't handle non-finite values.
Results may differ from a plain program's by a relative error of at most 0.0059.
Values may be sent and summed in bfloat16 or wider, within the bound.
No kernel may reach another device: no remote copies, remote signals or barrier semaphores. Data moves between devices by JAX's collectives and lax.ppermute only.
A program may use at most 128 MiB of HBM per device.

v0:
```python
import jax
import jax.numpy as jnp
from jax import lax
from jax.sharding import PartitionSpec as P


def extended(cells, sides, width):
    for axis, dim in sides:
        count = lax.axis_size(axis)
        ends = count - 1
        head = lax.slice_in_dim(cells, 0, width, axis=dim)
        tail = lax.slice_in_dim(cells, cells.shape[dim] - width, cells.shape[dim], axis=dim)
        cells = jnp.concatenate(
            [
                lax.ppermute(tail, axis, [(i, (i + 1) % count) for i in range(ends)]),
                cells,
                lax.ppermute(head, axis, [((i + 1) % count, i) for i in range(ends)]),
            ],
            axis=dim,
        )
    return cells


def from_behind(value, axis, steps):
    count = lax.axis_size(axis)
    initial, last = (max(0, -steps), min(count, count - steps))
    return lax.ppermute(value, axis, [(source, source + steps) for source in range(initial, last)])


def local(features, tile_values, tile_cols, tile_count, w_self, w_neigh, cotangent):
    feat_dev, node_dev = features.shape
    slots = tile_values.shape[1]
    tile = tile_values.shape[-1]
    block_count = node_dev // tile
    part = lax.axis_index("node")
    live = jnp.arange(slots, dtype=jnp.int32)[None, :] < tile_count[:, None]
    masked = jnp.where(live[:, :, None, None], tile_values, jnp.zeros_like(tile_values))
    window = extended(features, (("node", 1),), node_dev)
    window_blocks = window.reshape(feat_dev, 3 * block_count, tile)
    local_cols = tile_cols - (part - 1) * block_count
    picked = window_blocks[:, local_cols, :]
    agg = jnp.einsum("fbkj,bkji->fbi", picked, masked, preferred_element_type=jnp.float32)
    agg = agg.reshape(feat_dev, node_dev).astype(jnp.bfloat16)
    x_rows, agg_rows = (
        lax.all_to_all(features, "feat", split_axis=1, concat_axis=0, tiled=True),
        lax.all_to_all(agg, "feat", split_axis=1, concat_axis=0, tiled=True),
    )
    pre = jnp.dot(w_self, x_rows, preferred_element_type=jnp.float32) + jnp.dot(
        w_neigh, agg_rows, preferred_element_type=jnp.float32
    )
    sig = jax.nn.sigmoid(pre)
    hidden = (pre * sig).astype(jnp.bfloat16)
    dpre = (cotangent.astype(jnp.float32) * sig * (1.0 + pre * (1.0 - sig))).astype(jnp.bfloat16)
    rows_dims = (((1,), (1,)), ((), ()))
    part_neigh = lax.dot_general(dpre, agg_rows, rows_dims, preferred_element_type=jnp.float32)
    grad_w_neigh = lax.psum_scatter(part_neigh, ("node", "feat"), scatter_dimension=0, tiled=True)
    out_dims = (((0,), (0,)), ((), ()))
    dself = lax.dot_general(w_self, dpre, out_dims, preferred_element_type=jnp.float32).astype(
        jnp.bfloat16
    )
    dagg = lax.dot_general(w_neigh, dpre, out_dims, preferred_element_type=jnp.float32).astype(
        jnp.bfloat16
    )
    dself_cols, dagg_cols = (
        lax.all_to_all(dself, "feat", split_axis=0, concat_axis=1, tiled=True),
        lax.all_to_all(dagg, "feat", split_axis=0, concat_axis=1, tiled=True),
    )
    dagg_blocks = dagg_cols.reshape(feat_dev, block_count, tile)
    contrib = jnp.einsum("fbi,bkji->fbkj", dagg_blocks, masked, preferred_element_type=jnp.float32)
    spread = (
        jnp.zeros((feat_dev, 3 * block_count, tile), jnp.float32).at[:, local_cols, :].add(contrib)
    )
    from_after = from_behind(spread[:, :block_count].astype(jnp.bfloat16), "node", -1).astype(
        jnp.float32
    )
    from_before = from_behind(spread[:, 2 * block_count :].astype(jnp.bfloat16), "node", 1).astype(
        jnp.float32
    )
    total = spread[:, block_count : 2 * block_count] + from_after + from_before
    grad_features = (dself_cols.astype(jnp.float32) + total.reshape(feat_dev, node_dev)).astype(
        jnp.bfloat16
    )
    return (hidden, grad_features, grad_w_neigh)


def solution(mesh):
    placed = (
        P("feat", "node"),
        P("node", None, None, None),
        P("node", None),
        P("node"),
        P(),
        P(),
        P(None, ("node", "feat")),
    )
    return jax.shard_map(
        local,
        mesh=mesh,
        in_specs=placed,
        out_specs=(P(None, ("node", "feat")), P("feat", "node"), P(("node", "feat"), None)),
        check_vma=False,
    )
```

profile of v0, /device:TPU:2, one launch (start us, length us, event | category | flops | bytes accessed | tf_op | source)
XLA Modules:
  0.0 442.9 jit_solution(13064534037003442033)
XLA Ops:
  7.2 2.5 copy.61
  9.7 8.6 %all-to-all-start = ((bf16[64,16,512]{2,0,1:T(8,128)(2,1)}), bf16[64,16,512]{2,0,1:T(8,128)(2,1)}, u32[]{:S(2)}, u32[]{:S(2)}) async-start(bf16[64,16,512]{2,0,1:T(8,128)(2,1)} %bitcast.59), calls=%async_computation | async-start | bytes 2097152 | tf_op jit(solution)/shard_map/all_to_all | solution.py:45
  18.3 3.5 collective-permute-start
  21.8 4.5 %collective-permute-start.1 = (bf16[64,8192]{1,0:T(8,128)(2,1)S(1)}, bf16[64,8192]{1,0:T(8,128)(2,1)}, u32[]{:S(2)}, u32[]{:S(2)}) collective-permute-start(bf16[64,8192]{1,0:T(8,128)(2,1)S(1)} %copy-done.2), channel_id=1, source_target_pairs={{16,0},{32,16},{48,32},{64,48},{80,64},{96,80},{112,96},{128,112},... | collective-permute-start | bytes 3145736 | tf_op jit(solution)/shard_map/ppermute | solution.py:17
  26.6 21.2 %collective-permute-done = bf16[64,8192]{1,0:T(8,128)(2,1)} collective-permute-done((bf16[64,8192]{1,0:T(8,128)(2,1)S(1)}, bf16[64,8192]{1,0:T(8,128)(2,1)}, u32[]{:S(2)}, u32[]{:S(2)}) %collective-permute-start) | collective-permute-done | bytes 1048608 | tf_op jit(solution)/shard_map/ppermute | solution.py:15
  48.9 3.2 copy_bitcast_fusion
  52.1 4.1 gather_fusion
  56.2 3.6 fusion.9
  60.5 1.4 convert_element_type.53
  61.9 2.8 copy.39
  64.7 7.0 %all-to-all-start.1 = ((bf16[64,16,512]{2,0,1:T(8,128)(2,1)}), bf16[64,16,512]{2,0,1:T(8,128)(2,1)S(1)}, u32[]{:S(2)}, u32[]{:S(2)}) async-start(bf16[64,16,512]{2,0,1:T(8,128)(2,1)} %copy.39), calls=%async_computation.1 | async-start | bytes 2097152 | tf_op jit(solution)/shard_map/all_to_all | solution.py:46
  71.7 4.4 %fusion.14 = f32[1024,512]{1,0:T(8,128)} fusion(bf16[1024,1024]{1,0:T(8,128)(2,1)} %param.11, bf16[1024,512]{1,0:T(8,128)(2,1)} %bitcast.1), kind=kOutput, calls=%fused_computation.34 | convolution fusion | flops 1073741824 | bytes 5242880 | tf_op jit(solution)/shard_map/dot_general | solution.py:48
  76.1 22.2 %all-to-all-done.1 = bf16[64,16,512]{2,0,1:T(8,128)(2,1)S(1)} async-done(((bf16[64,16,512]{2,0,1:T(8,128)(2,1)}), bf16[64,16,512]{2,0,1:T(8,128)(2,1)S(1)}, u32[]{:S(2)}, u32[]{:S(2)}) %all-to-all-start.1) | async-done | bytes 1048608 | tf_op jit(solution)/shard_map/all_to_all | solution.py:46
  98.4 5.3 %multiply_convert_fusion = (bf16[1024,512]{1,0:T(8,128)(2,1)S(1)}, bf16[1024,512]{1,0:T(8,128)(2,1)}) fusion(bf16[1024,512]{1,0:T(8,128)(2,1)} %param.13, f32[1024,512]{1,0:T(8,128)} %fusion.14, bf16[1024,1024]{1,0:T(8,128)(2,1)S(1)} %copy-done, bf16[1024,512]{1,0:T(8,128)(2,1)S(1)} %bitcast.66), kind=kOutput, calls=%fused_computation.15 | convolution fusion | flops 1080557568 | bytes 8388608 | tf_op jit(solution)/shard_map/dot_general | solution.py:48
  105.9 1.3 copy.43
  107.3 4.9 %all-to-all-start.3 = ((bf16[16,64,512]{2,1,0:T(8,128)(2,1)}), bf16[16,64,512]{2,1,0:T(8,128)(2,1)S(1)}, u32[]{:S(2)}, u32[]{:S(2)}) async-start(bf16[16,64,512]{2,1,0:T(8,128)(2,1)} %bitcast.14), calls=%async_computation.3 | async-start | bytes 2097152 | tf_op jit(solution)/shard_map/all_to_all | solution.py:66
  112.2 2.9 fusion.7
  115.1 1.3 copy.41
  116.4 22.5 %all-to-all-done.3 = bf16[16,64,512]{2,1,0:T(8,128)(2,1)S(1)} async-done(((bf16[16,64,512]{2,1,0:T(8,128)(2,1)}), bf16[16,64,512]{2,1,0:T(8,128)(2,1)S(1)}, u32[]{:S(2)}, u32[]{:S(2)}) %all-to-all-start.3) | async-done | bytes 1048608 | tf_op jit(solution)/shard_map/all_to_all | solution.py:66
  138.9 4.8 %all-to-all-start.2 = ((bf16[16,64,512]{2,1,0:T(8,128)(2,1)}), bf16[16,64,512]{2,1,0:T(8,128)(2,1)S(1)}, u32[]{:S(2)}, u32[]{:S(2)}) async-start(bf16[16,64,512]{2,1,0:T(8,128)(2,1)} %bitcast.11), calls=%async_computation.2 | async-start | bytes 2097152 | tf_op jit(solution)/shard_map/all_to_all | solution.py:65
  143.9 4.5 %fusion.15 = f32[1024,1024]{1,0:T(8,128)} fusion(bf16[1024,512]{1,0:T(8,128)(2,1)S(1)} %copy-done.5, bf16[1024,512]{1,0:T(8,128)(2,1)} %bitcast.67), kind=kOutput, calls=%fused_computation.35 | convolution fusion | flops 1073741824 | bytes 6291456 | tf_op jit(solution)/shard_map/dot_general | solution.py:55
  149.7 5.7 %fusion = f32[64,2,128,64]{2,3,1,0:T(8,128)} fusion(bf16[64,2,128,128]{3,2,1,0:T(8,128)(2,1)} %param.8, pred[64,2]{1,0:T(8,128)(4,1)S(1)} %iota_compare_fusion, bf16[64,64,128,1]{2,1,0,3:T(8,128)(2,1)S(1)} %bitcast.64), kind=kOutput, calls=%fused_computation.3 | convolution fusion | flops 270532608 | bytes 9437312 | tf_op jit(solution)/shard_map/fbi,bkji->fbkj/dot_general | solution.py:69
  155.5 3.5 broadcast_in_dim.24
  158.9 20.3 %scatter_fusion = f32[64,192,128]{2,0,1:T(8,128)} fusion(f32[64,192,128]{2,0,1:T(8,128)} %broadcast_in_dim.24, s32[128]{0:T(128)S(1)} %reshape.60, f32[128,64,128]{2,1,0:T(8,128)} %bitcast.60), kind=kCustom, calls=%fused_computation.1 | custom fusion | flops 1048576 | bytes 12583424 | tf_op jit(solution)/shard_map/scatter-add | solution.py:71
  179.3 3.6 convert.6
  182.9 1.5 fusion.13
  184.4 6.8 %collective-permute-start.2 = (bf16[64,64,128]{2,0,1:T(8,128)(2,1)}, bf16[64,64,128]{2,0,1:T(8,128)(2,1)}, u32[]{:S(2)}, u32[]{:S(2)}) collective-permute-start(bf16[64,64,128]{2,0,1:T(8,128)(2,1)} %get-tuple-element.3), channel_id=1, source_target_pairs={{16,0},{32,16},{48,32},{64,48},{80,64},{96,80},{112,96},{128,112},... | collective-permute-start | bytes 3145736 | tf_op jit(solution)/shard_map/ppermute | solution.py:27
  191.2 1.9 collective-permute-start.3
  193.5 1.5 copy.54
  195.0 235.3 %all-reduce.3.cloned.1.call-done = f32[1024,1024]{1,0:T(8,128)} async-done(((f32[1024,1024]{1,0:T(8,128)}), f32[1024,1024]{1,0:T(8,128)}) %all-reduce.3.cloned.1.call-update) | async-done | bytes 4194320
  430.4 1.4 constant_dynamic-slice_fusion
  431.7 4.3 fusion.2
  (35 shorter events, 6.1 us)
Async XLA Ops:
  7.2 91.2 %copy-start = (bf16[1024,1024]{1,0:T(8,128)(2,1)S(1)}, bf16[1024,1024]{1,0:T(8,128)(2,1)}, u32[]{:S(2)}) copy-start(bf16[1024,1024]{1,0:T(8,128)(2,1)} %param.12) | copy-start | bytes 6291460
  7.2 11.1 %copy-start.2 = (bf16[64,8192]{1,0:T(8,128)(2,1)S(1)}, bf16[64,8192]{1,0:T(8,128)(2,1)}, u32[]{:S(2)}) copy-start(bf16[64,8192]{1,0:T(8,128)(2,1)} %param.7) | copy-start | bytes 3145732
  7.2 19.1 %copy-start.7 = (s32[64,2]{0,1:T(2,128)S(1)}, s32[64,2]{0,1:T(2,128)}, u32[]{:S(2)}) copy-start(s32[64,2]{0,1:T(2,128)} %param.9) | copy-start | bytes 1540
  7.2 19.4 %copy-start.8 = (s32[64]{0:T(128)S(1)}, s32[64]{0:T(128)}, u32[]{:S(2)}) copy-start(s32[64]{0:T(128)} %param.10) | copy-start | bytes 772
  9.7 55.1 %all-to-all-start = ((bf16[64,16,512]{2,0,1:T(8,128)(2,1)}), bf16[64,16,512]{2,0,1:T(8,128)(2,1)}, u32[]{:S(2)}, u32[]{:S(2)}) async-start(bf16[64,16,512]{2,0,1:T(8,128)(2,1)} %bitcast.59), calls=%async_computation | async-start | bytes 2097152 | tf_op jit(solution)/shard_map/all_to_all | solution.py:45
  18.3 29.5 %collective-permute-start = (bf16[64,8192]{1,0:T(8,128)(2,1)S(1)}, bf16[64,8192]{1,0:T(8,128)(2,1)}, u32[]{:S(2)}, u32[]{:S(2)}) collective-permute-start(bf16[64,8192]{1,0:T(8,128)(2,1)S(1)} %copy-done.2), channel_id=1, source_target_pairs={{0,16},{16,32},{32,48},{48,64},{64,80},{80,96},{96,112},{112,128},... | collective-permute-start | bytes 3145736 | tf_op jit(solution)/shard_map/ppermute | solution.py:15
  21.8 27.1 %collective-permute-start.1 = (bf16[64,8192]{1,0:T(8,128)(2,1)S(1)}, bf16[64,8192]{1,0:T(8,128)(2,1)}, u32[]{:S(2)}, u32[]{:S(2)}) collective-permute-start(bf16[64,8192]{1,0:T(8,128)(2,1)S(1)} %copy-done.2), channel_id=1, source_target_pairs={{16,0},{32,16},{48,32},{64,48},{80,64},{96,80},{112,96},{128,112},... | collective-permute-start | bytes 3145736 | tf_op jit(solution)/shard_map/ppermute | solution.py:17
  64.7 33.6 %all-to-all-start.1 = ((bf16[64,16,512]{2,0,1:T(8,128)(2,1)}), bf16[64,16,512]{2,0,1:T(8,128)(2,1)S(1)}, u32[]{:S(2)}, u32[]{:S(2)}) async-start(bf16[64,16,512]{2,0,1:T(8,128)(2,1)} %copy.39), calls=%async_computation.1 | async-start | bytes 2097152 | tf_op jit(solution)/shard_map/all_to_all | solution.py:46
  98.4 5.3 %copy-start.6 = (bf16[64,16,512]{2,0,1:T(8,128)(2,1)}, bf16[64,16,512]{2,0,1:T(8,128)(2,1)S(1)}, u32[]{:S(2)}) copy-start(bf16[64,16,512]{2,0,1:T(8,128)(2,1)S(1)} %all-to-all-done.1) | copy-start | bytes 3145732
  103.7 1.0 copy-start.3
  107.3 4.9 %copy-start.4 = (bf16[1024,512]{1,0:T(8,128)(2,1)S(1)}, bf16[1024,512]{1,0:T(8,128)(2,1)}, u32[]{:S(2)}) copy-start(bf16[1024,512]{1,0:T(8,128)(2,1)} %copy-done.3) | copy-start | bytes 3145732
  107.3 31.6 %all-to-all-start.3 = ((bf16[16,64,512]{2,1,0:T(8,128)(2,1)}), bf16[16,64,512]{2,1,0:T(8,128)(2,1)S(1)}, u32[]{:S(2)}, u32[]{:S(2)}) async-start(bf16[16,64,512]{2,1,0:T(8,128)(2,1)} %bitcast.14), calls=%async_computation.3 | async-start | bytes 2097152 | tf_op jit(solution)/shard_map/all_to_all | solution.py:66
  116.4 27.5 %copy-start.5 = (bf16[1024,512]{1,0:T(8,128)(2,1)S(1)}, bf16[1024,512]{1,0:T(8,128)(2,1)}, u32[]{:S(2)}) copy-start(bf16[1024,512]{1,0:T(8,128)(2,1)} %copy-done.3) | copy-start | bytes 3145732
  138.9 54.3 %all-to-all-start.2 = ((bf16[16,64,512]{2,1,0:T(8,128)(2,1)}), bf16[16,64,512]{2,1,0:T(8,128)(2,1)S(1)}, u32[]{:S(2)}, u32[]{:S(2)}) async-start(bf16[16,64,512]{2,1,0:T(8,128)(2,1)} %bitcast.11), calls=%async_computation.2 | async-start | bytes 2097152 | tf_op jit(solution)/shard_map/all_to_all | solution.py:65
  143.7 286.7 %all-reduce.3.cloned.1.call-start = ((), (), s32[]{:S(2)}) async-start(), calls=%async_computation.4 | async-start | bytes 8388608
  184.4 247.3 %collective-permute-start.2 = (bf16[64,64,128]{2,0,1:T(8,128)(2,1)}, bf16[64,64,128]{2,0,1:T(8,128)(2,1)}, u32[]{:S(2)}, u32[]{:S(2)}) collective-permute-start(bf16[64,64,128]{2,0,1:T(8,128)(2,1)} %get-tuple-element.3), channel_id=1, source_target_pairs={{16,0},{32,16},{48,32},{64,48},{80,64},{96,80},{112,96},{128,112},... | collective-permute-start | bytes 3145736 | tf_op jit(solution)/shard_map/ppermute | solution.py:27
  191.2 240.5 %collective-permute-start.3 = (bf16[64,64,128]{2,0,1:T(8,128)(2,1)}, bf16[64,64,128]{2,0,1:T(8,128)(2,1)}, u32[]{:S(2)}, u32[]{:S(2)}) collective-permute-start(bf16[64,64,128]{2,0,1:T(8,128)(2,1)} %get-tuple-element.4), channel_id=1, source_target_pairs={{0,16},{16,32},{32,48},{48,64},{64,80},{80,96},{96,112},{112,128},... | collective-permute-start | bytes 3145736 | tf_op jit(solution)/shard_map/ppermute | solution.py:27
  431.7 4.3 copy-start.1
Sparse Core Ops, SparseCore 0:
  150.0 280.3 all-reduce.2
where the time goes:
time: 444 us; the launch traced here: 443 us
  waiting for transfers between devices  302 us (68%)
  starting transfers between devices  42.2 us (10%)
  other arithmetic  31.8 us (7%)
  matrix products  27.8 us (6%)
  local copies, waits for them, and re-layouts  24.5 us (6%)
  between operations  14.3 us (3%)
    unnamed x2, waiting for transfers between devices  235 us
    all_to_all x1, waiting for transfers between devices, local(): lax.all_to_all(dagg, 'feat', split_axis=0, concat_axis=1, tiled=True)  22.5 us
    all_to_all x1, waiting for transfers between devices, local(): lax.all_to_all(agg, 'feat', split_axis=1, concat_axis=0, tiled=True)  22.2 us
    ppermute x1, waiting for transfers between devices, extended(): lax.ppermute(tail, axis, [(i, (i + 1) % count) for i in range(ends)])  21.2 us
    scatter-add x1, other arithmetic, local(): jnp.zeros((feat_dev, 3 * block_count, tile), jnp.float32)  20.3 us
  transfers between devices with their start and end apart: 9, of which 5 were waited for; matrix products, arithmetic and copies ran while one was open for 15% of the time, Pallas kernels for 0%

commit v1 on v0

v1 whole, which is shorter than its diff:
```python
import functools

import jax
import jax.numpy as jnp
from jax import lax
from jax.experimental import pallas as pl
from jax.experimental.pallas import tpu as pltpu
from jax.sharding import PartitionSpec as P

F32 = jnp.float32
BF16 = jnp.bfloat16
NT = (((1,), (1,)), ((), ()))
NN = (((1,), (0,)), ((), ()))
MIB = 1 << 20


def dot(a, b, dims=NN):
    return lax.dot_general(a, b, dims, preferred_element_type=F32)


def params(mib):
    return pltpu.CompilerParams(
        dimension_semantics=("arbitrary",), vmem_limit_bytes=mib * MIB
    )


def split_kernel(x_ref, out_ref):
    out_ref[0] = x_ref[...]


def split_columns(x, groups):
    rows, columns = x.shape
    width = columns // groups
    return pl.pallas_call(
        split_kernel,
        grid=(groups,),
        in_specs=[pl.BlockSpec((rows, width), lambda g: (0, g))],
        out_specs=pl.BlockSpec((1, rows, width), lambda g: (g, 0, 0)),
        out_shape=jax.ShapeDtypeStruct((groups, rows, width), x.dtype),
        compiler_params=params(16),
    )(x)


def agg_kernel(col_ref, live_ref, before, own, after, tiles_ref, out_ref, window, sems):
    step = pl.program_id(0)
    span = own.shape[1]
    tile = tiles_ref.shape[-1]
    blocks = span // tile
    group = tiles_ref.shape[0]
    per = out_ref.shape[2] // tile

    @pl.when(step == 0)
    def _():
        copies = [
            pltpu.make_async_copy(part, window.at[:, i * span : (i + 1) * span], sems.at[i])
            for i, part in enumerate((before, own, after))
        ]
        for copy in copies:
            copy.start()
        for copy in copies:
            copy.wait()

    for b in range(group):
        r = step * group + b
        here = pl.multiple_of((blocks + r) * tile, tile)
        there = pl.multiple_of(col_ref[r] * tile, tile)
        first = dot(window[:, pl.ds(here, tile)], tiles_ref[b, 0])
        second = dot(window[:, pl.ds(there, tile)], tiles_ref[b, 1])
        total = first + jnp.where(live_ref[r] > 0, second, 0.0)
        out_ref[b // per, :, (b % per) * tile : (b % per + 1) * tile] = total.astype(BF16)


def aggregate(col, live, before, own, after, tiles, groups):
    rows, span = own.shape
    blocks, slots, tile, _ = tiles.shape
    width = span // groups
    per = width // tile
    group = 2 * per
    anywhere = pl.BlockSpec(memory_space=pl.ANY)
    smem = pl.BlockSpec(memory_space=pltpu.SMEM)
    return pl.pallas_call(
        agg_kernel,
        grid=(blocks // group,),
        in_specs=[smem, smem, anywhere, anywhere, anywhere]
        + [pl.BlockSpec((group, slots, tile, tile), lambda g: (g, 0, 0, 0))],
        out_specs=pl.BlockSpec((group // per, rows, width), lambda g: (g, 0, 0)),
        out_shape=jax.ShapeDtypeStruct((groups, rows, width), BF16),
        scratch_shapes=[pltpu.VMEM((rows, 3 * span), BF16), pltpu.SemaphoreType.DMA((3,))],
        compiler_params=params(24),
        cost_estimate=pl.CostEstimate(
            flops=4 * rows * span * tile, bytes_accessed=9 * MIB, transcendentals=0
        ),
    )(col, live, before, own, after, tiles)


def spread_kernel(col_ref, live_ref, dagg_ref, tiles_ref, before_ref, own_ref, after_ref, acc):
    step = pl.program_id(0)
    tile = tiles_ref.shape[-1]
    blocks = own_ref.shape[0]
    group = tiles_ref.shape[0]
    per = dagg_ref.shape[2] // tile

    @pl.when(step == 0)
    def _():
        def clear(i, carry):
            acc[i] = jnp.zeros(acc.shape[1:], F32)
            return carry

        lax.fori_loop(0, acc.shape[0], clear, 0, unroll=8)

    for b in range(group):
        r = step * group + b
        grad = dagg_ref[b // per, :, (b % per) * tile : (b % per + 1) * tile]
        first = dot(grad, tiles_ref[b, 0], NT)
        second = dot(grad, tiles_ref[b, 1], NT)
        acc[blocks + r] += first
        acc[col_ref[r]] += jnp.where(live_ref[r] > 0, second, 0.0)

    @pl.when(step == pl.num_programs(0) - 1)
    def _():
        def store(i, carry):
            before_ref[i] = acc[i].astype(BF16)
            own_ref[i] = acc[blocks + i]
            after_ref[i] = acc[2 * blocks + i].astype(BF16)
            return carry

        lax.fori_loop(0, blocks, store, 0, unroll=4)


def spread(col, live, dagg, tiles):
    groups, rows, width = dagg.shape
    blocks, slots, tile, _ = tiles.shape
    per = width // tile
    group = 2 * per
    smem = pl.BlockSpec(memory_space=pltpu.SMEM)
    whole = pl.BlockSpec((blocks, rows, tile), lambda g: (0, 0, 0))
    shape = (blocks, rows, tile)
    return pl.pallas_call(
        spread_kernel,
        grid=(blocks // group,),
        in_specs=[
            smem,
            smem,
            pl.BlockSpec((group // per, rows, width), lambda g: (g, 0, 0)),
            pl.BlockSpec((group, slots, tile, tile), lambda g: (g, 0, 0, 0)),
        ],
        out_specs=[whole, whole, whole],
        out_shape=[
            jax.ShapeDtypeStruct(shape, BF16),
            jax.ShapeDtypeStruct(shape, F32),
            jax.ShapeDtypeStruct(shape, BF16),
        ],
        scratch_shapes=[pltpu.VMEM((3 * blocks, rows, tile), F32)],
        compiler_params=params(32),
        cost_estimate=pl.CostEstimate(
            flops=4 * rows * blocks * tile * tile, bytes_accessed=9 * MIB, transcendentals=0
        ),
    )(col, live, dagg, tiles)


def dense_kernel(chunk, w_self, w_neigh, w_back, x_ref, agg_ref, cot_ref, hidden, dpre, dagg):
    size = w_self.shape[0]

    def forward(i, carry):
        rows = pl.ds(pl.multiple_of(i * chunk, chunk), chunk)
        pre = dot(w_self[rows, :], x_ref[...]) + dot(w_neigh[rows, :], agg_ref[...])
        sig = jax.nn.sigmoid(pre)
        hidden[rows, :] = (pre * sig).astype(BF16)
        slope = sig * (1.0 + pre * (1.0 - sig))
        dpre[rows, :] = (cot_ref[rows, :].astype(F32) * slope).astype(BF16)
        return carry

    lax.fori_loop(0, size // chunk, forward, 0)

    def backward(i, carry):
        rows = pl.ds(pl.multiple_of(i * chunk, chunk), chunk)
        dagg[rows, :] = dot(w_back[rows, :], dpre[...]).astype(BF16)
        return carry

    lax.fori_loop(0, size // chunk, backward, 0)


def dense(w_self, w_neigh, w_back, x_rows, agg_rows, cot):
    size, width = x_rows.shape
    vmem = pl.BlockSpec(memory_space=pltpu.VMEM)
    out = jax.ShapeDtypeStruct((size, width), BF16)
    return pl.pallas_call(
        functools.partial(dense_kernel, 256),
        in_specs=[vmem] * 6,
        out_specs=[vmem] * 3,
        out_shape=[out] * 3,
        compiler_params=pltpu.CompilerParams(vmem_limit_bytes=24 * MIB),
        cost_estimate=pl.CostEstimate(
            flops=6 * size * size * width, bytes_accessed=12 * MIB, transcendentals=size * width
        ),
    )(w_self, w_neigh, w_back, x_rows, agg_rows, cot)


def late_kernel(chunk, w_back, dpre, ordered, agg_ref, dself, grad):
    def step(i, carry):
        rows = pl.ds(pl.multiple_of(i * chunk, chunk), chunk)
        dself[rows, :] = dot(w_back[rows, :], dpre[...]).astype(BF16)
        return carry

    lax.fori_loop(0, dself.shape[0] // chunk, step, 0)

    def weight(i, carry):
        rows = pl.ds(pl.multiple_of(i * chunk, chunk), chunk)
        grad[rows, :] = dot(ordered[rows, :], agg_ref[...], NT).astype(BF16)
        return carry

    lax.fori_loop(0, grad.shape[0] // chunk, weight, 0)


def late(w_back, dpre, ordered, agg_rows):
    size, width = dpre.shape
    vmem = pl.BlockSpec(memory_space=pltpu.VMEM)
    return pl.pallas_call(
        functools.partial(late_kernel, 256),
        in_specs=[vmem] * 4,
        out_specs=[vmem] * 2,
        out_shape=[
            jax.ShapeDtypeStruct((size, width), BF16),
            jax.ShapeDtypeStruct((size, size), BF16),
        ],
        compiler_params=pltpu.CompilerParams(vmem_limit_bytes=24 * MIB),
        cost_estimate=pl.CostEstimate(
            flops=4 * size * size * width, bytes_accessed=7 * MIB, transcendentals=0
        ),
    )(w_back, dpre, ordered, agg_rows)


def final_kernel(own_ref, before_ref, after_ref, dself_ref, out_ref):
    tile = own_ref.shape[2]
    for b in range(own_ref.shape[0]):
        columns = slice(b * tile, (b + 1) * tile)
        total = own_ref[b] + before_ref[b].astype(F32) + after_ref[b].astype(F32)
        out_ref[:, columns] = (dself_ref[0, :, columns].astype(F32) + total).astype(BF16)


def finish(own, before, after, dself):
    groups, rows, width = dself.shape
    blocks, _, tile = own.shape
    per = width // tile
    part = pl.BlockSpec((per, rows, tile), lambda g: (g, 0, 0))
    return pl.pallas_call(
        final_kernel,
        grid=(groups,),
        in_specs=[part, part, part, pl.BlockSpec((1, rows, width), lambda g: (g, 0, 0))],
        out_specs=pl.BlockSpec((rows, width), lambda g: (0, g)),
        out_shape=jax.ShapeDtypeStruct((rows, groups * width), BF16),
        compiler_params=params(16),
    )(own, before, after, dself)


def shifted(value, axis, steps):
    count = lax.axis_size(axis)
    first, last = max(0, -steps), min(count, count - steps)
    return lax.ppermute(value, axis, [(source, source + steps) for source in range(first, last)])


def exchange(value, axis):
    return lax.all_to_all(value, axis, split_axis=0, concat_axis=0, tiled=True)


SIDE = 4
CORES = 2


def by_owner(rows):
    size, width = rows.shape
    rows = rows.reshape(SIDE, SIDE, -1, CORES, size // (256), width)
    return rows.transpose(3, 1, 0, 2, 4, 5).reshape(size, width)


def exchange_sum(value, axis, count, index, partner):
    pieces = value.reshape(count, -1, value.shape[-1])
    total = lax.dynamic_index_in_dim(pieces, index, 0, keepdims=False).astype(F32)
    for step in range(1, count):
        target = (index + step) % count
        piece = lax.dynamic_index_in_dim(pieces, target, 0, keepdims=False).astype(BF16)
        pairs = [(i, partner(i, step)) for i in range(lax.axis_size(axis))]
        total = total + lax.ppermute(piece, axis, pairs).astype(F32)
    return total


def summed_over_all(value):
    feat, node = lax.axis_index("feat"), lax.axis_index("node")
    value = exchange_sum(value, "feat", CORES, feat % CORES, lambda i, s: i ^ 1)
    y = lambda i, s: i // SIDE * SIDE + (i + s) % SIDE
    value = exchange_sum(value, "node", SIDE, node % SIDE, y)
    x = lambda i, s: (i + s * SIDE) % (SIDE * SIDE)
    value = exchange_sum(value, "node", SIDE, node // SIDE, x)
    groups = lax.axis_size("feat")
    same = [[z * CORES + c for z in range(groups // CORES)] for c in range(CORES)]
    return lax.psum_scatter(value, "feat", scatter_dimension=0, tiled=True, axis_index_groups=same)


def local(features, tile_values, tile_cols, tile_count, w_self, w_neigh, cotangent):
    feat_dev, node_dev = features.shape
    tile = tile_values.shape[-1]
    block_count = node_dev // tile
    groups = lax.axis_size("feat")
    size = w_self.shape[0]
    part = lax.axis_index("node")
    col = tile_cols[:, 1] - (part - 1) * block_count
    live = (tile_count > 1).astype(jnp.int32)

    before = shifted(features, "node", 1)
    after = shifted(features, "node", -1)
    x_rows = exchange(split_columns(features, groups), "feat").reshape(size, -1)
    agg = aggregate(col, live, before, features, after, tile_values, groups)
    agg_rows = exchange(agg, "feat").reshape(size, -1)
    hidden, dpre, dagg = dense(w_self, w_neigh, w_neigh.T, x_rows, agg_rows, cotangent)
    dagg_cols = exchange(dagg.reshape(groups, feat_dev, -1), "feat")
    dself, part_neigh = late(w_self.T, dpre, by_owner(dpre), agg_rows)
    dself_cols = exchange(dself.reshape(groups, feat_dev, -1), "feat")

    grad_w_neigh = summed_over_all(part_neigh)

    to_before, own, to_after = spread(col, live, dagg_cols, tile_values)
    from_after = shifted(to_before, "node", -1)
    from_before = shifted(to_after, "node", 1)
    grad_features = finish(own, from_before, from_after, dself_cols)
    return (hidden, grad_features, grad_w_neigh)


def solution(mesh):
    placed = (
        P("feat", "node"),
        P("node", None, None, None),
        P("node", None),
        P("node"),
        P(),
        P(),
        P(None, ("node", "feat")),
    )
    return jax.shard_map(
        local,
        mesh=mesh,
        in_specs=placed,
        out_specs=(P(None, ("node", "feat")), P("feat", "node"), P(("node", "feat"), None)),
        check_vma=False,
    )
```

time: 444 us -> 289 us (0.65)
  waiting for transfers between devices: 302 us -> 143 us
  Pallas kernels: 0 us -> 37.5 us
  matrix products: 27.8 us -> 0 us
  other arithmetic: 31.8 us -> 4.81 us
  starting transfers between devices: 42.2 us -> 52.7 us
  local copies, waits for them, and re-layouts: 24.5 us -> 34.5 us
    unnamed x2, waiting for transfers between devices: 235 us -> 69.4 us
    pallas_call x0 -> x6, Pallas kernels: none -> 37.5 us  [the longest x1 9.31 us: finish(): pl.pallas_call(final_kernel, grid=(groups,), in_specs=[part, part, part,...]
    dot_general x7 -> x0, matrix products: 27.8 us -> none  [the longest x1 5.74 us: local(): jnp.einsum('fbi,bkji->fbkj', dagg_blocks, masked, preferred_element_type=...]
    unnamed x19 -> x52, local copies, waits for them, and re-layouts: 2.38 us -> 26.1 us
    scatter-add x1 -> x0, other arithmetic: 20.3 us -> none  [local(): jnp.zeros((feat_dev, 3 * block_count, tile), jnp.float32)]
    ppermute x4 -> x11, waiting for transfers between devices: 22.3 us -> 42.3 us  [the longest x4 22.6 us: shifted(): lax.ppermute(value, axis, [(source, source + steps) for source in range(f...]
    all_to_all x4, waiting for transfers between devices: 44.7 us -> 31.1 us  [exchange(): return lax.all_to_all(value, axis, split_axis=0, concat_axis=0, tiled=True)]
    ppermute x4 -> x11, starting transfers between devices: 16.7 us -> 27.3 us  [the longest x4 16 us: shifted(): lax.ppermute(value, axis, [(source, source + steps) for source in range(f...]
  transfers between devices with their start and end apart: 9 -> 16, of which waited for: 5 -> 7; matrix products, arithmetic and copies ran while one was open for 15% -> 8% of each run, Pallas kernels for 0% -> 6%
where the time goes in v1:
time: 289 us; the launch traced here: 287 us
  waiting for transfers between devices  143 us (49%)
  starting transfers between devices  52.7 us (18%)
  Pallas kernels  37.5 us (13%)
  local copies, waits for them, and re-layouts  34.5 us (12%)
  between operations  15.2 us (5%)
  other arithmetic  4.81 us (2%)
    unnamed x2, waiting for transfers between devices  69.4 us
    all_to_all x4, waiting for transfers between devices, exchange(): return lax.all_to_all(value, axis, split_axis=0, concat_axis=0, tiled=True)  31.1 us
    unnamed x52, local copies, waits for them, and re-layouts  26.1 us
    all_to_all x4, starting transfers between devices, exchange(): return lax.all_to_all(value, axis, split_axis=0, concat_axis=0, tiled=True)  25.3 us
    ppermute x4, waiting for transfers between devices, shifted(): lax.ppermute(value, axis, [(source, source + steps) for source in range(f...  22.6 us
    ppermute x7, waiting for transfers between devices, exchange_sum(): total = total + lax.ppermute(piece, axis, pairs).astype(F32)  19.7 us
    ppermute x4, starting transfers between devices, shifted(): lax.ppermute(value, axis, [(source, source + steps) for source in range(f...  16 us
    ppermute x7, starting transfers between devices, exchange_sum(): total = total + lax.ppermute(piece, axis, pairs).astype(F32)  11.3 us
  transfers between devices with their start and end apart: 16, of which 7 were waited for; matrix products, arithmetic and copies ran while one was open for 8% of the time, Pallas kernels for 6%

profile of v1, /device:TPU:2, one launch (start us, length us, event | category | flops | bytes accessed | tf_op | source)
XLA Modules:
  0.0 287.3 jit_solution(2456918547789175714)
XLA Ops:
  8.4 5.1 %shard_map.94 = bf16[16,64,512]{2,1,0:T(8,128)(2,1)} custom-call(bf16[64,8192]{1,0:T(8,128)(2,1)S(1)} %copy-done.2), custom_call_target="tpu_custom_call" | custom-call | tf_op jit(solution)/shard_map/pallas_call | solution.py:34
  13.5 8.6 %all-to-all-start = ((bf16[16,64,512]{2,1,0:T(8,128)(2,1)}), bf16[16,64,512]{2,1,0:T(8,128)(2,1)}, u32[]{:S(2)}, u32[]{:S(2)}) async-start(bf16[16,64,512]{2,1,0:T(8,128)(2,1)} %shard_map.94), calls=%async_computation | async-start | bytes 2097152 | tf_op jit(solution)/shard_map/all_to_all | solution.py:263
  22.2 3.5 %collective-permute-start = (bf16[64,8192]{1,0:T(8,128)(2,1)S(1)}, bf16[64,8192]{1,0:T(8,128)(2,1)S(1)}, u32[]{:S(2)}, u32[]{:S(2)}) collective-permute-start(bf16[64,8192]{1,0:T(8,128)(2,1)S(1)} %copy-done.3), channel_id=1, source_target_pairs={{0,16},{16,32},{32,48},{48,64},{64,80},{80,96},{96,112},{112,128},... | collective-permute-start | bytes 3145736 | tf_op jit(solution)/shard_map/ppermute | solution.py:259
  25.7 4.5 %collective-permute-start.1 = (bf16[64,8192]{1,0:T(8,128)(2,1)S(1)}, bf16[64,8192]{1,0:T(8,128)(2,1)S(1)}, u32[]{:S(2)}, u32[]{:S(2)}) collective-permute-start(bf16[64,8192]{1,0:T(8,128)(2,1)S(1)} %copy-done.3), channel_id=1, source_target_pairs={{16,0},{32,16},{48,32},{64,48},{80,64},{96,80},{112,96},{128,112},... | collective-permute-start | bytes 3145736 | tf_op jit(solution)/shard_map/ppermute | solution.py:259
  30.2 21.4 %collective-permute-done.before = bf16[64,8192]{1,0:T(8,128)(2,1)S(1)} collective-permute-done((bf16[64,8192]{1,0:T(8,128)(2,1)S(1)}, bf16[64,8192]{1,0:T(8,128)(2,1)S(1)}, u32[]{:S(2)}, u32[]{:S(2)}) %collective-permute-start) | collective-permute-done | bytes 1048608 | tf_op jit(solution)/shard_map/ppermute | solution.py:259
  52.8 2.2 copy-done
  55.0 4.9 %shard_map.95 = bf16[16,64,512]{2,1,0:T(8,128)(2,1)} custom-call(s32[64]{0:T(128)S(1)} %subtract_bitcast_fusion.col_ref, s32[64]{0:T(128)S(1)} %compare_convert_fusion.live_ref, bf16[64,8192]{1,0:T(8,128)(2,1)S(1)} %collective-permute-done.before, bf16[64,8192]{1,0:T(8,128)(2,1)S(1)} %copy-done.3, bf16[64,8192]{1,0:T(8,128)(2,1)S(1)} %collective-permute-done.1.after, ...), custom_call_target="tpu_custom_call" | custom-call | flops 268435456 | bytes 9437184 | tf_op jit(solution)/shard_map/pallas_call | solution.py:81
  59.9 7.1 %all-to-all-start.1 = ((bf16[16,64,512]{2,1,0:T(8,128)(2,1)}), bf16[16,64,512]{2,1,0:T(8,128)(2,1)S(1)}, u32[]{:S(2)}, u32[]{:S(2)}) async-start(bf16[16,64,512]{2,1,0:T(8,128)(2,1)} %shard_map.95), calls=%async_computation.1 | async-start | bytes 2097152 | tf_op jit(solution)/shard_map/all_to_all | solution.py:263
  67.0 2.6 copy.13
  69.6 24.0 %all-to-all-done.1 = bf16[16,64,512]{2,1,0:T(8,128)(2,1)S(1)} async-done(((bf16[16,64,512]{2,1,0:T(8,128)(2,1)}), bf16[16,64,512]{2,1,0:T(8,128)(2,1)S(1)}, u32[]{:S(2)}, u32[]{:S(2)}) %all-to-all-start.1) | async-done | bytes 1048608 | tf_op jit(solution)/shard_map/all_to_all | solution.py:263
  94.6 1.6 copy-done.8
  96.2 1.6 copy-done.10
  100.3 7.1 %shard_map.96 = (bf16[1024,512]{1,0:T(8,128)(2,1)}, bf16[1024,512]{1,0:T(8,128)(2,1)S(1)}, bf16[1024,512]{1,0:T(8,128)(2,1)S(1)}) custom-call(bf16[1024,1024]{1,0:T(8,128)(2,1)S(1)} %copy-done.8, bf16[1024,1024]{1,0:T(8,128)(2,1)S(1)} %copy-done.7, bf16[1024,1024]{1,0:T(8,128)(2,1)S(1)} %bitcast.47, bf16[1024,512]{1,0:T(8,128)(2,1)} %bitcast.1.x_ref, ...), custom_call_target="tpu_custom_call" | custom-call | flops 3221225472 | bytes 12582912 | tf_op jit(solution)/shard_map/pallas_call | solution.py:187
  109.3 4.8 %all-to-all-start.2 = ((bf16[16,64,512]{2,1,0:T(8,128)(2,1)}), bf16[16,64,512]{2,1,0:T(8,128)(2,1)S(1)}, u32[]{:S(2)}, u32[]{:S(2)}) async-start(bf16[16,64,512]{2,1,0:T(8,128)(2,1)} %bitcast.50), calls=%async_computation.2 | async-start | bytes 2097152 | tf_op jit(solution)/shard_map/all_to_all | solution.py:263
  114.1 4.1 %copy.14 = bf16[1024,1024]{0,1:T(8,128)(2,1)} copy(bf16[1024,1024]{1,0:T(8,128)(2,1)} %w_self.1) | data formatting | bytes 4194304 | tf_op args[4]
  119.3 2.9 copy.17
  122.2 2.2 reshape.47.ordered
  124.3 1.6 copy-done.9
  127.1 4.5 %shard_map.98 = (bf16[1024,512]{1,0:T(8,128)(2,1)}, bf16[1024,1024]{1,0:T(8,128)(2,1)S(1)}) custom-call(bf16[1024,1024]{1,0:T(8,128)(2,1)S(1)} %bitcast.46, bf16[1024,512]{1,0:T(8,128)(2,1)S(1)} %copy-done.16, bf16[1024,512]{1,0:T(8,128)(2,1)S(1)} %copy-done.17, bf16[1024,512]{1,0:T(8,128)(2,1)S(1)} %bitcast.49), custom_call_target="tpu_custom_call" | custom-call | flops 2147483648 | bytes 7340032 | tf_op jit(solution)/shard_map/pallas_call | solution.py:218
  133.7 7.0 %all-to-all-done.2.dagg_ref = bf16[16,64,512]{2,1,0:T(8,128)(2,1)S(1)} async-done(((bf16[16,64,512]{2,1,0:T(8,128)(2,1)}), bf16[16,64,512]{2,1,0:T(8,128)(2,1)S(1)}, u32[]{:S(2)}, u32[]{:S(2)}) %all-to-all-start.2) | async-done | bytes 1048608 | tf_op jit(solution)/shard_map/all_to_all | solution.py:263
  140.8 4.8 %all-to-all-start.3 = ((bf16[16,64,512]{2,1,0:T(8,128)(2,1)}), bf16[16,64,512]{2,1,0:T(8,128)(2,1)S(1)}, u32[]{:S(2)}, u32[]{:S(2)}) async-start(bf16[16,64,512]{2,1,0:T(8,128)(2,1)} %bitcast.7), calls=%async_computation.3 | async-start | bytes 2097152 | tf_op jit(solution)/shard_map/all_to_all | solution.py:263
  145.7 1.8 convert_add_fusion
  150.0 4.6 %collective-permute-start.6 = (bf16[128,1024]{1,0:T(8,128)(2,1)}, bf16[128,1024]{1,0:T(8,128)(2,1)}, u32[]{:S(2)}, u32[]{:S(2)}) collective-permute-start(bf16[128,1024]{1,0:T(8,128)(2,1)} %get-tuple-element.21), channel_id=1, source_target_pairs={{0,32},{16,48},{32,0},{48,16},{64,96},{80,112},{96,64},{112,80},{1... | collective-permute-start | bytes 786440 | tf_op jit(solution)/shard_map/ppermute | solution.py:283
  154.6 6.6 %shard_map.97 = (bf16[64,64,128]{2,1,0:T(8,128)(2,1)}, f32[64,64,128]{2,1,0:T(8,128)S(1)}, bf16[64,64,128]{2,1,0:T(8,128)(2,1)}) custom-call(s32[64]{0:T(128)S(1)} %subtract_bitcast_fusion.col_ref, s32[64]{0:T(128)S(1)} %compare_convert_fusion.live_ref, bf16[16,64,512]{2,1,0:T(8,128)(2,1)S(1)} %all-to-all-done.2.dagg_ref, bf16[64,2,128,128]{3,2,1,0:T(8,128)(2,1)S(1)} %copy-done.1), custom_call_target="tpu_custom_call" | custom-call | flops 268435456 | bytes 9437184 | tf_op jit(solution)/shard_map/pallas_call | solution.py:138
  162.6 4.0 %collective-permute-start.2 = (bf16[64,64,128]{2,1,0:T(8,128)(2,1)}, bf16[64,64,128]{2,1,0:T(8,128)(2,1)}, u32[]{:S(2)}, u32[]{:S(2)}) collective-permute-start(bf16[64,64,128]{2,1,0:T(8,128)(2,1)} %get-tuple-element.14), channel_id=1, source_target_pairs={{0,16},{16,32},{32,48},{48,64},{64,80},{80,96},{96,112},{112,128},... | collective-permute-start | bytes 3145736 | tf_op jit(solution)/shard_map/ppermute | solution.py:259
  166.6 4.0 %collective-permute-start.3 = (bf16[64,64,128]{2,1,0:T(8,128)(2,1)}, bf16[64,64,128]{2,1,0:T(8,128)(2,1)}, u32[]{:S(2)}, u32[]{:S(2)}) collective-permute-start(bf16[64,64,128]{2,1,0:T(8,128)(2,1)} %get-tuple-element.15), channel_id=1, source_target_pairs={{16,0},{32,16},{48,32},{64,48},{80,64},{96,80},{112,96},{128,112},... | collective-permute-start | bytes 3145736 | tf_op jit(solution)/shard_map/ppermute | solution.py:259
  173.1 2.0 collective-permute-start.8
  175.1 2.7 collective-permute-start.9
  177.8 19.0 %collective-permute-done.10 = bf16[32,1024]{1,0:T(8,128)(2,1)S(1)} collective-permute-done((bf16[32,1024]{1,0:T(8,128)(2,1)S(1)}, bf16[32,1024]{1,0:T(8,128)(2,1)S(1)}, u32[]{:S(2)}, u32[]{:S(2)}) %collective-permute-start.10) | collective-permute-done | bytes 65568 | tf_op jit(solution)/shard_map/ppermute | solution.py:283
  197.5 1.6 fusion.6
  200.4 69.4 %all-reduce.3.cloned.1.call-done = f32[32,1024]{1,0:T(8,128)} async-done(((f32[32,1024]{1,0:T(8,128)}), f32[32,1024]{1,0:T(8,128)}) %all-reduce.3.cloned.1.call-update) | async-done | bytes 131088
  271.2 9.3 %shard_map.99 = bf16[64,8192]{1,0:T(8,128)(2,1)} custom-call(f32[64,64,128]{2,1,0:T(8,128)S(1)} %copy-done.5, bf16[64,64,128]{2,1,0:T(8,128)(2,1)} %collective-permute-done.2.before_ref, bf16[64,64,128]{2,1,0:T(8,128)(2,1)} %collective-permute-done.3.after_ref, bf16[16,64,512]{2,1,0:T(8,128)(2,1)S(1)} %all-to-all-done.3.dself_ref), custom_call_target="tpu_custom_call" | custom-call | tf_op jit(solution)/shard_map/pallas_call | solution.py:246
  (70 shorter events, 21.2 us)
Async XLA Ops:
  8.4 13.8 %copy-start.3 = (bf16[64,8192]{1,0:T(8,128)(2,1)S(1)}, bf16[64,8192]{1,0:T(8,128)(2,1)}, u32[]{:S(2)}) copy-start(bf16[64,8192]{1,0:T(8,128)(2,1)} %own.1) | copy-start | bytes 3145732
  8.4 21.8 %copy-start.22 = (s32[64]{0:T(128)S(1)}, s32[64]{0:T(128)}, u32[]{:S(2)}) copy-start(s32[64]{0:T(128)} %param.10) | copy-start | bytes 772
  8.4 21.8 %copy-start.21 = (s32[64,2]{0,1:T(2,128)S(1)}, s32[64,2]{0,1:T(2,128)}, u32[]{:S(2)}) copy-start(s32[64,2]{0,1:T(2,128)} %param.9) | copy-start | bytes 1540
  13.5 46.4 %all-to-all-start = ((bf16[16,64,512]{2,1,0:T(8,128)(2,1)}), bf16[16,64,512]{2,1,0:T(8,128)(2,1)}, u32[]{:S(2)}, u32[]{:S(2)}) async-start(bf16[16,64,512]{2,1,0:T(8,128)(2,1)} %shard_map.94), calls=%async_computation | async-start | bytes 2097152 | tf_op jit(solution)/shard_map/all_to_all | solution.py:263
  22.2 29.4 %collective-permute-start = (bf16[64,8192]{1,0:T(8,128)(2,1)S(1)}, bf16[64,8192]{1,0:T(8,128)(2,1)S(1)}, u32[]{:S(2)}, u32[]{:S(2)}) collective-permute-start(bf16[64,8192]{1,0:T(8,128)(2,1)S(1)} %copy-done.3), channel_id=1, source_target_pairs={{0,16},{16,32},{32,48},{48,64},{64,80},{80,96},{96,112},{112,128},... | collective-permute-start | bytes 3145736 | tf_op jit(solution)/shard_map/ppermute | solution.py:259
  25.7 27.1 %collective-permute-start.1 = (bf16[64,8192]{1,0:T(8,128)(2,1)S(1)}, bf16[64,8192]{1,0:T(8,128)(2,1)S(1)}, u32[]{:S(2)}, u32[]{:S(2)}) collective-permute-start(bf16[64,8192]{1,0:T(8,128)(2,1)S(1)} %copy-done.3), channel_id=1, source_target_pairs={{16,0},{32,16},{48,32},{64,48},{80,64},{96,80},{112,96},{128,112},... | collective-permute-start | bytes 3145736 | tf_op jit(solution)/shard_map/ppermute | solution.py:259
  52.8 2.2 copy-start
  59.9 7.1 %copy-start.7 = (bf16[1024,1024]{1,0:T(8,128)(2,1)S(1)}, bf16[1024,1024]{1,0:T(8,128)(2,1)}, u32[]{:S(2)}) copy-start(bf16[1024,1024]{1,0:T(8,128)(2,1)} %w_neigh.1) | copy-start | bytes 6291460
  59.9 33.8 %all-to-all-start.1 = ((bf16[16,64,512]{2,1,0:T(8,128)(2,1)}), bf16[16,64,512]{2,1,0:T(8,128)(2,1)S(1)}, u32[]{:S(2)}, u32[]{:S(2)}) async-start(bf16[16,64,512]{2,1,0:T(8,128)(2,1)} %shard_map.95), calls=%async_computation.1 | async-start | bytes 2097152 | tf_op jit(solution)/shard_map/all_to_all | solution.py:263
  94.6 1.6 copy-start.8
  96.2 1.6 copy-start.10
  109.3 31.5 %all-to-all-start.2 = ((bf16[16,64,512]{2,1,0:T(8,128)(2,1)}), bf16[16,64,512]{2,1,0:T(8,128)(2,1)S(1)}, u32[]{:S(2)}, u32[]{:S(2)}) async-start(bf16[16,64,512]{2,1,0:T(8,128)(2,1)} %bitcast.50), calls=%async_computation.2 | async-start | bytes 2097152 | tf_op jit(solution)/shard_map/all_to_all | solution.py:263
  114.1 4.1 %copy-start.16 = (bf16[1024,512]{1,0:T(8,128)(2,1)S(1)}, bf16[1024,512]{1,0:T(8,128)(2,1)}, u32[]{:S(2)}) copy-start(bf16[1024,512]{1,0:T(8,128)(2,1)} %copy-done.15) | copy-start | bytes 3145732
  119.3 5.0 %copy-start.13 = (bf16[16,64,512]{2,1,0:T(8,128)(2,1)S(1)}, bf16[16,64,512]{2,1,0:T(8,128)(2,1)}, u32[]{:S(2)}) copy-start(bf16[16,64,512]{2,1,0:T(8,128)(2,1)} %copy-done.11) | copy-start | bytes 3145732
  124.3 1.6 copy-start.9
  131.6 1.7 copy-start.6
  133.3 12.4 %collective-permute-start.4 = (bf16[512,1024]{1,0:T(8,128)(2,1)}, bf16[512,1024]{1,0:T(8,128)(2,1)S(1)}, u32[]{:S(2)}, u32[]{:S(2)}) collective-permute-start(bf16[512,1024]{1,0:T(8,128)(2,1)} %dynamic-slice_bitcast_fusion), channel_id=1, source_target_pairs={{0,1},{1,0},{2,3},{3,2},{4,5},{5,4},{6,7},{7,6},{8,9},{9,8},{10,11... | collective-permute-start | bytes 3145736 | tf_op jit(solution)/shard_map/ppermute | solution.py:283
  140.8 130.4 %all-to-all-start.3 = ((bf16[16,64,512]{2,1,0:T(8,128)(2,1)}), bf16[16,64,512]{2,1,0:T(8,128)(2,1)S(1)}, u32[]{:S(2)}, u32[]{:S(2)}) async-start(bf16[16,64,512]{2,1,0:T(8,128)(2,1)} %bitcast.7), calls=%async_computation.3 | async-start | bytes 2097152 | tf_op jit(solution)/shard_map/all_to_all | solution.py:263
  145.5 124.2 %all-reduce.3.cloned.1.call-start = ((), (), s32[]{:S(2)}) async-start(), calls=%async_computation.4 | async-start | bytes 262144
  145.7 9.0 %copy-start.1 = (bf16[64,2,128,128]{3,2,1,0:T(8,128)(2,1)S(1)}, bf16[64,2,128,128]{3,2,1,0:T(8,128)(2,1)}, u32[]{:S(2)}) copy-start(bf16[64,2,128,128]{3,2,1,0:T(8,128)(2,1)} %tiles_ref.3) | copy-start | bytes 12582916
  147.5 7.2 %copy-start.19 = (f32[512,1024]{1,0:T(8,128)}, f32[512,1024]{1,0:T(8,128)S(1)}, u32[]{:S(2)}) copy-start(f32[512,1024]{1,0:T(8,128)S(1)} %convert_add_fusion) | copy-start | bytes 6291460
  148.5 22.2 %collective-permute-start.5 = (bf16[128,1024]{1,0:T(8,128)(2,1)}, bf16[128,1024]{1,0:T(8,128)(2,1)}, u32[]{:S(2)}, u32[]{:S(2)}) collective-permute-start(bf16[128,1024]{1,0:T(8,128)(2,1)} %get-tuple-element.19), channel_id=1, source_target_pairs={{0,16},{16,32},{32,48},{48,0},{64,80},{80,96},{96,112},{112,64},{1... | collective-permute-start | bytes 786440 | tf_op jit(solution)/shard_map/ppermute | solution.py:283
  150.0 20.7 %collective-permute-start.6 = (bf16[128,1024]{1,0:T(8,128)(2,1)}, bf16[128,1024]{1,0:T(8,128)(2,1)}, u32[]{:S(2)}, u32[]{:S(2)}) collective-permute-start(bf16[128,1024]{1,0:T(8,128)(2,1)} %get-tuple-element.21), channel_id=1, source_target_pairs={{0,32},{16,48},{32,0},{48,16},{64,96},{80,112},{96,64},{112,80},{1... | collective-permute-start | bytes 786440 | tf_op jit(solution)/shard_map/ppermute | solution.py:283
  154.6 16.1 %collective-permute-start.7 = (bf16[128,1024]{1,0:T(8,128)(2,1)S(1)}, bf16[128,1024]{1,0:T(8,128)(2,1)}, u32[]{:S(2)}, u32[]{:S(2)}) collective-permute-start(bf16[128,1024]{1,0:T(8,128)(2,1)S(1)} %get-tuple-element.20), channel_id=1, source_target_pairs={{0,48},{16,0},{32,16},{48,32},{64,112},{80,64},{96,80},{112,96},{1... | collective-permute-start | bytes 786440 | tf_op jit(solution)/shard_map/ppermute | solution.py:283
  161.2 1.3 copy-start.4
  162.6 36.6 %copy-start.23 = (u32[256]{0:T(256)S(1)}, u32[256]{0:T(256)}, u32[]{:S(2)}) copy-start(u32[256]{0:T(256)} %constant.103) | copy-start | bytes 3076
  162.6 108.6 %copy-start.5 = (f32[64,64,128]{2,1,0:T(8,128)S(1)}, f32[64,64,128]{2,1,0:T(8,128)}, u32[]{:S(2)}) copy-start(f32[64,64,128]{2,1,0:T(8,128)} %copy-done.4) | copy-start | bytes 6291460
  162.6 108.6 %collective-permute-start.2 = (bf16[64,64,128]{2,1,0:T(8,128)(2,1)}, bf16[64,64,128]{2,1,0:T(8,128)(2,1)}, u32[]{:S(2)}, u32[]{:S(2)}) collective-permute-start(bf16[64,64,128]{2,1,0:T(8,128)(2,1)} %get-tuple-element.14), channel_id=1, source_target_pairs={{0,16},{16,32},{32,48},{48,64},{64,80},{80,96},{96,112},{112,128},... | collective-permute-start | bytes 3145736 | tf_op jit(solution)/shard_map/ppermute | solution.py:259
  166.6 104.6 %collective-permute-start.3 = (bf16[64,64,128]{2,1,0:T(8,128)(2,1)}, bf16[64,64,128]{2,1,0:T(8,128)(2,1)}, u32[]{:S(2)}, u32[]{:S(2)}) collective-permute-start(bf16[64,64,128]{2,1,0:T(8,128)(2,1)} %get-tuple-element.15), channel_id=1, source_target_pairs={{16,0},{32,16},{48,32},{64,48},{80,64},{96,80},{112,96},{128,112},... | collective-permute-start | bytes 3145736 | tf_op jit(solution)/shard_map/ppermute | solution.py:259
  173.0 23.7 %collective-permute-start.10 = (bf16[32,1024]{1,0:T(8,128)(2,1)S(1)}, bf16[32,1024]{1,0:T(8,128)(2,1)S(1)}, u32[]{:S(2)}, u32[]{:S(2)}) collective-permute-start(bf16[32,1024]{1,0:T(8,128)(2,1)S(1)} %get-tuple-element.23), channel_id=1, source_target_pairs={{0,192},{16,208},{32,224},{48,240},{64,0},{80,16},{96,32},{112,48}... | collective-permute-start | bytes 196616 | tf_op jit(solution)/shard_map/ppermute | solution.py:283
  173.1 23.7 %collective-permute-start.8 = (bf16[32,1024]{1,0:T(8,128)(2,1)S(1)}, bf16[32,1024]{1,0:T(8,128)(2,1)S(1)}, u32[]{:S(2)}, u32[]{:S(2)}) collective-permute-start(bf16[32,1024]{1,0:T(8,128)(2,1)S(1)} %get-tuple-element.22), channel_id=1, source_target_pairs={{0,64},{16,80},{32,96},{48,112},{64,128},{80,144},{96,160},{112,17... | collective-permute-start | bytes 196616 | tf_op jit(solution)/shard_map/ppermute | solution.py:283
  175.1 22.3 %collective-permute-start.9 = (bf16[32,1024]{1,0:T(8,128)(2,1)S(1)}, bf16[32,1024]{1,0:T(8,128)(2,1)S(1)}, u32[]{:S(2)}, u32[]{:S(2)}) collective-permute-start(bf16[32,1024]{1,0:T(8,128)(2,1)S(1)} %get-tuple-element.24), channel_id=1, source_target_pairs={{0,128},{16,144},{32,160},{48,176},{64,192},{80,208},{96,224},{112... | collective-permute-start | bytes 196616 | tf_op jit(solution)/shard_map/ppermute | solution.py:283
  (8 other events, 8.6 us)
Sparse Core Ops, SparseCore 0:
  199.2 70.4 all-reduce.2

commit v2 on v1

--- a/solution.py
+++ b/solution.py
@@ -25,19 +25,22 @@
 
 
 def split_kernel(x_ref, out_ref):
-    out_ref[0] = x_ref[...]
+    width = out_ref.shape[2]
+    for g in range(out_ref.shape[0]):
+        out_ref[g] = x_ref[:, g * width : (g + 1) * width]
 
 
 def split_columns(x, groups):
     rows, columns = x.shape
     width = columns // groups
+    steps = 4
     return pl.pallas_call(
         split_kernel,
-        grid=(groups,),
-        in_specs=[pl.BlockSpec((rows, width), lambda g: (0, g))],
-        out_specs=pl.BlockSpec((1, rows, width), lambda g: (g, 0, 0)),
+        grid=(steps,),
+        in_specs=[pl.BlockSpec((rows, columns // steps), lambda g: (0, g))],
+        out_specs=pl.BlockSpec((groups // steps, rows, width), lambda g: (g, 0, 0)),
         out_shape=jax.ShapeDtypeStruct((groups, rows, width), x.dtype),
-        compiler_params=params(16),
+        compiler_params=params(56),
     )(x)
 
 
@@ -75,7 +78,7 @@
     blocks, slots, tile, _ = tiles.shape
     width = span // groups
     per = width // tile
-    group = 2 * per
+    group = 4 * per
     anywhere = pl.BlockSpec(memory_space=pl.ANY)
     smem = pl.BlockSpec(memory_space=pltpu.SMEM)
     return pl.pallas_call(
@@ -86,7 +89,7 @@
         out_specs=pl.BlockSpec((group // per, rows, width), lambda g: (g, 0, 0)),
         out_shape=jax.ShapeDtypeStruct((groups, rows, width), BF16),
         scratch_shapes=[pltpu.VMEM((rows, 3 * span), BF16), pltpu.SemaphoreType.DMA((3,))],
-        compiler_params=params(24),
+        compiler_params=params(56),
         cost_estimate=pl.CostEstimate(
             flops=4 * rows * span * tile, bytes_accessed=9 * MIB, transcendentals=0
         ),
@@ -131,7 +134,7 @@
     groups, rows, width = dagg.shape
     blocks, slots, tile, _ = tiles.shape
     per = width // tile
-    group = 2 * per
+    group = 4 * per
     smem = pl.BlockSpec(memory_space=pltpu.SMEM)
     whole = pl.BlockSpec((blocks, rows, tile), lambda g: (0, 0, 0))
     shape = (blocks, rows, tile)
@@ -151,49 +154,124 @@
             jax.ShapeDtypeStruct(shape, BF16),
         ],
         scratch_shapes=[pltpu.VMEM((3 * blocks, rows, tile), F32)],
-        compiler_params=params(32),
+        compiler_params=params(56),
         cost_estimate=pl.CostEstimate(
             flops=4 * rows * blocks * tile * tile, bytes_accessed=9 * MIB, transcendentals=0
         ),
     )(col, live, dagg, tiles)
 
 
-def dense_kernel(chunk, w_self, w_neigh, w_back, x_ref, agg_ref, cot_ref, hidden, dpre, dagg):
-    size = w_self.shape[0]
-
-    def forward(i, carry):
+def self_kernel(chunk, w_self, x_ref, out):
+    def step(i, carry):
         rows = pl.ds(pl.multiple_of(i * chunk, chunk), chunk)
-        pre = dot(w_self[rows, :], x_ref[...]) + dot(w_neigh[rows, :], agg_ref[...])
-        sig = jax.nn.sigmoid(pre)
-        hidden[rows, :] = (pre * sig).astype(BF16)
-        slope = sig * (1.0 + pre * (1.0 - sig))
-        dpre[rows, :] = (cot_ref[rows, :].astype(F32) * slope).astype(BF16)
+        out[rows, :] = dot(w_self[rows, :], x_ref[...])
         return carry
 
-    lax.fori_loop(0, size // chunk, forward, 0)
-
-    def backward(i, carry):
-        rows = pl.ds(pl.multiple_of(i * chunk, chunk), chunk)
-        dagg[rows, :] = dot(w_back[rows, :], dpre[...]).astype(BF16)
-        return carry
-
-    lax.fori_loop(0, size // chunk, backward, 0)
-
-
-def dense(w_self, w_neigh, w_back, x_rows, agg_rows, cot):
+    lax.fori_loop(0, out.shape[0] // chunk, step, 0)
+
+
+def self_product(w_self, x_rows):
     size, width = x_rows.shape
     vmem = pl.BlockSpec(memory_space=pltpu.VMEM)
+    return pl.pallas_call(
+        functools.partial(self_kernel, 256),
+        in_specs=[vmem] * 2,
+        out_specs=vmem,
+        out_shape=jax.ShapeDtypeStruct((size, width), F32),
+        compiler_params=pltpu.CompilerParams(vmem_limit_bytes=56 * MIB),
+        cost_estimate=pl.CostEstimate(
+            flops=2 * size * size * width, bytes_accessed=5 * MIB, transcendentals=0
+        ),
+    )(w_self, x_rows)
+
+
+def dense_kernel(
+    chunk,
+    w_neigh_hbm,
+    w_back_hbm,
+    pre_hbm,
+    agg_hbm,
+    cot_hbm,
+    hidden_hbm,
+    dpre_hbm,
+    dagg_hbm,
+    w_neigh,
+    w_back,
+    pre_ref,
+    agg_ref,
+    cot_ref,
+    hidden,
+    dpre,
+    dagg,
+    in_sems,
+    out_sems,
+):
+    steps = w_neigh.shape[0] // chunk
+    part = [slice(i * chunk, (i + 1) * chunk) for i in range(steps)]
+    whole = pltpu.make_async_copy(agg_hbm, agg_ref, in_sems.at[4, 0])
+    whole.start()
+    sources = ((w_neigh_hbm, w_neigh), (pre_hbm, pre_ref), (cot_hbm, cot_ref), (w_back_hbm, w_back))
+    loads = [
+        [
+            pltpu.make_async_copy(src.at[part[i]], dst.at[part[i]], in_sems.at[k, i])
+            for i in range(steps)
+        ]
+        for k, (src, dst) in enumerate(sources)
+    ]
+    for i in range(steps):
+        for k in range(3):
+            loads[k][i].start()
+    for i in range(steps):
+        loads[3][i].start()
+    whole.wait()
+    stores = []
+
+    def store(k, src, dst, i):
+        copy = pltpu.make_async_copy(src.at[part[i]], dst.at[part[i]], out_sems.at[k, i])
+        copy.start()
+        stores.append(copy)
+
+    for i in range(steps):
+        for k in range(3):
+            loads[k][i].wait()
+        pre = pre_ref[part[i], :] + dot(w_neigh[part[i], :], agg_ref[...])
+        sig = jax.nn.sigmoid(pre)
+        hidden[part[i], :] = (pre * sig).astype(BF16)
+        slope = sig * (1.0 + pre * (1.0 - sig))
+        dpre[part[i], :] = (cot_ref[part[i], :].astype(F32) * slope).astype(BF16)
+        store(0, hidden, hidden_hbm, i)
+        store(1, dpre, dpre_hbm, i)
+    for i in range(steps):
+        loads[3][i].wait()
+        dagg[part[i], :] = dot(w_back[part[i], :], dpre[...]).astype(BF16)
+        store(2, dagg, dagg_hbm, i)
+    for copy in stores:
+        copy.wait()
+
+
+def dense(w_neigh, w_back, pre_self, agg_rows, cot):
+    size, width = agg_rows.shape
+    chunk = 256
+    steps = size // chunk
+    anywhere = pl.BlockSpec(memory_space=pl.ANY)
     out = jax.ShapeDtypeStruct((size, width), BF16)
     return pl.pallas_call(
-        functools.partial(dense_kernel, 256),
-        in_specs=[vmem] * 6,
-        out_specs=[vmem] * 3,
+        functools.partial(dense_kernel, chunk),
+        in_specs=[anywhere] * 5,
+        out_specs=[anywhere] * 3,
         out_shape=[out] * 3,
-        compiler_params=pltpu.CompilerParams(vmem_limit_bytes=24 * MIB),
+        scratch_shapes=[
+            pltpu.VMEM((size, size), BF16),
+            pltpu.VMEM((size, size), BF16),
+            pltpu.VMEM((size, width), F32),
+        ]
+        + [pltpu.VMEM((size, width), BF16)] * 5
+        + [pltpu.SemaphoreType.DMA((5, steps)), pltpu.SemaphoreType.DMA((3, steps))],
+        compiler_params=pltpu.CompilerParams(vmem_limit_bytes=56 * MIB),
         cost_estimate=pl.CostEstimate(
-            flops=6 * size * size * width, bytes_accessed=12 * MIB, transcendentals=size * width
+            flops=4 * size * size * width, bytes_accessed=12 * MIB, transcendentals=size * width
         ),
-    )(w_self, w_neigh, w_back, x_rows, agg_rows, cot)
+    )(w_neigh, w_back, pre_self, agg_rows, cot)
 
 
 def late_kernel(chunk, w_back, dpre, ordered, agg_ref, dself, grad):
@@ -223,7 +301,7 @@
             jax.ShapeDtypeStruct((size, width), BF16),
             jax.ShapeDtypeStruct((size, size), BF16),
         ],
-        compiler_params=pltpu.CompilerParams(vmem_limit_bytes=24 * MIB),
+        compiler_params=pltpu.CompilerParams(vmem_limit_bytes=56 * MIB),
         cost_estimate=pl.CostEstimate(
             flops=4 * size * size * width, bytes_accessed=7 * MIB, transcendentals=0
         ),
@@ -232,24 +310,26 @@
 
 def final_kernel(own_ref, before_ref, after_ref, dself_ref, out_ref):
     tile = own_ref.shape[2]
+    per = dself_ref.shape[2] // tile
     for b in range(own_ref.shape[0]):
-        columns = slice(b * tile, (b + 1) * tile)
+        grad = dself_ref[b // per, :, (b % per) * tile : (b % per + 1) * tile]
         total = own_ref[b] + before_ref[b].astype(F32) + after_ref[b].astype(F32)
-        out_ref[:, columns] = (dself_ref[0, :, columns].astype(F32) + total).astype(BF16)
+        out_ref[:, b * tile : (b + 1) * tile] = (grad.astype(F32) + total).astype(BF16)
 
 
 def finish(own, before, after, dself):
     groups, rows, width = dself.shape
     blocks, _, tile = own.shape
-    per = width // tile
-    part = pl.BlockSpec((per, rows, tile), lambda g: (g, 0, 0))
+    steps = 4
+    part = pl.BlockSpec((blocks // steps, rows, tile), lambda g: (g, 0, 0))
     return pl.pallas_call(
         final_kernel,
-        grid=(groups,),
-        in_specs=[part, part, part, pl.BlockSpec((1, rows, width), lambda g: (g, 0, 0))],
-        out_specs=pl.BlockSpec((rows, width), lambda g: (0, g)),
+        grid=(steps,),
+        in_specs=[part, part, part]
+        + [pl.BlockSpec((groups // steps, rows, width), lambda g: (g, 0, 0))],
+        out_specs=pl.BlockSpec((rows, groups * width // steps), lambda g: (0, g)),
         out_shape=jax.ShapeDtypeStruct((rows, groups * width), BF16),
-        compiler_params=params(16),
+        compiler_params=params(56),
     )(own, before, after, dself)
 
 
@@ -269,16 +349,20 @@
 
 def by_owner(rows):
     size, width = rows.shape
-    rows = rows.reshape(SIDE, SIDE, -1, CORES, size // (256), width)
+    owners = lax.axis_size("node") * lax.axis_size("feat")
+    rows = rows.reshape(SIDE, SIDE, -1, CORES, size // owners, width)
     return rows.transpose(3, 1, 0, 2, 4, 5).reshape(size, width)
 
 
-def exchange_sum(value, axis, count, index, partner):
+def piece_at(pieces, index):
+    return lax.dynamic_index_in_dim(pieces, index, 0, keepdims=False)
+
+
+def exchange_sum(value, axis, count, index, partner, sent):
     pieces = value.reshape(count, -1, value.shape[-1])
-    total = lax.dynamic_index_in_dim(pieces, index, 0, keepdims=False).astype(F32)
+    total = piece_at(pieces, index).astype(F32)
     for step in range(1, count):
-        target = (index + step) % count
-        piece = lax.dynamic_index_in_dim(pieces, target, 0, keepdims=False).astype(BF16)
+        piece = piece_at(pieces, lax.rem(index + step, count)).astype(sent)
         pairs = [(i, partner(i, step)) for i in range(lax.axis_size(axis))]
         total = total + lax.ppermute(piece, axis, pairs).astype(F32)
     return total
@@ -286,14 +370,17 @@
 
 def summed_over_all(value):
     feat, node = lax.axis_index("feat"), lax.axis_index("node")
-    value = exchange_sum(value, "feat", CORES, feat % CORES, lambda i, s: i ^ 1)
+    value = exchange_sum(value, "feat", CORES, lax.rem(feat, CORES), lambda i, s: i ^ 1, BF16)
     y = lambda i, s: i // SIDE * SIDE + (i + s) % SIDE
-    value = exchange_sum(value, "node", SIDE, node % SIDE, y)
+    value = exchange_sum(value, "node", SIDE, lax.rem(node, SIDE), y, BF16)
     x = lambda i, s: (i + s * SIDE) % (SIDE * SIDE)
-    value = exchange_sum(value, "node", SIDE, node // SIDE, x)
-    groups = lax.axis_size("feat")
-    same = [[z * CORES + c for z in range(groups // CORES)] for c in range(CORES)]
-    return lax.psum_scatter(value, "feat", scatter_dimension=0, tiled=True, axis_index_groups=same)
+    value = exchange_sum(value, "node", SIDE, lax.div(node, SIDE), x, BF16)
+    half = lax.axis_size("feat") // 2
+    while half >= CORES:
+        flip = lambda i, s, half=half: i ^ half
+        value = exchange_sum(value, "feat", 2, lax.rem(lax.div(feat, half), 2), flip, F32)
+        half //= 2
+    return value
 
 
 def local(features, tile_values, tile_cols, tile_count, w_self, w_neigh, cotangent):
@@ -311,7 +398,8 @@
     x_rows = exchange(split_columns(features, groups), "feat").reshape(size, -1)
     agg = aggregate(col, live, before, features, after, tile_values, groups)
     agg_rows = exchange(agg, "feat").reshape(size, -1)
-    hidden, dpre, dagg = dense(w_self, w_neigh, w_neigh.T, x_rows, agg_rows, cotangent)
+    pre_self = self_product(w_self, x_rows)
+    hidden, dpre, dagg = dense(w_neigh, w_neigh.T, pre_self, agg_rows, cotangent)
     dagg_cols = exchange(dagg.reshape(groups, feat_dev, -1), "feat")
     dself, part_neigh = late(w_self.T, dpre, by_owner(dpre), agg_rows)
     dself_cols = exchange(dself.reshape(groups, feat_dev, -1), "feat")

time: 289 us -> 191 us (0.66)
  waiting for transfers between devices: 143 us -> 63.6 us
  local copies, waits for them, and re-layouts: 34.5 us -> 12.6 us
  between operations: 15.2 us -> 0.96 us
  starting transfers between devices: 52.7 us -> 63.5 us
  Pallas kernels: 37.5 us -> 41.6 us
    unnamed x2 -> x0, waiting for transfers between devices: 69.4 us -> none
    unnamed x52 -> x22, local copies, waits for them, and re-layouts: 26.1 us -> 6.18 us
    all_to_all x4, waiting for transfers between devices: 31.1 us -> 19.4 us  [exchange(): return lax.all_to_all(value, axis, split_axis=0, concat_axis=0, tiled=True)]
    ppermute x7 -> x10, starting transfers between devices: 11.3 us -> 19.8 us  [exchange_sum(): total = total + lax.ppermute(piece, axis, pairs).astype(F32)]
    pallas_call x1, Pallas kernels: 4.48 us -> 7.46 us  [late(): pl.pallas_call(functools.partial(late_kernel, 256), in_specs=[vmem] * 4,...]
    pallas_call x3 -> x4, Pallas kernels: 21.5 us -> 19.2 us  [the longest x1 6.59 us: dense(): pl.pallas_call(functools.partial(dense_kernel, chunk), in_specs=[anywhere...]
    ppermute x7 -> x10, waiting for transfers between devices: 19.7 us -> 19.8 us  [exchange_sum(): total = total + lax.ppermute(piece, axis, pairs).astype(F32)]
  transfers between devices with their start and end apart: 16 -> 18, of which waited for: 7 -> 14; matrix products, arithmetic and copies ran while one was open for 8% -> 10% of each run, Pallas kernels for 6% -> 14%
where the time goes in v2:
time: 191 us; the launch traced here: 189 us
  waiting for transfers between devices  63.6 us (33%)
  starting transfers between devices  63.5 us (33%)
  Pallas kernels  41.6 us (22%)
  local copies, waits for them, and re-layouts  12.6 us (7%)
  other arithmetic  6.52 us (3%)
    all_to_all x4, starting transfers between devices, exchange(): return lax.all_to_all(value, axis, split_axis=0, concat_axis=0, tiled=True)  27.8 us
    ppermute x4, waiting for transfers between devices, shifted(): lax.ppermute(value, axis, [(source, source + steps) for source in range(f...  24.4 us
    ppermute x10, starting transfers between devices, exchange_sum(): total = total + lax.ppermute(piece, axis, pairs).astype(F32)  19.8 us
    ppermute x10, waiting for transfers between devices, exchange_sum(): total = total + lax.ppermute(piece, axis, pairs).astype(F32)  19.8 us
    all_to_all x4, waiting for transfers between devices, exchange(): return lax.all_to_all(value, axis, split_axis=0, concat_axis=0, tiled=True)  19.4 us
    ppermute x4, starting transfers between devices, shifted(): lax.ppermute(value, axis, [(source, source + steps) for source in range(f...  15.9 us
    pallas_call x1, Pallas kernels, spread(): pl.pallas_call(spread_kernel, grid=(blocks // group,), in_specs=[smem, sm...  8.13 us
    pallas_call x1, Pallas kernels, late(): pl.pallas_call(functools.partial(late_kernel, 256), in_specs=[vmem] * 4,...  7.46 us
  transfers between devices with their start and end apart: 18, of which 14 were waited for; matrix products, arithmetic and copies ran while one was open for 10% of the time, Pallas kernels for 14%

profile of v2, /device:TPU:2, one launch (start us, length us, event | category | flops | bytes accessed | tf_op | source)
XLA Modules:
  0.0 188.9 jit_solution(11974326233257280611)
XLA Ops:
  0.7 3.4 %shard_map.94 = bf16[16,64,512]{2,1,0:T(8,128)(2,1)} custom-call(bf16[64,8192]{1,0:T(8,128)(2,1)} %own.1), custom_call_target="tpu_custom_call" | custom-call | tf_op jit(solution)/shard_map/pallas_call | solution.py:37
  4.1 8.6 %all-to-all-start = ((bf16[16,64,512]{2,1,0:T(8,128)(2,1)}), bf16[16,64,512]{2,1,0:T(8,128)(2,1)S(1)}, u32[]{:S(2)}, u32[]{:S(2)}) async-start(bf16[16,64,512]{2,1,0:T(8,128)(2,1)} %shard_map.94), calls=%async_computation | async-start | bytes 2097152 | tf_op jit(solution)/shard_map/all_to_all | solution.py:343
  12.7 3.5 %collective-permute-start = (bf16[64,8192]{1,0:T(8,128)(2,1)S(1)}, bf16[64,8192]{1,0:T(8,128)(2,1)S(1)}, u32[]{:S(2)}, u32[]{:S(2)}) collective-permute-start(bf16[64,8192]{1,0:T(8,128)(2,1)S(1)} %copy-done.2), channel_id=1, source_target_pairs={{0,16},{16,32},{32,48},{48,64},{64,80},{80,96},{96,112},{112,128},... | collective-permute-start | bytes 3145736 | tf_op jit(solution)/shard_map/ppermute | solution.py:339
  16.2 4.5 %collective-permute-start.1 = (bf16[64,8192]{1,0:T(8,128)(2,1)S(1)}, bf16[64,8192]{1,0:T(8,128)(2,1)}, u32[]{:S(2)}, u32[]{:S(2)}) collective-permute-start(bf16[64,8192]{1,0:T(8,128)(2,1)S(1)} %copy-done.2), channel_id=1, source_target_pairs={{16,0},{32,16},{48,32},{64,48},{80,64},{96,80},{112,96},{128,112},... | collective-permute-start | bytes 3145736 | tf_op jit(solution)/shard_map/ppermute | solution.py:339
  21.7 20.5 %collective-permute-done.before = bf16[64,8192]{1,0:T(8,128)(2,1)S(1)} collective-permute-done((bf16[64,8192]{1,0:T(8,128)(2,1)S(1)}, bf16[64,8192]{1,0:T(8,128)(2,1)S(1)}, u32[]{:S(2)}, u32[]{:S(2)}) %collective-permute-start) | collective-permute-done | bytes 1048608 | tf_op jit(solution)/shard_map/ppermute | solution.py:339
  43.4 6.8 %shard_map.96 = bf16[16,64,512]{2,1,0:T(8,128)(2,1)} custom-call(s32[64]{0:T(128)} %subtract_bitcast_fusion.col_ref, s32[64]{0:T(128)} %compare_convert_fusion.live_ref, bf16[64,8192]{1,0:T(8,128)(2,1)} %copy-done.5, bf16[64,8192]{1,0:T(8,128)(2,1)} %own.1, bf16[64,8192]{1,0:T(8,128)(2,1)} %collective-permute-done.1.after, bf16[64,2,128,128]{3,2,1,0:T(8,128)(2,1)} %tiles_ref.3), custom_call_target="tpu_custom_call" | custom-call | flops 268435456 | bytes 9437184 | tf_op jit(solution)/shard_map/pallas_call | solution.py:84
  50.2 7.3 %all-to-all-start.1 = ((bf16[16,64,512]{2,1,0:T(8,128)(2,1)}), bf16[16,64,512]{2,1,0:T(8,128)(2,1)}, u32[]{:S(2)}, u32[]{:S(2)}) async-start(bf16[16,64,512]{2,1,0:T(8,128)(2,1)} %shard_map.96), calls=%async_computation.1 | async-start | bytes 2097152 | tf_op jit(solution)/shard_map/all_to_all | solution.py:343
  57.5 2.6 %copy.10 = bf16[1024,1024]{0,1:T(8,128)(2,1)} copy(bf16[1024,1024]{1,0:T(8,128)(2,1)S(1)} %copy-done.1) | data formatting | bytes 4194304 | tf_op args[5]
  60.1 4.9 %shard_map.95.pre_hbm = f32[1024,512]{1,0:T(8,128)} custom-call(bf16[1024,1024]{1,0:T(8,128)(2,1)} %w_self.1, bf16[1024,512]{1,0:T(8,128)(2,1)} %bitcast.63), custom_call_target="tpu_custom_call" | custom-call | flops 1073741824 | bytes 5242880 | tf_op jit(solution)/shard_map/pallas_call | solution.py:176
  65.0 19.2 %all-to-all-done.1 = bf16[16,64,512]{2,1,0:T(8,128)(2,1)} async-done(((bf16[16,64,512]{2,1,0:T(8,128)(2,1)}), bf16[16,64,512]{2,1,0:T(8,128)(2,1)}, u32[]{:S(2)}, u32[]{:S(2)}) %all-to-all-start.1) | async-done | bytes 1048608 | tf_op jit(solution)/shard_map/all_to_all | solution.py:343
  84.2 6.6 %shard_map.97 = (bf16[1024,512]{1,0:T(8,128)(2,1)}, bf16[1024,512]{1,0:T(8,128)(2,1)}, bf16[1024,512]{1,0:T(8,128)(2,1)}) custom-call(bf16[1024,1024]{1,0:T(8,128)(2,1)} %w_neigh_hbm.1, bf16[1024,1024]{1,0:T(8,128)(2,1)} %bitcast.60, f32[1024,512]{1,0:T(8,128)} %shard_map.95.pre_hbm, bf16[1024,512]{1,0:T(8,128)(2,1)} %bitcast.3.agg_hbm.agg_ref, ...), custom_call_target="tpu_custom_call" | custom-call | flops 2147483648 | bytes 12582912 | tf_op jit(solution)/shard_map/pallas_call | solution.py:258
  90.8 4.9 %all-to-all-start.2 = ((bf16[16,64,512]{2,1,0:T(8,128)(2,1)}), bf16[16,64,512]{2,1,0:T(8,128)(2,1)S(1)}, u32[]{:S(2)}, u32[]{:S(2)}) async-start(bf16[16,64,512]{2,1,0:T(8,128)(2,1)} %bitcast.69), calls=%async_computation.2 | async-start | bytes 2097152 | tf_op jit(solution)/shard_map/all_to_all | solution.py:343
  95.8 2.6 %copy.11 = bf16[1024,1024]{0,1:T(8,128)(2,1)} copy(bf16[1024,1024]{1,0:T(8,128)(2,1)S(1)} %copy-done) | data formatting | bytes 4194304 | tf_op args[4]
  101.5 7.5 %shard_map.99 = (bf16[1024,512]{1,0:T(8,128)(2,1)}, bf16[1024,1024]{1,0:T(8,128)(2,1)}) custom-call(bf16[1024,1024]{1,0:T(8,128)(2,1)} %bitcast.67, bf16[1024,512]{1,0:T(8,128)(2,1)} %get-tuple-element.16.dpre, bf16[1024,512]{1,0:T(8,128)(2,1)} %reshape.56.ordered, bf16[1024,512]{1,0:T(8,128)(2,1)} %bitcast.3.agg_hbm.agg_ref), custom_call_target="tpu_custom_call" | custom-call | flops 2147483648 | bytes 7340032 | tf_op jit(solution)/shard_map/pallas_call | solution.py:296
  110.8 2.4 %collective-permute-done.4 = bf16[512,1024]{1,0:T(8,128)(2,1)} collective-permute-done((bf16[512,1024]{1,0:T(8,128)(2,1)S(1)}, bf16[512,1024]{1,0:T(8,128)(2,1)}, u32[]{:S(2)}, u32[]{:S(2)}) %collective-permute-start.4) | collective-permute-done | bytes 1048608 | tf_op jit(solution)/shard_map/ppermute | solution.py:367
  113.3 1.9 %convert_add_fusion = f32[512,1024]{1,0:T(8,128)S(1)} fusion(bf16[512,1024]{1,0:T(8,128)(2,1)} %collective-permute-done.4, bf16[2,512,1024]{2,1,0:T(8,128)(2,1)} %bitcast.66, s32[]{:T(128)S(6)} %select_n.54), kind=kLoop, calls=%fused_computation | loop fusion | flops 1572864 | bytes 4194308 | tf_op jit(solution)/shard_map/add | solution.py:367
  116.1 1.6 collective-permute-start.5
  117.7 4.6 %collective-permute-start.6 = (bf16[128,1024]{1,0:T(8,128)(2,1)}, bf16[128,1024]{1,0:T(8,128)(2,1)}, u32[]{:S(2)}, u32[]{:S(2)}) collective-permute-start(bf16[128,1024]{1,0:T(8,128)(2,1)} %get-tuple-element.21), channel_id=1, source_target_pairs={{0,32},{16,48},{32,0},{48,16},{64,96},{80,112},{96,64},{112,80},{1... | collective-permute-start | bytes 786440 | tf_op jit(solution)/shard_map/ppermute | solution.py:367
  122.4 7.0 %all-to-all-start.3 = ((bf16[16,64,512]{2,1,0:T(8,128)(2,1)}), bf16[16,64,512]{2,1,0:T(8,128)(2,1)}, u32[]{:S(2)}, u32[]{:S(2)}) async-start(bf16[16,64,512]{2,1,0:T(8,128)(2,1)} %bitcast.68), calls=%async_computation.3 | async-start | bytes 2097152 | tf_op jit(solution)/shard_map/all_to_all | solution.py:343
  129.6 5.2 %collective-permute-done.6 = bf16[128,1024]{1,0:T(8,128)(2,1)} collective-permute-done((bf16[128,1024]{1,0:T(8,128)(2,1)}, bf16[128,1024]{1,0:T(8,128)(2,1)}, u32[]{:S(2)}, u32[]{:S(2)}) %collective-permute-start.6) | collective-permute-done | bytes 262176 | tf_op jit(solution)/shard_map/ppermute | solution.py:367
  134.8 2.0 %fusion.1 = f32[128,1024]{1,0:T(8,128)} fusion(bf16[128,1024]{1,0:T(8,128)(2,1)} %collective-permute-done.7, bf16[128,1024]{1,0:T(8,128)(2,1)} %collective-permute-done.6, bf16[128,1024]{1,0:T(8,128)(2,1)} %collective-permute-done.5, f32[4,128,1024]{2,1,0:T(8,128)S(1)} %bitcast.62, s32[]{:T(128)S(6)} %select_n.56), kind=kLoop, calls=%fused_computation.5 | loop fusion | flops 786432 | bytes 1835012 | tf_op jit(solution)/shard_map/add | solution.py:367
  138.5 1.5 collective-permute-start.8
  142.7 3.0 %collective-permute-done.9 = bf16[32,1024]{1,0:T(8,128)(2,1)S(1)} collective-permute-done((bf16[32,1024]{1,0:T(8,128)(2,1)S(1)}, bf16[32,1024]{1,0:T(8,128)(2,1)S(1)}, u32[]{:S(2)}, u32[]{:S(2)}) %collective-permute-start.9) | collective-permute-done | bytes 65568 | tf_op jit(solution)/shard_map/ppermute | solution.py:367
  146.7 8.1 %shard_map.98 = (bf16[64,64,128]{2,1,0:T(8,128)(2,1)}, f32[64,64,128]{2,1,0:T(8,128)}, bf16[64,64,128]{2,1,0:T(8,128)(2,1)}) custom-call(s32[64]{0:T(128)} %subtract_bitcast_fusion.col_ref, s32[64]{0:T(128)} %compare_convert_fusion.live_ref, bf16[16,64,512]{2,1,0:T(8,128)(2,1)} %copy-done.4, bf16[64,2,128,128]{3,2,1,0:T(8,128)(2,1)} %tiles_ref.3), custom_call_target="tpu_custom_call" | custom-call | flops 268435456 | bytes 9437184 | tf_op jit(solution)/shard_map/pallas_call | solution.py:141
  154.8 1.9 %collective-permute-start.2 = (bf16[64,64,128]{2,1,0:T(8,128)(2,1)}, bf16[64,64,128]{2,1,0:T(8,128)(2,1)S(1)}, u32[]{:S(2)}, u32[]{:S(2)}) collective-permute-start(bf16[64,64,128]{2,1,0:T(8,128)(2,1)} %get-tuple-element.14), channel_id=1, source_target_pairs={{0,16},{16,32},{32,48},{48,64},{64,80},{80,96},{96,112},{112,128},... | collective-permute-start | bytes 3145736 | tf_op jit(solution)/shard_map/ppermute | solution.py:339
  156.7 6.0 %collective-permute-start.3 = (bf16[64,64,128]{2,1,0:T(8,128)(2,1)}, bf16[64,64,128]{2,1,0:T(8,128)(2,1)S(1)}, u32[]{:S(2)}, u32[]{:S(2)}) collective-permute-start(bf16[64,64,128]{2,1,0:T(8,128)(2,1)} %get-tuple-element.15), channel_id=1, source_target_pairs={{16,0},{32,16},{48,32},{64,48},{80,64},{96,80},{112,96},{128,112},... | collective-permute-start | bytes 3145736 | tf_op jit(solution)/shard_map/ppermute | solution.py:339
  162.8 5.6 %collective-permute-start.11 = (f32[16,1024]{1,0:T(8,128)S(1)}, f32[16,1024]{1,0:T(8,128)S(1)}, u32[]{:S(2)}, u32[]{:S(2)}) collective-permute-start(f32[16,1024]{1,0:T(8,128)S(1)} %dynamic-slice_bitcast_fusion.1), channel_id=1, source_target_pairs={{0,8},{1,9},{2,10},{3,11},{4,12},{5,13},{6,14},{7,15},{8,0},{9,1},... | collective-permute-start | bytes 196616 | tf_op jit(solution)/shard_map/ppermute | solution.py:367
  168.4 3.1 %collective-permute-done.11 = f32[16,1024]{1,0:T(8,128)S(1)} collective-permute-done((f32[16,1024]{1,0:T(8,128)S(1)}, f32[16,1024]{1,0:T(8,128)S(1)}, u32[]{:S(2)}, u32[]{:S(2)}) %collective-permute-start.11) | collective-permute-done | bytes 65568 | tf_op jit(solution)/shard_map/ppermute | solution.py:367
  171.5 2.9 %collective-permute-start.12 = (f32[8,1024]{1,0:T(8,128)S(1)}, f32[8,1024]{1,0:T(8,128)S(1)}, u32[]{:S(2)}, u32[]{:S(2)}) collective-permute-start(f32[8,1024]{1,0:T(8,128)S(1)} %dynamic-slice_bitcast_fusion.2), channel_id=1, source_target_pairs={{0,4},{1,5},{2,6},{3,7},{4,0},{5,1},{6,2},{7,3},{8,12},{9,13},{10,... | collective-permute-start | bytes 98312 | tf_op jit(solution)/shard_map/ppermute | solution.py:367
  174.5 2.0 %collective-permute-done.12 = f32[8,1024]{1,0:T(8,128)S(1)} collective-permute-done((f32[8,1024]{1,0:T(8,128)S(1)}, f32[8,1024]{1,0:T(8,128)S(1)}, u32[]{:S(2)}, u32[]{:S(2)}) %collective-permute-start.12) | collective-permute-done | bytes 32800 | tf_op jit(solution)/shard_map/ppermute | solution.py:367
  177.9 2.4 %collective-permute-done.13 = f32[4,1024]{1,0:T(4,128)S(1)} collective-permute-done((f32[4,1024]{1,0:T(4,128)S(1)}, f32[4,1024]{1,0:T(4,128)S(1)}, u32[]{:S(2)}, u32[]{:S(2)}) %collective-permute-start.13) | collective-permute-done | bytes 16416 | tf_op jit(solution)/shard_map/ppermute | solution.py:367
  184.6 4.3 %shard_map.100 = bf16[64,8192]{1,0:T(8,128)(2,1)} custom-call(f32[64,64,128]{2,1,0:T(8,128)} %get-tuple-element.13.own_ref, bf16[64,64,128]{2,1,0:T(8,128)(2,1)} %copy-done.6, bf16[64,64,128]{2,1,0:T(8,128)(2,1)} %copy-done.7, bf16[16,64,512]{2,1,0:T(8,128)(2,1)} %all-to-all-done.3.dself_ref), custom_call_target="tpu_custom_call" | custom-call | tf_op jit(solution)/shard_map/pallas_call | solution.py:325
  (51 shorter events, 19.4 us)
Async XLA Ops:
  0.6 12.1 %copy-start.2 = (bf16[64,8192]{1,0:T(8,128)(2,1)S(1)}, bf16[64,8192]{1,0:T(8,128)(2,1)}, u32[]{:S(2)}) copy-start(bf16[64,8192]{1,0:T(8,128)(2,1)} %own.1) | copy-start | bytes 3145732
  0.6 20.0 %copy-start.9 = (s32[64]{0:T(128)S(1)}, s32[64]{0:T(128)}, u32[]{:S(2)}) copy-start(s32[64]{0:T(128)} %param.10) | copy-start | bytes 772
  0.7 20.5 %copy-start.8 = (s32[64,2]{0,1:T(2,128)S(1)}, s32[64,2]{0,1:T(2,128)}, u32[]{:S(2)}) copy-start(s32[64,2]{0,1:T(2,128)} %param.9) | copy-start | bytes 1540
  4.1 46.1 %all-to-all-start = ((bf16[16,64,512]{2,1,0:T(8,128)(2,1)}), bf16[16,64,512]{2,1,0:T(8,128)(2,1)S(1)}, u32[]{:S(2)}, u32[]{:S(2)}) async-start(bf16[16,64,512]{2,1,0:T(8,128)(2,1)} %shard_map.94), calls=%async_computation | async-start | bytes 2097152 | tf_op jit(solution)/shard_map/all_to_all | solution.py:343
  12.7 29.5 %collective-permute-start = (bf16[64,8192]{1,0:T(8,128)(2,1)S(1)}, bf16[64,8192]{1,0:T(8,128)(2,1)S(1)}, u32[]{:S(2)}, u32[]{:S(2)}) collective-permute-start(bf16[64,8192]{1,0:T(8,128)(2,1)S(1)} %copy-done.2), channel_id=1, source_target_pairs={{0,16},{16,32},{32,48},{48,64},{64,80},{80,96},{96,112},{112,128},... | collective-permute-start | bytes 3145736 | tf_op jit(solution)/shard_map/ppermute | solution.py:339
  16.2 27.2 %collective-permute-start.1 = (bf16[64,8192]{1,0:T(8,128)(2,1)S(1)}, bf16[64,8192]{1,0:T(8,128)(2,1)}, u32[]{:S(2)}, u32[]{:S(2)}) collective-permute-start(bf16[64,8192]{1,0:T(8,128)(2,1)S(1)} %copy-done.2), channel_id=1, source_target_pairs={{16,0},{32,16},{48,32},{64,48},{80,64},{96,80},{112,96},{128,112},... | collective-permute-start | bytes 3145736 | tf_op jit(solution)/shard_map/ppermute | solution.py:339
  42.2 1.2 copy-start.5
  50.2 7.3 %copy-start.1 = (bf16[1024,1024]{1,0:T(8,128)(2,1)S(1)}, bf16[1024,1024]{1,0:T(8,128)(2,1)}, u32[]{:S(2)}) copy-start(bf16[1024,1024]{1,0:T(8,128)(2,1)} %w_neigh_hbm.1) | copy-start | bytes 6291460
  50.2 9.9 %copy-start.3 = (bf16[16,64,512]{2,1,0:T(8,128)(2,1)}, bf16[16,64,512]{2,1,0:T(8,128)(2,1)S(1)}, u32[]{:S(2)}) copy-start(bf16[16,64,512]{2,1,0:T(8,128)(2,1)S(1)} %all-to-all-done) | copy-start | bytes 3145732
  50.2 34.0 %all-to-all-start.1 = ((bf16[16,64,512]{2,1,0:T(8,128)(2,1)}), bf16[16,64,512]{2,1,0:T(8,128)(2,1)}, u32[]{:S(2)}, u32[]{:S(2)}) async-start(bf16[16,64,512]{2,1,0:T(8,128)(2,1)} %shard_map.96), calls=%async_computation.1 | async-start | bytes 2097152 | tf_op jit(solution)/shard_map/all_to_all | solution.py:343
  90.8 5.0 %copy-start = (bf16[1024,1024]{1,0:T(8,128)(2,1)S(1)}, bf16[1024,1024]{1,0:T(8,128)(2,1)}, u32[]{:S(2)}) copy-start(bf16[1024,1024]{1,0:T(8,128)(2,1)} %w_self.1) | copy-start | bytes 6291460
  90.8 31.6 %all-to-all-start.2 = ((bf16[16,64,512]{2,1,0:T(8,128)(2,1)}), bf16[16,64,512]{2,1,0:T(8,128)(2,1)S(1)}, u32[]{:S(2)}, u32[]{:S(2)}) async-start(bf16[16,64,512]{2,1,0:T(8,128)(2,1)} %bitcast.69), calls=%async_computation.2 | async-start | bytes 2097152 | tf_op jit(solution)/shard_map/all_to_all | solution.py:343
  110.3 2.9 %collective-permute-start.4 = (bf16[512,1024]{1,0:T(8,128)(2,1)S(1)}, bf16[512,1024]{1,0:T(8,128)(2,1)}, u32[]{:S(2)}, u32[]{:S(2)}) collective-permute-start(bf16[512,1024]{1,0:T(8,128)(2,1)S(1)} %dynamic-slice_bitcast_fusion), channel_id=1, source_target_pairs={{0,1},{1,0},{2,3},{3,2},{4,5},{5,4},{6,7},{7,6},{8,9},{9,8},{10,11... | collective-permute-start | bytes 3145736 | tf_op jit(solution)/shard_map/ppermute | solution.py:367
  116.1 13.4 %collective-permute-start.5 = (bf16[128,1024]{1,0:T(8,128)(2,1)}, bf16[128,1024]{1,0:T(8,128)(2,1)}, u32[]{:S(2)}, u32[]{:S(2)}) collective-permute-start(bf16[128,1024]{1,0:T(8,128)(2,1)} %get-tuple-element.19), channel_id=1, source_target_pairs={{0,16},{16,32},{32,48},{48,0},{64,80},{80,96},{96,112},{112,64},{1... | collective-permute-start | bytes 786440 | tf_op jit(solution)/shard_map/ppermute | solution.py:367
  117.7 17.1 %collective-permute-start.6 = (bf16[128,1024]{1,0:T(8,128)(2,1)}, bf16[128,1024]{1,0:T(8,128)(2,1)}, u32[]{:S(2)}, u32[]{:S(2)}) collective-permute-start(bf16[128,1024]{1,0:T(8,128)(2,1)} %get-tuple-element.21), channel_id=1, source_target_pairs={{0,32},{16,48},{32,0},{48,16},{64,96},{80,112},{96,64},{112,80},{1... | collective-permute-start | bytes 786440 | tf_op jit(solution)/shard_map/ppermute | solution.py:367
  122.3 12.5 %collective-permute-start.7 = (bf16[128,1024]{1,0:T(8,128)(2,1)S(1)}, bf16[128,1024]{1,0:T(8,128)(2,1)}, u32[]{:S(2)}, u32[]{:S(2)}) collective-permute-start(bf16[128,1024]{1,0:T(8,128)(2,1)S(1)} %get-tuple-element.20), channel_id=1, source_target_pairs={{0,48},{16,0},{32,16},{48,32},{64,112},{80,64},{96,80},{112,96},{1... | collective-permute-start | bytes 786440 | tf_op jit(solution)/shard_map/ppermute | solution.py:367
  122.4 15.4 %copy-start.4 = (bf16[16,64,512]{2,1,0:T(8,128)(2,1)}, bf16[16,64,512]{2,1,0:T(8,128)(2,1)S(1)}, u32[]{:S(2)}) copy-start(bf16[16,64,512]{2,1,0:T(8,128)(2,1)S(1)} %all-to-all-done.2.dagg_ref) | copy-start | bytes 3145732
  122.4 58.5 %all-to-all-start.3 = ((bf16[16,64,512]{2,1,0:T(8,128)(2,1)}), bf16[16,64,512]{2,1,0:T(8,128)(2,1)}, u32[]{:S(2)}, u32[]{:S(2)}) async-start(bf16[16,64,512]{2,1,0:T(8,128)(2,1)} %bitcast.68), calls=%async_computation.3 | async-start | bytes 2097152 | tf_op jit(solution)/shard_map/all_to_all | solution.py:343
  137.9 4.3 %collective-permute-start.10 = (bf16[32,1024]{1,0:T(8,128)(2,1)S(1)}, bf16[32,1024]{1,0:T(8,128)(2,1)S(1)}, u32[]{:S(2)}, u32[]{:S(2)}) collective-permute-start(bf16[32,1024]{1,0:T(8,128)(2,1)S(1)} %get-tuple-element.23), channel_id=1, source_target_pairs={{0,192},{16,208},{32,224},{48,240},{64,0},{80,16},{96,32},{112,48}... | collective-permute-start | bytes 196616 | tf_op jit(solution)/shard_map/ppermute | solution.py:367
  138.5 4.3 %collective-permute-start.8 = (bf16[32,1024]{1,0:T(8,128)(2,1)S(1)}, bf16[32,1024]{1,0:T(8,128)(2,1)S(1)}, u32[]{:S(2)}, u32[]{:S(2)}) collective-permute-start(bf16[32,1024]{1,0:T(8,128)(2,1)S(1)} %get-tuple-element.22), channel_id=1, source_target_pairs={{0,64},{16,80},{32,96},{48,112},{64,128},{80,144},{96,160},{112,17... | collective-permute-start | bytes 196616 | tf_op jit(solution)/shard_map/ppermute | solution.py:367
  140.0 5.8 %collective-permute-start.9 = (bf16[32,1024]{1,0:T(8,128)(2,1)S(1)}, bf16[32,1024]{1,0:T(8,128)(2,1)S(1)}, u32[]{:S(2)}, u32[]{:S(2)}) collective-permute-start(bf16[32,1024]{1,0:T(8,128)(2,1)S(1)} %get-tuple-element.24), channel_id=1, source_target_pairs={{0,128},{16,144},{32,160},{48,176},{64,192},{80,208},{96,224},{112... | collective-permute-start | bytes 196616 | tf_op jit(solution)/shard_map/ppermute | solution.py:367
  154.8 27.5 %collective-permute-start.2 = (bf16[64,64,128]{2,1,0:T(8,128)(2,1)}, bf16[64,64,128]{2,1,0:T(8,128)(2,1)S(1)}, u32[]{:S(2)}, u32[]{:S(2)}) collective-permute-start(bf16[64,64,128]{2,1,0:T(8,128)(2,1)} %get-tuple-element.14), channel_id=1, source_target_pairs={{0,16},{16,32},{32,48},{48,64},{64,80},{80,96},{96,112},{112,128},... | collective-permute-start | bytes 3145736 | tf_op jit(solution)/shard_map/ppermute | solution.py:339
  156.7 26.9 %collective-permute-start.3 = (bf16[64,64,128]{2,1,0:T(8,128)(2,1)}, bf16[64,64,128]{2,1,0:T(8,128)(2,1)S(1)}, u32[]{:S(2)}, u32[]{:S(2)}) collective-permute-start(bf16[64,64,128]{2,1,0:T(8,128)(2,1)} %get-tuple-element.15), channel_id=1, source_target_pairs={{16,0},{32,16},{48,32},{64,48},{80,64},{96,80},{112,96},{128,112},... | collective-permute-start | bytes 3145736 | tf_op jit(solution)/shard_map/ppermute | solution.py:339
  162.8 8.7 %collective-permute-start.11 = (f32[16,1024]{1,0:T(8,128)S(1)}, f32[16,1024]{1,0:T(8,128)S(1)}, u32[]{:S(2)}, u32[]{:S(2)}) collective-permute-start(f32[16,1024]{1,0:T(8,128)S(1)} %dynamic-slice_bitcast_fusion.1), channel_id=1, source_target_pairs={{0,8},{1,9},{2,10},{3,11},{4,12},{5,13},{6,14},{7,15},{8,0},{9,1},... | collective-permute-start | bytes 196616 | tf_op jit(solution)/shard_map/ppermute | solution.py:367
  171.5 4.9 %collective-permute-start.12 = (f32[8,1024]{1,0:T(8,128)S(1)}, f32[8,1024]{1,0:T(8,128)S(1)}, u32[]{:S(2)}, u32[]{:S(2)}) collective-permute-start(f32[8,1024]{1,0:T(8,128)S(1)} %dynamic-slice_bitcast_fusion.2), channel_id=1, source_target_pairs={{0,4},{1,5},{2,6},{3,7},{4,0},{5,1},{6,2},{7,3},{8,12},{9,13},{10,... | collective-permute-start | bytes 98312 | tf_op jit(solution)/shard_map/ppermute | solution.py:367
  176.5 3.8 %collective-permute-start.13 = (f32[4,1024]{1,0:T(4,128)S(1)}, f32[4,1024]{1,0:T(4,128)S(1)}, u32[]{:S(2)}, u32[]{:S(2)}) collective-permute-start(f32[4,1024]{1,0:T(4,128)S(1)} %dynamic-slice_bitcast_fusion.3), channel_id=1, source_target_pairs={{0,2},{1,3},{2,0},{3,1},{4,6},{5,7},{6,4},{7,5},{8,10},{9,11},{10,... | collective-permute-start | bytes 49160 | tf_op jit(solution)/shard_map/ppermute | solution.py:367
  182.3 1.3 copy-start.6
  183.6 1.0 copy-start.7

commit v3 on v0

v3 whole, which is shorter than its diff:
```python
import functools

import jax
import jax.numpy as jnp
from jax import lax
from jax.experimental import pallas as pl
from jax.experimental.pallas import tpu as pltpu
from jax.sharding import PartitionSpec as P

F32 = jnp.float32
BF16 = jnp.bfloat16
NT = (((1,), (1,)), ((), ()))
NN = (((1,), (0,)), ((), ()))
MIB = 1 << 20


def dot(a, b, dims=NN):
    return lax.dot_general(a, b, dims, preferred_element_type=F32)


def whole_params(mib):
    return pltpu.CompilerParams(vmem_limit_bytes=mib * MIB)


def params(mib):
    return pltpu.CompilerParams(
        dimension_semantics=("arbitrary",), vmem_limit_bytes=mib * MIB
    )


def split_kernel(x_hbm, out_hbm, sems):
    width = out_hbm.shape[2]
    copies = [
        pltpu.make_async_copy(x_hbm.at[:, g * width : (g + 1) * width], out_hbm.at[g], sems.at[g])
        for g in range(out_hbm.shape[0])
    ]
    for copy in copies:
        copy.start()
    for copy in copies:
        copy.wait()


ANYWHERE = pl.BlockSpec(memory_space=pl.ANY)
SMEM = pl.BlockSpec(memory_space=pltpu.SMEM)
VMEM = pl.BlockSpec(memory_space=pltpu.VMEM)


def split_columns(x, groups):
    rows, columns = x.shape
    return pl.pallas_call(
        split_kernel,
        in_specs=[ANYWHERE],
        out_specs=ANYWHERE,
        out_shape=jax.ShapeDtypeStruct((groups, rows, columns // groups), x.dtype),
        scratch_shapes=[pltpu.SemaphoreType.DMA((groups,))],
        compiler_params=whole_params(60),
    )(x)


def gather_kernel(col_ref, before, own, after, out_hbm, sems):
    tile = 128
    blocks = own.shape[1] // tile
    per = out_hbm.shape[2] // tile

    def target(r):
        place = pl.ds(pl.multiple_of(lax.rem(r, per) * tile, tile), tile)
        return out_hbm.at[lax.div(r, per), :, place]

    def start(r, carry):
        col = col_ref[r]
        for i, part in enumerate((before, own, after)):

            @pl.when((col >= i * blocks) & (col < (i + 1) * blocks))
            def _(i=i, part=part):
                place = pl.ds(pl.multiple_of((col - i * blocks) * tile, tile), tile)
                pltpu.make_async_copy(part.at[:, place], target(r), sems.at[r]).start()

        return carry

    def wait(r, carry):
        pltpu.make_async_copy(own.at[:, :tile], target(r), sems.at[r]).wait()
        return carry

    lax.fori_loop(0, blocks, start, 0)
    lax.fori_loop(0, blocks, wait, 0)


def gather(col, before, own, after, groups):
    rows, span = own.shape
    return pl.pallas_call(
        gather_kernel,
        in_specs=[SMEM] + [ANYWHERE] * 3,
        out_specs=ANYWHERE,
        out_shape=jax.ShapeDtypeStruct((groups, rows, span // groups), BF16),
        scratch_shapes=[pltpu.SemaphoreType.DMA((col.shape[0],))],
        compiler_params=whole_params(2),
        cost_estimate=pl.CostEstimate(flops=0, bytes_accessed=8 * MIB, transcendentals=0),
    )(col, before, own, after)


def scatter_kernel(col_ref, parts_ref, before_hbm, own_hbm, after_hbm, acc, before, after, sems):
    tile = acc.shape[2]
    blocks = own_hbm.shape[0]
    per = parts_ref.shape[2] // tile

    def clear(i, carry):
        acc[i] = jnp.zeros(acc.shape[1:], F32)
        return carry

    lax.fori_loop(0, acc.shape[0], clear, 0, unroll=8)

    def add(g, carry):
        for b in range(per):
            acc[col_ref[g * per + b]] += parts_ref[g, :, b * tile : (b + 1) * tile].astype(F32)
        return carry

    lax.fori_loop(0, parts_ref.shape[0], add, 0)

    def cast(i, carry):
        before[i] = acc[i].astype(BF16)
        after[i] = acc[2 * blocks + i].astype(BF16)
        return carry

    lax.fori_loop(0, blocks, cast, 0, unroll=4)
    copies = [
        pltpu.make_async_copy(before, before_hbm, sems.at[0]),
        pltpu.make_async_copy(after, after_hbm, sems.at[1]),
        pltpu.make_async_copy(acc.at[blocks : 2 * blocks], own_hbm, sems.at[2]),
    ]
    for copy in copies:
        copy.start()
    for copy in copies:
        copy.wait()


def scatter(col, parts):
    groups, rows, width = parts.shape
    blocks = col.shape[0]
    tile = groups * width // blocks
    shape = (blocks, rows, tile)
    return pl.pallas_call(
        scatter_kernel,
        in_specs=[SMEM, VMEM],
        out_specs=[ANYWHERE] * 3,
        out_shape=[
            jax.ShapeDtypeStruct(shape, BF16),
            jax.ShapeDtypeStruct(shape, F32),
            jax.ShapeDtypeStruct(shape, BF16),
        ],
        scratch_shapes=[
            pltpu.VMEM((3 * blocks, rows, tile), F32),
            pltpu.VMEM(shape, BF16),
            pltpu.VMEM(shape, BF16),
            pltpu.SemaphoreType.DMA((3,)),
        ],
        compiler_params=whole_params(60),
        cost_estimate=pl.CostEstimate(flops=0, bytes_accessed=8 * MIB, transcendentals=0),
    )(col, parts)


def self_kernel(chunk, w_self, x_ref, tiles, pre, agg):
    tile = tiles.shape[-1]
    for i in range(pre.shape[0] // chunk):
        rows = slice(i * chunk, (i + 1) * chunk)
        pre[rows, :] = dot(w_self[rows, :], x_ref[...])
        for b in range(tiles.shape[0]):
            here = slice(b * tile, (b + 1) * tile)
            agg[rows, here] = dot(x_ref[rows, here], tiles[b, 0])


def self_products(w_self, x_rows, tiles):
    size, width = x_rows.shape
    out = jax.ShapeDtypeStruct((size, width), F32)
    return pl.pallas_call(
        functools.partial(self_kernel, 256),
        in_specs=[VMEM] * 3,
        out_specs=[VMEM] * 2,
        out_shape=[out, out],
        compiler_params=whole_params(60),
        cost_estimate=pl.CostEstimate(
            flops=2 * size * size * width, bytes_accessed=7 * MIB, transcendentals=0
        ),
    )(w_self, x_rows, tiles)


def dense_kernel(
    chunk,
    live_ref,
    tiles_hbm,
    picked_hbm,
    agg_self_hbm,
    w_neigh_hbm,
    pre_hbm,
    cot_hbm,
    w_back_hbm,
    agg_hbm,
    hidden_hbm,
    dpre_hbm,
    dagg_hbm,
    second_hbm,
    tiles,
    picked,
    agg_self,
    w_neigh,
    pre_ref,
    cot_ref,
    w_back,
    agg,
    hidden,
    dpre,
    dagg,
    second,
    in_sems,
    out_sems,
    tile_sem,
):
    steps = w_neigh.shape[0] // chunk
    tile = tiles.shape[-1]
    count = tiles.shape[0]
    part = [slice(i * chunk, (i + 1) * chunk) for i in range(steps)]
    here = [slice(b * tile, (b + 1) * tile) for b in range(count)]
    first = pltpu.make_async_copy(tiles_hbm, tiles, tile_sem)
    first.start()
    loads = {}
    order = (
        (picked_hbm, picked),
        (agg_self_hbm, agg_self),
        (w_neigh_hbm, w_neigh),
        (pre_hbm, pre_ref),
        (cot_hbm, cot_ref),
        (w_back_hbm, w_back),
    )
    for stage in ((0, 1), (2, 3, 4), (5,)):
        for i in range(steps):
            for k in stage:
                src, dst = order[k]
                copy = pltpu.make_async_copy(src.at[part[i]], dst.at[part[i]], in_sems.at[k, i])
                copy.start()
                loads[k, i] = copy
    stores = []

    def store(k, src, dst, i):
        copy = pltpu.make_async_copy(src.at[part[i]], dst.at[part[i]], out_sems.at[k, i])
        copy.start()
        stores.append(copy)

    first.wait()
    for i in range(steps):
        loads[0, i].wait()
        loads[1, i].wait()
        for b in range(count):
            other = dot(picked[part[i], here[b]], tiles[b, 1])
            total = agg_self[part[i], here[b]] + jnp.where(live_ref[b] > 0, other, 0.0)
            agg[part[i], here[b]] = total.astype(BF16)
        store(0, agg, agg_hbm, i)
    for i in range(steps):
        for k in (2, 3, 4):
            loads[k, i].wait()
        pre = pre_ref[part[i], :] + dot(w_neigh[part[i], :], agg[...])
        sig = jax.nn.sigmoid(pre)
        hidden[part[i], :] = (pre * sig).astype(BF16)
        slope = sig * (1.0 + pre * (1.0 - sig))
        dpre[part[i], :] = (cot_ref[part[i], :].astype(F32) * slope).astype(BF16)
        store(1, hidden, hidden_hbm, i)
        store(2, dpre, dpre_hbm, i)
    for i in range(steps):
        loads[5, i].wait()
        dagg[part[i], :] = dot(w_back[part[i], :], dpre[...]).astype(BF16)
        for b in range(count):
            other = dot(dagg[part[i], here[b]], tiles[b, 1], NT)
            second[part[i], here[b]] = jnp.where(live_ref[b] > 0, other, 0.0).astype(BF16)
        store(3, dagg, dagg_hbm, i)
        store(4, second, second_hbm, i)
    for copy in stores:
        copy.wait()


def dense(live, tiles, picked, agg_self, w_neigh, pre_self, cot, w_back):
    size, width = picked.shape
    chunk = 256
    steps = size // chunk
    out = jax.ShapeDtypeStruct((size, width), BF16)
    wide, narrow = pltpu.VMEM((size, width), F32), pltpu.VMEM((size, width), BF16)
    square = pltpu.VMEM((size, size), BF16)
    return pl.pallas_call(
        functools.partial(dense_kernel, chunk),
        in_specs=[SMEM] + [ANYWHERE] * 7,
        out_specs=[ANYWHERE] * 5,
        out_shape=[out] * 5,
        scratch_shapes=[pltpu.VMEM(tiles.shape, BF16), narrow, wide, square, wide, narrow, square]
        + [narrow] * 5
        + [
            pltpu.SemaphoreType.DMA((6, steps)),
            pltpu.SemaphoreType.DMA((5, steps)),
            pltpu.SemaphoreType.DMA(()),
        ],
        compiler_params=whole_params(60),
        cost_estimate=pl.CostEstimate(
            flops=4 * size * size * width, bytes_accessed=16 * MIB, transcendentals=size * width
        ),
    )(live, tiles, picked, agg_self, w_neigh, pre_self, cot, w_back)


def own_kernel(chunk, w_back, dpre, dagg_ref, tiles, own):
    tile = tiles.shape[-1]
    for i in range(own.shape[0] // chunk):
        rows = slice(i * chunk, (i + 1) * chunk)
        dself = dot(w_back[rows, :], dpre[...])
        for b in range(tiles.shape[0]):
            here = slice(b * tile, (b + 1) * tile)
            total = dself[:, here] + dot(dagg_ref[rows, here], tiles[b, 0], NT)
            own[rows, here] = total.astype(BF16)


def own_part(w_back, dpre, dagg, tiles):
    size, width = dpre.shape
    return pl.pallas_call(
        functools.partial(own_kernel, 256),
        in_specs=[VMEM] * 4,
        out_specs=VMEM,
        out_shape=jax.ShapeDtypeStruct((size, width), BF16),
        compiler_params=whole_params(12),
        cost_estimate=pl.CostEstimate(
            flops=2 * size * size * width, bytes_accessed=5 * MIB, transcendentals=0
        ),
    )(w_back, dpre, dagg, tiles)


def weight_kernel(chunk, half_ref, dpre, agg_ref, grad):
    rows = grad.shape[1]
    half = agg_ref.at[pl.ds(pl.multiple_of(half_ref[0] * rows, rows), rows)]
    for i in range(grad.shape[0] // chunk):
        here = slice(i * chunk, (i + 1) * chunk)
        grad[here, :] = dot(dpre[here, :], half[...], NT).astype(BF16)


def weight_sum_kernel(chunk, half_ref, dpre, agg_ref, other_ref, grad):
    rows = grad.shape[1]
    half = agg_ref.at[pl.ds(pl.multiple_of(half_ref[0] * rows, rows), rows)]
    for i in range(grad.shape[0] // chunk):
        here = slice(i * chunk, (i + 1) * chunk)
        total = dot(dpre[here, :], half[...], NT) + other_ref[here, :].astype(F32)
        grad[here, :] = total.astype(BF16)


def weight_part(half, dpre, agg_rows, other=None):
    size, width = dpre.shape
    body = weight_kernel if other is None else weight_sum_kernel
    more = () if other is None else (other,)
    return pl.pallas_call(
        functools.partial(body, 256),
        in_specs=[SMEM] + [VMEM] * (2 + len(more)),
        out_specs=VMEM,
        out_shape=jax.ShapeDtypeStruct((size, size // CORES), BF16),
        compiler_params=whole_params(12),
        cost_estimate=pl.CostEstimate(
            flops=size * size * width, bytes_accessed=3 * MIB, transcendentals=0
        ),
    )(half, dpre, agg_rows, *more)


def final_kernel(own_ref, before_ref, after_ref, dself_ref, out_ref):
    tile = own_ref.shape[2]
    per = dself_ref.shape[2] // tile
    for b in range(own_ref.shape[0]):
        grad = dself_ref[b // per, :, (b % per) * tile : (b % per + 1) * tile]
        total = own_ref[b] + before_ref[b].astype(F32) + after_ref[b].astype(F32)
        out_ref[:, b * tile : (b + 1) * tile] = (grad.astype(F32) + total).astype(BF16)


def finish(own, before, after, dself):
    groups, rows, width = dself.shape
    blocks, _, tile = own.shape
    steps = 4
    part = pl.BlockSpec((blocks // steps, rows, tile), lambda g: (g, 0, 0))
    return pl.pallas_call(
        final_kernel,
        grid=(steps,),
        in_specs=[part, part, part]
        + [pl.BlockSpec((groups // steps, rows, width), lambda g: (g, 0, 0))],
        out_specs=pl.BlockSpec((rows, groups * width // steps), lambda g: (0, g)),
        out_shape=jax.ShapeDtypeStruct((rows, groups * width), BF16),
        compiler_params=params(16),
    )(own, before, after, dself)


def shifted(value, axis, steps):
    count = lax.axis_size(axis)
    first, last = max(0, -steps), min(count, count - steps)
    return lax.ppermute(value, axis, [(source, source + steps) for source in range(first, last)])


def exchange(value, axis):
    return lax.all_to_all(value, axis, split_axis=0, concat_axis=0, tiled=True)


SIDE = 4
CORES = 2


def piece_at(pieces, index):
    return lax.dynamic_index_in_dim(pieces, index, 0, keepdims=False)


def exchange_sum(value, axis, count, index, partner, sent):
    pieces = value.reshape(count, -1, value.shape[-1])
    total = piece_at(pieces, index).astype(F32)
    for step in range(1, count):
        piece = piece_at(pieces, lax.rem(index + step, count)).astype(sent)
        pairs = [(i, partner(i, step)) for i in range(lax.axis_size(axis))]
        total = total + lax.ppermute(piece, axis, pairs).astype(F32)
    return total


def after(value, other):
    return lax.optimization_barrier((value, other))[0]


def weight_gradient(dpre, agg_rows, spread, halo):
    feat, node = lax.axis_index("feat"), lax.axis_index("node")
    core = lax.rem(feat, CORES)
    pairs = [(i, i ^ 1) for i in range(lax.axis_size("feat"))]
    sent = weight_part(1 - core[None], dpre, agg_rows)
    value = weight_part(core[None], dpre, agg_rows, lax.ppermute(sent, "feat", pairs))
    x = lambda i, s: (i + s * SIDE) % (SIDE * SIDE)
    value = exchange_sum(value, "node", SIDE, lax.div(node, SIDE), x, BF16)
    value = after(value, spread)
    y = lambda i, s: i // SIDE * SIDE + (i + s) % SIDE
    value = exchange_sum(value, "node", SIDE, lax.rem(node, SIDE), y, BF16)
    half = lax.axis_size("feat") // 2
    while half > 1:
        if half == CORES:
            value = after(value, halo)
        flip = lambda i, s, half=half: i ^ half
        value = exchange_sum(value, "feat", 2, lax.rem(lax.div(feat, half), 2), flip, F32)
        half //= 2
    pieces = value.reshape(CORES, -1, value.shape[-1])
    other = lax.ppermute(piece_at(pieces, 1 - core), "feat", pairs)
    kept = piece_at(pieces, core)
    first, second = jnp.where(core == 0, kept, other), jnp.where(core == 0, other, kept)
    return jnp.concatenate([first, second], axis=1)


def local(features, tile_values, tile_cols, tile_count, w_self, w_neigh, cotangent):
    feat_dev, node_dev = features.shape
    tile = tile_values.shape[-1]
    block_count = node_dev // tile
    groups = lax.axis_size("feat")
    size = w_self.shape[0]
    part, feat = lax.axis_index("node"), lax.axis_index("feat")
    col = tile_cols[:, 1] - (part - 1) * block_count
    mine = block_count // groups
    live = (lax.dynamic_slice_in_dim(tile_count, feat * mine, mine) > 1).astype(jnp.int32)
    tiles = lax.dynamic_slice_in_dim(tile_values, feat * mine, mine)

    before = shifted(features, "node", 1)
    after = shifted(features, "node", -1)
    x_rows = exchange(split_columns(features, groups), "feat").reshape(size, -1)
    picked = exchange(gather(col, before, features, after, groups), "feat").reshape(size, -1)
    pre_self, agg_self = self_products(w_self, x_rows, tiles)
    agg_rows, hidden, dpre, dagg, second = dense(
        live, tiles, picked, agg_self, w_neigh, pre_self, cotangent, w_neigh.T
    )
    second_cols = exchange(second.reshape(groups, feat_dev, -1), "feat")
    own_rows = own_part(w_self.T, dpre, dagg, tiles)
    second_cols, own_rows = lax.optimization_barrier((second_cols, own_rows))
    own_cols = exchange(own_rows.reshape(groups, feat_dev, -1), "feat")
    to_before, spread, to_after = scatter(col, second_cols)
    from_after = shifted(to_before, "node", -1)
    from_before = shifted(to_after, "node", 1)
    grad_w_neigh = weight_gradient(dpre, agg_rows, spread, (from_after, from_before))
    grad_features = finish(spread, from_before, from_after, own_cols)
    return (hidden, grad_features, grad_w_neigh)


def solution(mesh):
    placed = (
        P("feat", "node"),
        P("node", None, None, None),
        P("node", None),
        P("node"),
        P(),
        P(),
        P(None, ("node", "feat")),
    )
    return jax.shard_map(
        local,
        mesh=mesh,
        in_specs=placed,
        out_specs=(P(None, ("node", "feat")), P("feat", "node"), P(("node", "feat"), None)),
        check_vma=False,
    )
```

time: 444 us -> 215 us (0.48)
  waiting for transfers between devices: 302 us -> 65.7 us
  Pallas kernels: 0 us -> 65.6 us
  matrix products: 27.8 us -> 0 us
  other arithmetic: 31.8 us -> 4.33 us
  starting transfers between devices: 42.2 us -> 63 us
  between operations: 14.3 us -> 1.07 us
  local copies, waits for them, and re-layouts: 24.5 us -> 12.4 us
    unnamed x2 -> x0, waiting for transfers between devices: 235 us -> none
    pallas_call x0 -> x9, Pallas kernels: none -> 65.6 us  [the longest x1 33 us: split_columns(): pl.pallas_call(split_kernel, in_specs=[ANYWHERE], out_specs=ANYWHERE, out...]
    all_to_all x4, waiting for transfers between devices: 44.7 us -> 16.4 us  [exchange(): return lax.all_to_all(value, axis, split_axis=0, concat_axis=0, tiled=True)]
    dot_general x7 -> x0, matrix products: 27.8 us -> none  [the longest x1 5.74 us: local(): jnp.einsum('fbi,bkji->fbkj', dagg_blocks, masked, preferred_element_type=...]
    ppermute x4 -> x15, waiting for transfers between devices: 22.3 us -> 49.2 us  [the longest x4 24.7 us: shifted(): lax.ppermute(value, axis, [(source, source + steps) for source in range(f...]
    scatter-add x1 -> x0, other arithmetic: 20.3 us -> none  [local(): jnp.zeros((feat_dev, 3 * block_count, tile), jnp.float32)]
    ppermute x4 -> x15, starting transfers between devices: 16.7 us -> 35.9 us  [the longest x9 18.8 us: exchange_sum(): total = total + lax.ppermute(piece, axis, pairs).astype(F32)]
    convert_element_type x6 -> x1, local copies, waits for them, and re-layouts: 9.11 us -> 1.07 us  [exchange_sum(): piece = piece_at(pieces, lax.rem(index + step, count)).astype(sent)]
  transfers between devices with their start and end apart: 9 -> 19, of which waited for: 5 -> 12; matrix products, arithmetic and copies ran while one was open for 15% -> 6% of each run, Pallas kernels for 0% -> 6%
where the time goes in v3:
time: 215 us; the launch traced here: 212 us
  waiting for transfers between devices  65.7 us (31%)
  Pallas kernels  65.6 us (31%)
  starting transfers between devices  63 us (29%)
  local copies, waits for them, and re-layouts  12.4 us (6%)
  other arithmetic  4.33 us (2%)
    pallas_call x1, Pallas kernels, split_columns(): pl.pallas_call(split_kernel, in_specs=[ANYWHERE], out_specs=ANYWHERE, out...  33 us
    all_to_all x4, starting transfers between devices, exchange(): return lax.all_to_all(value, axis, split_axis=0, concat_axis=0, tiled=True)  27.1 us
    ppermute x4, waiting for transfers between devices, shifted(): lax.ppermute(value, axis, [(source, source + steps) for source in range(f...  24.7 us
    ppermute x9, waiting for transfers between devices, exchange_sum(): total = total + lax.ppermute(piece, axis, pairs).astype(F32)  20.9 us
    ppermute x9, starting transfers between devices, exchange_sum(): total = total + lax.ppermute(piece, axis, pairs).astype(F32)  18.8 us
    all_to_all x4, waiting for transfers between devices, exchange(): return lax.all_to_all(value, axis, split_axis=0, concat_axis=0, tiled=True)  16.4 us
    ppermute x4, starting transfers between devices, shifted(): lax.ppermute(value, axis, [(source, source + steps) for source in range(f...  15.9 us
    pallas_call x1, Pallas kernels, dense(): pl.pallas_call(functools.partial(dense_kernel, chunk), in_specs=[SMEM] +...  11.3 us
  transfers between devices with their start and end apart: 19, of which 12 were waited for; matrix products, arithmetic and copies ran while one was open for 6% of the time, Pallas kernels for 6%

profile of v3, /device:TPU:2, one launch (start us, length us, event | category | flops | bytes accessed | tf_op | source)
XLA Modules:
  0.0 212.1 jit_solution(11530609913957019064)
XLA Ops:
  0.6 33.0 %shard_map.95 = bf16[16,64,512]{2,1,0:T(8,128)(2,1)} custom-call(bf16[64,8192]{1,0:T(8,128)(2,1)} %x_hbm.1), custom_call_target="tpu_custom_call" | custom-call | tf_op jit(solution)/shard_map/pallas_call | solution.py:50
  33.7 8.6 %all-to-all-start.1 = ((bf16[16,64,512]{2,1,0:T(8,128)(2,1)}), bf16[16,64,512]{2,1,0:T(8,128)(2,1)}, u32[]{:S(2)}, u32[]{:S(2)}) async-start(bf16[16,64,512]{2,1,0:T(8,128)(2,1)} %shard_map.95), calls=%async_computation.1 | async-start | bytes 2097152 | tf_op jit(solution)/shard_map/all_to_all | solution.py:394
  42.3 3.5 %collective-permute-start = (bf16[64,8192]{1,0:T(8,128)(2,1)S(1)}, bf16[64,8192]{1,0:T(8,128)(2,1)S(1)}, u32[]{:S(2)}, u32[]{:S(2)}) collective-permute-start(bf16[64,8192]{1,0:T(8,128)(2,1)S(1)} %copy-done.1), channel_id=1, source_target_pairs={{0,16},{16,32},{32,48},{48,64},{64,80},{80,96},{96,112},{112,128},... | collective-permute-start | bytes 3145736 | tf_op jit(solution)/shard_map/ppermute | solution.py:390
  45.8 4.5 %collective-permute-start.1 = (bf16[64,8192]{1,0:T(8,128)(2,1)S(1)}, bf16[64,8192]{1,0:T(8,128)(2,1)S(1)}, u32[]{:S(2)}, u32[]{:S(2)}) collective-permute-start(bf16[64,8192]{1,0:T(8,128)(2,1)S(1)} %copy-done.1), channel_id=1, source_target_pairs={{16,0},{32,16},{48,32},{64,48},{80,64},{96,80},{112,96},{128,112},... | collective-permute-start | bytes 3145736 | tf_op jit(solution)/shard_map/ppermute | solution.py:390
  50.3 21.4 %collective-permute-done.before = bf16[64,8192]{1,0:T(8,128)(2,1)S(1)} collective-permute-done((bf16[64,8192]{1,0:T(8,128)(2,1)S(1)}, bf16[64,8192]{1,0:T(8,128)(2,1)S(1)}, u32[]{:S(2)}, u32[]{:S(2)}) %collective-permute-start) | collective-permute-done | bytes 1048608 | tf_op jit(solution)/shard_map/ppermute | solution.py:390
  72.9 2.9 %shard_map.94 = bf16[16,64,512]{2,1,0:T(8,128)(2,1)} custom-call(s32[64]{0:T(128)S(1)} %subtract_bitcast_fusion.col_ref, bf16[64,8192]{1,0:T(8,128)(2,1)S(1)} %collective-permute-done.before, bf16[64,8192]{1,0:T(8,128)(2,1)S(1)} %copy-done.1, bf16[64,8192]{1,0:T(8,128)(2,1)S(1)} %collective-permute-done.1.after), custom_call_target="tpu_custom_call" | custom-call | bytes 8388608 | tf_op jit(solution)/shard_map/pallas_call | solution.py:90
  75.8 7.1 %all-to-all-start = ((bf16[16,64,512]{2,1,0:T(8,128)(2,1)}), bf16[16,64,512]{2,1,0:T(8,128)(2,1)S(1)}, u32[]{:S(2)}, u32[]{:S(2)}) async-start(bf16[16,64,512]{2,1,0:T(8,128)(2,1)} %shard_map.94), calls=%async_computation | async-start | bytes 2097152 | tf_op jit(solution)/shard_map/all_to_all | solution.py:394
  83.0 2.6 %copy.10 = bf16[1024,1024]{0,1:T(8,128)(2,1)} copy(bf16[1024,1024]{1,0:T(8,128)(2,1)S(1)} %copy-done.8) | data formatting | bytes 4194304 | tf_op args[5]
  86.1 1.7 constant_dynamic-slice_fusion.tiles.tiles_hbm
  87.8 5.4 %shard_map.96 = (f32[1024,512]{1,0:T(8,128)}, f32[1024,512]{1,0:T(8,128)}) custom-call(bf16[1024,1024]{1,0:T(8,128)(2,1)} %w_self.1, bf16[1024,512]{1,0:T(8,128)(2,1)} %bitcast.2.x_ref, bf16[4,2,128,128]{3,2,1,0:T(8,128)(2,1)} %constant_dynamic-slice_fusion.tiles.tiles_hbm), custom_call_target="tpu_custom_call" | custom-call | flops 1073741824 | bytes 7340032 | tf_op jit(solution)/shard_map/pallas_call | solution.py:174
  93.2 16.4 %all-to-all-done = bf16[16,64,512]{2,1,0:T(8,128)(2,1)S(1)} async-done(((bf16[16,64,512]{2,1,0:T(8,128)(2,1)}), bf16[16,64,512]{2,1,0:T(8,128)(2,1)S(1)}, u32[]{:S(2)}, u32[]{:S(2)}) %all-to-all-start) | async-done | bytes 1048608 | tf_op jit(solution)/shard_map/all_to_all | solution.py:394
  110.6 11.3 %shard_map.97 = (bf16[1024,512]{1,0:T(8,128)(2,1)}, bf16[1024,512]{1,0:T(8,128)(2,1)}, bf16[1024,512]{1,0:T(8,128)(2,1)}, bf16[1024,512]{1,0:T(8,128)(2,1)}, bf16[1024,512]{1,0:T(8,128)(2,1)}) custom-call(s32[4]{0:T(128)} %compare_convert_fusion.live_ref, bf16[4,2,128,128]{3,2,1,0:T(8,128)(2,1)} %constant_dynamic-slice_fusion.tiles.tiles_hbm, ...), custom_call_target="tpu_custom_call" | custom-call | flops 2147483648 | bytes 16777216 | tf_op jit(solution)/shard_map/pallas_call | solution.py:285
  121.9 5.0 %all-to-all-start.2 = ((bf16[16,64,512]{2,1,0:T(8,128)(2,1)}), bf16[16,64,512]{2,1,0:T(8,128)(2,1)}, u32[]{:S(2)}, u32[]{:S(2)}) async-start(bf16[16,64,512]{2,1,0:T(8,128)(2,1)} %bitcast.59), calls=%async_computation.2 | async-start | bytes 2097152 | tf_op jit(solution)/shard_map/all_to_all | solution.py:394
  126.9 1.7 shard_map.101
  129.7 2.5 %collective-permute-done.4.other_ref = bf16[1024,512]{1,0:T(8,128)(2,1)S(1)} collective-permute-done((bf16[1024,512]{1,0:T(8,128)(2,1)}, bf16[1024,512]{1,0:T(8,128)(2,1)S(1)}, u32[]{:S(2)}, u32[]{:S(2)}) %collective-permute-start.4) | collective-permute-done | bytes 1048608 | tf_op jit(solution)/shard_map/ppermute | solution.py:424
  137.4 2.2 %collective-permute-start.7 = (bf16[256,512]{1,0:T(8,128)(2,1)}, bf16[256,512]{1,0:T(8,128)(2,1)}, u32[]{:S(2)}, u32[]{:S(2)}) collective-permute-start(bf16[256,512]{1,0:T(8,128)(2,1)} %get-tuple-element.32), channel_id=1, source_target_pairs={{0,192},{16,208},{32,224},{48,240},{64,0},{80,16},{96,32},{112,48}... | collective-permute-start | bytes 786440 | tf_op jit(solution)/shard_map/ppermute | solution.py:411
  139.6 2.9 %copy.11 = bf16[1024,1024]{0,1:T(8,128)(2,1)S(1)} copy(bf16[1024,1024]{1,0:T(8,128)(2,1)} %w_self.1) | data formatting | bytes 4194304 | tf_op args[4]
  143.8 2.5 %shard_map.98 = bf16[1024,512]{1,0:T(8,128)(2,1)} custom-call(bf16[1024,1024]{1,0:T(8,128)(2,1)S(1)} %bitcast.52, bf16[1024,512]{1,0:T(8,128)(2,1)S(1)} %copy-done, bf16[1024,512]{1,0:T(8,128)(2,1)S(1)} %copy-done.6, bf16[4,2,128,128]{3,2,1,0:T(8,128)(2,1)S(1)} %copy-done.4), custom_call_target="tpu_custom_call" | custom-call | flops 1073741824 | bytes 5242880 | tf_op jit(solution)/shard_map/pallas_call | solution.py:317
  147.4 4.0 %collective-permute-done.7 = bf16[256,512]{1,0:T(8,128)(2,1)} collective-permute-done((bf16[256,512]{1,0:T(8,128)(2,1)}, bf16[256,512]{1,0:T(8,128)(2,1)}, u32[]{:S(2)}, u32[]{:S(2)}) %collective-permute-start.7) | collective-permute-done | bytes 262176 | tf_op jit(solution)/shard_map/ppermute | solution.py:411
  151.4 2.2 %fusion.1 = f32[256,512]{1,0:T(8,128)} fusion(bf16[256,512]{1,0:T(8,128)(2,1)} %collective-permute-done.7, bf16[256,512]{1,0:T(8,128)(2,1)} %collective-permute-done.6, bf16[256,512]{1,0:T(8,128)(2,1)} %collective-permute-done.5, bf16[4,256,512]{2,1,0:T(8,128)(2,1)} %bitcast.54, s32[]{:T(128)S(6)} %select_n.72), kind=kLoop, calls=%fused_computation.2 | loop fusion | flops 917504 | bytes 1572868 | tf_op jit(solution)/shard_map/add | solution.py:411
  153.6 4.4 %shard_map.99 = (bf16[64,64,128]{2,1,0:T(8,128)(2,1)}, f32[64,64,128]{2,1,0:T(8,128)}, bf16[64,64,128]{2,1,0:T(8,128)(2,1)}) custom-call(s32[64]{0:T(128)} %copy-done.7, bf16[16,64,512]{2,1,0:T(8,128)(2,1)} %all-to-all-done.2.parts_ref), custom_call_target="tpu_custom_call" | custom-call | bytes 8388608 | tf_op jit(solution)/shard_map/pallas_call | solution.py:141
  157.9 6.3 %all-to-all-start.3 = ((bf16[16,64,512]{2,1,0:T(8,128)(2,1)}), bf16[16,64,512]{2,1,0:T(8,128)(2,1)S(1)}, u32[]{:S(2)}, u32[]{:S(2)}) async-start(bf16[16,64,512]{2,1,0:T(8,128)(2,1)} %bitcast.6), calls=%async_computation.3 | async-start | bytes 2097152 | tf_op jit(solution)/shard_map/all_to_all | solution.py:394
  165.4 4.7 %collective-permute-start.10 = (bf16[64,512]{1,0:T(8,128)(2,1)S(1)}, bf16[64,512]{1,0:T(8,128)(2,1)S(1)}, u32[]{:S(2)}, u32[]{:S(2)}) collective-permute-start(bf16[64,512]{1,0:T(8,128)(2,1)S(1)} %get-tuple-element.35), channel_id=1, source_target_pairs={{0,48},{16,0},{32,16},{48,32},{64,112},{80,64},{96,80},{112,96},{1... | collective-permute-start | bytes 196616 | tf_op jit(solution)/shard_map/ppermute | solution.py:411
  171.6 4.4 %collective-permute-start.2 = (bf16[64,64,128]{2,1,0:T(8,128)(2,1)}, bf16[64,64,128]{2,1,0:T(8,128)(2,1)}, u32[]{:S(2)}, u32[]{:S(2)}) collective-permute-start(bf16[64,64,128]{2,1,0:T(8,128)(2,1)} %get-tuple-element.25), channel_id=1, source_target_pairs={{0,16},{16,32},{32,48},{48,64},{64,80},{80,96},{96,112},{112,128},... | collective-permute-start | bytes 3145736 | tf_op jit(solution)/shard_map/ppermute | solution.py:390
  176.1 3.5 %collective-permute-start.3 = (bf16[64,64,128]{2,1,0:T(8,128)(2,1)}, bf16[64,64,128]{2,1,0:T(8,128)(2,1)}, u32[]{:S(2)}, u32[]{:S(2)}) collective-permute-start(bf16[64,64,128]{2,1,0:T(8,128)(2,1)} %get-tuple-element.26), channel_id=1, source_target_pairs={{16,0},{32,16},{48,32},{64,48},{80,64},{96,80},{112,96},{128,112},... | collective-permute-start | bytes 3145736 | tf_op jit(solution)/shard_map/ppermute | solution.py:390
  180.6 5.9 %collective-permute-start.11 = (f32[32,512]{1,0:T(8,128)S(1)}, f32[32,512]{1,0:T(8,128)S(1)}, u32[]{:S(2)}, u32[]{:S(2)}) collective-permute-start(f32[32,512]{1,0:T(8,128)S(1)} %dynamic-slice_bitcast_fusion.3), channel_id=1, source_target_pairs={{0,8},{1,9},{2,10},{3,11},{4,12},{5,13},{6,14},{7,15},{8,0},{9,1},... | collective-permute-start | bytes 196616 | tf_op jit(solution)/shard_map/ppermute | solution.py:411
  186.5 9.1 %collective-permute-done.11 = f32[32,512]{1,0:T(8,128)S(1)} collective-permute-done((f32[32,512]{1,0:T(8,128)S(1)}, f32[32,512]{1,0:T(8,128)S(1)}, u32[]{:S(2)}, u32[]{:S(2)}) %collective-permute-start.11) | collective-permute-done | bytes 65568 | tf_op jit(solution)/shard_map/ppermute | solution.py:411
  195.9 4.6 %collective-permute-done.12 = f32[16,512]{1,0:T(8,128)S(1)} collective-permute-done((f32[16,512]{1,0:T(8,128)S(1)}, f32[16,512]{1,0:T(8,128)S(1)}, u32[]{:S(2)}, u32[]{:S(2)}) %collective-permute-start.12) | collective-permute-done | bytes 32800 | tf_op jit(solution)/shard_map/ppermute | solution.py:411
  200.9 1.8 collective-permute-done.3.after_ref
  202.7 1.6 collective-permute-start.13
  204.3 2.1 collective-permute-done.13
  208.3 3.8 %shard_map.100 = bf16[64,8192]{1,0:T(8,128)(2,1)} custom-call(f32[64,64,128]{2,1,0:T(8,128)S(1)} %copy-done.5, bf16[64,64,128]{2,1,0:T(8,128)(2,1)} %collective-permute-done.2.before_ref, bf16[64,64,128]{2,1,0:T(8,128)(2,1)} %collective-permute-done.3.after_ref, bf16[16,64,512]{2,1,0:T(8,128)(2,1)S(1)} %all-to-all-done.3.dself_ref), custom_call_target="tpu_custom_call" | custom-call | tf_op jit(solution)/shard_map/pallas_call | solution.py:376
  (58 shorter events, 17.4 us)
Async XLA Ops:
  0.6 41.7 %copy-start.1 = (bf16[64,8192]{1,0:T(8,128)(2,1)S(1)}, bf16[64,8192]{1,0:T(8,128)(2,1)}, u32[]{:S(2)}) copy-start(bf16[64,8192]{1,0:T(8,128)(2,1)} %x_hbm.1) | copy-start | bytes 3145732
  0.6 49.7 %copy-start.10 = (s32[64,2]{0,1:T(2,128)S(1)}, s32[64,2]{0,1:T(2,128)}, u32[]{:S(2)}) copy-start(s32[64,2]{0,1:T(2,128)} %param.9) | copy-start | bytes 1540
  33.7 42.1 %all-to-all-start.1 = ((bf16[16,64,512]{2,1,0:T(8,128)(2,1)}), bf16[16,64,512]{2,1,0:T(8,128)(2,1)}, u32[]{:S(2)}, u32[]{:S(2)}) async-start(bf16[16,64,512]{2,1,0:T(8,128)(2,1)} %shard_map.95), calls=%async_computation.1 | async-start | bytes 2097152 | tf_op jit(solution)/shard_map/all_to_all | solution.py:394
  42.3 29.4 %collective-permute-start = (bf16[64,8192]{1,0:T(8,128)(2,1)S(1)}, bf16[64,8192]{1,0:T(8,128)(2,1)S(1)}, u32[]{:S(2)}, u32[]{:S(2)}) collective-permute-start(bf16[64,8192]{1,0:T(8,128)(2,1)S(1)} %copy-done.1), channel_id=1, source_target_pairs={{0,16},{16,32},{32,48},{48,64},{64,80},{80,96},{96,112},{112,128},... | collective-permute-start | bytes 3145736 | tf_op jit(solution)/shard_map/ppermute | solution.py:390
  45.8 27.1 %collective-permute-start.1 = (bf16[64,8192]{1,0:T(8,128)(2,1)S(1)}, bf16[64,8192]{1,0:T(8,128)(2,1)S(1)}, u32[]{:S(2)}, u32[]{:S(2)}) collective-permute-start(bf16[64,8192]{1,0:T(8,128)(2,1)S(1)} %copy-done.1), channel_id=1, source_target_pairs={{16,0},{32,16},{48,32},{64,48},{80,64},{96,80},{112,96},{128,112},... | collective-permute-start | bytes 3145736 | tf_op jit(solution)/shard_map/ppermute | solution.py:390
  50.3 25.5 %copy-start.7 = (s32[64]{0:T(128)}, s32[64]{0:T(128)S(1)}, u32[]{:S(2)}) copy-start(s32[64]{0:T(128)S(1)} %subtract_bitcast_fusion.col_ref) | copy-start | bytes 772
  75.8 7.1 %copy-start.8 = (bf16[1024,1024]{1,0:T(8,128)(2,1)S(1)}, bf16[1024,1024]{1,0:T(8,128)(2,1)}, u32[]{:S(2)}) copy-start(bf16[1024,1024]{1,0:T(8,128)(2,1)} %w_neigh_hbm.1) | copy-start | bytes 6291460
  75.8 33.8 %all-to-all-start = ((bf16[16,64,512]{2,1,0:T(8,128)(2,1)}), bf16[16,64,512]{2,1,0:T(8,128)(2,1)S(1)}, u32[]{:S(2)}, u32[]{:S(2)}) async-start(bf16[16,64,512]{2,1,0:T(8,128)(2,1)} %shard_map.94), calls=%async_computation | async-start | bytes 2097152 | tf_op jit(solution)/shard_map/all_to_all | solution.py:394
  82.9 2.6 %copy-start.11 = (s32[64]{0:T(128)S(1)}, s32[64]{0:T(128)}, u32[]{:S(2)}) copy-start(s32[64]{0:T(128)} %param.10) | copy-start | bytes 772
  109.6 1.0 copy-start.9
  121.9 5.0 %copy-start = (bf16[1024,512]{1,0:T(8,128)(2,1)S(1)}, bf16[1024,512]{1,0:T(8,128)(2,1)}, u32[]{:S(2)}) copy-start(bf16[1024,512]{1,0:T(8,128)(2,1)} %get-tuple-element.21.dpre) | copy-start | bytes 3145732
  121.9 5.0 %copy-start.3 = (bf16[1024,512]{1,0:T(8,128)(2,1)S(1)}, bf16[1024,512]{1,0:T(8,128)(2,1)}, u32[]{:S(2)}) copy-start(bf16[1024,512]{1,0:T(8,128)(2,1)} %get-tuple-element.28.agg_ref) | copy-start | bytes 3145732
  121.9 31.7 %all-to-all-start.2 = ((bf16[16,64,512]{2,1,0:T(8,128)(2,1)}), bf16[16,64,512]{2,1,0:T(8,128)(2,1)}, u32[]{:S(2)}, u32[]{:S(2)}) async-start(bf16[16,64,512]{2,1,0:T(8,128)(2,1)} %bitcast.59), calls=%async_computation.2 | async-start | bytes 2097152 | tf_op jit(solution)/shard_map/all_to_all | solution.py:394
  128.6 3.6 %collective-permute-start.4 = (bf16[1024,512]{1,0:T(8,128)(2,1)}, bf16[1024,512]{1,0:T(8,128)(2,1)S(1)}, u32[]{:S(2)}, u32[]{:S(2)}) collective-permute-start(bf16[1024,512]{1,0:T(8,128)(2,1)} %shard_map.101), channel_id=1, source_target_pairs={{0,1},{1,0},{2,3},{3,2},{4,5},{5,4},{6,7},{7,6},{8,9},{9,8},{10,11... | collective-permute-start | bytes 3145736 | tf_op jit(solution)/shard_map/ppermute | solution.py:424
  132.9 1.0 copy-start.2
  134.8 11.5 %collective-permute-start.5 = (bf16[256,512]{1,0:T(8,128)(2,1)}, bf16[256,512]{1,0:T(8,128)(2,1)}, u32[]{:S(2)}, u32[]{:S(2)}) collective-permute-start(bf16[256,512]{1,0:T(8,128)(2,1)} %get-tuple-element.31), channel_id=1, source_target_pairs={{0,64},{16,80},{32,96},{48,112},{64,128},{80,144},{96,160},{112,17... | collective-permute-start | bytes 786440 | tf_op jit(solution)/shard_map/ppermute | solution.py:411
  136.3 11.0 %collective-permute-start.6 = (bf16[256,512]{1,0:T(8,128)(2,1)}, bf16[256,512]{1,0:T(8,128)(2,1)}, u32[]{:S(2)}, u32[]{:S(2)}) collective-permute-start(bf16[256,512]{1,0:T(8,128)(2,1)} %get-tuple-element.33), channel_id=1, source_target_pairs={{0,128},{16,144},{32,160},{48,176},{64,192},{80,208},{96,224},{112... | collective-permute-start | bytes 786440 | tf_op jit(solution)/shard_map/ppermute | solution.py:411
  137.4 13.9 %collective-permute-start.7 = (bf16[256,512]{1,0:T(8,128)(2,1)}, bf16[256,512]{1,0:T(8,128)(2,1)}, u32[]{:S(2)}, u32[]{:S(2)}) collective-permute-start(bf16[256,512]{1,0:T(8,128)(2,1)} %get-tuple-element.32), channel_id=1, source_target_pairs={{0,192},{16,208},{32,224},{48,240},{64,0},{80,16},{96,32},{112,48}... | collective-permute-start | bytes 786440 | tf_op jit(solution)/shard_map/ppermute | solution.py:411
  139.6 3.0 %copy-start.4 = (bf16[4,2,128,128]{3,2,1,0:T(8,128)(2,1)S(1)}, bf16[4,2,128,128]{3,2,1,0:T(8,128)(2,1)}, u32[]{:S(2)}) copy-start(bf16[4,2,128,128]{3,2,1,0:T(8,128)(2,1)} %constant_dynamic-slice_fusion.tiles.tiles_hbm) | copy-start | bytes 786436
  142.5 1.2 copy-start.6
  157.9 50.4 %copy-start.5 = (f32[64,64,128]{2,1,0:T(8,128)S(1)}, f32[64,64,128]{2,1,0:T(8,128)}, u32[]{:S(2)}) copy-start(f32[64,64,128]{2,1,0:T(8,128)} %get-tuple-element.24.own_ref) | copy-start | bytes 6291460
  157.9 50.4 %all-to-all-start.3 = ((bf16[16,64,512]{2,1,0:T(8,128)(2,1)}), bf16[16,64,512]{2,1,0:T(8,128)(2,1)S(1)}, u32[]{:S(2)}, u32[]{:S(2)}) async-start(bf16[16,64,512]{2,1,0:T(8,128)(2,1)} %bitcast.6), calls=%async_computation.3 | async-start | bytes 2097152 | tf_op jit(solution)/shard_map/all_to_all | solution.py:394
  165.4 14.2 %collective-permute-start.10 = (bf16[64,512]{1,0:T(8,128)(2,1)S(1)}, bf16[64,512]{1,0:T(8,128)(2,1)S(1)}, u32[]{:S(2)}, u32[]{:S(2)}) collective-permute-start(bf16[64,512]{1,0:T(8,128)(2,1)S(1)} %get-tuple-element.35), channel_id=1, source_target_pairs={{0,48},{16,0},{32,16},{48,32},{64,112},{80,64},{96,80},{112,96},{1... | collective-permute-start | bytes 196616 | tf_op jit(solution)/shard_map/ppermute | solution.py:411
  170.1 9.6 %collective-permute-start.8 = (bf16[64,512]{1,0:T(8,128)(2,1)S(1)}, bf16[64,512]{1,0:T(8,128)(2,1)S(1)}, u32[]{:S(2)}, u32[]{:S(2)}) collective-permute-start(bf16[64,512]{1,0:T(8,128)(2,1)S(1)} %get-tuple-element.34), channel_id=1, source_target_pairs={{0,16},{16,32},{32,48},{48,0},{64,80},{80,96},{96,112},{112,64},{1... | collective-permute-start | bytes 196616 | tf_op jit(solution)/shard_map/ppermute | solution.py:411
  170.1 9.6 %collective-permute-start.9 = (bf16[64,512]{1,0:T(8,128)(2,1)S(1)}, bf16[64,512]{1,0:T(8,128)(2,1)S(1)}, u32[]{:S(2)}, u32[]{:S(2)}) collective-permute-start(bf16[64,512]{1,0:T(8,128)(2,1)S(1)} %get-tuple-element.36), channel_id=1, source_target_pairs={{0,32},{16,48},{32,0},{48,16},{64,96},{80,112},{96,64},{112,80},{1... | collective-permute-start | bytes 196616 | tf_op jit(solution)/shard_map/ppermute | solution.py:411
  171.6 29.2 %collective-permute-start.2 = (bf16[64,64,128]{2,1,0:T(8,128)(2,1)}, bf16[64,64,128]{2,1,0:T(8,128)(2,1)}, u32[]{:S(2)}, u32[]{:S(2)}) collective-permute-start(bf16[64,64,128]{2,1,0:T(8,128)(2,1)} %get-tuple-element.25), channel_id=1, source_target_pairs={{0,16},{16,32},{32,48},{48,64},{64,80},{80,96},{96,112},{112,128},... | collective-permute-start | bytes 3145736 | tf_op jit(solution)/shard_map/ppermute | solution.py:390
  176.1 26.6 %collective-permute-start.3 = (bf16[64,64,128]{2,1,0:T(8,128)(2,1)}, bf16[64,64,128]{2,1,0:T(8,128)(2,1)}, u32[]{:S(2)}, u32[]{:S(2)}) collective-permute-start(bf16[64,64,128]{2,1,0:T(8,128)(2,1)} %get-tuple-element.26), channel_id=1, source_target_pairs={{16,0},{32,16},{48,32},{64,48},{80,64},{96,80},{112,96},{128,112},... | collective-permute-start | bytes 3145736 | tf_op jit(solution)/shard_map/ppermute | solution.py:390
  180.6 15.0 %collective-permute-start.11 = (f32[32,512]{1,0:T(8,128)S(1)}, f32[32,512]{1,0:T(8,128)S(1)}, u32[]{:S(2)}, u32[]{:S(2)}) collective-permute-start(f32[32,512]{1,0:T(8,128)S(1)} %dynamic-slice_bitcast_fusion.3), channel_id=1, source_target_pairs={{0,8},{1,9},{2,10},{3,11},{4,12},{5,13},{6,14},{7,15},{8,0},{9,1},... | collective-permute-start | bytes 196616 | tf_op jit(solution)/shard_map/ppermute | solution.py:411
  195.7 4.9 %collective-permute-start.12 = (f32[16,512]{1,0:T(8,128)S(1)}, f32[16,512]{1,0:T(8,128)S(1)}, u32[]{:S(2)}, u32[]{:S(2)}) collective-permute-start(f32[16,512]{1,0:T(8,128)S(1)} %dynamic-slice_bitcast_fusion.4), channel_id=1, source_target_pairs={{0,4},{1,5},{2,6},{3,7},{4,0},{5,1},{6,2},{7,3},{8,12},{9,13},{10,... | collective-permute-start | bytes 98312 | tf_op jit(solution)/shard_map/ppermute | solution.py:411
  202.7 3.7 %collective-permute-start.13 = (f32[8,512]{1,0:T(8,128)S(1)}, f32[8,512]{1,0:T(8,128)S(1)}, u32[]{:S(2)}, u32[]{:S(2)}) collective-permute-start(f32[8,512]{1,0:T(8,128)S(1)} %dynamic-slice_bitcast_fusion.5), channel_id=1, source_target_pairs={{0,2},{1,3},{2,0},{3,1},{4,6},{5,7},{6,4},{7,5},{8,10},{9,11},{10,... | collective-permute-start | bytes 49160 | tf_op jit(solution)/shard_map/ppermute | solution.py:411
  206.4 1.3 collective-permute-start.14

commit v4 on v3

--- a/solution.py
+++ b/solution.py
@@ -12,6 +12,7 @@
 NT = (((1,), (1,)), ((), ()))
 NN = (((1,), (0,)), ((), ()))
 MIB = 1 << 20
+DENSE_MIB = 60
 
 
 def dot(a, b, dims=NN):
@@ -28,15 +29,20 @@
     )
 
 
-def split_kernel(x_hbm, out_hbm, sems):
+def split_kernel(x_hbm, out_hbm, held, in_sems, out_sems):
     width = out_hbm.shape[2]
-    copies = [
-        pltpu.make_async_copy(x_hbm.at[:, g * width : (g + 1) * width], out_hbm.at[g], sems.at[g])
-        for g in range(out_hbm.shape[0])
+    groups = range(out_hbm.shape[0])
+    loads = [
+        pltpu.make_async_copy(x_hbm.at[:, g * width : (g + 1) * width], held.at[g], in_sems.at[g])
+        for g in groups
     ]
-    for copy in copies:
+    stores = [pltpu.make_async_copy(held.at[g], out_hbm.at[g], out_sems.at[g]) for g in groups]
+    for copy in loads:
         copy.start()
-    for copy in copies:
+    for load, store in zip(loads, stores):
+        load.wait()
+        store.start()
+    for copy in stores:
         copy.wait()
 
 
@@ -52,7 +58,11 @@
         in_specs=[ANYWHERE],
         out_specs=ANYWHERE,
         out_shape=jax.ShapeDtypeStruct((groups, rows, columns // groups), x.dtype),
-        scratch_shapes=[pltpu.SemaphoreType.DMA((groups,))],
+        scratch_shapes=[
+            pltpu.VMEM((groups, rows, columns // groups), x.dtype),
+            pltpu.SemaphoreType.DMA((groups,)),
+            pltpu.SemaphoreType.DMA((groups,)),
+        ],
         compiler_params=whole_params(60),
     )(x)
 
@@ -158,85 +168,40 @@
     )(col, parts)
 
 
-def self_kernel(chunk, w_self, x_ref, tiles, pre, agg):
-    tile = tiles.shape[-1]
+def self_kernel(chunk, w_self, x_ref, pre):
     for i in range(pre.shape[0] // chunk):
         rows = slice(i * chunk, (i + 1) * chunk)
         pre[rows, :] = dot(w_self[rows, :], x_ref[...])
-        for b in range(tiles.shape[0]):
-            here = slice(b * tile, (b + 1) * tile)
-            agg[rows, here] = dot(x_ref[rows, here], tiles[b, 0])
-
-
-def self_products(w_self, x_rows, tiles):
+
+
+def self_product(w_self, x_rows):
     size, width = x_rows.shape
-    out = jax.ShapeDtypeStruct((size, width), F32)
     return pl.pallas_call(
         functools.partial(self_kernel, 256),
-        in_specs=[VMEM] * 3,
-        out_specs=[VMEM] * 2,
-        out_shape=[out, out],
+        in_specs=[VMEM] * 2,
+        out_specs=VMEM,
+        out_shape=jax.ShapeDtypeStruct((size, width), F32),
         compiler_params=whole_params(60),
         cost_estimate=pl.CostEstimate(
-            flops=2 * size * size * width, bytes_accessed=7 * MIB, transcendentals=0
+            flops=2 * size * size * width, bytes_accessed=5 * MIB, transcendentals=0
         ),
-    )(w_self, x_rows, tiles)
-
-
-def dense_kernel(
-    chunk,
-    live_ref,
-    tiles_hbm,
-    picked_hbm,
-    agg_self_hbm,
-    w_neigh_hbm,
-    pre_hbm,
-    cot_hbm,
-    w_back_hbm,
-    agg_hbm,
-    hidden_hbm,
-    dpre_hbm,
-    dagg_hbm,
-    second_hbm,
-    tiles,
-    picked,
-    agg_self,
-    w_neigh,
-    pre_ref,
-    cot_ref,
-    w_back,
-    agg,
-    hidden,
-    dpre,
-    dagg,
-    second,
-    in_sems,
-    out_sems,
-    tile_sem,
-):
-    steps = w_neigh.shape[0] // chunk
-    tile = tiles.shape[-1]
-    count = tiles.shape[0]
-    part = [slice(i * chunk, (i + 1) * chunk) for i in range(steps)]
-    here = [slice(b * tile, (b + 1) * tile) for b in range(count)]
-    first = pltpu.make_async_copy(tiles_hbm, tiles, tile_sem)
-    first.start()
-    loads = {}
-    order = (
-        (picked_hbm, picked),
-        (agg_self_hbm, agg_self),
-        (w_neigh_hbm, w_neigh),
-        (pre_hbm, pre_ref),
-        (cot_hbm, cot_ref),
-        (w_back_hbm, w_back),
-    )
-    for stage in ((0, 1), (2, 3, 4), (5,)):
-        for i in range(steps):
-            for k in stage:
-                src, dst = order[k]
-                copy = pltpu.make_async_copy(src.at[part[i]], dst.at[part[i]], in_sems.at[k, i])
-                copy.start()
-                loads[k, i] = copy
+    )(w_self, x_rows)
+
+
+def dense_kernel(chunk, *refs):
+    (tiles_hbm, turned_hbm, x_hbm, picked_hbm, w_neigh_hbm, pre_hbm, cot_hbm, w_back_hbm) = refs[:8]
+    (agg_hbm, hidden_hbm, dpre_hbm, dagg_hbm, second_hbm) = refs[8:13]
+    (tiles, turned, x_ref, picked, w_neigh, pre_ref, cot_ref, w_back) = refs[13:21]
+    (agg, hidden, dpre, dagg, second, in_sems, out_sems) = refs[21:]
+    size = w_neigh.shape[0]
+    pair = tiles.shape[-1]
+    part = [slice(i, i + chunk) for i in range(0, size, chunk)]
+    here = [slice(i, i + pair) for i in range(0, agg.shape[1], pair)]
+    loads = [
+        pltpu.make_async_copy(refs[k], refs[13 + k], in_sems.at[k]) for k in (0, 2, 3, 4, 5, 6, 7, 1)
+    ]
+    for copy in loads:
+        copy.start()
     stores = []
 
     def store(k, src, dst, i):
@@ -244,75 +209,68 @@
         copy.start()
         stores.append(copy)
 
-    first.wait()
-    for i in range(steps):
-        loads[0, i].wait()
-        loads[1, i].wait()
-        for b in range(count):
-            other = dot(picked[part[i], here[b]], tiles[b, 1])
-            total = agg_self[part[i], here[b]] + jnp.where(live_ref[b] > 0, other, 0.0)
-            agg[part[i], here[b]] = total.astype(BF16)
+    for copy in loads[:3]:
+        copy.wait()
+    for i in range(len(part)):
+        for p in range(len(here)):
+            total = dot(x_ref[part[i], here[p]], tiles[0, p])
+            total = total + dot(picked[part[i], here[p]], tiles[1, p])
+            agg[part[i], here[p]] = total.astype(BF16)
+    for copy in loads[3:6]:
+        copy.wait()
+    for i in range(len(part)):
         store(0, agg, agg_hbm, i)
-    for i in range(steps):
-        for k in (2, 3, 4):
-            loads[k, i].wait()
         pre = pre_ref[part[i], :] + dot(w_neigh[part[i], :], agg[...])
-        sig = jax.nn.sigmoid(pre)
+        sig = 0.5 + 0.5 * jnp.tanh(0.5 * pre)
         hidden[part[i], :] = (pre * sig).astype(BF16)
         slope = sig * (1.0 + pre * (1.0 - sig))
         dpre[part[i], :] = (cot_ref[part[i], :].astype(F32) * slope).astype(BF16)
+    for copy in loads[6:]:
+        copy.wait()
+    for i in range(len(part)):
         store(1, hidden, hidden_hbm, i)
         store(2, dpre, dpre_hbm, i)
-    for i in range(steps):
-        loads[5, i].wait()
         dagg[part[i], :] = dot(w_back[part[i], :], dpre[...]).astype(BF16)
-        for b in range(count):
-            other = dot(dagg[part[i], here[b]], tiles[b, 1], NT)
-            second[part[i], here[b]] = jnp.where(live_ref[b] > 0, other, 0.0).astype(BF16)
+        for p in range(len(here)):
+            second[part[i], here[p]] = dot(dagg[part[i], here[p]], turned[1, p]).astype(BF16)
         store(3, dagg, dagg_hbm, i)
         store(4, second, second_hbm, i)
     for copy in stores:
         copy.wait()
 
 
-def dense(live, tiles, picked, agg_self, w_neigh, pre_self, cot, w_back):
+def dense(tiles, turned, x_rows, picked, w_neigh, pre_self, cot, w_back):
     size, width = picked.shape
     chunk = 256
-    steps = size // chunk
     out = jax.ShapeDtypeStruct((size, width), BF16)
-    wide, narrow = pltpu.VMEM((size, width), F32), pltpu.VMEM((size, width), BF16)
-    square = pltpu.VMEM((size, size), BF16)
+    args = (tiles, turned, x_rows, picked, w_neigh, pre_self, cot, w_back)
     return pl.pallas_call(
         functools.partial(dense_kernel, chunk),
-        in_specs=[SMEM] + [ANYWHERE] * 7,
+        in_specs=[ANYWHERE] * len(args),
         out_specs=[ANYWHERE] * 5,
         out_shape=[out] * 5,
-        scratch_shapes=[pltpu.VMEM(tiles.shape, BF16), narrow, wide, square, wide, narrow, square]
-        + [narrow] * 5
-        + [
-            pltpu.SemaphoreType.DMA((6, steps)),
-            pltpu.SemaphoreType.DMA((5, steps)),
-            pltpu.SemaphoreType.DMA(()),
-        ],
-        compiler_params=whole_params(60),
+        scratch_shapes=[pltpu.VMEM(arg.shape, arg.dtype) for arg in args]
+        + [pltpu.VMEM((size, width), BF16)] * 5
+        + [pltpu.SemaphoreType.DMA((len(args),)), pltpu.SemaphoreType.DMA((5, size // chunk))],
+        compiler_params=whole_params(DENSE_MIB),
         cost_estimate=pl.CostEstimate(
             flops=4 * size * size * width, bytes_accessed=16 * MIB, transcendentals=size * width
         ),
-    )(live, tiles, picked, agg_self, w_neigh, pre_self, cot, w_back)
-
-
-def own_kernel(chunk, w_back, dpre, dagg_ref, tiles, own):
-    tile = tiles.shape[-1]
-    for i in range(own.shape[0] // chunk):
-        rows = slice(i * chunk, (i + 1) * chunk)
+    )(*args)
+
+
+def own_kernel(chunk, w_back, dpre, dagg_ref, turned, own):
+    pair = turned.shape[-1]
+    for i in range(0, own.shape[0], chunk):
+        rows = slice(i, i + chunk)
         dself = dot(w_back[rows, :], dpre[...])
-        for b in range(tiles.shape[0]):
-            here = slice(b * tile, (b + 1) * tile)
-            total = dself[:, here] + dot(dagg_ref[rows, here], tiles[b, 0], NT)
+        for p in range(own.shape[1] // pair):
+            here = slice(p * pair, (p + 1) * pair)
+            total = dself[:, here] + dot(dagg_ref[rows, here], turned[0, p])
             own[rows, here] = total.astype(BF16)
 
 
-def own_part(w_back, dpre, dagg, tiles):
+def own_part(w_back, dpre, dagg, turned):
     size, width = dpre.shape
     return pl.pallas_call(
         functools.partial(own_kernel, 256),
@@ -323,7 +281,7 @@
         cost_estimate=pl.CostEstimate(
             flops=2 * size * size * width, bytes_accessed=5 * MIB, transcendentals=0
         ),
-    )(w_back, dpre, dagg, tiles)
+    )(w_back, dpre, dagg, turned)
 
 
 def weight_kernel(chunk, half_ref, dpre, agg_ref, grad):
@@ -416,29 +374,34 @@
     return lax.optimization_barrier((value, other))[0]
 
 
-def weight_gradient(dpre, agg_rows, spread, halo):
+def weight_first(dpre, agg_rows):
     feat, node = lax.axis_index("feat"), lax.axis_index("node")
     core = lax.rem(feat, CORES)
     pairs = [(i, i ^ 1) for i in range(lax.axis_size("feat"))]
     sent = weight_part(1 - core[None], dpre, agg_rows)
     value = weight_part(core[None], dpre, agg_rows, lax.ppermute(sent, "feat", pairs))
     x = lambda i, s: (i + s * SIDE) % (SIDE * SIDE)
-    value = exchange_sum(value, "node", SIDE, lax.div(node, SIDE), x, BF16)
-    value = after(value, spread)
+    return exchange_sum(value, "node", SIDE, lax.div(node, SIDE), x, BF16)
+
+
+def weight_rest(value, last):
+    node, groups = lax.axis_index("node"), lax.axis_size("feat")
     y = lambda i, s: i // SIDE * SIDE + (i + s) % SIDE
     value = exchange_sum(value, "node", SIDE, lax.rem(node, SIDE), y, BF16)
-    half = lax.axis_size("feat") // 2
-    while half > 1:
-        if half == CORES:
-            value = after(value, halo)
-        flip = lambda i, s, half=half: i ^ half
-        value = exchange_sum(value, "feat", 2, lax.rem(lax.div(feat, half), 2), flip, F32)
-        half //= 2
-    pieces = value.reshape(CORES, -1, value.shape[-1])
-    other = lax.ppermute(piece_at(pieces, 1 - core), "feat", pairs)
-    kept = piece_at(pieces, core)
-    first, second = jnp.where(core == 0, kept, other), jnp.where(core == 0, other, kept)
-    return jnp.concatenate([first, second], axis=1)
+    value = after(value, last)
+    rows, half = value.shape
+    pieces = exchange(value.reshape(groups, rows // groups, half), "feat")
+    total = jnp.sum(pieces.reshape(groups // CORES, CORES, rows // groups, half), axis=0)
+    return jnp.concatenate([total[i] for i in range(CORES)], axis=1)
+
+
+def paired(tiles):
+    blocks, tile, _ = tiles.shape
+    tiles = tiles.reshape(blocks // 2, 2, tile, tile)
+    empty = jnp.zeros_like(tiles[:, 0])
+    upper = jnp.concatenate([tiles[:, 0], empty], axis=2)
+    lower = jnp.concatenate([empty, tiles[:, 1]], axis=2)
+    return jnp.concatenate([upper, lower], axis=1)
 
 
 def local(features, tile_values, tile_cols, tile_count, w_self, w_neigh, cotangent):
@@ -450,25 +413,32 @@
     part, feat = lax.axis_index("node"), lax.axis_index("feat")
     col = tile_cols[:, 1] - (part - 1) * block_count
     mine = block_count // groups
-    live = (lax.dynamic_slice_in_dim(tile_count, feat * mine, mine) > 1).astype(jnp.int32)
+    live = lax.dynamic_slice_in_dim(tile_count, feat * mine, mine) > 1
     tiles = lax.dynamic_slice_in_dim(tile_values, feat * mine, mine)
+    other = jnp.where(live[:, None, None], tiles[:, 1], jnp.zeros_like(tiles[:, 1]))
+    straight = jnp.stack([paired(tiles[:, 0]), paired(other)])
+    turned = straight.swapaxes(2, 3)
 
     before = shifted(features, "node", 1)
-    after = shifted(features, "node", -1)
+    behind = shifted(features, "node", -1)
     x_rows = exchange(split_columns(features, groups), "feat").reshape(size, -1)
-    picked = exchange(gather(col, before, features, after, groups), "feat").reshape(size, -1)
-    pre_self, agg_self = self_products(w_self, x_rows, tiles)
+    picked = exchange(gather(col, before, features, behind, groups), "feat").reshape(size, -1)
+    x_rows, self_back, neigh_back, straight, turned = lax.optimization_barrier(
+        (x_rows, w_self.T, w_neigh.T, straight, turned)
+    )
+    pre_self = self_product(w_self, x_rows)
     agg_rows, hidden, dpre, dagg, second = dense(
-        live, tiles, picked, agg_self, w_neigh, pre_self, cotangent, w_neigh.T
+        straight, turned, x_rows, picked, w_neigh, pre_self, cotangent, neigh_back
     )
     second_cols = exchange(second.reshape(groups, feat_dev, -1), "feat")
-    own_rows = own_part(w_self.T, dpre, dagg, tiles)
-    second_cols, own_rows = lax.optimization_barrier((second_cols, own_rows))
+    own_rows = own_part(self_back, dpre, dagg, turned)
+    weight = weight_first(dpre, agg_rows)
+    second_cols, own_rows, weight = lax.optimization_barrier((second_cols, own_rows, weight))
     own_cols = exchange(own_rows.reshape(groups, feat_dev, -1), "feat")
     to_before, spread, to_after = scatter(col, second_cols)
     from_after = shifted(to_before, "node", -1)
     from_before = shifted(to_after, "node", 1)
-    grad_w_neigh = weight_gradient(dpre, agg_rows, spread, (from_after, from_before))
+    grad_w_neigh = weight_rest(after(weight, spread), (from_after, from_before, own_cols))
     grad_features = finish(spread, from_before, from_after, own_cols)
     return (hidden, grad_features, grad_w_neigh)
 

time: 215 us -> 190 us (0.88)
  Pallas kernels: 65.6 us -> 28.8 us
  local copies, waits for them, and re-layouts: 12.4 us -> 22.4 us
  waiting for transfers between devices: 65.7 us -> 70 us
  starting transfers between devices: 63 us -> 59.6 us
    pallas_call x1, Pallas kernels: 33 us -> 2.24 us  [split_columns(): pl.pallas_call(split_kernel, in_specs=[ANYWHERE], out_specs=ANYWHERE, out...]
    ppermute x9 -> x6, starting transfers between devices: 18.8 us -> 8.44 us  [exchange_sum(): total = total + lax.ppermute(piece, axis, pairs).astype(F32)]
    ppermute x9 -> x6, waiting for transfers between devices: 20.9 us -> 28.9 us  [exchange_sum(): total = total + lax.ppermute(piece, axis, pairs).astype(F32)]
    unnamed x26 -> x30, local copies, waits for them, and re-layouts: 8.68 us -> 16.3 us
    all_to_all x4 -> x5, starting transfers between devices: 27.1 us -> 33.8 us  [exchange(): return lax.all_to_all(value, axis, split_axis=0, concat_axis=0, tiled=True)]
    pallas_call x2, Pallas kernels: 16.7 us -> 12.4 us  [the longest x1 7.97 us: dense(): pl.pallas_call(functools.partial(dense_kernel, chunk), in_specs=[ANYWHERE...]
    all_to_all x4 -> x5, waiting for transfers between devices: 16.4 us -> 15.8 us  [exchange(): return lax.all_to_all(value, axis, split_axis=0, concat_axis=0, tiled=True)]
  transfers between devices with their start and end apart: 19 -> 16, of which waited for: 12 -> 8; matrix products, arithmetic and copies ran while one was open for 6% -> 9% of each run, Pallas kernels for 6% -> 10%
where the time goes in v4:
time: 190 us; the launch traced here: 187 us
  waiting for transfers between devices  70 us (37%)
  starting transfers between devices  59.6 us (31%)
  Pallas kernels  28.8 us (15%)
  local copies, waits for them, and re-layouts  22.4 us (12%)
  other arithmetic  4.92 us (3%)
    all_to_all x5, starting transfers between devices, exchange(): return lax.all_to_all(value, axis, split_axis=0, concat_axis=0, tiled=True)  33.8 us
    ppermute x6, waiting for transfers between devices, exchange_sum(): total = total + lax.ppermute(piece, axis, pairs).astype(F32)  28.9 us
    ppermute x4, waiting for transfers between devices, shifted(): lax.ppermute(value, axis, [(source, source + steps) for source in range(f...  22.6 us
    ppermute x4, starting transfers between devices, shifted(): lax.ppermute(value, axis, [(source, source + steps) for source in range(f...  16.4 us
    unnamed x30, local copies, waits for them, and re-layouts  16.3 us
    all_to_all x5, waiting for transfers between devices, exchange(): return lax.all_to_all(value, axis, split_axis=0, concat_axis=0, tiled=True)  15.8 us
    ppermute x6, starting transfers between devices, exchange_sum(): total = total + lax.ppermute(piece, axis, pairs).astype(F32)  8.44 us
    pallas_call x1, Pallas kernels, dense(): pl.pallas_call(functools.partial(dense_kernel, chunk), in_specs=[ANYWHERE...  7.97 us
  transfers between devices with their start and end apart: 16, of which 8 were waited for; matrix products, arithmetic and copies ran while one was open for 9% of the time, Pallas kernels for 10%

profile of v4, /device:TPU:2, one launch (start us, length us, event | category | flops | bytes accessed | tf_op | source)
XLA Modules:
  0.0 186.8 jit_solution(18176275759303652289)
XLA Ops:
  0.7 2.2 %shard_map.94 = bf16[16,64,512]{2,1,0:T(8,128)(2,1)} custom-call(bf16[64,8192]{1,0:T(8,128)(2,1)} %own.1), custom_call_target="tpu_custom_call" | custom-call | tf_op jit(solution)/shard_map/pallas_call | solution.py:56
  2.9 8.6 %all-to-all-start = ((bf16[16,64,512]{2,1,0:T(8,128)(2,1)}), bf16[16,64,512]{2,1,0:T(8,128)(2,1)}, u32[]{:S(2)}, u32[]{:S(2)}) async-start(bf16[16,64,512]{2,1,0:T(8,128)(2,1)} %shard_map.94), calls=%async_computation | async-start | bytes 2097152 | tf_op jit(solution)/shard_map/all_to_all | solution.py:352
  11.5 3.5 %collective-permute-start = (bf16[64,8192]{1,0:T(8,128)(2,1)S(1)}, bf16[64,8192]{1,0:T(8,128)(2,1)S(1)}, u32[]{:S(2)}, u32[]{:S(2)}) collective-permute-start(bf16[64,8192]{1,0:T(8,128)(2,1)S(1)} %copy-done.2), channel_id=1, source_target_pairs={{0,16},{16,32},{32,48},{48,64},{64,80},{80,96},{96,112},{112,128},... | collective-permute-start | bytes 3145736 | tf_op jit(solution)/shard_map/ppermute | solution.py:348
  15.0 4.5 %collective-permute-start.1 = (bf16[64,8192]{1,0:T(8,128)(2,1)S(1)}, bf16[64,8192]{1,0:T(8,128)(2,1)S(1)}, u32[]{:S(2)}, u32[]{:S(2)}) collective-permute-start(bf16[64,8192]{1,0:T(8,128)(2,1)S(1)} %copy-done.2), channel_id=1, source_target_pairs={{16,0},{32,16},{48,32},{64,48},{80,64},{96,80},{112,96},{128,112},... | collective-permute-start | bytes 3145736 | tf_op jit(solution)/shard_map/ppermute | solution.py:348
  19.6 21.4 %collective-permute-done.before = bf16[64,8192]{1,0:T(8,128)(2,1)S(1)} collective-permute-done((bf16[64,8192]{1,0:T(8,128)(2,1)S(1)}, bf16[64,8192]{1,0:T(8,128)(2,1)S(1)}, u32[]{:S(2)}, u32[]{:S(2)}) %collective-permute-start) | collective-permute-done | bytes 1048608 | tf_op jit(solution)/shard_map/ppermute | solution.py:348
  42.2 2.9 %shard_map.95 = bf16[16,64,512]{2,1,0:T(8,128)(2,1)} custom-call(s32[64]{0:T(128)S(1)} %subtract_bitcast_fusion.col_ref, bf16[64,8192]{1,0:T(8,128)(2,1)S(1)} %collective-permute-done.before, bf16[64,8192]{1,0:T(8,128)(2,1)S(1)} %copy-done.2, bf16[64,8192]{1,0:T(8,128)(2,1)S(1)} %collective-permute-done.1.after), custom_call_target="tpu_custom_call" | custom-call | bytes 8388608 | tf_op jit(solution)/shard_map/pallas_call | solution.py:100
  45.0 7.0 %all-to-all-start.1 = ((bf16[16,64,512]{2,1,0:T(8,128)(2,1)}), bf16[16,64,512]{2,1,0:T(8,128)(2,1)S(1)}, u32[]{:S(2)}, u32[]{:S(2)}) async-start(bf16[16,64,512]{2,1,0:T(8,128)(2,1)} %shard_map.95), calls=%async_computation.1 | async-start | bytes 2097152 | tf_op jit(solution)/shard_map/all_to_all | solution.py:352
  53.7 2.9 %copy.14 = bf16[1024,1024]{0,1:T(8,128)(2,1)S(1)} copy(bf16[1024,1024]{1,0:T(8,128)(2,1)} %w_self.1) | data formatting | bytes 4194304 | tf_op args[4]
  56.6 4.0 %copy.15 = bf16[1024,1024]{0,1:T(8,128)(2,1)} copy(bf16[1024,1024]{1,0:T(8,128)(2,1)} %refs_4_.1) | data formatting | bytes 4194304 | tf_op args[5]
  61.7 2.1 %copy.21.refs_0_ = bf16[2,2,256,256]{3,2,1,0:T(8,128)(2,1)} copy(bf16[2,2,256,256]{2,3,1,0:T(8,128)(2,1)} %get-tuple-element.21) | data formatting | bytes 1048576 | tf_op jit(solution)/shard_map/optimization_barrier | solution.py:426
  63.8 4.4 %shard_map.96.refs_5_ = f32[1024,512]{1,0:T(8,128)} custom-call(bf16[1024,1024]{1,0:T(8,128)(2,1)} %w_self.1, bf16[1024,512]{1,0:T(8,128)(2,1)} %bitcast.x_ref.refs_2_), custom_call_target="tpu_custom_call" | custom-call | flops 1073741824 | bytes 5242880 | tf_op jit(solution)/shard_map/pallas_call | solution.py:179
  68.2 10.4 %all-to-all-done.1 = bf16[16,64,512]{2,1,0:T(8,128)(2,1)S(1)} async-done(((bf16[16,64,512]{2,1,0:T(8,128)(2,1)}), bf16[16,64,512]{2,1,0:T(8,128)(2,1)S(1)}, u32[]{:S(2)}, u32[]{:S(2)}) %all-to-all-start.1) | async-done | bytes 1048608 | tf_op jit(solution)/shard_map/all_to_all | solution.py:352
  79.7 8.0 %shard_map.97 = (bf16[1024,512]{1,0:T(8,128)(2,1)}, bf16[1024,512]{1,0:T(8,128)(2,1)}, bf16[1024,512]{1,0:T(8,128)(2,1)}, bf16[1024,512]{1,0:T(8,128)(2,1)}, bf16[1024,512]{1,0:T(8,128)(2,1)}) custom-call(bf16[2,2,256,256]{3,2,1,0:T(8,128)(2,1)} %copy.21.refs_0_, bf16[2,2,256,256]{3,2,1,0:T(8,128)(2,1)} %get-tuple-element.22.refs_1_.turned, ...), custom_call_target="tpu_custom_call" | custom-call | flops 2147483648 | bytes 16777216 | tf_op jit(solution)/shard_map/pallas_call | solution.py:247
  87.6 5.0 %all-to-all-start.2 = ((bf16[16,64,512]{2,1,0:T(8,128)(2,1)}), bf16[16,64,512]{2,1,0:T(8,128)(2,1)}, u32[]{:S(2)}, u32[]{:S(2)}) async-start(bf16[16,64,512]{2,1,0:T(8,128)(2,1)} %bitcast.63), calls=%async_computation.2 | async-start | bytes 2097152 | tf_op jit(solution)/shard_map/all_to_all | solution.py:352
  93.9 1.7 shard_map.99
  96.7 2.6 %collective-permute-done.2.other_ref = bf16[1024,512]{1,0:T(8,128)(2,1)} collective-permute-done((bf16[1024,512]{1,0:T(8,128)(2,1)}, bf16[1024,512]{1,0:T(8,128)(2,1)}, u32[]{:S(2)}, u32[]{:S(2)}) %collective-permute-start.2) | collective-permute-done | bytes 1048608 | tf_op jit(solution)/shard_map/ppermute | solution.py:382
  100.5 2.0 %shard_map.100 = bf16[1024,512]{1,0:T(8,128)(2,1)S(1)} custom-call(s32[1]{0:T(128)} %bitcast.15.half_ref, bf16[1024,512]{1,0:T(8,128)(2,1)S(1)} %copy-done, bf16[1024,512]{1,0:T(8,128)(2,1)S(1)} %copy-done.4, bf16[1024,512]{1,0:T(8,128)(2,1)} %collective-permute-done.2.other_ref), custom_call_target="tpu_custom_call" | custom-call | flops 536870912 | bytes 3145728 | tf_op jit(solution)/shard_map/pallas_call | solution.py:308
  106.9 2.2 %collective-permute-start.5 = (bf16[256,512]{1,0:T(8,128)(2,1)S(1)}, bf16[256,512]{1,0:T(8,128)(2,1)}, u32[]{:S(2)}, u32[]{:S(2)}) collective-permute-start(bf16[256,512]{1,0:T(8,128)(2,1)S(1)} %get-tuple-element.42), channel_id=1, source_target_pairs={{0,192},{16,208},{32,224},{48,240},{64,0},{80,16},{96,32},{112,48}... | collective-permute-start | bytes 786440 | tf_op jit(solution)/shard_map/ppermute | solution.py:369
  113.9 3.0 %collective-permute-done.4 = bf16[256,512]{1,0:T(8,128)(2,1)} collective-permute-done((bf16[256,512]{1,0:T(8,128)(2,1)}, bf16[256,512]{1,0:T(8,128)(2,1)}, u32[]{:S(2)}, u32[]{:S(2)}) %collective-permute-start.4) | collective-permute-done | bytes 262176 | tf_op jit(solution)/shard_map/ppermute | solution.py:369
  116.9 3.8 %collective-permute-done.5 = bf16[256,512]{1,0:T(8,128)(2,1)} collective-permute-done((bf16[256,512]{1,0:T(8,128)(2,1)S(1)}, bf16[256,512]{1,0:T(8,128)(2,1)}, u32[]{:S(2)}, u32[]{:S(2)}) %collective-permute-start.5) | collective-permute-done | bytes 262176 | tf_op jit(solution)/shard_map/ppermute | solution.py:369
  120.7 2.1 %fusion.5 = f32[256,512]{1,0:T(8,128)} fusion(bf16[256,512]{1,0:T(8,128)(2,1)} %collective-permute-done.5, bf16[256,512]{1,0:T(8,128)(2,1)} %collective-permute-done.4, bf16[256,512]{1,0:T(8,128)(2,1)} %collective-permute-done.3, bf16[4,256,512]{2,1,0:T(8,128)(2,1)} %bitcast.57, s32[]{:T(128)S(6)} %select_n.37), kind=kLoop, calls=%fused_computation.9 | loop fusion | flops 917504 | bytes 1572868 | tf_op jit(solution)/shard_map/add | solution.py:369
  122.8 6.2 %all-to-all-start.3 = ((bf16[16,64,512]{2,1,0:T(8,128)(2,1)}), bf16[16,64,512]{2,1,0:T(8,128)(2,1)S(1)}, u32[]{:S(2)}, u32[]{:S(2)}) async-start(bf16[16,64,512]{2,1,0:T(8,128)(2,1)} %bitcast.58), calls=%async_computation.3 | async-start | bytes 2097152 | tf_op jit(solution)/shard_map/all_to_all | solution.py:352
  129.0 4.4 %shard_map.101 = (bf16[64,64,128]{2,1,0:T(8,128)(2,1)}, f32[64,64,128]{2,1,0:T(8,128)}, bf16[64,64,128]{2,1,0:T(8,128)(2,1)}) custom-call(s32[64]{0:T(128)} %copy-done.9, bf16[16,64,512]{2,1,0:T(8,128)(2,1)} %all-to-all-done.2.parts_ref), custom_call_target="tpu_custom_call" | custom-call | bytes 8388608 | tf_op jit(solution)/shard_map/pallas_call | solution.py:151
  133.4 3.4 %collective-permute-start.6 = (bf16[64,64,128]{2,1,0:T(8,128)(2,1)}, bf16[64,64,128]{2,1,0:T(8,128)(2,1)S(1)}, u32[]{:S(2)}, u32[]{:S(2)}) collective-permute-start(bf16[64,64,128]{2,1,0:T(8,128)(2,1)} %get-tuple-element.33), channel_id=1, source_target_pairs={{0,16},{16,32},{32,48},{48,64},{64,80},{80,96},{96,112},{112,128},... | collective-permute-start | bytes 3145736 | tf_op jit(solution)/shard_map/ppermute | solution.py:348
  136.8 5.0 %collective-permute-start.7 = (bf16[64,64,128]{2,1,0:T(8,128)(2,1)}, bf16[64,64,128]{2,1,0:T(8,128)(2,1)S(1)}, u32[]{:S(2)}, u32[]{:S(2)}) collective-permute-start(bf16[64,64,128]{2,1,0:T(8,128)(2,1)} %get-tuple-element.34), channel_id=1, source_target_pairs={{16,0},{32,16},{48,32},{64,48},{80,64},{96,80},{112,96},{128,112},... | collective-permute-start | bytes 3145736 | tf_op jit(solution)/shard_map/ppermute | solution.py:348
  142.9 2.1 %collective-permute-start.10 = (bf16[64,512]{1,0:T(8,128)(2,1)S(1)}, bf16[64,512]{1,0:T(8,128)(2,1)S(1)}, u32[]{:S(2)}, u32[]{:S(2)}) collective-permute-start(bf16[64,512]{1,0:T(8,128)(2,1)S(1)} %get-tuple-element.45), channel_id=1, source_target_pairs={{0,48},{16,0},{32,16},{48,32},{64,112},{80,64},{96,80},{112,96},{1... | collective-permute-start | bytes 196616 | tf_op jit(solution)/shard_map/ppermute | solution.py:369
  145.0 1.6 collective-permute-start.9
  146.6 22.2 %collective-permute-done.10 = bf16[64,512]{1,0:T(8,128)(2,1)S(1)} collective-permute-done((bf16[64,512]{1,0:T(8,128)(2,1)S(1)}, bf16[64,512]{1,0:T(8,128)(2,1)S(1)}, u32[]{:S(2)}, u32[]{:S(2)}) %collective-permute-start.10) | collective-permute-done | bytes 65568 | tf_op jit(solution)/shard_map/ppermute | solution.py:369
  170.4 6.9 %all-to-all-start.4 = ((f32[16,4,512]{2,1,0:T(4,128)}), f32[16,4,512]{2,1,0:T(4,128)S(1)}, u32[]{:S(2)}, u32[]{:S(2)}) async-start(f32[16,4,512]{2,1,0:T(4,128)} %reshape.48), calls=%async_computation.4 | async-start | bytes 262144 | tf_op jit(solution)/shard_map/all_to_all | solution.py:352
  177.4 1.6 copy-done.7
  179.0 1.8 shard_map.102
  180.7 5.4 %all-to-all-done.4 = f32[16,4,512]{2,1,0:T(4,128)S(1)} async-done(((f32[16,4,512]{2,1,0:T(4,128)}), f32[16,4,512]{2,1,0:T(4,128)S(1)}, u32[]{:S(2)}, u32[]{:S(2)}) %all-to-all-start.4) | async-done | bytes 131104 | tf_op jit(solution)/shard_map/all_to_all | solution.py:352
  (59 shorter events, 21.1 us)
Async XLA Ops:
  0.6 10.9 %copy-start.2 = (bf16[64,8192]{1,0:T(8,128)(2,1)S(1)}, bf16[64,8192]{1,0:T(8,128)(2,1)}, u32[]{:S(2)}) copy-start(bf16[64,8192]{1,0:T(8,128)(2,1)} %own.1) | copy-start | bytes 3145732
  0.6 18.9 %copy-start.11 = (s32[64,2]{0,1:T(2,128)S(1)}, s32[64,2]{0,1:T(2,128)}, u32[]{:S(2)}) copy-start(s32[64,2]{0,1:T(2,128)} %param.9) | copy-start | bytes 1540
  2.9 42.1 %all-to-all-start = ((bf16[16,64,512]{2,1,0:T(8,128)(2,1)}), bf16[16,64,512]{2,1,0:T(8,128)(2,1)}, u32[]{:S(2)}, u32[]{:S(2)}) async-start(bf16[16,64,512]{2,1,0:T(8,128)(2,1)} %shard_map.94), calls=%async_computation | async-start | bytes 2097152 | tf_op jit(solution)/shard_map/all_to_all | solution.py:352
  11.5 29.4 %collective-permute-start = (bf16[64,8192]{1,0:T(8,128)(2,1)S(1)}, bf16[64,8192]{1,0:T(8,128)(2,1)S(1)}, u32[]{:S(2)}, u32[]{:S(2)}) collective-permute-start(bf16[64,8192]{1,0:T(8,128)(2,1)S(1)} %copy-done.2), channel_id=1, source_target_pairs={{0,16},{16,32},{32,48},{48,64},{64,80},{80,96},{96,112},{112,128},... | collective-permute-start | bytes 3145736 | tf_op jit(solution)/shard_map/ppermute | solution.py:348
  15.0 27.1 %collective-permute-start.1 = (bf16[64,8192]{1,0:T(8,128)(2,1)S(1)}, bf16[64,8192]{1,0:T(8,128)(2,1)S(1)}, u32[]{:S(2)}, u32[]{:S(2)}) collective-permute-start(bf16[64,8192]{1,0:T(8,128)(2,1)S(1)} %copy-done.2), channel_id=1, source_target_pairs={{16,0},{32,16},{48,32},{64,48},{80,64},{96,80},{112,96},{128,112},... | collective-permute-start | bytes 3145736 | tf_op jit(solution)/shard_map/ppermute | solution.py:348
  19.5 25.5 %copy-start.9 = (s32[64]{0:T(128)}, s32[64]{0:T(128)S(1)}, u32[]{:S(2)}) copy-start(s32[64]{0:T(128)S(1)} %subtract_bitcast_fusion.col_ref) | copy-start | bytes 772
  45.0 8.1 %copy-start.12 = (s32[64]{0:T(128)S(1)}, s32[64]{0:T(128)}, u32[]{:S(2)}) copy-start(s32[64]{0:T(128)} %param.10) | copy-start | bytes 772
  45.0 33.6 %all-to-all-start.1 = ((bf16[16,64,512]{2,1,0:T(8,128)(2,1)}), bf16[16,64,512]{2,1,0:T(8,128)(2,1)S(1)}, u32[]{:S(2)}, u32[]{:S(2)}) async-start(bf16[16,64,512]{2,1,0:T(8,128)(2,1)} %shard_map.95), calls=%async_computation.1 | async-start | bytes 2097152 | tf_op jit(solution)/shard_map/all_to_all | solution.py:352
  78.7 1.0 copy-start.10
  87.6 5.0 %copy-start = (bf16[1024,512]{1,0:T(8,128)(2,1)S(1)}, bf16[1024,512]{1,0:T(8,128)(2,1)}, u32[]{:S(2)}) copy-start(bf16[1024,512]{1,0:T(8,128)(2,1)} %get-tuple-element.28.dpre) | copy-start | bytes 3145732
  87.6 35.1 %all-to-all-start.2 = ((bf16[16,64,512]{2,1,0:T(8,128)(2,1)}), bf16[16,64,512]{2,1,0:T(8,128)(2,1)}, u32[]{:S(2)}, u32[]{:S(2)}) async-start(bf16[16,64,512]{2,1,0:T(8,128)(2,1)} %bitcast.63), calls=%async_computation.2 | async-start | bytes 2097152 | tf_op jit(solution)/shard_map/all_to_all | solution.py:352
  92.7 1.2 copy-start.3
  95.6 3.7 %collective-permute-start.2 = (bf16[1024,512]{1,0:T(8,128)(2,1)}, bf16[1024,512]{1,0:T(8,128)(2,1)}, u32[]{:S(2)}, u32[]{:S(2)}) collective-permute-start(bf16[1024,512]{1,0:T(8,128)(2,1)} %shard_map.99), channel_id=1, source_target_pairs={{0,1},{1,0},{2,3},{3,2},{4,5},{5,4},{6,7},{7,6},{8,9},{9,8},{10,11... | collective-permute-start | bytes 3145736 | tf_op jit(solution)/shard_map/ppermute | solution.py:382
  99.3 1.2 copy-start.4
  102.5 1.0 copy-start.5
  104.3 9.6 %collective-permute-start.3 = (bf16[256,512]{1,0:T(8,128)(2,1)}, bf16[256,512]{1,0:T(8,128)(2,1)}, u32[]{:S(2)}, u32[]{:S(2)}) collective-permute-start(bf16[256,512]{1,0:T(8,128)(2,1)} %get-tuple-element.41), channel_id=1, source_target_pairs={{0,64},{16,80},{32,96},{48,112},{64,128},{80,144},{96,160},{112,17... | collective-permute-start | bytes 786440 | tf_op jit(solution)/shard_map/ppermute | solution.py:369
  105.8 11.0 %collective-permute-start.4 = (bf16[256,512]{1,0:T(8,128)(2,1)}, bf16[256,512]{1,0:T(8,128)(2,1)}, u32[]{:S(2)}, u32[]{:S(2)}) collective-permute-start(bf16[256,512]{1,0:T(8,128)(2,1)} %get-tuple-element.43), channel_id=1, source_target_pairs={{0,128},{16,144},{32,160},{48,176},{64,192},{80,208},{96,224},{112... | collective-permute-start | bytes 786440 | tf_op jit(solution)/shard_map/ppermute | solution.py:369
  106.9 13.7 %collective-permute-start.5 = (bf16[256,512]{1,0:T(8,128)(2,1)S(1)}, bf16[256,512]{1,0:T(8,128)(2,1)}, u32[]{:S(2)}, u32[]{:S(2)}) collective-permute-start(bf16[256,512]{1,0:T(8,128)(2,1)S(1)} %get-tuple-element.42), channel_id=1, source_target_pairs={{0,192},{16,208},{32,224},{48,240},{64,0},{80,16},{96,32},{112,48}... | collective-permute-start | bytes 786440 | tf_op jit(solution)/shard_map/ppermute | solution.py:369
  109.1 1.0 copy-start.1
  110.2 1.2 copy-start.8
  112.9 1.0 copy-start.6
  122.8 46.9 %all-to-all-start.3 = ((bf16[16,64,512]{2,1,0:T(8,128)(2,1)}), bf16[16,64,512]{2,1,0:T(8,128)(2,1)S(1)}, u32[]{:S(2)}, u32[]{:S(2)}) async-start(bf16[16,64,512]{2,1,0:T(8,128)(2,1)} %bitcast.58), calls=%async_computation.3 | async-start | bytes 2097152 | tf_op jit(solution)/shard_map/all_to_all | solution.py:352
  133.4 36.3 %collective-permute-start.6 = (bf16[64,64,128]{2,1,0:T(8,128)(2,1)}, bf16[64,64,128]{2,1,0:T(8,128)(2,1)S(1)}, u32[]{:S(2)}, u32[]{:S(2)}) collective-permute-start(bf16[64,64,128]{2,1,0:T(8,128)(2,1)} %get-tuple-element.33), channel_id=1, source_target_pairs={{0,16},{16,32},{32,48},{48,64},{64,80},{80,96},{96,112},{112,128},... | collective-permute-start | bytes 3145736 | tf_op jit(solution)/shard_map/ppermute | solution.py:348
  136.8 32.9 %collective-permute-start.7 = (bf16[64,64,128]{2,1,0:T(8,128)(2,1)}, bf16[64,64,128]{2,1,0:T(8,128)(2,1)S(1)}, u32[]{:S(2)}, u32[]{:S(2)}) collective-permute-start(bf16[64,64,128]{2,1,0:T(8,128)(2,1)} %get-tuple-element.34), channel_id=1, source_target_pairs={{16,0},{32,16},{48,32},{64,48},{80,64},{96,80},{112,96},{128,112},... | collective-permute-start | bytes 3145736 | tf_op jit(solution)/shard_map/ppermute | solution.py:348
  142.9 25.8 %collective-permute-start.10 = (bf16[64,512]{1,0:T(8,128)(2,1)S(1)}, bf16[64,512]{1,0:T(8,128)(2,1)S(1)}, u32[]{:S(2)}, u32[]{:S(2)}) collective-permute-start(bf16[64,512]{1,0:T(8,128)(2,1)S(1)} %get-tuple-element.45), channel_id=1, source_target_pairs={{0,48},{16,0},{32,16},{48,32},{64,112},{80,64},{96,80},{112,96},{1... | collective-permute-start | bytes 196616 | tf_op jit(solution)/shard_map/ppermute | solution.py:369
  145.0 23.7 %collective-permute-start.8 = (bf16[64,512]{1,0:T(8,128)(2,1)S(1)}, bf16[64,512]{1,0:T(8,128)(2,1)S(1)}, u32[]{:S(2)}, u32[]{:S(2)}) collective-permute-start(bf16[64,512]{1,0:T(8,128)(2,1)S(1)} %get-tuple-element.44), channel_id=1, source_target_pairs={{0,16},{16,32},{32,48},{48,0},{64,80},{80,96},{96,112},{112,64},{1... | collective-permute-start | bytes 196616 | tf_op jit(solution)/shard_map/ppermute | solution.py:369
  145.0 23.7 %collective-permute-start.9 = (bf16[64,512]{1,0:T(8,128)(2,1)S(1)}, bf16[64,512]{1,0:T(8,128)(2,1)S(1)}, u32[]{:S(2)}, u32[]{:S(2)}) collective-permute-start(bf16[64,512]{1,0:T(8,128)(2,1)S(1)} %get-tuple-element.46), channel_id=1, source_target_pairs={{0,32},{16,48},{32,0},{48,16},{64,96},{80,112},{96,64},{112,80},{1... | collective-permute-start | bytes 196616 | tf_op jit(solution)/shard_map/ppermute | solution.py:369
  170.4 15.7 %all-to-all-start.4 = ((f32[16,4,512]{2,1,0:T(4,128)}), f32[16,4,512]{2,1,0:T(4,128)S(1)}, u32[]{:S(2)}, u32[]{:S(2)}) async-start(f32[16,4,512]{2,1,0:T(4,128)} %reshape.48), calls=%async_computation.4 | async-start | bytes 262144 | tf_op jit(solution)/shard_map/all_to_all | solution.py:352
  177.4 1.6 copy-start.7

commit v5 on v4

--- a/solution.py
+++ b/solution.py
@@ -13,6 +13,9 @@
 NN = (((1,), (0,)), ((), ()))
 MIB = 1 << 20
 DENSE_MIB = 60
+OWN_MIB = 60
+WEIGHT_MIB = 60
+FINAL_MIB = 60
 
 
 def dot(a, b, dims=NN):
@@ -189,16 +192,16 @@
 
 
 def dense_kernel(chunk, *refs):
-    (tiles_hbm, turned_hbm, x_hbm, picked_hbm, w_neigh_hbm, pre_hbm, cot_hbm, w_back_hbm) = refs[:8]
-    (agg_hbm, hidden_hbm, dpre_hbm, dagg_hbm, second_hbm) = refs[8:13]
-    (tiles, turned, x_ref, picked, w_neigh, pre_ref, cot_ref, w_back) = refs[13:21]
-    (agg, hidden, dpre, dagg, second, in_sems, out_sems) = refs[21:]
+    half_ref, sources, targets, held = refs[0], refs[1:9], refs[9:15], refs[15:23]
+    (agg_hbm, hidden_hbm, dpre_hbm, dagg_hbm, second_hbm, sent_hbm) = targets
+    (tiles, turned, x_ref, picked, w_neigh, pre_ref, cot_ref, w_back) = held
+    (agg, hidden, dpre, dagg, second, sent, in_sems, out_sems) = refs[23:]
     size = w_neigh.shape[0]
     pair = tiles.shape[-1]
     part = [slice(i, i + chunk) for i in range(0, size, chunk)]
     here = [slice(i, i + pair) for i in range(0, agg.shape[1], pair)]
     loads = [
-        pltpu.make_async_copy(refs[k], refs[13 + k], in_sems.at[k]) for k in (0, 2, 3, 4, 5, 6, 7, 1)
+        pltpu.make_async_copy(sources[k], held[k], in_sems.at[k]) for k in (0, 2, 3, 4, 5, 6, 7, 1)
     ]
     for copy in loads:
         copy.start()
@@ -235,110 +238,139 @@
             second[part[i], here[p]] = dot(dagg[part[i], here[p]], turned[1, p]).astype(BF16)
         store(3, dagg, dagg_hbm, i)
         store(4, second, second_hbm, i)
+    width = sent.shape[1]
+    half = agg.at[pl.ds(pl.multiple_of(half_ref[0] * width, width), width)]
+    for i in range(len(part)):
+        sent[part[i], :] = dot(dpre[part[i], :], half[...], NT).astype(BF16)
+        store(5, sent, sent_hbm, i)
     for copy in stores:
         copy.wait()
 
 
-def dense(tiles, turned, x_rows, picked, w_neigh, pre_self, cot, w_back):
+def dense(half, tiles, turned, x_rows, picked, w_neigh, pre_self, cot, w_back):
     size, width = picked.shape
     chunk = 256
     out = jax.ShapeDtypeStruct((size, width), BF16)
     args = (tiles, turned, x_rows, picked, w_neigh, pre_self, cot, w_back)
     return pl.pallas_call(
         functools.partial(dense_kernel, chunk),
-        in_specs=[ANYWHERE] * len(args),
-        out_specs=[ANYWHERE] * 5,
-        out_shape=[out] * 5,
+        in_specs=[SMEM] + [ANYWHERE] * len(args),
+        out_specs=[ANYWHERE] * 6,
+        out_shape=[out] * 5 + [jax.ShapeDtypeStruct((size, size // CORES), BF16)],
         scratch_shapes=[pltpu.VMEM(arg.shape, arg.dtype) for arg in args]
         + [pltpu.VMEM((size, width), BF16)] * 5
-        + [pltpu.SemaphoreType.DMA((len(args),)), pltpu.SemaphoreType.DMA((5, size // chunk))],
+        + [pltpu.VMEM((size, size // CORES), BF16)]
+        + [pltpu.SemaphoreType.DMA((len(args),)), pltpu.SemaphoreType.DMA((6, size // chunk))],
         compiler_params=whole_params(DENSE_MIB),
         cost_estimate=pl.CostEstimate(
             flops=4 * size * size * width, bytes_accessed=16 * MIB, transcendentals=size * width
         ),
-    )(*args)
+    )(half, *args)
+
+
+EXTRA = 8
 
 
 def own_kernel(chunk, w_back, dpre, dagg_ref, turned, own):
     pair = turned.shape[-1]
-    for i in range(0, own.shape[0], chunk):
+    each = own.shape[1] - EXTRA
+    for i in range(0, dpre.shape[0], chunk):
         rows = slice(i, i + chunk)
         dself = dot(w_back[rows, :], dpre[...])
-        for p in range(own.shape[1] // pair):
+        for p in range(own.shape[2] // pair):
             here = slice(p * pair, (p + 1) * pair)
             total = dself[:, here] + dot(dagg_ref[rows, here], turned[0, p])
-            own[rows, here] = total.astype(BF16)
-
-
-def own_part(w_back, dpre, dagg, turned):
+            for g in range(chunk // each):
+                own[i // each + g, :each, here] = total[g * each : (g + 1) * each].astype(BF16)
+
+
+def own_part(w_back, dpre, dagg, turned, groups):
     size, width = dpre.shape
     return pl.pallas_call(
         functools.partial(own_kernel, 256),
         in_specs=[VMEM] * 4,
         out_specs=VMEM,
-        out_shape=jax.ShapeDtypeStruct((size, width), BF16),
-        compiler_params=whole_params(12),
+        out_shape=jax.ShapeDtypeStruct((groups, size // groups + EXTRA, width), BF16),
+        compiler_params=whole_params(OWN_MIB),
         cost_estimate=pl.CostEstimate(
             flops=2 * size * size * width, bytes_accessed=5 * MIB, transcendentals=0
         ),
     )(w_back, dpre, dagg, turned)
 
 
-def weight_kernel(chunk, half_ref, dpre, agg_ref, grad):
-    rows = grad.shape[1]
-    half = agg_ref.at[pl.ds(pl.multiple_of(half_ref[0] * rows, rows), rows)]
-    for i in range(grad.shape[0] // chunk):
-        here = slice(i * chunk, (i + 1) * chunk)
-        grad[here, :] = dot(dpre[here, :], half[...], NT).astype(BF16)
-
-
-def weight_sum_kernel(chunk, half_ref, dpre, agg_ref, other_ref, grad):
-    rows = grad.shape[1]
-    half = agg_ref.at[pl.ds(pl.multiple_of(half_ref[0] * rows, rows), rows)]
-    for i in range(grad.shape[0] // chunk):
-        here = slice(i * chunk, (i + 1) * chunk)
+def weight_kernel(index_ref, dpre, agg_ref, other_ref, *outs):
+    core, me = index_ref[0], index_ref[1]
+    rows, width = outs[0].shape
+    half = agg_ref.at[pl.ds(pl.multiple_of(core * width, width), width)]
+    for step, out in enumerate(outs):
+        here = pl.ds(pl.multiple_of(lax.rem(me + step, len(outs)) * rows, rows), rows)
         total = dot(dpre[here, :], half[...], NT) + other_ref[here, :].astype(F32)
-        grad[here, :] = total.astype(BF16)
-
-
-def weight_part(half, dpre, agg_rows, other=None):
+        out[...] = total.astype(out.dtype)
+
+
+def weight_pieces(core, me, dpre, agg_rows, other):
     size, width = dpre.shape
-    body = weight_kernel if other is None else weight_sum_kernel
-    more = () if other is None else (other,)
-    return pl.pallas_call(
-        functools.partial(body, 256),
-        in_specs=[SMEM] + [VMEM] * (2 + len(more)),
-        out_specs=VMEM,
-        out_shape=jax.ShapeDtypeStruct((size, size // CORES), BF16),
-        compiler_params=whole_params(12),
+    shape = (size // SIDE, size // CORES)
+    return pl.pallas_call(
+        weight_kernel,
+        in_specs=[SMEM] + [VMEM] * 3,
+        out_specs=[VMEM] * SIDE,
+        out_shape=[jax.ShapeDtypeStruct(shape, F32)]
+        + [jax.ShapeDtypeStruct(shape, BF16)] * (SIDE - 1),
+        compiler_params=whole_params(WEIGHT_MIB),
         cost_estimate=pl.CostEstimate(
-            flops=size * size * width, bytes_accessed=3 * MIB, transcendentals=0
+            flops=size * size * width, bytes_accessed=4 * MIB, transcendentals=0
         ),
-    )(half, dpre, agg_rows, *more)
+    )(jnp.stack([core, me]), dpre, agg_rows, other)
+
+
+def add_kernel(index_ref, *refs):
+    parts, outs = refs[:SIDE], refs[SIDE:]
+    rows = outs[0].shape[0]
+    for step, out in enumerate(outs):
+        here = pl.ds(pl.multiple_of(lax.rem(index_ref[0] + step, SIDE) * rows, rows), rows)
+        total = parts[0][here, :]
+        for part in parts[1:]:
+            total = total + part[here, :].astype(F32)
+        out[...] = total.astype(out.dtype)
+
+
+def added_pieces(me, parts):
+    rows, width = parts[0].shape
+    shape = (rows // SIDE, width)
+    return pl.pallas_call(
+        add_kernel,
+        in_specs=[SMEM] + [VMEM] * SIDE,
+        out_specs=[VMEM] * SIDE,
+        out_shape=[jax.ShapeDtypeStruct(shape, F32)]
+        + [jax.ShapeDtypeStruct(shape, BF16)] * (SIDE - 1),
+        compiler_params=whole_params(WEIGHT_MIB),
+        cost_estimate=pl.CostEstimate(flops=0, bytes_accessed=2 * MIB, transcendentals=0),
+    )(me[None], *parts)
 
 
 def final_kernel(own_ref, before_ref, after_ref, dself_ref, out_ref):
     tile = own_ref.shape[2]
     per = dself_ref.shape[2] // tile
     for b in range(own_ref.shape[0]):
-        grad = dself_ref[b // per, :, (b % per) * tile : (b % per + 1) * tile]
+        grad = dself_ref[b // per, : own_ref.shape[1], (b % per) * tile : (b % per + 1) * tile]
         total = own_ref[b] + before_ref[b].astype(F32) + after_ref[b].astype(F32)
         out_ref[:, b * tile : (b + 1) * tile] = (grad.astype(F32) + total).astype(BF16)
 
 
 def finish(own, before, after, dself):
-    groups, rows, width = dself.shape
-    blocks, _, tile = own.shape
+    groups, high, width = dself.shape
+    blocks, rows, tile = own.shape
     steps = 4
     part = pl.BlockSpec((blocks // steps, rows, tile), lambda g: (g, 0, 0))
     return pl.pallas_call(
         final_kernel,
         grid=(steps,),
         in_specs=[part, part, part]
-        + [pl.BlockSpec((groups // steps, rows, width), lambda g: (g, 0, 0))],
+        + [pl.BlockSpec((groups // steps, high, width), lambda g: (g, 0, 0))],
         out_specs=pl.BlockSpec((rows, groups * width // steps), lambda g: (0, g)),
         out_shape=jax.ShapeDtypeStruct((rows, groups * width), BF16),
-        compiler_params=params(16),
+        compiler_params=params(FINAL_MIB),
     )(own, before, after, dself)
 
 
@@ -356,42 +388,34 @@
 CORES = 2
 
 
-def piece_at(pieces, index):
-    return lax.dynamic_index_in_dim(pieces, index, 0, keepdims=False)
-
-
-def exchange_sum(value, axis, count, index, partner, sent):
-    pieces = value.reshape(count, -1, value.shape[-1])
-    total = piece_at(pieces, index).astype(F32)
-    for step in range(1, count):
-        piece = piece_at(pieces, lax.rem(index + step, count)).astype(sent)
-        pairs = [(i, partner(i, step)) for i in range(lax.axis_size(axis))]
-        total = total + lax.ppermute(piece, axis, pairs).astype(F32)
-    return total
-
-
-def after(value, other):
-    return lax.optimization_barrier((value, other))[0]
-
-
-def weight_first(dpre, agg_rows):
+def sent_round(pieces, axis, partner):
+    count = lax.axis_size(axis)
+    return [pieces[0]] + [
+        lax.ppermute(piece, axis, [(i, partner(i, step + 1)) for i in range(count)])
+        for step, piece in enumerate(pieces[1:])
+    ]
+
+
+def weight_rows(sent, dpre, agg_rows, groups):
     feat, node = lax.axis_index("feat"), lax.axis_index("node")
-    core = lax.rem(feat, CORES)
-    pairs = [(i, i ^ 1) for i in range(lax.axis_size("feat"))]
-    sent = weight_part(1 - core[None], dpre, agg_rows)
-    value = weight_part(core[None], dpre, agg_rows, lax.ppermute(sent, "feat", pairs))
-    x = lambda i, s: (i + s * SIDE) % (SIDE * SIDE)
-    return exchange_sum(value, "node", SIDE, lax.div(node, SIDE), x, BF16)
-
-
-def weight_rest(value, last):
-    node, groups = lax.axis_index("node"), lax.axis_size("feat")
-    y = lambda i, s: i // SIDE * SIDE + (i + s) % SIDE
-    value = exchange_sum(value, "node", SIDE, lax.rem(node, SIDE), y, BF16)
-    value = after(value, last)
-    rows, half = value.shape
-    pieces = exchange(value.reshape(groups, rows // groups, half), "feat")
-    total = jnp.sum(pieces.reshape(groups // CORES, CORES, rows // groups, half), axis=0)
+    other = lax.ppermute(sent, "feat", [(i, i ^ 1) for i in range(groups)])
+    pieces = weight_pieces(lax.rem(feat, CORES), lax.div(node, SIDE), dpre, agg_rows, other)
+    parts = sent_round(pieces, "node", lambda i, s: (i + s * SIDE) % (SIDE * SIDE))
+    pieces = added_pieces(lax.rem(node, SIDE), parts)
+    parts = sent_round(pieces, "node", lambda i, s: i // SIDE * SIDE + (i + s) % SIDE)
+    total = parts[0]
+    for part in parts[1:]:
+        total = total + part.astype(F32)
+    total = total.reshape(groups, EXTRA // 2, -1)
+    high = total.astype(BF16)
+    low = (total - high.astype(F32)).astype(BF16)
+    return jnp.concatenate([high, low], axis=1)
+
+
+def weight_total(rows):
+    groups, count, width = rows.shape
+    rows = rows.astype(F32).reshape(groups // CORES, CORES, 2, count // 2, width)
+    total = jnp.sum(rows, axis=(0, 2))
     return jnp.concatenate([total[i] for i in range(CORES)], axis=1)
 
 
@@ -427,18 +451,19 @@
         (x_rows, w_self.T, w_neigh.T, straight, turned)
     )
     pre_self = self_product(w_self, x_rows)
-    agg_rows, hidden, dpre, dagg, second = dense(
-        straight, turned, x_rows, picked, w_neigh, pre_self, cotangent, neigh_back
+    core = lax.rem(feat, CORES)
+    agg_rows, hidden, dpre, dagg, second, sent = dense(
+        1 - core[None], straight, turned, x_rows, picked, w_neigh, pre_self, cotangent, neigh_back
     )
     second_cols = exchange(second.reshape(groups, feat_dev, -1), "feat")
-    own_rows = own_part(self_back, dpre, dagg, turned)
-    weight = weight_first(dpre, agg_rows)
-    second_cols, own_rows, weight = lax.optimization_barrier((second_cols, own_rows, weight))
-    own_cols = exchange(own_rows.reshape(groups, feat_dev, -1), "feat")
+    own_rows = own_part(self_back, dpre, dagg, turned, groups)
+    weight = weight_rows(sent, dpre, agg_rows, groups)
+    own_rows = lax.dynamic_update_slice(own_rows, weight, (0, feat_dev, 0))
+    own_cols = exchange(own_rows, "feat")
     to_before, spread, to_after = scatter(col, second_cols)
     from_after = shifted(to_before, "node", -1)
     from_before = shifted(to_after, "node", 1)
-    grad_w_neigh = weight_rest(after(weight, spread), (from_after, from_before, own_cols))
+    grad_w_neigh = weight_total(own_cols[:, feat_dev:])
     grad_features = finish(spread, from_before, from_after, own_cols)
     return (hidden, grad_features, grad_w_neigh)
 

time: 190 us -> 180 us (0.947)
  local copies, waits for them, and re-layouts: 22.4 us -> 13.9 us
  Pallas kernels: 28.8 us -> 37 us
  starting transfers between devices: 59.6 us -> 54.9 us
  waiting for transfers between devices: 70 us -> 66.8 us
    ppermute x7, waiting for transfers between devices: 31.6 us -> 11.6 us  [the longest x6 11.6 us: sent_round(): lax.ppermute(piece, axis, [(i, partner(i, step + 1)) for i in range(count)])]
    all_to_all x5 -> x4, waiting for transfers between devices: 15.8 us -> 29 us  [exchange(): return lax.all_to_all(value, axis, split_axis=0, concat_axis=0, tiled=True)]
    all_to_all x5 -> x4, starting transfers between devices: 33.8 us -> 26.4 us  [exchange(): return lax.all_to_all(value, axis, split_axis=0, concat_axis=0, tiled=True)]
    unnamed x30 -> x34, local copies, waits for them, and re-layouts: 16.3 us -> 10.5 us
    ppermute x4, waiting for transfers between devices: 22.6 us -> 26.2 us  [shifted(): lax.ppermute(value, axis, [(source, source + steps) for source in range(f...]
    pallas_call x1, Pallas kernels: 1.51 us -> 4.88 us  [own_part(): pl.pallas_call(functools.partial(own_kernel, 256), in_specs=[VMEM] * 4, o...]
    ppermute x7, starting transfers between devices: 9.51 us -> 12.6 us  [the longest x6 10.9 us: sent_round(): lax.ppermute(piece, axis, [(i, partner(i, step + 1)) for i in range(count)])]
    add x2 -> x1, other arithmetic: 3.03 us -> 0.03 us  [weight_rows(): total = total + part.astype(F32)]
  transfers between devices with their start and end apart: 16 -> 15, of which waited for: 8 -> 9; matrix products, arithmetic and copies ran while one was open for 9% -> 8% of each run, Pallas kernels for 10% -> 12%
where the time goes in v5:
time: 180 us; the launch traced here: 178 us
  waiting for transfers between devices  66.8 us (37%)
  starting transfers between devices  54.9 us (30%)
  Pallas kernels  37 us (21%)
  local copies, waits for them, and re-layouts  13.9 us (8%)
  other arithmetic  4 us (2%)
    all_to_all x4, waiting for transfers between devices, exchange(): return lax.all_to_all(value, axis, split_axis=0, concat_axis=0, tiled=True)  29 us
    all_to_all x4, starting transfers between devices, exchange(): return lax.all_to_all(value, axis, split_axis=0, concat_axis=0, tiled=True)  26.4 us
    ppermute x4, waiting for transfers between devices, shifted(): lax.ppermute(value, axis, [(source, source + steps) for source in range(f...  26.2 us
    ppermute x4, starting transfers between devices, shifted(): lax.ppermute(value, axis, [(source, source + steps) for source in range(f...  15.9 us
    ppermute x6, waiting for transfers between devices, sent_round(): lax.ppermute(piece, axis, [(i, partner(i, step + 1)) for i in range(count)])  11.6 us
    ppermute x6, starting transfers between devices, sent_round(): lax.ppermute(piece, axis, [(i, partner(i, step + 1)) for i in range(count)])  10.9 us
    unnamed x34, local copies, waits for them, and re-layouts  10.5 us
    pallas_call x1, Pallas kernels, dense(): pl.pallas_call(functools.partial(dense_kernel, chunk), in_specs=[SMEM] +...  8.56 us
  transfers between devices with their start and end apart: 15, of which 9 were waited for; matrix products, arithmetic and copies ran while one was open for 8% of the time, Pallas kernels for 12%

profile of v5, /device:TPU:2, one launch (start us, length us, event | category | flops | bytes accessed | tf_op | source)
XLA Modules:
  0.0 177.6 jit_solution(9660776678156119014)
XLA Ops:
  0.6 2.2 %shard_map.94 = bf16[16,64,512]{2,1,0:T(8,128)(2,1)} custom-call(bf16[64,8192]{1,0:T(8,128)(2,1)} %own.1), custom_call_target="tpu_custom_call" | custom-call | tf_op jit(solution)/shard_map/pallas_call | solution.py:59
  2.9 8.6 %all-to-all-start = ((bf16[16,64,512]{2,1,0:T(8,128)(2,1)}), bf16[16,64,512]{2,1,0:T(8,128)(2,1)}, u32[]{:S(2)}, u32[]{:S(2)}) async-start(bf16[16,64,512]{2,1,0:T(8,128)(2,1)} %shard_map.94), calls=%async_computation | async-start | bytes 2097152 | tf_op jit(solution)/shard_map/all_to_all | solution.py:384
  11.5 3.5 %collective-permute-start = (bf16[64,8192]{1,0:T(8,128)(2,1)S(1)}, bf16[64,8192]{1,0:T(8,128)(2,1)S(1)}, u32[]{:S(2)}, u32[]{:S(2)}) collective-permute-start(bf16[64,8192]{1,0:T(8,128)(2,1)S(1)} %copy-done), channel_id=1, source_target_pairs={{0,16},{16,32},{32,48},{48,64},{64,80},{80,96},{96,112},{112,128},... | collective-permute-start | bytes 3145736 | tf_op jit(solution)/shard_map/ppermute | solution.py:380
  15.0 4.5 %collective-permute-start.1 = (bf16[64,8192]{1,0:T(8,128)(2,1)S(1)}, bf16[64,8192]{1,0:T(8,128)(2,1)S(1)}, u32[]{:S(2)}, u32[]{:S(2)}) collective-permute-start(bf16[64,8192]{1,0:T(8,128)(2,1)S(1)} %copy-done), channel_id=1, source_target_pairs={{16,0},{32,16},{48,32},{64,48},{80,64},{96,80},{112,96},{128,112},... | collective-permute-start | bytes 3145736 | tf_op jit(solution)/shard_map/ppermute | solution.py:380
  19.6 21.4 %collective-permute-done.before = bf16[64,8192]{1,0:T(8,128)(2,1)S(1)} collective-permute-done((bf16[64,8192]{1,0:T(8,128)(2,1)S(1)}, bf16[64,8192]{1,0:T(8,128)(2,1)S(1)}, u32[]{:S(2)}, u32[]{:S(2)}) %collective-permute-start) | collective-permute-done | bytes 1048608 | tf_op jit(solution)/shard_map/ppermute | solution.py:380
  42.2 2.9 %shard_map.95 = bf16[16,64,512]{2,1,0:T(8,128)(2,1)} custom-call(s32[64]{0:T(128)S(1)} %subtract_bitcast_fusion.col_ref, bf16[64,8192]{1,0:T(8,128)(2,1)S(1)} %collective-permute-done.before, bf16[64,8192]{1,0:T(8,128)(2,1)S(1)} %copy-done, bf16[64,8192]{1,0:T(8,128)(2,1)S(1)} %collective-permute-done.1.after), custom_call_target="tpu_custom_call" | custom-call | bytes 8388608 | tf_op jit(solution)/shard_map/pallas_call | solution.py:103
  45.1 7.1 %all-to-all-start.1 = ((bf16[16,64,512]{2,1,0:T(8,128)(2,1)}), bf16[16,64,512]{2,1,0:T(8,128)(2,1)S(1)}, u32[]{:S(2)}, u32[]{:S(2)}) async-start(bf16[16,64,512]{2,1,0:T(8,128)(2,1)} %shard_map.95), calls=%async_computation.1 | async-start | bytes 2097152 | tf_op jit(solution)/shard_map/all_to_all | solution.py:384
  53.9 2.6 %copy.14 = bf16[1024,1024]{0,1:T(8,128)(2,1)} copy(bf16[1024,1024]{1,0:T(8,128)(2,1)S(1)} %copy-done.2) | data formatting | bytes 4194304 | tf_op args[4]
  56.5 3.9 %copy.15 = bf16[1024,1024]{0,1:T(8,128)(2,1)} copy(bf16[1024,1024]{1,0:T(8,128)(2,1)} %refs_5_.1) | data formatting | bytes 4194304 | tf_op args[5]
  62.5 4.5 %shard_map.96.refs_6_ = f32[1024,512]{1,0:T(8,128)} custom-call(bf16[1024,1024]{1,0:T(8,128)(2,1)} %w_self.1, bf16[1024,512]{1,0:T(8,128)(2,1)} %bitcast.1.x_ref.refs_3_), custom_call_target="tpu_custom_call" | custom-call | flops 1073741824 | bytes 5242880 | tf_op jit(solution)/shard_map/pallas_call | solution.py:182
  67.0 11.8 %all-to-all-done.1 = bf16[16,64,512]{2,1,0:T(8,128)(2,1)S(1)} async-done(((bf16[16,64,512]{2,1,0:T(8,128)(2,1)}), bf16[16,64,512]{2,1,0:T(8,128)(2,1)S(1)}, u32[]{:S(2)}, u32[]{:S(2)}) %all-to-all-start.1) | async-done | bytes 1048608 | tf_op jit(solution)/shard_map/all_to_all | solution.py:384
  79.8 8.6 %shard_map.97 = (bf16[1024,512]{1,0:T(8,128)(2,1)}, bf16[1024,512]{1,0:T(8,128)(2,1)}, bf16[1024,512]{1,0:T(8,128)(2,1)}, bf16[1024,512]{1,0:T(8,128)(2,1)}, bf1...) custom-call(s32[1]{0:T(128)S(6)} %sub.17.refs_0_, bf16[2,2,256,256]{3,2,1,0:T(8,128)(2,1)} %copy.21.refs_1_, ...), custom_call_target="tpu_custom_call" | custom-call | flops 2147483648 | bytes 16777216 | tf_op jit(solution)/shard_map/pallas_call | solution.py:255
  88.4 1.8 collective-permute-start.4
  90.1 3.7 %all-to-all-start.2 = ((bf16[16,64,512]{2,1,0:T(8,128)(2,1)}), bf16[16,64,512]{2,1,0:T(8,128)(2,1)S(1)}, u32[]{:S(2)}, u32[]{:S(2)}) async-start(bf16[16,64,512]{2,1,0:T(8,128)(2,1)} %bitcast.35), calls=%async_computation.2 | async-start | bytes 2097152 | tf_op jit(solution)/shard_map/all_to_all | solution.py:384
  95.4 3.3 %shard_map.100 = (f32[256,512]{1,0:T(8,128)}, bf16[256,512]{1,0:T(8,128)(2,1)}, bf16[256,512]{1,0:T(8,128)(2,1)}, bf16[256,512]{1,0:T(8,128)(2,1)}) custom-call(s32[2]{0:T(128)} %pad_add_fusion.index_ref, bf16[1024,512]{1,0:T(8,128)(2,1)} %get-tuple-element.35.dpre, bf16[1024,512]{1,0:T(8,128)(2,1)} %get-tuple-element.37.agg_ref, bf16[1024,512]{1,0:T(8,128)(2,1)} %copy-done.8), custom_call_target="tpu_custom_call" | custom-call | flops 536870912 | bytes 4194304 | tf_op jit(solution)/shard_map/pallas_call | solution.py:314
  98.7 1.5 collective-permute-start.5
  101.3 2.2 %collective-permute-start.7 = (bf16[256,512]{1,0:T(8,128)(2,1)}, bf16[256,512]{1,0:T(8,128)(2,1)S(1)}, u32[]{:S(2)}, u32[]{:S(2)}) collective-permute-start(bf16[256,512]{1,0:T(8,128)(2,1)} %get-tuple-element.42), channel_id=1, source_target_pairs={{0,192},{16,208},{32,224},{48,240},{64,0},{80,16},{96,32},{112,48}... | collective-permute-start | bytes 786440 | tf_op jit(solution)/shard_map/ppermute | solution.py:394
  103.5 4.6 %collective-permute-done.5.refs_1_ = bf16[256,512]{1,0:T(8,128)(2,1)S(1)} collective-permute-done((bf16[256,512]{1,0:T(8,128)(2,1)}, bf16[256,512]{1,0:T(8,128)(2,1)S(1)}, u32[]{:S(2)}, u32[]{:S(2)}) %collective-permute-start.5) | collective-permute-done | bytes 262176 | tf_op jit(solution)/shard_map/ppermute | solution.py:394
  108.1 3.1 %collective-permute-done.6.refs_2_ = bf16[256,512]{1,0:T(8,128)(2,1)S(1)} collective-permute-done((bf16[256,512]{1,0:T(8,128)(2,1)}, bf16[256,512]{1,0:T(8,128)(2,1)S(1)}, u32[]{:S(2)}, u32[]{:S(2)}) %collective-permute-start.6) | collective-permute-done | bytes 262176 | tf_op jit(solution)/shard_map/ppermute | solution.py:394
  111.1 3.9 %collective-permute-done.7.refs_3_ = bf16[256,512]{1,0:T(8,128)(2,1)S(1)} collective-permute-done((bf16[256,512]{1,0:T(8,128)(2,1)}, bf16[256,512]{1,0:T(8,128)(2,1)S(1)}, u32[]{:S(2)}, u32[]{:S(2)}) %collective-permute-start.7) | collective-permute-done | bytes 262176 | tf_op jit(solution)/shard_map/ppermute | solution.py:394
  115.8 2.1 %shard_map.101 = (f32[64,512]{1,0:T(8,128)}, bf16[64,512]{1,0:T(8,128)(2,1)}, bf16[64,512]{1,0:T(8,128)(2,1)}, bf16[64,512]{1,0:T(8,128)(2,1)}) custom-call(s32[1]{0:T(128)} %bitcast.16.index_ref, f32[256,512]{1,0:T(8,128)} %get-tuple-element.39.refs_0_, bf16[256,512]{1,0:T(8,128)(2,1)} %copy-done.9, bf16[256,512]{1,0:T(8,128)(2,1)} %copy-done.10, ...), custom_call_target="tpu_custom_call" | custom-call | bytes 2097152 | tf_op jit(solution)/shard_map/pallas_call | solution.py:341
  117.9 1.5 collective-permute-start.8
  119.4 4.6 %collective-permute-start.9 = (bf16[64,512]{1,0:T(8,128)(2,1)}, bf16[64,512]{1,0:T(8,128)(2,1)S(1)}, u32[]{:S(2)}, u32[]{:S(2)}) collective-permute-start(bf16[64,512]{1,0:T(8,128)(2,1)} %get-tuple-element.45), channel_id=1, source_target_pairs={{0,32},{16,48},{32,0},{48,16},{64,96},{80,112},{96,64},{112,80},{1... | collective-permute-start | bytes 196616 | tf_op jit(solution)/shard_map/ppermute | solution.py:394
  124.0 4.9 %shard_map.99 = bf16[16,72,512]{2,1,0:T(8,128)(2,1)} custom-call(bf16[1024,1024]{1,0:T(8,128)(2,1)} %bitcast.32, bf16[1024,512]{1,0:T(8,128)(2,1)} %get-tuple-element.35.dpre, bf16[1024,512]{1,0:T(8,128)(2,1)} %get-tuple-element.36.dagg_ref, bf16[2,2,256,256]{3,2,1,0:T(8,128)(2,1)} %get-tuple-element.26.refs_2_.turned), custom_call_target="tpu_custom_call" | custom-call | flops 1073741824 | bytes 5242880 | tf_op jit(solution)/shard_map/pallas_call | solution.py:289
  129.7 7.0 %all-to-all-start.3 = ((bf16[16,72,512]{2,1,0:T(8,128)(2,1)}), bf16[16,72,512]{2,1,0:T(8,128)(2,1)S(1)}, u32[]{:S(2)}, u32[]{:S(2)}) async-start(bf16[16,72,512]{2,1,0:T(8,128)(2,1)} %maximum_dynamic-update-slice_fusion), calls=%async_computation.3 | async-start | bytes 2359296 | tf_op jit(solution)/shard_map/all_to_all | solution.py:384
  136.8 4.3 %shard_map.98 = (bf16[64,64,128]{2,1,0:T(8,128)(2,1)}, f32[64,64,128]{2,1,0:T(8,128)}, bf16[64,64,128]{2,1,0:T(8,128)(2,1)}) custom-call(s32[64]{0:T(128)} %copy-done.1, bf16[16,64,512]{2,1,0:T(8,128)(2,1)} %copy-done.4), custom_call_target="tpu_custom_call" | custom-call | bytes 8388608 | tf_op jit(solution)/shard_map/pallas_call | solution.py:154
  141.1 3.9 %collective-permute-start.2 = (bf16[64,64,128]{2,1,0:T(8,128)(2,1)}, bf16[64,64,128]{2,1,0:T(8,128)(2,1)S(1)}, u32[]{:S(2)}, u32[]{:S(2)}) collective-permute-start(bf16[64,64,128]{2,1,0:T(8,128)(2,1)} %get-tuple-element.32), channel_id=1, source_target_pairs={{0,16},{16,32},{32,48},{48,64},{64,80},{80,96},{96,112},{112,128},... | collective-permute-start | bytes 3145736 | tf_op jit(solution)/shard_map/ppermute | solution.py:380
  145.0 4.0 %collective-permute-start.3 = (bf16[64,64,128]{2,1,0:T(8,128)(2,1)}, bf16[64,64,128]{2,1,0:T(8,128)(2,1)S(1)}, u32[]{:S(2)}, u32[]{:S(2)}) collective-permute-start(bf16[64,64,128]{2,1,0:T(8,128)(2,1)} %get-tuple-element.33), channel_id=1, source_target_pairs={{16,0},{32,16},{48,32},{64,48},{80,64},{96,80},{112,96},{128,112},... | collective-permute-start | bytes 3145736 | tf_op jit(solution)/shard_map/ppermute | solution.py:380
  149.0 17.2 %all-to-all-done.3.dself_ref = bf16[16,72,512]{2,1,0:T(8,128)(2,1)S(1)} async-done(((bf16[16,72,512]{2,1,0:T(8,128)(2,1)}), bf16[16,72,512]{2,1,0:T(8,128)(2,1)S(1)}, u32[]{:S(2)}, u32[]{:S(2)}) %all-to-all-start.3) | async-done | bytes 1179680 | tf_op jit(solution)/shard_map/all_to_all | solution.py:384
  168.7 2.1 %collective-permute-done.2.before_ref = bf16[64,64,128]{2,1,0:T(8,128)(2,1)S(1)} collective-permute-done((bf16[64,64,128]{2,1,0:T(8,128)(2,1)}, bf16[64,64,128]{2,1,0:T(8,128)(2,1)S(1)}, u32[]{:S(2)}, u32[]{:S(2)}) %collective-permute-start.2) | collective-permute-done | bytes 1048608 | tf_op jit(solution)/shard_map/ppermute | solution.py:380
  170.8 1.5 collective-permute-done.3.after_ref
  173.3 4.3 %shard_map.102 = bf16[64,8192]{1,0:T(8,128)(2,1)} custom-call(f32[64,64,128]{2,1,0:T(8,128)} %get-tuple-element.31.own_ref, bf16[64,64,128]{2,1,0:T(8,128)(2,1)} %copy-done.6, bf16[64,64,128]{2,1,0:T(8,128)(2,1)} %copy-done.7, bf16[16,72,512]{2,1,0:T(8,128)(2,1)} %copy-done.3), custom_call_target="tpu_custom_call" | custom-call | tf_op jit(solution)/shard_map/pallas_call | solution.py:366
  (63 shorter events, 13.6 us)
Async XLA Ops:
  0.6 10.9 %copy-start = (bf16[64,8192]{1,0:T(8,128)(2,1)S(1)}, bf16[64,8192]{1,0:T(8,128)(2,1)}, u32[]{:S(2)}) copy-start(bf16[64,8192]{1,0:T(8,128)(2,1)} %own.1) | copy-start | bytes 3145732
  0.6 18.9 %copy-start.13 = (s32[64,2]{0,1:T(2,128)S(1)}, s32[64,2]{0,1:T(2,128)}, u32[]{:S(2)}) copy-start(s32[64,2]{0,1:T(2,128)} %param.9) | copy-start | bytes 1540
  2.9 42.2 %all-to-all-start = ((bf16[16,64,512]{2,1,0:T(8,128)(2,1)}), bf16[16,64,512]{2,1,0:T(8,128)(2,1)}, u32[]{:S(2)}, u32[]{:S(2)}) async-start(bf16[16,64,512]{2,1,0:T(8,128)(2,1)} %shard_map.94), calls=%async_computation | async-start | bytes 2097152 | tf_op jit(solution)/shard_map/all_to_all | solution.py:384
  11.5 29.4 %collective-permute-start = (bf16[64,8192]{1,0:T(8,128)(2,1)S(1)}, bf16[64,8192]{1,0:T(8,128)(2,1)S(1)}, u32[]{:S(2)}, u32[]{:S(2)}) collective-permute-start(bf16[64,8192]{1,0:T(8,128)(2,1)S(1)} %copy-done), channel_id=1, source_target_pairs={{0,16},{16,32},{32,48},{48,64},{64,80},{80,96},{96,112},{112,128},... | collective-permute-start | bytes 3145736 | tf_op jit(solution)/shard_map/ppermute | solution.py:380
  15.0 27.1 %collective-permute-start.1 = (bf16[64,8192]{1,0:T(8,128)(2,1)S(1)}, bf16[64,8192]{1,0:T(8,128)(2,1)S(1)}, u32[]{:S(2)}, u32[]{:S(2)}) collective-permute-start(bf16[64,8192]{1,0:T(8,128)(2,1)S(1)} %copy-done), channel_id=1, source_target_pairs={{16,0},{32,16},{48,32},{64,48},{80,64},{96,80},{112,96},{128,112},... | collective-permute-start | bytes 3145736 | tf_op jit(solution)/shard_map/ppermute | solution.py:380
  19.5 25.5 %copy-start.1 = (s32[64]{0:T(128)}, s32[64]{0:T(128)S(1)}, u32[]{:S(2)}) copy-start(s32[64]{0:T(128)S(1)} %subtract_bitcast_fusion.col_ref) | copy-start | bytes 772
  45.0 7.2 %copy-start.14 = (s32[64]{0:T(128)S(1)}, s32[64]{0:T(128)}, u32[]{:S(2)}) copy-start(s32[64]{0:T(128)} %param.10) | copy-start | bytes 772
  45.0 8.8 %copy-start.2 = (bf16[1024,1024]{1,0:T(8,128)(2,1)S(1)}, bf16[1024,1024]{1,0:T(8,128)(2,1)}, u32[]{:S(2)}) copy-start(bf16[1024,1024]{1,0:T(8,128)(2,1)} %w_self.1) | copy-start | bytes 6291460
  45.1 33.8 %all-to-all-start.1 = ((bf16[16,64,512]{2,1,0:T(8,128)(2,1)}), bf16[16,64,512]{2,1,0:T(8,128)(2,1)S(1)}, u32[]{:S(2)}, u32[]{:S(2)}) async-start(bf16[16,64,512]{2,1,0:T(8,128)(2,1)} %shard_map.95), calls=%async_computation.1 | async-start | bytes 2097152 | tf_op jit(solution)/shard_map/all_to_all | solution.py:384
  78.8 1.0 copy-start.5
  88.4 6.1 %collective-permute-start.4 = (bf16[1024,512]{1,0:T(8,128)(2,1)}, bf16[1024,512]{1,0:T(8,128)(2,1)S(1)}, u32[]{:S(2)}, u32[]{:S(2)}) collective-permute-start(bf16[1024,512]{1,0:T(8,128)(2,1)} %get-tuple-element.38), channel_id=1, source_target_pairs={{0,1},{1,0},{2,3},{3,2},{4,5},{5,4},{6,7},{7,6},{8,9},{9,8},{10,11... | collective-permute-start | bytes 3145736 | tf_op jit(solution)/shard_map/ppermute | solution.py:401
  90.1 39.6 %all-to-all-start.2 = ((bf16[16,64,512]{2,1,0:T(8,128)(2,1)}), bf16[16,64,512]{2,1,0:T(8,128)(2,1)S(1)}, u32[]{:S(2)}, u32[]{:S(2)}) async-start(bf16[16,64,512]{2,1,0:T(8,128)(2,1)} %bitcast.35), calls=%async_computation.2 | async-start | bytes 2097152 | tf_op jit(solution)/shard_map/all_to_all | solution.py:384
  94.4 1.0 copy-start.8
  98.7 9.3 %collective-permute-start.5 = (bf16[256,512]{1,0:T(8,128)(2,1)}, bf16[256,512]{1,0:T(8,128)(2,1)S(1)}, u32[]{:S(2)}, u32[]{:S(2)}) collective-permute-start(bf16[256,512]{1,0:T(8,128)(2,1)} %get-tuple-element.40), channel_id=1, source_target_pairs={{0,64},{16,80},{32,96},{48,112},{64,128},{80,144},{96,160},{112,17... | collective-permute-start | bytes 786440 | tf_op jit(solution)/shard_map/ppermute | solution.py:394
  100.2 10.9 %collective-permute-start.6 = (bf16[256,512]{1,0:T(8,128)(2,1)}, bf16[256,512]{1,0:T(8,128)(2,1)S(1)}, u32[]{:S(2)}, u32[]{:S(2)}) collective-permute-start(bf16[256,512]{1,0:T(8,128)(2,1)} %get-tuple-element.41), channel_id=1, source_target_pairs={{0,128},{16,144},{32,160},{48,176},{64,192},{80,208},{96,224},{112... | collective-permute-start | bytes 786440 | tf_op jit(solution)/shard_map/ppermute | solution.py:394
  101.3 13.8 %collective-permute-start.7 = (bf16[256,512]{1,0:T(8,128)(2,1)}, bf16[256,512]{1,0:T(8,128)(2,1)S(1)}, u32[]{:S(2)}, u32[]{:S(2)}) collective-permute-start(bf16[256,512]{1,0:T(8,128)(2,1)} %get-tuple-element.42), channel_id=1, source_target_pairs={{0,192},{16,208},{32,224},{48,240},{64,0},{80,16},{96,32},{112,48}... | collective-permute-start | bytes 786440 | tf_op jit(solution)/shard_map/ppermute | solution.py:394
  108.1 7.0 %copy-start.9 = (bf16[256,512]{1,0:T(8,128)(2,1)}, bf16[256,512]{1,0:T(8,128)(2,1)S(1)}, u32[]{:S(2)}) copy-start(bf16[256,512]{1,0:T(8,128)(2,1)S(1)} %collective-permute-done.5.refs_1_) | copy-start | bytes 786436
  111.1 3.9 %copy-start.10 = (bf16[256,512]{1,0:T(8,128)(2,1)}, bf16[256,512]{1,0:T(8,128)(2,1)S(1)}, u32[]{:S(2)}) copy-start(bf16[256,512]{1,0:T(8,128)(2,1)S(1)} %collective-permute-done.6.refs_2_) | copy-start | bytes 786436
  115.1 0.7 copy-start.11
  117.9 11.0 %collective-permute-start.8 = (bf16[64,512]{1,0:T(8,128)(2,1)}, bf16[64,512]{1,0:T(8,128)(2,1)S(1)}, u32[]{:S(2)}, u32[]{:S(2)}) collective-permute-start(bf16[64,512]{1,0:T(8,128)(2,1)} %get-tuple-element.44), channel_id=1, source_target_pairs={{0,16},{16,32},{32,48},{48,0},{64,80},{80,96},{96,112},{112,64},{1... | collective-permute-start | bytes 196616 | tf_op jit(solution)/shard_map/ppermute | solution.py:394
  119.4 9.5 %collective-permute-start.9 = (bf16[64,512]{1,0:T(8,128)(2,1)}, bf16[64,512]{1,0:T(8,128)(2,1)S(1)}, u32[]{:S(2)}, u32[]{:S(2)}) collective-permute-start(bf16[64,512]{1,0:T(8,128)(2,1)} %get-tuple-element.45), channel_id=1, source_target_pairs={{0,32},{16,48},{32,0},{48,16},{64,96},{80,112},{96,64},{112,80},{1... | collective-permute-start | bytes 196616 | tf_op jit(solution)/shard_map/ppermute | solution.py:394
  124.0 4.9 %collective-permute-start.10 = (bf16[64,512]{1,0:T(8,128)(2,1)}, bf16[64,512]{1,0:T(8,128)(2,1)S(1)}, u32[]{:S(2)}, u32[]{:S(2)}) collective-permute-start(bf16[64,512]{1,0:T(8,128)(2,1)} %get-tuple-element.46), channel_id=1, source_target_pairs={{0,48},{16,0},{32,16},{48,32},{64,112},{80,64},{96,80},{112,96},{1... | collective-permute-start | bytes 196616 | tf_op jit(solution)/shard_map/ppermute | solution.py:394
  124.0 4.9 %copy-start.12 = (f32[64,512]{1,0:T(8,128)S(1)}, f32[64,512]{1,0:T(8,128)}, u32[]{:S(2)}) copy-start(f32[64,512]{1,0:T(8,128)} %get-tuple-element.43) | copy-start | bytes 393220
  129.7 7.0 %copy-start.4 = (bf16[16,64,512]{2,1,0:T(8,128)(2,1)}, bf16[16,64,512]{2,1,0:T(8,128)(2,1)S(1)}, u32[]{:S(2)}) copy-start(bf16[16,64,512]{2,1,0:T(8,128)(2,1)S(1)} %all-to-all-done.2.parts_ref) | copy-start | bytes 3145732
  129.7 36.5 %all-to-all-start.3 = ((bf16[16,72,512]{2,1,0:T(8,128)(2,1)}), bf16[16,72,512]{2,1,0:T(8,128)(2,1)S(1)}, u32[]{:S(2)}, u32[]{:S(2)}) async-start(bf16[16,72,512]{2,1,0:T(8,128)(2,1)} %maximum_dynamic-update-slice_fusion), calls=%async_computation.3 | async-start | bytes 2359296 | tf_op jit(solution)/shard_map/all_to_all | solution.py:384
  141.1 29.7 %collective-permute-start.2 = (bf16[64,64,128]{2,1,0:T(8,128)(2,1)}, bf16[64,64,128]{2,1,0:T(8,128)(2,1)S(1)}, u32[]{:S(2)}, u32[]{:S(2)}) collective-permute-start(bf16[64,64,128]{2,1,0:T(8,128)(2,1)} %get-tuple-element.32), channel_id=1, source_target_pairs={{0,16},{16,32},{32,48},{48,64},{64,80},{80,96},{96,112},{112,128},... | collective-permute-start | bytes 3145736 | tf_op jit(solution)/shard_map/ppermute | solution.py:380
  145.0 27.3 %collective-permute-start.3 = (bf16[64,64,128]{2,1,0:T(8,128)(2,1)}, bf16[64,64,128]{2,1,0:T(8,128)(2,1)S(1)}, u32[]{:S(2)}, u32[]{:S(2)}) collective-permute-start(bf16[64,64,128]{2,1,0:T(8,128)(2,1)} %get-tuple-element.33), channel_id=1, source_target_pairs={{16,0},{32,16},{48,32},{64,48},{80,64},{96,80},{112,96},{128,112},... | collective-permute-start | bytes 3145736 | tf_op jit(solution)/shard_map/ppermute | solution.py:380
  166.2 6.1 %copy-start.3 = (bf16[16,72,512]{2,1,0:T(8,128)(2,1)}, bf16[16,72,512]{2,1,0:T(8,128)(2,1)S(1)}, u32[]{:S(2)}) copy-start(bf16[16,72,512]{2,1,0:T(8,128)(2,1)S(1)} %all-to-all-done.3.dself_ref) | copy-start | bytes 3538948
  170.8 1.6 copy-start.6
  172.3 1.0 copy-start.7

commit v6 on v5

--- a/solution.py
+++ b/solution.py
@@ -12,10 +12,12 @@
 NT = (((1,), (1,)), ((), ()))
 NN = (((1,), (0,)), ((), ()))
 MIB = 1 << 20
-DENSE_MIB = 60
+DENSE_MIB = 56
 OWN_MIB = 60
 WEIGHT_MIB = 60
-FINAL_MIB = 60
+FINAL_MIB = 50
+SCATTER_MIB = 56
+CHUNK = 512
 
 
 def dot(a, b, dims=NN):
@@ -111,36 +113,41 @@
     )(col, before, own, after)
 
 
-def scatter_kernel(col_ref, parts_ref, before_hbm, own_hbm, after_hbm, acc, before, after, sems):
+def scatter_kernel(
+    col_ref, parts_hbm, before_hbm, own_hbm, after_hbm, parts_ref, acc, before, after, load_sem, sems
+):
     tile = acc.shape[2]
     blocks = own_hbm.shape[0]
     per = parts_ref.shape[2] // tile
+    load = pltpu.make_async_copy(parts_hbm, parts_ref, load_sem)
+    load.start()
 
     def clear(i, carry):
         acc[i] = jnp.zeros(acc.shape[1:], F32)
         return carry
 
     lax.fori_loop(0, acc.shape[0], clear, 0, unroll=8)
+    load.wait()
 
     def add(g, carry):
         for b in range(per):
             acc[col_ref[g * per + b]] += parts_ref[g, :, b * tile : (b + 1) * tile].astype(F32)
         return carry
 
-    lax.fori_loop(0, parts_ref.shape[0], add, 0)
-
-    def cast(i, carry):
-        before[i] = acc[i].astype(BF16)
-        after[i] = acc[2 * blocks + i].astype(BF16)
-        return carry
-
-    lax.fori_loop(0, blocks, cast, 0, unroll=4)
+    lax.fori_loop(0, parts_ref.shape[0], add, 0, unroll=2)
     copies = [
-        pltpu.make_async_copy(before, before_hbm, sems.at[0]),
-        pltpu.make_async_copy(after, after_hbm, sems.at[1]),
-        pltpu.make_async_copy(acc.at[blocks : 2 * blocks], own_hbm, sems.at[2]),
+        pltpu.make_async_copy(acc.at[blocks : 2 * blocks], own_hbm, sems.at[0]),
+        pltpu.make_async_copy(before, before_hbm, sems.at[1]),
+        pltpu.make_async_copy(after, after_hbm, sems.at[2]),
     ]
-    for copy in copies:
+    copies[0].start()
+    for first, out, copy in ((0, before, copies[1]), (2 * blocks, after, copies[2])):
+
+        def cast(i, carry, first=first, out=out):
+            out[i] = acc[first + i].astype(BF16)
+            return carry
+
+        lax.fori_loop(0, blocks, cast, 0, unroll=8)
         copy.start()
     for copy in copies:
         copy.wait()
@@ -153,7 +160,7 @@
     shape = (blocks, rows, tile)
     return pl.pallas_call(
         scatter_kernel,
-        in_specs=[SMEM, VMEM],
+        in_specs=[SMEM, ANYWHERE],
         out_specs=[ANYWHERE] * 3,
         out_shape=[
             jax.ShapeDtypeStruct(shape, BF16),
@@ -161,12 +168,14 @@
             jax.ShapeDtypeStruct(shape, BF16),
         ],
         scratch_shapes=[
+            pltpu.VMEM(parts.shape, BF16),
             pltpu.VMEM((3 * blocks, rows, tile), F32),
             pltpu.VMEM(shape, BF16),
             pltpu.VMEM(shape, BF16),
+            pltpu.SemaphoreType.DMA(()),
             pltpu.SemaphoreType.DMA((3,)),
         ],
-        compiler_params=whole_params(60),
+        compiler_params=whole_params(SCATTER_MIB),
         cost_estimate=pl.CostEstimate(flops=0, bytes_accessed=8 * MIB, transcendentals=0),
     )(col, parts)
 
@@ -249,7 +258,7 @@
 
 def dense(half, tiles, turned, x_rows, picked, w_neigh, pre_self, cot, w_back):
     size, width = picked.shape
-    chunk = 256
+    chunk = CHUNK
     out = jax.ShapeDtypeStruct((size, width), BF16)
     args = (tiles, turned, x_rows, picked, w_neigh, pre_self, cot, w_back)
     return pl.pallas_call(
@@ -396,11 +405,12 @@
     ]
 
 
-def weight_rows(sent, dpre, agg_rows, groups):
+def weight_rows(sent, dpre, agg_rows, groups, own_rows):
     feat, node = lax.axis_index("feat"), lax.axis_index("node")
     other = lax.ppermute(sent, "feat", [(i, i ^ 1) for i in range(groups)])
     pieces = weight_pieces(lax.rem(feat, CORES), lax.div(node, SIDE), dpre, agg_rows, other)
     parts = sent_round(pieces, "node", lambda i, s: (i + s * SIDE) % (SIDE * SIDE))
+    parts, own_rows = lax.optimization_barrier((parts, own_rows))
     pieces = added_pieces(lax.rem(node, SIDE), parts)
     parts = sent_round(pieces, "node", lambda i, s: i // SIDE * SIDE + (i + s) % SIDE)
     total = parts[0]
@@ -409,7 +419,8 @@
     total = total.reshape(groups, EXTRA // 2, -1)
     high = total.astype(BF16)
     low = (total - high.astype(F32)).astype(BF16)
-    return jnp.concatenate([high, low], axis=1)
+    rows = jnp.concatenate([high, low], axis=1)
+    return lax.dynamic_update_slice(own_rows, rows, (0, own_rows.shape[1] - EXTRA, 0))
 
 
 def weight_total(rows):
@@ -457,9 +468,7 @@
     )
     second_cols = exchange(second.reshape(groups, feat_dev, -1), "feat")
     own_rows = own_part(self_back, dpre, dagg, turned, groups)
-    weight = weight_rows(sent, dpre, agg_rows, groups)
-    own_rows = lax.dynamic_update_slice(own_rows, weight, (0, feat_dev, 0))
-    own_cols = exchange(own_rows, "feat")
+    own_cols = exchange(weight_rows(sent, dpre, agg_rows, groups, own_rows), "feat")
     to_before, spread, to_after = scatter(col, second_cols)
     from_after = shifted(to_before, "node", -1)
     from_before = shifted(to_after, "node", 1)

time: 180 us -> 178 us (0.989)
    unnamed x34 -> x26, local copies, waits for them, and re-layouts: 10.5 us -> 9.43 us
  transfers between devices with their start and end apart: 15 -> 15, of which waited for: 9 -> 11; matrix products, arithmetic and copies ran while one was open for 8% -> 9% of each run, Pallas kernels for 12% -> 12%
where the time goes in v6:
time: 178 us; the launch traced here: 176 us
  waiting for transfers between devices  66.3 us (37%)
  starting transfers between devices  54.9 us (31%)
  Pallas kernels  36 us (20%)
  local copies, waits for them, and re-layouts  12.8 us (7%)
  other arithmetic  4.78 us (3%)
    all_to_all x4, waiting for transfers between devices, exchange(): return lax.all_to_all(value, axis, split_axis=0, concat_axis=0, tiled=True)  29.2 us
    all_to_all x4, starting transfers between devices, exchange(): return lax.all_to_all(value, axis, split_axis=0, concat_axis=0, tiled=True)  26.4 us
    ppermute x4, waiting for transfers between devices, shifted(): lax.ppermute(value, axis, [(source, source + steps) for source in range(f...  25.9 us
    ppermute x4, starting transfers between devices, shifted(): lax.ppermute(value, axis, [(source, source + steps) for source in range(f...  15.9 us
    ppermute x6, waiting for transfers between devices, sent_round(): lax.ppermute(piece, axis, [(i, partner(i, step + 1)) for i in range(count)])  11.2 us
    ppermute x6, starting transfers between devices, sent_round(): lax.ppermute(piece, axis, [(i, partner(i, step + 1)) for i in range(count)])  10.8 us
    unnamed x26, local copies, waits for them, and re-layouts  9.43 us
    pallas_call x1, Pallas kernels, dense(): pl.pallas_call(functools.partial(dense_kernel, chunk), in_specs=[SMEM] +...  8.21 us
  transfers between devices with their start and end apart: 15, of which 11 were waited for; matrix products, arithmetic and copies ran while one was open for 9% of the time, Pallas kernels for 12%

profile of v6, /device:TPU:2, one launch (start us, length us, event | category | flops | bytes accessed | tf_op | source)
XLA Modules:
  0.0 175.8 jit_solution(7930095589657770449)
XLA Ops:
  0.6 2.2 %shard_map.94 = bf16[16,64,512]{2,1,0:T(8,128)(2,1)} custom-call(bf16[64,8192]{1,0:T(8,128)(2,1)} %own.1), custom_call_target="tpu_custom_call" | custom-call | tf_op jit(solution)/shard_map/pallas_call | solution.py:61
  2.9 8.6 %all-to-all-start = ((bf16[16,64,512]{2,1,0:T(8,128)(2,1)}), bf16[16,64,512]{2,1,0:T(8,128)(2,1)}, u32[]{:S(2)}, u32[]{:S(2)}) async-start(bf16[16,64,512]{2,1,0:T(8,128)(2,1)} %shard_map.94), calls=%async_computation | async-start | bytes 2097152 | tf_op jit(solution)/shard_map/all_to_all | solution.py:393
  11.5 3.5 %collective-permute-start = (bf16[64,8192]{1,0:T(8,128)(2,1)S(1)}, bf16[64,8192]{1,0:T(8,128)(2,1)S(1)}, u32[]{:S(2)}, u32[]{:S(2)}) collective-permute-start(bf16[64,8192]{1,0:T(8,128)(2,1)S(1)} %copy-done), channel_id=1, source_target_pairs={{0,16},{16,32},{32,48},{48,64},{64,80},{80,96},{96,112},{112,128},... | collective-permute-start | bytes 3145736 | tf_op jit(solution)/shard_map/ppermute | solution.py:389
  15.0 4.5 %collective-permute-start.1 = (bf16[64,8192]{1,0:T(8,128)(2,1)S(1)}, bf16[64,8192]{1,0:T(8,128)(2,1)S(1)}, u32[]{:S(2)}, u32[]{:S(2)}) collective-permute-start(bf16[64,8192]{1,0:T(8,128)(2,1)S(1)} %copy-done), channel_id=1, source_target_pairs={{16,0},{32,16},{48,32},{64,48},{80,64},{96,80},{112,96},{128,112},... | collective-permute-start | bytes 3145736 | tf_op jit(solution)/shard_map/ppermute | solution.py:389
  19.6 21.4 %collective-permute-done.before = bf16[64,8192]{1,0:T(8,128)(2,1)S(1)} collective-permute-done((bf16[64,8192]{1,0:T(8,128)(2,1)S(1)}, bf16[64,8192]{1,0:T(8,128)(2,1)S(1)}, u32[]{:S(2)}, u32[]{:S(2)}) %collective-permute-start) | collective-permute-done | bytes 1048608 | tf_op jit(solution)/shard_map/ppermute | solution.py:389
  42.2 2.9 %shard_map.95 = bf16[16,64,512]{2,1,0:T(8,128)(2,1)} custom-call(s32[64]{0:T(128)S(1)} %subtract_bitcast_fusion.col_ref, bf16[64,8192]{1,0:T(8,128)(2,1)S(1)} %collective-permute-done.before, bf16[64,8192]{1,0:T(8,128)(2,1)S(1)} %copy-done, bf16[64,8192]{1,0:T(8,128)(2,1)S(1)} %collective-permute-done.1.after), custom_call_target="tpu_custom_call" | custom-call | bytes 8388608 | tf_op jit(solution)/shard_map/pallas_call | solution.py:105
  45.1 7.1 %all-to-all-start.1 = ((bf16[16,64,512]{2,1,0:T(8,128)(2,1)}), bf16[16,64,512]{2,1,0:T(8,128)(2,1)S(1)}, u32[]{:S(2)}, u32[]{:S(2)}) async-start(bf16[16,64,512]{2,1,0:T(8,128)(2,1)} %shard_map.95), calls=%async_computation.1 | async-start | bytes 2097152 | tf_op jit(solution)/shard_map/all_to_all | solution.py:393
  53.9 2.6 %copy.14 = bf16[1024,1024]{0,1:T(8,128)(2,1)} copy(bf16[1024,1024]{1,0:T(8,128)(2,1)S(1)} %copy-done.2) | data formatting | bytes 4194304 | tf_op args[4]
  56.5 3.9 %copy.15 = bf16[1024,1024]{0,1:T(8,128)(2,1)} copy(bf16[1024,1024]{1,0:T(8,128)(2,1)} %refs_5_.1) | data formatting | bytes 4194304 | tf_op args[5]
  62.4 4.5 %shard_map.96.refs_6_ = f32[1024,512]{1,0:T(8,128)} custom-call(bf16[1024,1024]{1,0:T(8,128)(2,1)} %w_self.1, bf16[1024,512]{1,0:T(8,128)(2,1)} %bitcast.1.x_ref.refs_3_), custom_call_target="tpu_custom_call" | custom-call | flops 1073741824 | bytes 5242880 | tf_op jit(solution)/shard_map/pallas_call | solution.py:191
  66.9 11.9 %all-to-all-done.1 = bf16[16,64,512]{2,1,0:T(8,128)(2,1)S(1)} async-done(((bf16[16,64,512]{2,1,0:T(8,128)(2,1)}), bf16[16,64,512]{2,1,0:T(8,128)(2,1)S(1)}, u32[]{:S(2)}, u32[]{:S(2)}) %all-to-all-start.1) | async-done | bytes 1048608 | tf_op jit(solution)/shard_map/all_to_all | solution.py:393
  79.8 8.2 %shard_map.97 = (bf16[1024,512]{1,0:T(8,128)(2,1)}, bf16[1024,512]{1,0:T(8,128)(2,1)}, bf16[1024,512]{1,0:T(8,128)(2,1)}, bf16[1024,512]{1,0:T(8,128)(2,1)}, bf1...) custom-call(s32[1]{0:T(128)S(6)} %sub.17.refs_0_, bf16[2,2,256,256]{3,2,1,0:T(8,128)(2,1)} %copy.21.refs_1_, ...), custom_call_target="tpu_custom_call" | custom-call | flops 2147483648 | bytes 16777216 | tf_op jit(solution)/shard_map/pallas_call | solution.py:264
  88.0 1.8 %collective-permute-start.4 = (bf16[1024,512]{1,0:T(8,128)(2,1)}, bf16[1024,512]{1,0:T(8,128)(2,1)S(1)}, u32[]{:S(2)}, u32[]{:S(2)}) collective-permute-start(bf16[1024,512]{1,0:T(8,128)(2,1)} %get-tuple-element.41), channel_id=1, source_target_pairs={{0,1},{1,0},{2,3},{3,2},{4,5},{5,4},{6,7},{7,6},{8,9},{9,8},{10,11... | collective-permute-start | bytes 3145736 | tf_op jit(solution)/shard_map/ppermute | solution.py:410
  89.8 3.7 %all-to-all-start.2 = ((bf16[16,64,512]{2,1,0:T(8,128)(2,1)}), bf16[16,64,512]{2,1,0:T(8,128)(2,1)S(1)}, u32[]{:S(2)}, u32[]{:S(2)}) async-start(bf16[16,64,512]{2,1,0:T(8,128)(2,1)} %bitcast.35), calls=%async_computation.2 | async-start | bytes 2097152 | tf_op jit(solution)/shard_map/all_to_all | solution.py:393
  95.0 3.3 %shard_map.99 = (f32[256,512]{1,0:T(8,128)}, bf16[256,512]{1,0:T(8,128)(2,1)}, bf16[256,512]{1,0:T(8,128)(2,1)}, bf16[256,512]{1,0:T(8,128)(2,1)}) custom-call(s32[2]{0:T(128)} %pad_add_fusion.index_ref, bf16[1024,512]{1,0:T(8,128)(2,1)} %get-tuple-element.39.dpre, bf16[1024,512]{1,0:T(8,128)(2,1)} %get-tuple-element.40.agg_ref, bf16[1024,512]{1,0:T(8,128)(2,1)} %copy-done.5), custom_call_target="tpu_custom_call" | custom-call | flops 536870912 | bytes 4194304 | tf_op jit(solution)/shard_map/pallas_call | solution.py:323
  98.3 1.5 collective-permute-start.5
  100.9 2.2 %collective-permute-start.7 = (bf16[256,512]{1,0:T(8,128)(2,1)}, bf16[256,512]{1,0:T(8,128)(2,1)S(1)}, u32[]{:S(2)}, u32[]{:S(2)}) collective-permute-start(bf16[256,512]{1,0:T(8,128)(2,1)} %get-tuple-element.45), channel_id=1, source_target_pairs={{0,192},{16,208},{32,224},{48,240},{64,0},{80,16},{96,32},{112,48}... | collective-permute-start | bytes 786440 | tf_op jit(solution)/shard_map/ppermute | solution.py:403
  103.1 4.9 %shard_map.100 = bf16[16,72,512]{2,1,0:T(8,128)(2,1)} custom-call(bf16[1024,1024]{1,0:T(8,128)(2,1)} %bitcast.32, bf16[1024,512]{1,0:T(8,128)(2,1)} %get-tuple-element.39.dpre, bf16[1024,512]{1,0:T(8,128)(2,1)} %get-tuple-element.47.dagg_ref, bf16[2,2,256,256]{3,2,1,0:T(8,128)(2,1)} %get-tuple-element.31.refs_2_.turned), custom_call_target="tpu_custom_call" | custom-call | flops 1073741824 | bytes 5242880 | tf_op jit(solution)/shard_map/pallas_call | solution.py:298
  107.9 2.8 %collective-permute-done.6.refs_2_ = bf16[256,512]{1,0:T(8,128)(2,1)S(1)} collective-permute-done((bf16[256,512]{1,0:T(8,128)(2,1)}, bf16[256,512]{1,0:T(8,128)(2,1)S(1)}, u32[]{:S(2)}, u32[]{:S(2)}) %collective-permute-start.6) | collective-permute-done | bytes 262176 | tf_op jit(solution)/shard_map/ppermute | solution.py:403
  110.7 3.9 %collective-permute-done.7.refs_3_ = bf16[256,512]{1,0:T(8,128)(2,1)S(1)} collective-permute-done((bf16[256,512]{1,0:T(8,128)(2,1)}, bf16[256,512]{1,0:T(8,128)(2,1)S(1)}, u32[]{:S(2)}, u32[]{:S(2)}) %collective-permute-start.7) | collective-permute-done | bytes 262176 | tf_op jit(solution)/shard_map/ppermute | solution.py:403
  115.4 2.1 %shard_map.101 = (f32[64,512]{1,0:T(8,128)}, bf16[64,512]{1,0:T(8,128)(2,1)}, bf16[64,512]{1,0:T(8,128)(2,1)}, bf16[64,512]{1,0:T(8,128)(2,1)}) custom-call(s32[1]{0:T(128)} %bitcast.17.index_ref, f32[256,512]{1,0:T(8,128)} %get-tuple-element.49.refs_0_, bf16[256,512]{1,0:T(8,128)(2,1)} %copy-done.6, bf16[256,512]{1,0:T(8,128)(2,1)} %copy-done.7, ...), custom_call_target="tpu_custom_call" | custom-call | bytes 2097152 | tf_op jit(solution)/shard_map/pallas_call | solution.py:350
  117.4 1.5 collective-permute-start.8
  118.9 4.6 %collective-permute-start.9 = (bf16[64,512]{1,0:T(8,128)(2,1)}, bf16[64,512]{1,0:T(8,128)(2,1)S(1)}, u32[]{:S(2)}, u32[]{:S(2)}) collective-permute-start(bf16[64,512]{1,0:T(8,128)(2,1)} %get-tuple-element.55), channel_id=1, source_target_pairs={{0,32},{16,48},{32,0},{48,16},{64,96},{80,112},{96,64},{112,80},{1... | collective-permute-start | bytes 196616 | tf_op jit(solution)/shard_map/ppermute | solution.py:403
  124.5 2.2 %collective-permute-done.9 = bf16[64,512]{1,0:T(8,128)(2,1)S(1)} collective-permute-done((bf16[64,512]{1,0:T(8,128)(2,1)}, bf16[64,512]{1,0:T(8,128)(2,1)S(1)}, u32[]{:S(2)}, u32[]{:S(2)}) %collective-permute-start.9) | collective-permute-done | bytes 65568 | tf_op jit(solution)/shard_map/ppermute | solution.py:403
  126.7 1.3 collective-permute-done.10
  129.8 7.0 %all-to-all-start.3 = ((bf16[16,72,512]{2,1,0:T(8,128)(2,1)}), bf16[16,72,512]{2,1,0:T(8,128)(2,1)S(1)}, u32[]{:S(2)}, u32[]{:S(2)}) async-start(bf16[16,72,512]{2,1,0:T(8,128)(2,1)} %maximum_dynamic-update-slice_fusion), calls=%async_computation.3 | async-start | bytes 2359296 | tf_op jit(solution)/shard_map/all_to_all | solution.py:393
  136.8 4.2 %shard_map.98 = (bf16[64,64,128]{2,1,0:T(8,128)(2,1)}, f32[64,64,128]{2,1,0:T(8,128)}, bf16[64,64,128]{2,1,0:T(8,128)(2,1)}) custom-call(s32[64]{0:T(128)} %copy-done.1, bf16[16,64,512]{2,1,0:T(8,128)(2,1)} %copy-done.3), custom_call_target="tpu_custom_call" | custom-call | bytes 8388608 | tf_op jit(solution)/shard_map/pallas_call | solution.py:161
  141.0 1.9 %collective-permute-start.2 = (bf16[64,64,128]{2,1,0:T(8,128)(2,1)}, bf16[64,64,128]{2,1,0:T(8,128)(2,1)S(1)}, u32[]{:S(2)}, u32[]{:S(2)}) collective-permute-start(bf16[64,64,128]{2,1,0:T(8,128)(2,1)} %get-tuple-element.37), channel_id=1, source_target_pairs={{0,16},{16,32},{32,48},{48,64},{64,80},{80,96},{96,112},{112,128},... | collective-permute-start | bytes 3145736 | tf_op jit(solution)/shard_map/ppermute | solution.py:389
  142.9 6.0 %collective-permute-start.3 = (bf16[64,64,128]{2,1,0:T(8,128)(2,1)}, bf16[64,64,128]{2,1,0:T(8,128)(2,1)S(1)}, u32[]{:S(2)}, u32[]{:S(2)}) collective-permute-start(bf16[64,64,128]{2,1,0:T(8,128)(2,1)} %get-tuple-element.38), channel_id=1, source_target_pairs={{16,0},{32,16},{48,32},{64,48},{80,64},{96,80},{112,96},{128,112},... | collective-permute-start | bytes 3145736 | tf_op jit(solution)/shard_map/ppermute | solution.py:389
  149.0 17.3 %all-to-all-done.3.dself_ref = bf16[16,72,512]{2,1,0:T(8,128)(2,1)S(1)} async-done(((bf16[16,72,512]{2,1,0:T(8,128)(2,1)}), bf16[16,72,512]{2,1,0:T(8,128)(2,1)S(1)}, u32[]{:S(2)}, u32[]{:S(2)}) %all-to-all-start.3) | async-done | bytes 1179680 | tf_op jit(solution)/shard_map/all_to_all | solution.py:393
  168.7 2.0 %collective-permute-done.2.before_ref = bf16[64,64,128]{2,1,0:T(8,128)(2,1)S(1)} collective-permute-done((bf16[64,64,128]{2,1,0:T(8,128)(2,1)}, bf16[64,64,128]{2,1,0:T(8,128)(2,1)S(1)}, u32[]{:S(2)}, u32[]{:S(2)}) %collective-permute-start.2) | collective-permute-done | bytes 1048608 | tf_op jit(solution)/shard_map/ppermute | solution.py:389
  172.0 3.8 %shard_map.102 = bf16[64,8192]{1,0:T(8,128)(2,1)} custom-call(f32[64,64,128]{2,1,0:T(8,128)} %get-tuple-element.36.own_ref, bf16[64,64,128]{2,1,0:T(8,128)(2,1)S(1)} %collective-permute-done.2.before_ref, bf16[64,64,128]{2,1,0:T(8,128)(2,1)S(1)} %collective-permute-done.3.after_ref, bf16[16,72,512]{2,1,0:T(8,128)(2,1)S(1)} %all-to-all-done.3.dself_ref), custom_call_target="tpu_custom_call" | custom-call | tf_op jit(solution)/shard_map/pallas_call | solution.py:375
  (55 shorter events, 15.7 us)
Async XLA Ops:
  0.6 10.9 %copy-start = (bf16[64,8192]{1,0:T(8,128)(2,1)S(1)}, bf16[64,8192]{1,0:T(8,128)(2,1)}, u32[]{:S(2)}) copy-start(bf16[64,8192]{1,0:T(8,128)(2,1)} %own.1) | copy-start | bytes 3145732
  0.6 18.9 %copy-start.9 = (s32[64,2]{0,1:T(2,128)S(1)}, s32[64,2]{0,1:T(2,128)}, u32[]{:S(2)}) copy-start(s32[64,2]{0,1:T(2,128)} %param.9) | copy-start | bytes 1540
  2.9 42.2 %all-to-all-start = ((bf16[16,64,512]{2,1,0:T(8,128)(2,1)}), bf16[16,64,512]{2,1,0:T(8,128)(2,1)}, u32[]{:S(2)}, u32[]{:S(2)}) async-start(bf16[16,64,512]{2,1,0:T(8,128)(2,1)} %shard_map.94), calls=%async_computation | async-start | bytes 2097152 | tf_op jit(solution)/shard_map/all_to_all | solution.py:393
  11.5 29.4 %collective-permute-start = (bf16[64,8192]{1,0:T(8,128)(2,1)S(1)}, bf16[64,8192]{1,0:T(8,128)(2,1)S(1)}, u32[]{:S(2)}, u32[]{:S(2)}) collective-permute-start(bf16[64,8192]{1,0:T(8,128)(2,1)S(1)} %copy-done), channel_id=1, source_target_pairs={{0,16},{16,32},{32,48},{48,64},{64,80},{80,96},{96,112},{112,128},... | collective-permute-start | bytes 3145736 | tf_op jit(solution)/shard_map/ppermute | solution.py:389
  15.0 27.1 %collective-permute-start.1 = (bf16[64,8192]{1,0:T(8,128)(2,1)S(1)}, bf16[64,8192]{1,0:T(8,128)(2,1)S(1)}, u32[]{:S(2)}, u32[]{:S(2)}) collective-permute-start(bf16[64,8192]{1,0:T(8,128)(2,1)S(1)} %copy-done), channel_id=1, source_target_pairs={{16,0},{32,16},{48,32},{64,48},{80,64},{96,80},{112,96},{128,112},... | collective-permute-start | bytes 3145736 | tf_op jit(solution)/shard_map/ppermute | solution.py:389
  19.5 25.5 %copy-start.1 = (s32[64]{0:T(128)}, s32[64]{0:T(128)S(1)}, u32[]{:S(2)}) copy-start(s32[64]{0:T(128)S(1)} %subtract_bitcast_fusion.col_ref) | copy-start | bytes 772
  45.0 7.2 %copy-start.10 = (s32[64]{0:T(128)S(1)}, s32[64]{0:T(128)}, u32[]{:S(2)}) copy-start(s32[64]{0:T(128)} %param.10) | copy-start | bytes 772
  45.0 8.8 %copy-start.2 = (bf16[1024,1024]{1,0:T(8,128)(2,1)S(1)}, bf16[1024,1024]{1,0:T(8,128)(2,1)}, u32[]{:S(2)}) copy-start(bf16[1024,1024]{1,0:T(8,128)(2,1)} %w_self.1) | copy-start | bytes 6291460
  45.1 33.8 %all-to-all-start.1 = ((bf16[16,64,512]{2,1,0:T(8,128)(2,1)}), bf16[16,64,512]{2,1,0:T(8,128)(2,1)S(1)}, u32[]{:S(2)}, u32[]{:S(2)}) async-start(bf16[16,64,512]{2,1,0:T(8,128)(2,1)} %shard_map.95), calls=%async_computation.1 | async-start | bytes 2097152 | tf_op jit(solution)/shard_map/all_to_all | solution.py:393
  78.8 1.0 copy-start.4
  88.0 6.0 %collective-permute-start.4 = (bf16[1024,512]{1,0:T(8,128)(2,1)}, bf16[1024,512]{1,0:T(8,128)(2,1)S(1)}, u32[]{:S(2)}, u32[]{:S(2)}) collective-permute-start(bf16[1024,512]{1,0:T(8,128)(2,1)} %get-tuple-element.41), channel_id=1, source_target_pairs={{0,1},{1,0},{2,3},{3,2},{4,5},{5,4},{6,7},{7,6},{8,9},{9,8},{10,11... | collective-permute-start | bytes 3145736 | tf_op jit(solution)/shard_map/ppermute | solution.py:410
  89.8 40.0 %all-to-all-start.2 = ((bf16[16,64,512]{2,1,0:T(8,128)(2,1)}), bf16[16,64,512]{2,1,0:T(8,128)(2,1)S(1)}, u32[]{:S(2)}, u32[]{:S(2)}) async-start(bf16[16,64,512]{2,1,0:T(8,128)(2,1)} %bitcast.35), calls=%async_computation.2 | async-start | bytes 2097152 | tf_op jit(solution)/shard_map/all_to_all | solution.py:393
  94.0 1.0 copy-start.5
  98.3 9.6 %collective-permute-start.5 = (bf16[256,512]{1,0:T(8,128)(2,1)}, bf16[256,512]{1,0:T(8,128)(2,1)S(1)}, u32[]{:S(2)}, u32[]{:S(2)}) collective-permute-start(bf16[256,512]{1,0:T(8,128)(2,1)} %get-tuple-element.43), channel_id=1, source_target_pairs={{0,64},{16,80},{32,96},{48,112},{64,128},{80,144},{96,160},{112,17... | collective-permute-start | bytes 786440 | tf_op jit(solution)/shard_map/ppermute | solution.py:403
  99.8 10.9 %collective-permute-start.6 = (bf16[256,512]{1,0:T(8,128)(2,1)}, bf16[256,512]{1,0:T(8,128)(2,1)S(1)}, u32[]{:S(2)}, u32[]{:S(2)}) collective-permute-start(bf16[256,512]{1,0:T(8,128)(2,1)} %get-tuple-element.44), channel_id=1, source_target_pairs={{0,128},{16,144},{32,160},{48,176},{64,192},{80,208},{96,224},{112... | collective-permute-start | bytes 786440 | tf_op jit(solution)/shard_map/ppermute | solution.py:403
  100.9 13.8 %collective-permute-start.7 = (bf16[256,512]{1,0:T(8,128)(2,1)}, bf16[256,512]{1,0:T(8,128)(2,1)S(1)}, u32[]{:S(2)}, u32[]{:S(2)}) collective-permute-start(bf16[256,512]{1,0:T(8,128)(2,1)} %get-tuple-element.45), channel_id=1, source_target_pairs={{0,192},{16,208},{32,224},{48,240},{64,0},{80,16},{96,32},{112,48}... | collective-permute-start | bytes 786440 | tf_op jit(solution)/shard_map/ppermute | solution.py:403
  107.9 6.7 %copy-start.6 = (bf16[256,512]{1,0:T(8,128)(2,1)}, bf16[256,512]{1,0:T(8,128)(2,1)S(1)}, u32[]{:S(2)}) copy-start(bf16[256,512]{1,0:T(8,128)(2,1)S(1)} %collective-permute-done.5.refs_1_) | copy-start | bytes 786436
  110.7 3.9 %copy-start.7 = (bf16[256,512]{1,0:T(8,128)(2,1)}, bf16[256,512]{1,0:T(8,128)(2,1)S(1)}, u32[]{:S(2)}) copy-start(bf16[256,512]{1,0:T(8,128)(2,1)S(1)} %collective-permute-done.6.refs_2_) | copy-start | bytes 786436
  114.7 0.7 copy-start.8
  117.4 7.1 %collective-permute-start.8 = (bf16[64,512]{1,0:T(8,128)(2,1)}, bf16[64,512]{1,0:T(8,128)(2,1)S(1)}, u32[]{:S(2)}, u32[]{:S(2)}) collective-permute-start(bf16[64,512]{1,0:T(8,128)(2,1)} %get-tuple-element.54), channel_id=1, source_target_pairs={{0,16},{16,32},{32,48},{48,0},{64,80},{80,96},{96,112},{112,64},{1... | collective-permute-start | bytes 196616 | tf_op jit(solution)/shard_map/ppermute | solution.py:403
  118.9 7.8 %collective-permute-start.9 = (bf16[64,512]{1,0:T(8,128)(2,1)}, bf16[64,512]{1,0:T(8,128)(2,1)S(1)}, u32[]{:S(2)}, u32[]{:S(2)}) collective-permute-start(bf16[64,512]{1,0:T(8,128)(2,1)} %get-tuple-element.55), channel_id=1, source_target_pairs={{0,32},{16,48},{32,0},{48,16},{64,96},{80,112},{96,64},{112,80},{1... | collective-permute-start | bytes 196616 | tf_op jit(solution)/shard_map/ppermute | solution.py:403
  123.5 4.5 %collective-permute-start.10 = (bf16[64,512]{1,0:T(8,128)(2,1)}, bf16[64,512]{1,0:T(8,128)(2,1)S(1)}, u32[]{:S(2)}, u32[]{:S(2)}) collective-permute-start(bf16[64,512]{1,0:T(8,128)(2,1)} %get-tuple-element.56), channel_id=1, source_target_pairs={{0,48},{16,0},{32,16},{48,32},{64,112},{80,64},{96,80},{112,96},{1... | collective-permute-start | bytes 196616 | tf_op jit(solution)/shard_map/ppermute | solution.py:403
  129.8 7.0 %copy-start.3 = (bf16[16,64,512]{2,1,0:T(8,128)(2,1)}, bf16[16,64,512]{2,1,0:T(8,128)(2,1)S(1)}, u32[]{:S(2)}) copy-start(bf16[16,64,512]{2,1,0:T(8,128)(2,1)S(1)} %all-to-all-done.2.parts_hbm) | copy-start | bytes 3145732
  129.8 36.5 %all-to-all-start.3 = ((bf16[16,72,512]{2,1,0:T(8,128)(2,1)}), bf16[16,72,512]{2,1,0:T(8,128)(2,1)S(1)}, u32[]{:S(2)}, u32[]{:S(2)}) async-start(bf16[16,72,512]{2,1,0:T(8,128)(2,1)} %maximum_dynamic-update-slice_fusion), calls=%async_computation.3 | async-start | bytes 2359296 | tf_op jit(solution)/shard_map/all_to_all | solution.py:393
  141.0 29.7 %collective-permute-start.2 = (bf16[64,64,128]{2,1,0:T(8,128)(2,1)}, bf16[64,64,128]{2,1,0:T(8,128)(2,1)S(1)}, u32[]{:S(2)}, u32[]{:S(2)}) collective-permute-start(bf16[64,64,128]{2,1,0:T(8,128)(2,1)} %get-tuple-element.37), channel_id=1, source_target_pairs={{0,16},{16,32},{32,48},{48,64},{64,80},{80,96},{96,112},{112,128},... | collective-permute-start | bytes 3145736 | tf_op jit(solution)/shard_map/ppermute | solution.py:389
  142.9 29.1 %collective-permute-start.3 = (bf16[64,64,128]{2,1,0:T(8,128)(2,1)}, bf16[64,64,128]{2,1,0:T(8,128)(2,1)S(1)}, u32[]{:S(2)}, u32[]{:S(2)}) collective-permute-start(bf16[64,64,128]{2,1,0:T(8,128)(2,1)} %get-tuple-element.38), channel_id=1, source_target_pairs={{16,0},{32,16},{48,32},{64,48},{80,64},{96,80},{112,96},{128,112},... | collective-permute-start | bytes 3145736 | tf_op jit(solution)/shard_map/ppermute | solution.py:389

commit v7 on v6

--- a/solution.py
+++ b/solution.py
@@ -277,12 +277,9 @@
     )(half, *args)
 
 
-EXTRA = 8
-
-
 def own_kernel(chunk, w_back, dpre, dagg_ref, turned, own):
     pair = turned.shape[-1]
-    each = own.shape[1] - EXTRA
+    each = own.shape[1]
     for i in range(0, dpre.shape[0], chunk):
         rows = slice(i, i + chunk)
         dself = dot(w_back[rows, :], dpre[...])
@@ -290,7 +287,7 @@
             here = slice(p * pair, (p + 1) * pair)
             total = dself[:, here] + dot(dagg_ref[rows, here], turned[0, p])
             for g in range(chunk // each):
-                own[i // each + g, :each, here] = total[g * each : (g + 1) * each].astype(BF16)
+                own[i // each + g, :, here] = total[g * each : (g + 1) * each].astype(BF16)
 
 
 def own_part(w_back, dpre, dagg, turned, groups):
@@ -299,7 +296,7 @@
         functools.partial(own_kernel, 256),
         in_specs=[VMEM] * 4,
         out_specs=VMEM,
-        out_shape=jax.ShapeDtypeStruct((groups, size // groups + EXTRA, width), BF16),
+        out_shape=jax.ShapeDtypeStruct((groups, size // groups, width), BF16),
         compiler_params=whole_params(OWN_MIB),
         cost_estimate=pl.CostEstimate(
             flops=2 * size * size * width, bytes_accessed=5 * MIB, transcendentals=0
@@ -307,8 +304,8 @@
     )(w_back, dpre, dagg, turned)
 
 
-def weight_kernel(index_ref, dpre, agg_ref, other_ref, *outs):
-    core, me = index_ref[0], index_ref[1]
+def weight_kernel(core_ref, me_ref, dpre, agg_ref, other_ref, *outs):
+    core, me = core_ref[0], me_ref[0]
     rows, width = outs[0].shape
     half = agg_ref.at[pl.ds(pl.multiple_of(core * width, width), width)]
     for step, out in enumerate(outs):
@@ -322,7 +319,7 @@
     shape = (size // SIDE, size // CORES)
     return pl.pallas_call(
         weight_kernel,
-        in_specs=[SMEM] + [VMEM] * 3,
+        in_specs=[SMEM] * 2 + [VMEM] * 3,
         out_specs=[VMEM] * SIDE,
         out_shape=[jax.ShapeDtypeStruct(shape, F32)]
         + [jax.ShapeDtypeStruct(shape, BF16)] * (SIDE - 1),
@@ -330,7 +327,7 @@
         cost_estimate=pl.CostEstimate(
             flops=size * size * width, bytes_accessed=4 * MIB, transcendentals=0
         ),
-    )(jnp.stack([core, me]), dpre, agg_rows, other)
+    )(core[None], me[None], dpre, agg_rows, other)
 
 
 def add_kernel(index_ref, *refs):
@@ -405,29 +402,44 @@
     ]
 
 
-def weight_rows(sent, dpre, agg_rows, groups, own_rows):
+def weight_parts(sent, dpre, agg_rows, groups, own_rows, second_cols):
     feat, node = lax.axis_index("feat"), lax.axis_index("node")
     other = lax.ppermute(sent, "feat", [(i, i ^ 1) for i in range(groups)])
     pieces = weight_pieces(lax.rem(feat, CORES), lax.div(node, SIDE), dpre, agg_rows, other)
     parts = sent_round(pieces, "node", lambda i, s: (i + s * SIDE) % (SIDE * SIDE))
     parts, own_rows = lax.optimization_barrier((parts, own_rows))
     pieces = added_pieces(lax.rem(node, SIDE), parts)
+    _, second_cols, own_rows = lax.optimization_barrier((pieces, second_cols, own_rows))
     parts = sent_round(pieces, "node", lambda i, s: i // SIDE * SIDE + (i + s) % SIDE)
-    total = parts[0]
+    return parts, own_rows, second_cols
+
+
+def piece_at(pieces, index):
+    return lax.dynamic_index_in_dim(pieces, index, 0, keepdims=False)
+
+
+def weight_total(parts, groups, halo):
+    feat = lax.axis_index("feat")
+    value = parts[0]
     for part in parts[1:]:
-        total = total + part.astype(F32)
-    total = total.reshape(groups, EXTRA // 2, -1)
-    high = total.astype(BF16)
-    low = (total - high.astype(F32)).astype(BF16)
-    rows = jnp.concatenate([high, low], axis=1)
-    return lax.dynamic_update_slice(own_rows, rows, (0, own_rows.shape[1] - EXTRA, 0))
-
-
-def weight_total(rows):
-    groups, count, width = rows.shape
-    rows = rows.astype(F32).reshape(groups // CORES, CORES, 2, count // 2, width)
-    total = jnp.sum(rows, axis=(0, 2))
-    return jnp.concatenate([total[i] for i in range(CORES)], axis=1)
+        value = value + part.astype(F32)
+    width = value.shape[1]
+    half = groups // 2
+    while half >= CORES:
+        if half == CORES:
+            value, _ = lax.optimization_barrier((value, halo))
+        bit = lax.rem(lax.div(feat, half), 2)
+        pieces = value.reshape(2, -1, width)
+        flip = [(i, i ^ half) for i in range(groups)]
+        value = piece_at(pieces, bit) + lax.ppermute(piece_at(pieces, 1 - bit), "feat", flip)
+        half //= 2
+    core = lax.rem(feat, CORES)
+    pieces = value.reshape(CORES, -1, width)
+    flip = [(i, i ^ 1) for i in range(groups)]
+    other = lax.ppermute(piece_at(pieces, 1 - core), "feat", flip)
+    kept = piece_at(pieces, core)
+    first, second = jnp.where(core == 0, kept, other), jnp.where(core == 0, other, kept)
+    return jnp.concatenate([first, second], axis=1)
 
 
 def paired(tiles):
@@ -468,11 +480,15 @@
     )
     second_cols = exchange(second.reshape(groups, feat_dev, -1), "feat")
     own_rows = own_part(self_back, dpre, dagg, turned, groups)
-    own_cols = exchange(weight_rows(sent, dpre, agg_rows, groups, own_rows), "feat")
+    parts, own_rows, second_cols = weight_parts(
+        sent, dpre, agg_rows, groups, own_rows, second_cols
+    )
+    own_cols = exchange(own_rows, "feat")
     to_before, spread, to_after = scatter(col, second_cols)
     from_after = shifted(to_before, "node", -1)
     from_before = shifted(to_after, "node", 1)
-    grad_w_neigh = weight_total(own_cols[:, feat_dev:])
+    parts, _ = lax.optimization_barrier((parts, spread))
+    grad_w_neigh = weight_total(parts, groups, (from_after, from_before))
     grad_features = finish(spread, from_before, from_after, own_cols)
     return (hidden, grad_features, grad_w_neigh)
 

time: 178 us -> 179 us (level)
  starting transfers between devices: 54.9 us -> 62.5 us
  waiting for transfers between devices: 66.3 us -> 62.5 us
  other arithmetic: 4.78 us -> 2.61 us
    ppermute x1 -> x5, waiting for transfers between devices: 0.01 us -> 17.1 us  [the longest x3 13.7 us: weight_total(): lax.ppermute(piece_at(pieces, 1 - bit), 'feat', flip)]
    all_to_all x4, waiting for transfers between devices: 29.2 us -> 12.2 us  [exchange(): return lax.all_to_all(value, axis, split_axis=0, concat_axis=0, tiled=True)]
    ppermute x1 -> x5, starting transfers between devices: 1.77 us -> 8.22 us  [the longest x3 7.6 us: weight_total(): lax.ppermute(piece_at(pieces, 1 - bit), 'feat', flip)]
    ppermute x6, waiting for transfers between devices: 11.2 us -> 6.88 us  [sent_round(): lax.ppermute(piece, axis, [(i, partner(i, step + 1)) for i in range(count)])]
    unnamed x26 -> x34, local copies, waits for them, and re-layouts: 9.43 us -> 10.1 us
  transfers between devices with their start and end apart: 15 -> 19, of which waited for: 11 -> 13; matrix products, arithmetic and copies ran while one was open for 9% -> 7% of each run, Pallas kernels for 12% -> 12%
where the time goes in v7:
time: 179 us; the launch traced here: 177 us
  starting transfers between devices  62.5 us (35%)
  waiting for transfers between devices  62.5 us (35%)
  Pallas kernels  35.9 us (20%)
  local copies, waits for them, and re-layouts  12.5 us (7%)
  other arithmetic  2.61 us (1%)
    all_to_all x4, starting transfers between devices, exchange(): return lax.all_to_all(value, axis, split_axis=0, concat_axis=0, tiled=True)  27.4 us
    ppermute x4, waiting for transfers between devices, shifted(): lax.ppermute(value, axis, [(source, source + steps) for source in range(f...  26.3 us
    ppermute x4, starting transfers between devices, shifted(): lax.ppermute(value, axis, [(source, source + steps) for source in range(f...  15.9 us
    ppermute x3, waiting for transfers between devices, weight_total(): lax.ppermute(piece_at(pieces, 1 - bit), 'feat', flip)  13.7 us
    all_to_all x4, waiting for transfers between devices, exchange(): return lax.all_to_all(value, axis, split_axis=0, concat_axis=0, tiled=True)  12.2 us
    ppermute x6, starting transfers between devices, sent_round(): lax.ppermute(piece, axis, [(i, partner(i, step + 1)) for i in range(count)])  11 us
    unnamed x34, local copies, waits for them, and re-layouts  10.1 us
    pallas_call x1, Pallas kernels, dense(): pl.pallas_call(functools.partial(dense_kernel, chunk), in_specs=[SMEM] +...  8.23 us
  transfers between devices with their start and end apart: 19, of which 13 were waited for; matrix products, arithmetic and copies ran while one was open for 7% of the time, Pallas kernels for 12%

profile of v7, /device:TPU:2, one launch (start us, length us, event | category | flops | bytes accessed | tf_op | source)
XLA Modules:
  0.0 177.1 jit_solution(17357529731313546648)
XLA Ops:
  0.6 2.2 %shard_map.94 = bf16[16,64,512]{2,1,0:T(8,128)(2,1)} custom-call(bf16[64,8192]{1,0:T(8,128)(2,1)} %own.1), custom_call_target="tpu_custom_call" | custom-call | tf_op jit(solution)/shard_map/pallas_call | solution.py:61
  2.9 8.6 %all-to-all-start = ((bf16[16,64,512]{2,1,0:T(8,128)(2,1)}), bf16[16,64,512]{2,1,0:T(8,128)(2,1)}, u32[]{:S(2)}, u32[]{:S(2)}) async-start(bf16[16,64,512]{2,1,0:T(8,128)(2,1)} %shard_map.94), calls=%async_computation | async-start | bytes 2097152 | tf_op jit(solution)/shard_map/all_to_all | solution.py:390
  11.5 3.5 %collective-permute-start = (bf16[64,8192]{1,0:T(8,128)(2,1)S(1)}, bf16[64,8192]{1,0:T(8,128)(2,1)S(1)}, u32[]{:S(2)}, u32[]{:S(2)}) collective-permute-start(bf16[64,8192]{1,0:T(8,128)(2,1)S(1)} %copy-done), channel_id=1, source_target_pairs={{0,16},{16,32},{32,48},{48,64},{64,80},{80,96},{96,112},{112,128},... | collective-permute-start | bytes 3145736 | tf_op jit(solution)/shard_map/ppermute | solution.py:386
  15.0 4.5 %collective-permute-start.1 = (bf16[64,8192]{1,0:T(8,128)(2,1)S(1)}, bf16[64,8192]{1,0:T(8,128)(2,1)S(1)}, u32[]{:S(2)}, u32[]{:S(2)}) collective-permute-start(bf16[64,8192]{1,0:T(8,128)(2,1)S(1)} %copy-done), channel_id=1, source_target_pairs={{16,0},{32,16},{48,32},{64,48},{80,64},{96,80},{112,96},{128,112},... | collective-permute-start | bytes 3145736 | tf_op jit(solution)/shard_map/ppermute | solution.py:386
  19.6 21.4 %collective-permute-done.before = bf16[64,8192]{1,0:T(8,128)(2,1)S(1)} collective-permute-done((bf16[64,8192]{1,0:T(8,128)(2,1)S(1)}, bf16[64,8192]{1,0:T(8,128)(2,1)S(1)}, u32[]{:S(2)}, u32[]{:S(2)}) %collective-permute-start) | collective-permute-done | bytes 1048608 | tf_op jit(solution)/shard_map/ppermute | solution.py:386
  42.2 2.9 %shard_map.95 = bf16[16,64,512]{2,1,0:T(8,128)(2,1)} custom-call(s32[64]{0:T(128)S(1)} %subtract_bitcast_fusion.col_ref, bf16[64,8192]{1,0:T(8,128)(2,1)S(1)} %collective-permute-done.before, bf16[64,8192]{1,0:T(8,128)(2,1)S(1)} %copy-done, bf16[64,8192]{1,0:T(8,128)(2,1)S(1)} %collective-permute-done.1.after), custom_call_target="tpu_custom_call" | custom-call | bytes 8388608 | tf_op jit(solution)/shard_map/pallas_call | solution.py:105
  45.1 7.1 %all-to-all-start.1 = ((bf16[16,64,512]{2,1,0:T(8,128)(2,1)}), bf16[16,64,512]{2,1,0:T(8,128)(2,1)S(1)}, u32[]{:S(2)}, u32[]{:S(2)}) async-start(bf16[16,64,512]{2,1,0:T(8,128)(2,1)} %shard_map.95), calls=%async_computation.1 | async-start | bytes 2097152 | tf_op jit(solution)/shard_map/all_to_all | solution.py:390
  53.9 2.6 %copy.14 = bf16[1024,1024]{0,1:T(8,128)(2,1)} copy(bf16[1024,1024]{1,0:T(8,128)(2,1)S(1)} %copy-done.2) | data formatting | bytes 4194304 | tf_op args[4]
  56.5 3.9 %copy.15 = bf16[1024,1024]{0,1:T(8,128)(2,1)} copy(bf16[1024,1024]{1,0:T(8,128)(2,1)} %refs_5_.1) | data formatting | bytes 4194304 | tf_op args[5]
  62.5 4.5 %shard_map.96.refs_6_ = f32[1024,512]{1,0:T(8,128)} custom-call(bf16[1024,1024]{1,0:T(8,128)(2,1)} %w_self.1, bf16[1024,512]{1,0:T(8,128)(2,1)} %bitcast.1.x_ref.refs_3_), custom_call_target="tpu_custom_call" | custom-call | flops 1073741824 | bytes 5242880 | tf_op jit(solution)/shard_map/pallas_call | solution.py:191
  66.9 11.9 %all-to-all-done.1 = bf16[16,64,512]{2,1,0:T(8,128)(2,1)S(1)} async-done(((bf16[16,64,512]{2,1,0:T(8,128)(2,1)}), bf16[16,64,512]{2,1,0:T(8,128)(2,1)S(1)}, u32[]{:S(2)}, u32[]{:S(2)}) %all-to-all-start.1) | async-done | bytes 1048608 | tf_op jit(solution)/shard_map/all_to_all | solution.py:390
  79.8 8.2 %shard_map.97 = (bf16[1024,512]{1,0:T(8,128)(2,1)}, bf16[1024,512]{1,0:T(8,128)(2,1)}, bf16[1024,512]{1,0:T(8,128)(2,1)}, bf16[1024,512]{1,0:T(8,128)(2,1)}, bf1...) custom-call(s32[1]{0:T(128)S(6)} %sub.26.refs_0_, bf16[2,2,256,256]{3,2,1,0:T(8,128)(2,1)} %copy.21.refs_1_, ...), custom_call_target="tpu_custom_call" | custom-call | flops 2147483648 | bytes 16777216 | tf_op jit(solution)/shard_map/pallas_call | solution.py:264
  88.0 4.9 %all-to-all-start.2 = ((bf16[16,64,512]{2,1,0:T(8,128)(2,1)}), bf16[16,64,512]{2,1,0:T(8,128)(2,1)S(1)}, u32[]{:S(2)}, u32[]{:S(2)}) async-start(bf16[16,64,512]{2,1,0:T(8,128)(2,1)} %bitcast.51), calls=%async_computation.2 | async-start | bytes 2097152 | tf_op jit(solution)/shard_map/all_to_all | solution.py:390
  93.5 2.3 %collective-permute-done.2.other_ref = bf16[1024,512]{1,0:T(8,128)(2,1)S(1)} collective-permute-done((bf16[1024,512]{1,0:T(8,128)(2,1)S(1)}, bf16[1024,512]{1,0:T(8,128)(2,1)S(1)}, u32[]{:S(2)}, u32[]{:S(2)}) %collective-permute-start.2) | collective-permute-done | bytes 1048608 | tf_op jit(solution)/shard_map/ppermute | solution.py:407
  96.8 3.3 %shard_map.98 = (f32[256,512]{1,0:T(8,128)}, bf16[256,512]{1,0:T(8,128)(2,1)}, bf16[256,512]{1,0:T(8,128)(2,1)}, bf16[256,512]{1,0:T(8,128)(2,1)}) custom-call(s32[1]{0:T(128)} %bitcast.core_ref, s32[1]{0:T(128)} %bitcast.16.me_ref, bf16[1024,512]{1,0:T(8,128)(2,1)} %get-tuple-element.42.dpre, bf16[1024,512]{1,0:T(8,128)(2,1)} %get-tuple-element.43.agg_ref, ...), custom_call_target="tpu_custom_call" | custom-call | flops 536870912 | bytes 4194304 | tf_op jit(solution)/shard_map/pallas_call | solution.py:320
  102.7 2.2 %collective-permute-start.5 = (bf16[256,512]{1,0:T(8,128)(2,1)}, bf16[256,512]{1,0:T(8,128)(2,1)S(1)}, u32[]{:S(2)}, u32[]{:S(2)}) collective-permute-start(bf16[256,512]{1,0:T(8,128)(2,1)} %get-tuple-element.48), channel_id=1, source_target_pairs={{0,192},{16,208},{32,224},{48,240},{64,0},{80,16},{96,32},{112,48}... | collective-permute-start | bytes 786440 | tf_op jit(solution)/shard_map/ppermute | solution.py:400
  104.8 4.8 %shard_map.99 = bf16[16,64,512]{2,1,0:T(8,128)(2,1)} custom-call(bf16[1024,1024]{1,0:T(8,128)(2,1)} %bitcast.48, bf16[1024,512]{1,0:T(8,128)(2,1)} %get-tuple-element.42.dpre, bf16[1024,512]{1,0:T(8,128)(2,1)} %get-tuple-element.50.dagg_ref, bf16[2,2,256,256]{3,2,1,0:T(8,128)(2,1)} %get-tuple-element.38.refs_2_.turned), custom_call_target="tpu_custom_call" | custom-call | flops 1073741824 | bytes 5242880 | tf_op jit(solution)/shard_map/pallas_call | solution.py:295
  109.6 2.9 %collective-permute-done.4.refs_2_ = bf16[256,512]{1,0:T(8,128)(2,1)S(1)} collective-permute-done((bf16[256,512]{1,0:T(8,128)(2,1)}, bf16[256,512]{1,0:T(8,128)(2,1)S(1)}, u32[]{:S(2)}, u32[]{:S(2)}) %collective-permute-start.4) | collective-permute-done | bytes 262176 | tf_op jit(solution)/shard_map/ppermute | solution.py:400
  112.5 4.0 %collective-permute-done.5.refs_3_ = bf16[256,512]{1,0:T(8,128)(2,1)S(1)} collective-permute-done((bf16[256,512]{1,0:T(8,128)(2,1)}, bf16[256,512]{1,0:T(8,128)(2,1)S(1)}, u32[]{:S(2)}, u32[]{:S(2)}) %collective-permute-start.5) | collective-permute-done | bytes 262176 | tf_op jit(solution)/shard_map/ppermute | solution.py:400
  117.2 2.0 %shard_map.100 = (f32[64,512]{1,0:T(8,128)}, bf16[64,512]{1,0:T(8,128)(2,1)}, bf16[64,512]{1,0:T(8,128)(2,1)}, bf16[64,512]{1,0:T(8,128)(2,1)}) custom-call(s32[1]{0:T(128)} %bitcast.15.index_ref, f32[256,512]{1,0:T(8,128)} %get-tuple-element.51.refs_0_, bf16[256,512]{1,0:T(8,128)(2,1)} %copy-done.6, bf16[256,512]{1,0:T(8,128)(2,1)} %copy-done.7, ...), custom_call_target="tpu_custom_call" | custom-call | bytes 2097152 | tf_op jit(solution)/shard_map/pallas_call | solution.py:347
  119.6 6.7 %all-to-all-start.3 = ((bf16[16,64,512]{2,1,0:T(8,128)(2,1)}), bf16[16,64,512]{2,1,0:T(8,128)(2,1)S(1)}, u32[]{:S(2)}, u32[]{:S(2)}) async-start(bf16[16,64,512]{2,1,0:T(8,128)(2,1)} %shard_map.99), calls=%async_computation.3 | async-start | bytes 2097152 | tf_op jit(solution)/shard_map/all_to_all | solution.py:390
  126.4 4.7 %collective-permute-start.10 = (bf16[64,512]{1,0:T(8,128)(2,1)}, bf16[64,512]{1,0:T(8,128)(2,1)S(1)}, u32[]{:S(2)}, u32[]{:S(2)}) collective-permute-start(bf16[64,512]{1,0:T(8,128)(2,1)} %get-tuple-element.58), channel_id=1, source_target_pairs={{0,48},{16,0},{32,16},{48,32},{64,112},{80,64},{96,80},{112,96},{1... | collective-permute-start | bytes 196616 | tf_op jit(solution)/shard_map/ppermute | solution.py:400
  132.6 4.2 %shard_map.101 = (bf16[64,64,128]{2,1,0:T(8,128)(2,1)}, f32[64,64,128]{2,1,0:T(8,128)}, bf16[64,64,128]{2,1,0:T(8,128)(2,1)}) custom-call(s32[64]{0:T(128)} %copy-done.1, bf16[16,64,512]{2,1,0:T(8,128)(2,1)} %copy-done.3), custom_call_target="tpu_custom_call" | custom-call | bytes 8388608 | tf_op jit(solution)/shard_map/pallas_call | solution.py:161
  136.8 4.4 %collective-permute-start.6 = (bf16[64,64,128]{2,1,0:T(8,128)(2,1)}, bf16[64,64,128]{2,1,0:T(8,128)(2,1)S(1)}, u32[]{:S(2)}, u32[]{:S(2)}) collective-permute-start(bf16[64,64,128]{2,1,0:T(8,128)(2,1)} %get-tuple-element.63), channel_id=1, source_target_pairs={{0,16},{16,32},{32,48},{48,64},{64,80},{80,96},{96,112},{112,128},... | collective-permute-start | bytes 3145736 | tf_op jit(solution)/shard_map/ppermute | solution.py:386
  141.3 3.5 %collective-permute-start.7 = (bf16[64,64,128]{2,1,0:T(8,128)(2,1)}, bf16[64,64,128]{2,1,0:T(8,128)(2,1)S(1)}, u32[]{:S(2)}, u32[]{:S(2)}) collective-permute-start(bf16[64,64,128]{2,1,0:T(8,128)(2,1)} %get-tuple-element.64), channel_id=1, source_target_pairs={{16,0},{32,16},{48,32},{64,48},{80,64},{96,80},{112,96},{128,112},... | collective-permute-start | bytes 3145736 | tf_op jit(solution)/shard_map/ppermute | solution.py:386
  146.4 5.8 %collective-permute-start.11 = (f32[32,512]{1,0:T(8,128)S(1)}, f32[32,512]{1,0:T(8,128)S(1)}, u32[]{:S(2)}, u32[]{:S(2)}) collective-permute-start(f32[32,512]{1,0:T(8,128)S(1)} %dynamic-slice_bitcast_fusion), channel_id=1, source_target_pairs={{0,8},{1,9},{2,10},{3,11},{4,12},{5,13},{6,14},{7,15},{8,0},{9,1},... | collective-permute-start | bytes 196616 | tf_op jit(solution)/shard_map/ppermute | solution.py:434
  152.2 6.5 %collective-permute-done.11 = f32[32,512]{1,0:T(8,128)S(1)} collective-permute-done((f32[32,512]{1,0:T(8,128)S(1)}, f32[32,512]{1,0:T(8,128)S(1)}, u32[]{:S(2)}, u32[]{:S(2)}) %collective-permute-start.11) | collective-permute-done | bytes 65568 | tf_op jit(solution)/shard_map/ppermute | solution.py:434
  158.8 5.1 %collective-permute-done.12 = f32[16,512]{1,0:T(8,128)S(1)} collective-permute-done((f32[16,512]{1,0:T(8,128)S(1)}, f32[16,512]{1,0:T(8,128)S(1)}, u32[]{:S(2)}, u32[]{:S(2)}) %collective-permute-start.12) | collective-permute-done | bytes 32800 | tf_op jit(solution)/shard_map/ppermute | solution.py:434
  164.0 1.9 %collective-permute-done.6.before_ref = bf16[64,64,128]{2,1,0:T(8,128)(2,1)S(1)} collective-permute-done((bf16[64,64,128]{2,1,0:T(8,128)(2,1)}, bf16[64,64,128]{2,1,0:T(8,128)(2,1)S(1)}, u32[]{:S(2)}, u32[]{:S(2)}) %collective-permute-start.6) | collective-permute-done | bytes 1048608 | tf_op jit(solution)/shard_map/ppermute | solution.py:386
  165.9 1.8 %collective-permute-done.7.after_ref = bf16[64,64,128]{2,1,0:T(8,128)(2,1)S(1)} collective-permute-done((bf16[64,64,128]{2,1,0:T(8,128)(2,1)}, bf16[64,64,128]{2,1,0:T(8,128)(2,1)S(1)}, u32[]{:S(2)}, u32[]{:S(2)}) %collective-permute-start.7) | collective-permute-done | bytes 1048608 | tf_op jit(solution)/shard_map/ppermute | solution.py:386
  169.3 2.1 %collective-permute-done.13 = f32[8,512]{1,0:T(8,128)S(1)} collective-permute-done((f32[8,512]{1,0:T(8,128)S(1)}, f32[8,512]{1,0:T(8,128)S(1)}, u32[]{:S(2)}, u32[]{:S(2)}) %collective-permute-start.13) | collective-permute-done | bytes 16416 | tf_op jit(solution)/shard_map/ppermute | solution.py:434
  173.3 3.8 %shard_map.102 = bf16[64,8192]{1,0:T(8,128)(2,1)} custom-call(f32[64,64,128]{2,1,0:T(8,128)} %get-tuple-element.62.own_ref, bf16[64,64,128]{2,1,0:T(8,128)(2,1)S(1)} %collective-permute-done.6.before_ref, bf16[64,64,128]{2,1,0:T(8,128)(2,1)S(1)} %collective-permute-done.7.after_ref, bf16[16,64,512]{2,1,0:T(8,128)(2,1)S(1)} %all-to-all-done.3.dself_ref), custom_call_target="tpu_custom_call" | custom-call | tf_op jit(solution)/shard_map/pallas_call | solution.py:372
  (72 shorter events, 17.8 us)
Async XLA Ops:
  0.6 10.9 %copy-start = (bf16[64,8192]{1,0:T(8,128)(2,1)S(1)}, bf16[64,8192]{1,0:T(8,128)(2,1)}, u32[]{:S(2)}) copy-start(bf16[64,8192]{1,0:T(8,128)(2,1)} %own.1) | copy-start | bytes 3145732
  0.6 18.9 %copy-start.13 = (s32[64,2]{0,1:T(2,128)S(1)}, s32[64,2]{0,1:T(2,128)}, u32[]{:S(2)}) copy-start(s32[64,2]{0,1:T(2,128)} %param.9) | copy-start | bytes 1540
  2.9 42.2 %all-to-all-start = ((bf16[16,64,512]{2,1,0:T(8,128)(2,1)}), bf16[16,64,512]{2,1,0:T(8,128)(2,1)}, u32[]{:S(2)}, u32[]{:S(2)}) async-start(bf16[16,64,512]{2,1,0:T(8,128)(2,1)} %shard_map.94), calls=%async_computation | async-start | bytes 2097152 | tf_op jit(solution)/shard_map/all_to_all | solution.py:390
  11.5 29.4 %collective-permute-start = (bf16[64,8192]{1,0:T(8,128)(2,1)S(1)}, bf16[64,8192]{1,0:T(8,128)(2,1)S(1)}, u32[]{:S(2)}, u32[]{:S(2)}) collective-permute-start(bf16[64,8192]{1,0:T(8,128)(2,1)S(1)} %copy-done), channel_id=1, source_target_pairs={{0,16},{16,32},{32,48},{48,64},{64,80},{80,96},{96,112},{112,128},... | collective-permute-start | bytes 3145736 | tf_op jit(solution)/shard_map/ppermute | solution.py:386
  15.0 27.1 %collective-permute-start.1 = (bf16[64,8192]{1,0:T(8,128)(2,1)S(1)}, bf16[64,8192]{1,0:T(8,128)(2,1)S(1)}, u32[]{:S(2)}, u32[]{:S(2)}) collective-permute-start(bf16[64,8192]{1,0:T(8,128)(2,1)S(1)} %copy-done), channel_id=1, source_target_pairs={{16,0},{32,16},{48,32},{64,48},{80,64},{96,80},{112,96},{128,112},... | collective-permute-start | bytes 3145736 | tf_op jit(solution)/shard_map/ppermute | solution.py:386
  19.5 25.5 %copy-start.1 = (s32[64]{0:T(128)}, s32[64]{0:T(128)S(1)}, u32[]{:S(2)}) copy-start(s32[64]{0:T(128)S(1)} %subtract_bitcast_fusion.col_ref) | copy-start | bytes 772
  45.0 8.3 %copy-start.14 = (s32[64]{0:T(128)S(1)}, s32[64]{0:T(128)}, u32[]{:S(2)}) copy-start(s32[64]{0:T(128)} %param.10) | copy-start | bytes 772
  45.0 8.8 %copy-start.2 = (bf16[1024,1024]{1,0:T(8,128)(2,1)S(1)}, bf16[1024,1024]{1,0:T(8,128)(2,1)}, u32[]{:S(2)}) copy-start(bf16[1024,1024]{1,0:T(8,128)(2,1)} %w_self.1) | copy-start | bytes 6291460
  45.1 33.8 %all-to-all-start.1 = ((bf16[16,64,512]{2,1,0:T(8,128)(2,1)}), bf16[16,64,512]{2,1,0:T(8,128)(2,1)S(1)}, u32[]{:S(2)}, u32[]{:S(2)}) async-start(bf16[16,64,512]{2,1,0:T(8,128)(2,1)} %shard_map.95), calls=%async_computation.1 | async-start | bytes 2097152 | tf_op jit(solution)/shard_map/all_to_all | solution.py:390
  78.8 1.0 copy-start.4
  88.0 5.0 %copy-start.11 = (bf16[1024,512]{1,0:T(8,128)(2,1)S(1)}, bf16[1024,512]{1,0:T(8,128)(2,1)}, u32[]{:S(2)}) copy-start(bf16[1024,512]{1,0:T(8,128)(2,1)} %get-tuple-element.44) | copy-start | bytes 3145732
  88.0 31.6 %all-to-all-start.2 = ((bf16[16,64,512]{2,1,0:T(8,128)(2,1)}), bf16[16,64,512]{2,1,0:T(8,128)(2,1)S(1)}, u32[]{:S(2)}, u32[]{:S(2)}) async-start(bf16[16,64,512]{2,1,0:T(8,128)(2,1)} %bitcast.51), calls=%async_computation.2 | async-start | bytes 2097152 | tf_op jit(solution)/shard_map/all_to_all | solution.py:390
  93.0 2.8 %collective-permute-start.2 = (bf16[1024,512]{1,0:T(8,128)(2,1)S(1)}, bf16[1024,512]{1,0:T(8,128)(2,1)S(1)}, u32[]{:S(2)}, u32[]{:S(2)}) collective-permute-start(bf16[1024,512]{1,0:T(8,128)(2,1)S(1)} %copy-done.11), channel_id=1, source_target_pairs={{0,1},{1,0},{2,3},{3,2},{4,5},{5,4},{6,7},{7,6},{8,9},{9,8},{10,11... | collective-permute-start | bytes 3145736 | tf_op jit(solution)/shard_map/ppermute | solution.py:407
  95.8 1.0 copy-start.5
  100.1 9.6 %collective-permute-start.3 = (bf16[256,512]{1,0:T(8,128)(2,1)}, bf16[256,512]{1,0:T(8,128)(2,1)S(1)}, u32[]{:S(2)}, u32[]{:S(2)}) collective-permute-start(bf16[256,512]{1,0:T(8,128)(2,1)} %get-tuple-element.46), channel_id=1, source_target_pairs={{0,64},{16,80},{32,96},{48,112},{64,128},{80,144},{96,160},{112,17... | collective-permute-start | bytes 786440 | tf_op jit(solution)/shard_map/ppermute | solution.py:400
  101.6 10.9 %collective-permute-start.4 = (bf16[256,512]{1,0:T(8,128)(2,1)}, bf16[256,512]{1,0:T(8,128)(2,1)S(1)}, u32[]{:S(2)}, u32[]{:S(2)}) collective-permute-start(bf16[256,512]{1,0:T(8,128)(2,1)} %get-tuple-element.47), channel_id=1, source_target_pairs={{0,128},{16,144},{32,160},{48,176},{64,192},{80,208},{96,224},{112... | collective-permute-start | bytes 786440 | tf_op jit(solution)/shard_map/ppermute | solution.py:400
  102.7 13.8 %collective-permute-start.5 = (bf16[256,512]{1,0:T(8,128)(2,1)}, bf16[256,512]{1,0:T(8,128)(2,1)S(1)}, u32[]{:S(2)}, u32[]{:S(2)}) collective-permute-start(bf16[256,512]{1,0:T(8,128)(2,1)} %get-tuple-element.48), channel_id=1, source_target_pairs={{0,192},{16,208},{32,224},{48,240},{64,0},{80,16},{96,32},{112,48}... | collective-permute-start | bytes 786440 | tf_op jit(solution)/shard_map/ppermute | solution.py:400
  109.6 6.9 %copy-start.6 = (bf16[256,512]{1,0:T(8,128)(2,1)}, bf16[256,512]{1,0:T(8,128)(2,1)S(1)}, u32[]{:S(2)}) copy-start(bf16[256,512]{1,0:T(8,128)(2,1)S(1)} %collective-permute-done.3.refs_1_) | copy-start | bytes 786436
  112.5 4.0 %copy-start.7 = (bf16[256,512]{1,0:T(8,128)(2,1)}, bf16[256,512]{1,0:T(8,128)(2,1)S(1)}, u32[]{:S(2)}) copy-start(bf16[256,512]{1,0:T(8,128)(2,1)S(1)} %collective-permute-done.4.refs_2_) | copy-start | bytes 786436
  119.3 11.8 %copy-start.12 = (bf16[64,512]{1,0:T(8,128)(2,1)S(1)}, bf16[64,512]{1,0:T(8,128)(2,1)}, u32[]{:S(2)}) copy-start(bf16[64,512]{1,0:T(8,128)(2,1)} %get-tuple-element.57) | copy-start | bytes 196612
  119.3 26.2 %copy-start.9 = (f32[64,512]{1,0:T(8,128)S(1)}, f32[64,512]{1,0:T(8,128)}, u32[]{:S(2)}) copy-start(f32[64,512]{1,0:T(8,128)} %get-tuple-element.66) | copy-start | bytes 393220
  119.6 13.0 %copy-start.3 = (bf16[16,64,512]{2,1,0:T(8,128)(2,1)}, bf16[16,64,512]{2,1,0:T(8,128)(2,1)S(1)}, u32[]{:S(2)}) copy-start(bf16[16,64,512]{2,1,0:T(8,128)(2,1)S(1)} %all-to-all-done.2.parts_hbm) | copy-start | bytes 3145732
  119.6 53.7 %all-to-all-start.3 = ((bf16[16,64,512]{2,1,0:T(8,128)(2,1)}), bf16[16,64,512]{2,1,0:T(8,128)(2,1)S(1)}, u32[]{:S(2)}, u32[]{:S(2)}) async-start(bf16[16,64,512]{2,1,0:T(8,128)(2,1)} %shard_map.99), calls=%async_computation.3 | async-start | bytes 2097152 | tf_op jit(solution)/shard_map/all_to_all | solution.py:390
  126.4 18.4 %collective-permute-start.10 = (bf16[64,512]{1,0:T(8,128)(2,1)}, bf16[64,512]{1,0:T(8,128)(2,1)S(1)}, u32[]{:S(2)}, u32[]{:S(2)}) collective-permute-start(bf16[64,512]{1,0:T(8,128)(2,1)} %get-tuple-element.58), channel_id=1, source_target_pairs={{0,48},{16,0},{32,16},{48,32},{64,112},{80,64},{96,80},{112,96},{1... | collective-permute-start | bytes 196616 | tf_op jit(solution)/shard_map/ppermute | solution.py:400
  131.1 13.7 %collective-permute-start.8 = (bf16[64,512]{1,0:T(8,128)(2,1)}, bf16[64,512]{1,0:T(8,128)(2,1)S(1)}, u32[]{:S(2)}, u32[]{:S(2)}) collective-permute-start(bf16[64,512]{1,0:T(8,128)(2,1)} %get-tuple-element.56), channel_id=1, source_target_pairs={{0,16},{16,32},{32,48},{48,0},{64,80},{80,96},{96,112},{112,64},{1... | collective-permute-start | bytes 196616 | tf_op jit(solution)/shard_map/ppermute | solution.py:400
  131.1 13.7 %collective-permute-start.9 = (bf16[64,512]{1,0:T(8,128)(2,1)S(1)}, bf16[64,512]{1,0:T(8,128)(2,1)S(1)}, u32[]{:S(2)}, u32[]{:S(2)}) collective-permute-start(bf16[64,512]{1,0:T(8,128)(2,1)S(1)} %copy-done.12), channel_id=1, source_target_pairs={{0,32},{16,48},{32,0},{48,16},{64,96},{80,112},{96,64},{112,80},{1... | collective-permute-start | bytes 196616 | tf_op jit(solution)/shard_map/ppermute | solution.py:400
  136.8 29.0 %collective-permute-start.6 = (bf16[64,64,128]{2,1,0:T(8,128)(2,1)}, bf16[64,64,128]{2,1,0:T(8,128)(2,1)S(1)}, u32[]{:S(2)}, u32[]{:S(2)}) collective-permute-start(bf16[64,64,128]{2,1,0:T(8,128)(2,1)} %get-tuple-element.63), channel_id=1, source_target_pairs={{0,16},{16,32},{32,48},{48,64},{64,80},{80,96},{96,112},{112,128},... | collective-permute-start | bytes 3145736 | tf_op jit(solution)/shard_map/ppermute | solution.py:386
  141.3 26.4 %collective-permute-start.7 = (bf16[64,64,128]{2,1,0:T(8,128)(2,1)}, bf16[64,64,128]{2,1,0:T(8,128)(2,1)S(1)}, u32[]{:S(2)}, u32[]{:S(2)}) collective-permute-start(bf16[64,64,128]{2,1,0:T(8,128)(2,1)} %get-tuple-element.64), channel_id=1, source_target_pairs={{16,0},{32,16},{48,32},{64,48},{80,64},{96,80},{112,96},{128,112},... | collective-permute-start | bytes 3145736 | tf_op jit(solution)/shard_map/ppermute | solution.py:386
  146.4 12.3 %collective-permute-start.11 = (f32[32,512]{1,0:T(8,128)S(1)}, f32[32,512]{1,0:T(8,128)S(1)}, u32[]{:S(2)}, u32[]{:S(2)}) collective-permute-start(f32[32,512]{1,0:T(8,128)S(1)} %dynamic-slice_bitcast_fusion), channel_id=1, source_target_pairs={{0,8},{1,9},{2,10},{3,11},{4,12},{5,13},{6,14},{7,15},{8,0},{9,1},... | collective-permute-start | bytes 196616 | tf_op jit(solution)/shard_map/ppermute | solution.py:434
  158.7 5.3 %collective-permute-start.12 = (f32[16,512]{1,0:T(8,128)S(1)}, f32[16,512]{1,0:T(8,128)S(1)}, u32[]{:S(2)}, u32[]{:S(2)}) collective-permute-start(f32[16,512]{1,0:T(8,128)S(1)} %dynamic-slice_bitcast_fusion.1), channel_id=1, source_target_pairs={{0,4},{1,5},{2,6},{3,7},{4,0},{5,1},{6,2},{7,3},{8,12},{9,13},{10,... | collective-permute-start | bytes 98312 | tf_op jit(solution)/shard_map/ppermute | solution.py:434
  167.7 3.7 %collective-permute-start.13 = (f32[8,512]{1,0:T(8,128)S(1)}, f32[8,512]{1,0:T(8,128)S(1)}, u32[]{:S(2)}, u32[]{:S(2)}) collective-permute-start(f32[8,512]{1,0:T(8,128)S(1)} %dynamic-slice_bitcast_fusion.2), channel_id=1, source_target_pairs={{0,2},{1,3},{2,0},{3,1},{4,6},{5,7},{6,4},{7,5},{8,10},{9,11},{10,... | collective-permute-start | bytes 49160 | tf_op jit(solution)/shard_map/ppermute | solution.py:434
  171.4 1.3 collective-permute-start.14
  (2 other events, 1.4 us)

commit v8 on v7

--- a/solution.py
+++ b/solution.py
@@ -308,9 +308,15 @@
     core, me = core_ref[0], me_ref[0]
     rows, width = outs[0].shape
     half = agg_ref.at[pl.ds(pl.multiple_of(core * width, width), width)]
+    each = rows // SIDE
+
+    def picked(ref, there):
+        first = lax.rem(me + there, SIDE) * each
+        places = [pl.multiple_of(i * rows + first, each) for i in range(SIDE)]
+        return jnp.concatenate([ref[pl.ds(place, each), :] for place in places], axis=0)
+
     for step, out in enumerate(outs):
-        here = pl.ds(pl.multiple_of(lax.rem(me + step, len(outs)) * rows, rows), rows)
-        total = dot(dpre[here, :], half[...], NT) + other_ref[here, :].astype(F32)
+        total = dot(picked(dpre, step), half[...], NT) + picked(other_ref, step).astype(F32)
         out[...] = total.astype(out.dtype)
 
 
@@ -402,31 +408,29 @@
     ]
 
 
-def weight_parts(sent, dpre, agg_rows, groups, own_rows, second_cols):
+def weight_pieces_along_x(sent, dpre, agg_rows, groups, own_rows):
     feat, node = lax.axis_index("feat"), lax.axis_index("node")
     other = lax.ppermute(sent, "feat", [(i, i ^ 1) for i in range(groups)])
-    pieces = weight_pieces(lax.rem(feat, CORES), lax.div(node, SIDE), dpre, agg_rows, other)
-    parts = sent_round(pieces, "node", lambda i, s: (i + s * SIDE) % (SIDE * SIDE))
+    pieces = weight_pieces(lax.rem(feat, CORES), lax.rem(node, SIDE), dpre, agg_rows, other)
+    parts = sent_round(pieces, "node", lambda i, s: i // SIDE * SIDE + (i + s) % SIDE)
     parts, own_rows = lax.optimization_barrier((parts, own_rows))
-    pieces = added_pieces(lax.rem(node, SIDE), parts)
-    _, second_cols, own_rows = lax.optimization_barrier((pieces, second_cols, own_rows))
-    parts = sent_round(pieces, "node", lambda i, s: i // SIDE * SIDE + (i + s) % SIDE)
-    return parts, own_rows, second_cols
+    return added_pieces(lax.div(node, SIDE), parts)
 
 
 def piece_at(pieces, index):
     return lax.dynamic_index_in_dim(pieces, index, 0, keepdims=False)
 
 
-def weight_total(parts, groups, halo):
+def weight_total(pieces, groups, halo):
     feat = lax.axis_index("feat")
+    parts = sent_round(pieces, "node", lambda i, s: (i + s * SIDE) % (SIDE * SIDE))
     value = parts[0]
     for part in parts[1:]:
         value = value + part.astype(F32)
     width = value.shape[1]
     half = groups // 2
     while half >= CORES:
-        if half == CORES:
+        if half == 2 * CORES:
             value, _ = lax.optimization_barrier((value, halo))
         bit = lax.rem(lax.div(feat, half), 2)
         pieces = value.reshape(2, -1, width)
@@ -480,15 +484,14 @@
     )
     second_cols = exchange(second.reshape(groups, feat_dev, -1), "feat")
     own_rows = own_part(self_back, dpre, dagg, turned, groups)
-    parts, own_rows, second_cols = weight_parts(
-        sent, dpre, agg_rows, groups, own_rows, second_cols
-    )
+    pieces = weight_pieces_along_x(sent, dpre, agg_rows, groups, own_rows)
+    _, second_cols, own_rows = lax.optimization_barrier((pieces, second_cols, own_rows))
     own_cols = exchange(own_rows, "feat")
     to_before, spread, to_after = scatter(col, second_cols)
     from_after = shifted(to_before, "node", -1)
     from_before = shifted(to_after, "node", 1)
-    parts, _ = lax.optimization_barrier((parts, spread))
-    grad_w_neigh = weight_total(parts, groups, (from_after, from_before))
+    pieces, _ = lax.optimization_barrier((pieces, spread))
+    grad_w_neigh = weight_total(pieces, groups, (from_after, from_before))
     grad_features = finish(spread, from_before, from_after, own_cols)
     return (hidden, grad_features, grad_w_neigh)
 

time: 179 us -> 190 us (1.061)
  waiting for transfers between devices: 62.5 us -> 76.9 us
  starting transfers between devices: 62.5 us -> 58.6 us
    ppermute x6, waiting for transfers between devices: 6.88 us -> 24.6 us  [sent_round(): lax.ppermute(piece, axis, [(i, partner(i, step + 1)) for i in range(count)])]
    ppermute x4, waiting for transfers between devices: 26.3 us -> 22.6 us  [shifted(): lax.ppermute(value, axis, [(source, source + steps) for source in range(f...]
    ppermute x3, starting transfers between devices: 7.6 us -> 4.97 us  [weight_total(): lax.ppermute(piece_at(pieces, 1 - bit), 'feat', flip)]
  transfers between devices with their start and end apart: 19 -> 19, of which waited for: 13 -> 12; matrix products, arithmetic and copies ran while one was open for 7% -> 6% of each run, Pallas kernels for 12% -> 9%
where the time goes in v8:
time: 190 us; the launch traced here: 188 us
  waiting for transfers between devices  76.9 us (40%)
  starting transfers between devices  58.6 us (31%)
  Pallas kernels  36 us (19%)
  local copies, waits for them, and re-layouts  12.9 us (7%)
  other arithmetic  2.61 us (1%)
    all_to_all x4, starting transfers between devices, exchange(): return lax.all_to_all(value, axis, split_axis=0, concat_axis=0, tiled=True)  27.6 us
    ppermute x6, waiting for transfers between devices, sent_round(): lax.ppermute(piece, axis, [(i, partner(i, step + 1)) for i in range(count)])  24.6 us
    ppermute x4, waiting for transfers between devices, shifted(): lax.ppermute(value, axis, [(source, source + steps) for source in range(f...  22.6 us
    ppermute x4, starting transfers between devices, shifted(): lax.ppermute(value, axis, [(source, source + steps) for source in range(f...  15.9 us
    ppermute x3, waiting for transfers between devices, weight_total(): lax.ppermute(piece_at(pieces, 1 - bit), 'feat', flip)  14.4 us
    all_to_all x4, waiting for transfers between devices, exchange(): return lax.all_to_all(value, axis, split_axis=0, concat_axis=0, tiled=True)  11.9 us
    unnamed x34, local copies, waits for them, and re-layouts  10.5 us
    ppermute x6, starting transfers between devices, sent_round(): lax.ppermute(piece, axis, [(i, partner(i, step + 1)) for i in range(count)])  9.54 us
  transfers between devices with their start and end apart: 19, of which 12 were waited for; matrix products, arithmetic and copies ran while one was open for 6% of the time, Pallas kernels for 9%

profile of v8, /device:TPU:2, one launch (start us, length us, event | category | flops | bytes accessed | tf_op | source)
XLA Modules:
  0.0 188.1 jit_solution(10389409412727981492)
XLA Ops:
  0.6 2.2 %shard_map.94 = bf16[16,64,512]{2,1,0:T(8,128)(2,1)} custom-call(bf16[64,8192]{1,0:T(8,128)(2,1)} %own.1), custom_call_target="tpu_custom_call" | custom-call | tf_op jit(solution)/shard_map/pallas_call | solution.py:61
  2.9 8.6 %all-to-all-start = ((bf16[16,64,512]{2,1,0:T(8,128)(2,1)}), bf16[16,64,512]{2,1,0:T(8,128)(2,1)}, u32[]{:S(2)}, u32[]{:S(2)}) async-start(bf16[16,64,512]{2,1,0:T(8,128)(2,1)} %shard_map.94), calls=%async_computation | async-start | bytes 2097152 | tf_op jit(solution)/shard_map/all_to_all | solution.py:396
  11.5 3.5 %collective-permute-start = (bf16[64,8192]{1,0:T(8,128)(2,1)S(1)}, bf16[64,8192]{1,0:T(8,128)(2,1)S(1)}, u32[]{:S(2)}, u32[]{:S(2)}) collective-permute-start(bf16[64,8192]{1,0:T(8,128)(2,1)S(1)} %copy-done), channel_id=1, source_target_pairs={{0,16},{16,32},{32,48},{48,64},{64,80},{80,96},{96,112},{112,128},... | collective-permute-start | bytes 3145736 | tf_op jit(solution)/shard_map/ppermute | solution.py:392
  15.0 4.5 %collective-permute-start.1 = (bf16[64,8192]{1,0:T(8,128)(2,1)S(1)}, bf16[64,8192]{1,0:T(8,128)(2,1)S(1)}, u32[]{:S(2)}, u32[]{:S(2)}) collective-permute-start(bf16[64,8192]{1,0:T(8,128)(2,1)S(1)} %copy-done), channel_id=1, source_target_pairs={{16,0},{32,16},{48,32},{64,48},{80,64},{96,80},{112,96},{128,112},... | collective-permute-start | bytes 3145736 | tf_op jit(solution)/shard_map/ppermute | solution.py:392
  19.6 21.4 %collective-permute-done.before = bf16[64,8192]{1,0:T(8,128)(2,1)S(1)} collective-permute-done((bf16[64,8192]{1,0:T(8,128)(2,1)S(1)}, bf16[64,8192]{1,0:T(8,128)(2,1)S(1)}, u32[]{:S(2)}, u32[]{:S(2)}) %collective-permute-start) | collective-permute-done | bytes 1048608 | tf_op jit(solution)/shard_map/ppermute | solution.py:392
  42.2 2.9 %shard_map.95 = bf16[16,64,512]{2,1,0:T(8,128)(2,1)} custom-call(s32[64]{0:T(128)S(1)} %subtract_bitcast_fusion.col_ref, bf16[64,8192]{1,0:T(8,128)(2,1)S(1)} %collective-permute-done.before, bf16[64,8192]{1,0:T(8,128)(2,1)S(1)} %copy-done, bf16[64,8192]{1,0:T(8,128)(2,1)S(1)} %collective-permute-done.1.after), custom_call_target="tpu_custom_call" | custom-call | bytes 8388608 | tf_op jit(solution)/shard_map/pallas_call | solution.py:105
  45.1 7.1 %all-to-all-start.1 = ((bf16[16,64,512]{2,1,0:T(8,128)(2,1)}), bf16[16,64,512]{2,1,0:T(8,128)(2,1)S(1)}, u32[]{:S(2)}, u32[]{:S(2)}) async-start(bf16[16,64,512]{2,1,0:T(8,128)(2,1)} %shard_map.95), calls=%async_computation.1 | async-start | bytes 2097152 | tf_op jit(solution)/shard_map/all_to_all | solution.py:396
  53.9 2.6 %copy.14 = bf16[1024,1024]{0,1:T(8,128)(2,1)} copy(bf16[1024,1024]{1,0:T(8,128)(2,1)S(1)} %copy-done.2) | data formatting | bytes 4194304 | tf_op args[4]
  56.5 3.9 %copy.15 = bf16[1024,1024]{0,1:T(8,128)(2,1)} copy(bf16[1024,1024]{1,0:T(8,128)(2,1)} %refs_5_.1) | data formatting | bytes 4194304 | tf_op args[5]
  62.5 4.5 %shard_map.96.refs_6_ = f32[1024,512]{1,0:T(8,128)} custom-call(bf16[1024,1024]{1,0:T(8,128)(2,1)} %w_self.1, bf16[1024,512]{1,0:T(8,128)(2,1)} %bitcast.1.x_ref.refs_3_), custom_call_target="tpu_custom_call" | custom-call | flops 1073741824 | bytes 5242880 | tf_op jit(solution)/shard_map/pallas_call | solution.py:191
  66.9 11.9 %all-to-all-done.1 = bf16[16,64,512]{2,1,0:T(8,128)(2,1)S(1)} async-done(((bf16[16,64,512]{2,1,0:T(8,128)(2,1)}), bf16[16,64,512]{2,1,0:T(8,128)(2,1)S(1)}, u32[]{:S(2)}, u32[]{:S(2)}) %all-to-all-start.1) | async-done | bytes 1048608 | tf_op jit(solution)/shard_map/all_to_all | solution.py:396
  79.8 8.2 %shard_map.97 = (bf16[1024,512]{1,0:T(8,128)(2,1)}, bf16[1024,512]{1,0:T(8,128)(2,1)}, bf16[1024,512]{1,0:T(8,128)(2,1)}, bf16[1024,512]{1,0:T(8,128)(2,1)}, bf1...) custom-call(s32[1]{0:T(128)S(6)} %sub.26.refs_0_, bf16[2,2,256,256]{3,2,1,0:T(8,128)(2,1)} %copy.21.refs_1_, ...), custom_call_target="tpu_custom_call" | custom-call | flops 2147483648 | bytes 16777216 | tf_op jit(solution)/shard_map/pallas_call | solution.py:264
  88.0 4.9 %all-to-all-start.2 = ((bf16[16,64,512]{2,1,0:T(8,128)(2,1)}), bf16[16,64,512]{2,1,0:T(8,128)(2,1)S(1)}, u32[]{:S(2)}, u32[]{:S(2)}) async-start(bf16[16,64,512]{2,1,0:T(8,128)(2,1)} %bitcast.54), calls=%async_computation.2 | async-start | bytes 2097152 | tf_op jit(solution)/shard_map/all_to_all | solution.py:396
  93.5 2.3 %collective-permute-done.2.other_ref = bf16[1024,512]{1,0:T(8,128)(2,1)S(1)} collective-permute-done((bf16[1024,512]{1,0:T(8,128)(2,1)S(1)}, bf16[1024,512]{1,0:T(8,128)(2,1)S(1)}, u32[]{:S(2)}, u32[]{:S(2)}) %collective-permute-start.2) | collective-permute-done | bytes 1048608 | tf_op jit(solution)/shard_map/ppermute | solution.py:413
  96.8 3.4 %shard_map.98 = (f32[256,512]{1,0:T(8,128)}, bf16[256,512]{1,0:T(8,128)(2,1)}, bf16[256,512]{1,0:T(8,128)(2,1)}, bf16[256,512]{1,0:T(8,128)(2,1)}) custom-call(s32[1]{0:T(128)} %bitcast.core_ref, s32[1]{0:T(128)} %bitcast.16.me_ref, bf16[1024,512]{1,0:T(8,128)(2,1)} %get-tuple-element.41.dpre, bf16[1024,512]{1,0:T(8,128)(2,1)} %get-tuple-element.42.agg_ref, ...), custom_call_target="tpu_custom_call" | custom-call | flops 536870912 | bytes 4194304 | tf_op jit(solution)/shard_map/pallas_call | solution.py:326
  100.2 1.5 collective-permute-start.3
  101.7 4.6 %collective-permute-start.4 = (bf16[256,512]{1,0:T(8,128)(2,1)}, bf16[256,512]{1,0:T(8,128)(2,1)S(1)}, u32[]{:S(2)}, u32[]{:S(2)}) collective-permute-start(bf16[256,512]{1,0:T(8,128)(2,1)} %get-tuple-element.46), channel_id=1, source_target_pairs={{0,32},{16,48},{32,0},{48,16},{64,96},{80,112},{96,64},{112,80},{1... | collective-permute-start | bytes 786440 | tf_op jit(solution)/shard_map/ppermute | solution.py:406
  106.3 4.8 %shard_map.99 = bf16[16,64,512]{2,1,0:T(8,128)(2,1)} custom-call(bf16[1024,1024]{1,0:T(8,128)(2,1)} %bitcast.51, bf16[1024,512]{1,0:T(8,128)(2,1)} %get-tuple-element.41.dpre, bf16[1024,512]{1,0:T(8,128)(2,1)} %get-tuple-element.49.dagg_ref, bf16[2,2,256,256]{3,2,1,0:T(8,128)(2,1)} %get-tuple-element.37.refs_2_.turned), custom_call_target="tpu_custom_call" | custom-call | flops 1073741824 | bytes 5242880 | tf_op jit(solution)/shard_map/pallas_call | solution.py:295
  111.8 6.8 %collective-permute-done.4.refs_2_ = bf16[256,512]{1,0:T(8,128)(2,1)S(1)} collective-permute-done((bf16[256,512]{1,0:T(8,128)(2,1)}, bf16[256,512]{1,0:T(8,128)(2,1)S(1)}, u32[]{:S(2)}, u32[]{:S(2)}) %collective-permute-start.4) | collective-permute-done | bytes 262176 | tf_op jit(solution)/shard_map/ppermute | solution.py:406
  119.4 2.0 %shard_map.100 = (f32[64,512]{1,0:T(8,128)}, bf16[64,512]{1,0:T(8,128)(2,1)}, bf16[64,512]{1,0:T(8,128)(2,1)}, bf16[64,512]{1,0:T(8,128)(2,1)}) custom-call(s32[1]{0:T(128)} %bitcast.15.index_ref, f32[256,512]{1,0:T(8,128)} %get-tuple-element.50.refs_0_, bf16[256,512]{1,0:T(8,128)(2,1)} %copy-done.6, bf16[256,512]{1,0:T(8,128)(2,1)} %copy-done.7, ...), custom_call_target="tpu_custom_call" | custom-call | bytes 2097152 | tf_op jit(solution)/shard_map/pallas_call | solution.py:353
  122.5 4.2 %shard_map.101 = (bf16[64,64,128]{2,1,0:T(8,128)(2,1)}, f32[64,64,128]{2,1,0:T(8,128)}, bf16[64,64,128]{2,1,0:T(8,128)(2,1)}) custom-call(s32[64]{0:T(128)} %copy-done.1, bf16[16,64,512]{2,1,0:T(8,128)(2,1)} %copy-done.3), custom_call_target="tpu_custom_call" | custom-call | bytes 8388608 | tf_op jit(solution)/shard_map/pallas_call | solution.py:161
  126.7 2.1 %collective-permute-start.6 = (bf16[64,64,128]{2,1,0:T(8,128)(2,1)}, bf16[64,64,128]{2,1,0:T(8,128)(2,1)S(1)}, u32[]{:S(2)}, u32[]{:S(2)}) collective-permute-start(bf16[64,64,128]{2,1,0:T(8,128)(2,1)} %get-tuple-element.61), channel_id=1, source_target_pairs={{0,16},{16,32},{32,48},{48,64},{64,80},{80,96},{96,112},{112,128},... | collective-permute-start | bytes 3145736 | tf_op jit(solution)/shard_map/ppermute | solution.py:392
  128.8 5.9 %collective-permute-start.7 = (bf16[64,64,128]{2,1,0:T(8,128)(2,1)}, bf16[64,64,128]{2,1,0:T(8,128)(2,1)S(1)}, u32[]{:S(2)}, u32[]{:S(2)}) collective-permute-start(bf16[64,64,128]{2,1,0:T(8,128)(2,1)} %get-tuple-element.62), channel_id=1, source_target_pairs={{16,0},{32,16},{48,32},{64,48},{80,64},{96,80},{112,96},{128,112},... | collective-permute-start | bytes 3145736 | tf_op jit(solution)/shard_map/ppermute | solution.py:392
  134.6 6.9 %all-to-all-start.3 = ((bf16[16,64,512]{2,1,0:T(8,128)(2,1)}), bf16[16,64,512]{2,1,0:T(8,128)(2,1)S(1)}, u32[]{:S(2)}, u32[]{:S(2)}) async-start(bf16[16,64,512]{2,1,0:T(8,128)(2,1)} %shard_map.99), calls=%async_computation.3 | async-start | bytes 2097152 | tf_op jit(solution)/shard_map/all_to_all | solution.py:396
  141.7 2.0 %collective-permute-start.8 = (bf16[64,512]{1,0:T(8,128)(2,1)S(1)}, bf16[64,512]{1,0:T(8,128)(2,1)S(1)}, u32[]{:S(2)}, u32[]{:S(2)}) collective-permute-start(bf16[64,512]{1,0:T(8,128)(2,1)S(1)} %copy-done.12), channel_id=1, source_target_pairs={{0,64},{16,80},{32,96},{48,112},{64,128},{80,144},{96,160},{112,17... | collective-permute-start | bytes 196616 | tf_op jit(solution)/shard_map/ppermute | solution.py:406
  143.7 1.4 collective-permute-start.9
  145.0 16.9 %collective-permute-done.10 = bf16[64,512]{1,0:T(8,128)(2,1)S(1)} collective-permute-done((bf16[64,512]{1,0:T(8,128)(2,1)}, bf16[64,512]{1,0:T(8,128)(2,1)S(1)}, u32[]{:S(2)}, u32[]{:S(2)}) %collective-permute-start.10) | collective-permute-done | bytes 65568 | tf_op jit(solution)/shard_map/ppermute | solution.py:406
  163.0 4.6 %collective-permute-start.11 = (f32[32,512]{1,0:T(8,128)S(1)}, f32[32,512]{1,0:T(8,128)S(1)}, u32[]{:S(2)}, u32[]{:S(2)}) collective-permute-start(f32[32,512]{1,0:T(8,128)S(1)} %dynamic-slice_bitcast_fusion), channel_id=1, source_target_pairs={{0,8},{1,9},{2,10},{3,11},{4,12},{5,13},{6,14},{7,15},{8,0},{9,1},... | collective-permute-start | bytes 196616 | tf_op jit(solution)/shard_map/ppermute | solution.py:438
  167.5 5.9 %collective-permute-done.11 = f32[32,512]{1,0:T(8,128)S(1)} collective-permute-done((f32[32,512]{1,0:T(8,128)S(1)}, f32[32,512]{1,0:T(8,128)S(1)}, u32[]{:S(2)}, u32[]{:S(2)}) %collective-permute-start.11) | collective-permute-done | bytes 65568 | tf_op jit(solution)/shard_map/ppermute | solution.py:438
  173.7 4.9 %collective-permute-done.12 = f32[16,512]{1,0:T(8,128)S(1)} collective-permute-done((f32[16,512]{1,0:T(8,128)S(1)}, f32[16,512]{1,0:T(8,128)S(1)}, u32[]{:S(2)}, u32[]{:S(2)}) %collective-permute-start.12) | collective-permute-done | bytes 32800 | tf_op jit(solution)/shard_map/ppermute | solution.py:438
  178.9 3.5 %collective-permute-done.13 = f32[8,512]{1,0:T(8,128)S(1)} collective-permute-done((f32[8,512]{1,0:T(8,128)S(1)}, f32[8,512]{1,0:T(8,128)S(1)}, u32[]{:S(2)}, u32[]{:S(2)}) %collective-permute-start.13) | collective-permute-done | bytes 16416 | tf_op jit(solution)/shard_map/ppermute | solution.py:438
  184.3 3.8 %shard_map.102 = bf16[64,8192]{1,0:T(8,128)(2,1)} custom-call(f32[64,64,128]{2,1,0:T(8,128)} %get-tuple-element.60.own_ref, bf16[64,64,128]{2,1,0:T(8,128)(2,1)S(1)} %collective-permute-done.6.before_ref, bf16[64,64,128]{2,1,0:T(8,128)(2,1)S(1)} %collective-permute-done.7.after_ref, bf16[16,64,512]{2,1,0:T(8,128)(2,1)S(1)} %all-to-all-done.3.dself_ref), custom_call_target="tpu_custom_call" | custom-call | tf_op jit(solution)/shard_map/pallas_call | solution.py:378
  (72 shorter events, 13.4 us)
Async XLA Ops:
  0.6 10.9 %copy-start = (bf16[64,8192]{1,0:T(8,128)(2,1)S(1)}, bf16[64,8192]{1,0:T(8,128)(2,1)}, u32[]{:S(2)}) copy-start(bf16[64,8192]{1,0:T(8,128)(2,1)} %own.1) | copy-start | bytes 3145732
  0.6 18.9 %copy-start.13 = (s32[64,2]{0,1:T(2,128)S(1)}, s32[64,2]{0,1:T(2,128)}, u32[]{:S(2)}) copy-start(s32[64,2]{0,1:T(2,128)} %param.9) | copy-start | bytes 1540
  2.9 42.2 %all-to-all-start = ((bf16[16,64,512]{2,1,0:T(8,128)(2,1)}), bf16[16,64,512]{2,1,0:T(8,128)(2,1)}, u32[]{:S(2)}, u32[]{:S(2)}) async-start(bf16[16,64,512]{2,1,0:T(8,128)(2,1)} %shard_map.94), calls=%async_computation | async-start | bytes 2097152 | tf_op jit(solution)/shard_map/all_to_all | solution.py:396
  11.5 29.4 %collective-permute-start = (bf16[64,8192]{1,0:T(8,128)(2,1)S(1)}, bf16[64,8192]{1,0:T(8,128)(2,1)S(1)}, u32[]{:S(2)}, u32[]{:S(2)}) collective-permute-start(bf16[64,8192]{1,0:T(8,128)(2,1)S(1)} %copy-done), channel_id=1, source_target_pairs={{0,16},{16,32},{32,48},{48,64},{64,80},{80,96},{96,112},{112,128},... | collective-permute-start | bytes 3145736 | tf_op jit(solution)/shard_map/ppermute | solution.py:392
  15.0 27.1 %collective-permute-start.1 = (bf16[64,8192]{1,0:T(8,128)(2,1)S(1)}, bf16[64,8192]{1,0:T(8,128)(2,1)S(1)}, u32[]{:S(2)}, u32[]{:S(2)}) collective-permute-start(bf16[64,8192]{1,0:T(8,128)(2,1)S(1)} %copy-done), channel_id=1, source_target_pairs={{16,0},{32,16},{48,32},{64,48},{80,64},{96,80},{112,96},{128,112},... | collective-permute-start | bytes 3145736 | tf_op jit(solution)/shard_map/ppermute | solution.py:392
  19.5 25.5 %copy-start.1 = (s32[64]{0:T(128)}, s32[64]{0:T(128)S(1)}, u32[]{:S(2)}) copy-start(s32[64]{0:T(128)S(1)} %subtract_bitcast_fusion.col_ref) | copy-start | bytes 772
  45.0 8.3 %copy-start.14 = (s32[64]{0:T(128)S(1)}, s32[64]{0:T(128)}, u32[]{:S(2)}) copy-start(s32[64]{0:T(128)} %param.10) | copy-start | bytes 772
  45.0 8.8 %copy-start.2 = (bf16[1024,1024]{1,0:T(8,128)(2,1)S(1)}, bf16[1024,1024]{1,0:T(8,128)(2,1)}, u32[]{:S(2)}) copy-start(bf16[1024,1024]{1,0:T(8,128)(2,1)} %w_self.1) | copy-start | bytes 6291460
  45.1 33.8 %all-to-all-start.1 = ((bf16[16,64,512]{2,1,0:T(8,128)(2,1)}), bf16[16,64,512]{2,1,0:T(8,128)(2,1)S(1)}, u32[]{:S(2)}, u32[]{:S(2)}) async-start(bf16[16,64,512]{2,1,0:T(8,128)(2,1)} %shard_map.95), calls=%async_computation.1 | async-start | bytes 2097152 | tf_op jit(solution)/shard_map/all_to_all | solution.py:396
  78.8 1.0 copy-start.4
  88.0 5.0 %copy-start.10 = (bf16[1024,512]{1,0:T(8,128)(2,1)S(1)}, bf16[1024,512]{1,0:T(8,128)(2,1)}, u32[]{:S(2)}) copy-start(bf16[1024,512]{1,0:T(8,128)(2,1)} %get-tuple-element.43) | copy-start | bytes 3145732
  88.0 33.5 %all-to-all-start.2 = ((bf16[16,64,512]{2,1,0:T(8,128)(2,1)}), bf16[16,64,512]{2,1,0:T(8,128)(2,1)S(1)}, u32[]{:S(2)}, u32[]{:S(2)}) async-start(bf16[16,64,512]{2,1,0:T(8,128)(2,1)} %bitcast.54), calls=%async_computation.2 | async-start | bytes 2097152 | tf_op jit(solution)/shard_map/all_to_all | solution.py:396
  93.0 2.8 %collective-permute-start.2 = (bf16[1024,512]{1,0:T(8,128)(2,1)S(1)}, bf16[1024,512]{1,0:T(8,128)(2,1)S(1)}, u32[]{:S(2)}, u32[]{:S(2)}) collective-permute-start(bf16[1024,512]{1,0:T(8,128)(2,1)S(1)} %copy-done.10), channel_id=1, source_target_pairs={{0,1},{1,0},{2,3},{3,2},{4,5},{5,4},{6,7},{7,6},{8,9},{9,8},{10,11... | collective-permute-start | bytes 3145736 | tf_op jit(solution)/shard_map/ppermute | solution.py:413
  95.8 1.0 copy-start.5
  100.2 11.7 %collective-permute-start.3 = (bf16[256,512]{1,0:T(8,128)(2,1)}, bf16[256,512]{1,0:T(8,128)(2,1)S(1)}, u32[]{:S(2)}, u32[]{:S(2)}) collective-permute-start(bf16[256,512]{1,0:T(8,128)(2,1)} %get-tuple-element.45), channel_id=1, source_target_pairs={{0,16},{16,32},{32,48},{48,0},{64,80},{80,96},{96,112},{112,64},{1... | collective-permute-start | bytes 786440 | tf_op jit(solution)/shard_map/ppermute | solution.py:406
  101.7 17.0 %collective-permute-start.4 = (bf16[256,512]{1,0:T(8,128)(2,1)}, bf16[256,512]{1,0:T(8,128)(2,1)S(1)}, u32[]{:S(2)}, u32[]{:S(2)}) collective-permute-start(bf16[256,512]{1,0:T(8,128)(2,1)} %get-tuple-element.46), channel_id=1, source_target_pairs={{0,32},{16,48},{32,0},{48,16},{64,96},{80,112},{96,64},{112,80},{1... | collective-permute-start | bytes 786440 | tf_op jit(solution)/shard_map/ppermute | solution.py:406
  106.3 12.4 %collective-permute-start.5 = (bf16[256,512]{1,0:T(8,128)(2,1)}, bf16[256,512]{1,0:T(8,128)(2,1)S(1)}, u32[]{:S(2)}, u32[]{:S(2)}) collective-permute-start(bf16[256,512]{1,0:T(8,128)(2,1)} %get-tuple-element.47), channel_id=1, source_target_pairs={{0,48},{16,0},{32,16},{48,32},{64,112},{80,64},{96,80},{112,96},{1... | collective-permute-start | bytes 786440 | tf_op jit(solution)/shard_map/ppermute | solution.py:406
  111.8 6.8 %copy-start.6 = (bf16[256,512]{1,0:T(8,128)(2,1)}, bf16[256,512]{1,0:T(8,128)(2,1)S(1)}, u32[]{:S(2)}) copy-start(bf16[256,512]{1,0:T(8,128)(2,1)S(1)} %collective-permute-done.3.refs_1_) | copy-start | bytes 786436
  121.5 20.2 %copy-start.12 = (bf16[64,512]{1,0:T(8,128)(2,1)S(1)}, bf16[64,512]{1,0:T(8,128)(2,1)}, u32[]{:S(2)}) copy-start(bf16[64,512]{1,0:T(8,128)(2,1)} %get-tuple-element.65) | copy-start | bytes 196612
  121.5 22.2 %copy-start.11 = (bf16[64,512]{1,0:T(8,128)(2,1)S(1)}, bf16[64,512]{1,0:T(8,128)(2,1)}, u32[]{:S(2)}) copy-start(bf16[64,512]{1,0:T(8,128)(2,1)} %get-tuple-element.66) | copy-start | bytes 196612
  121.5 40.6 %copy-start.9 = (f32[64,512]{1,0:T(8,128)S(1)}, f32[64,512]{1,0:T(8,128)}, u32[]{:S(2)}) copy-start(f32[64,512]{1,0:T(8,128)} %get-tuple-element.64) | copy-start | bytes 393220
  121.5 1.0 copy-start.3
  126.7 46.8 %collective-permute-start.6 = (bf16[64,64,128]{2,1,0:T(8,128)(2,1)}, bf16[64,64,128]{2,1,0:T(8,128)(2,1)S(1)}, u32[]{:S(2)}, u32[]{:S(2)}) collective-permute-start(bf16[64,64,128]{2,1,0:T(8,128)(2,1)} %get-tuple-element.61), channel_id=1, source_target_pairs={{0,16},{16,32},{32,48},{48,64},{64,80},{80,96},{96,112},{112,128},... | collective-permute-start | bytes 3145736 | tf_op jit(solution)/shard_map/ppermute | solution.py:392
  128.8 44.7 %collective-permute-start.7 = (bf16[64,64,128]{2,1,0:T(8,128)(2,1)}, bf16[64,64,128]{2,1,0:T(8,128)(2,1)S(1)}, u32[]{:S(2)}, u32[]{:S(2)}) collective-permute-start(bf16[64,64,128]{2,1,0:T(8,128)(2,1)} %get-tuple-element.62), channel_id=1, source_target_pairs={{16,0},{32,16},{48,32},{64,48},{80,64},{96,80},{112,96},{128,112},... | collective-permute-start | bytes 3145736 | tf_op jit(solution)/shard_map/ppermute | solution.py:392
  134.6 49.7 %all-to-all-start.3 = ((bf16[16,64,512]{2,1,0:T(8,128)(2,1)}), bf16[16,64,512]{2,1,0:T(8,128)(2,1)S(1)}, u32[]{:S(2)}, u32[]{:S(2)}) async-start(bf16[16,64,512]{2,1,0:T(8,128)(2,1)} %shard_map.99), calls=%async_computation.3 | async-start | bytes 2097152 | tf_op jit(solution)/shard_map/all_to_all | solution.py:396
  141.6 20.3 %collective-permute-start.10 = (bf16[64,512]{1,0:T(8,128)(2,1)}, bf16[64,512]{1,0:T(8,128)(2,1)S(1)}, u32[]{:S(2)}, u32[]{:S(2)}) collective-permute-start(bf16[64,512]{1,0:T(8,128)(2,1)} %get-tuple-element.67), channel_id=1, source_target_pairs={{0,192},{16,208},{32,224},{48,240},{64,0},{80,16},{96,32},{112,48}... | collective-permute-start | bytes 196616 | tf_op jit(solution)/shard_map/ppermute | solution.py:406
  141.7 20.2 %collective-permute-start.8 = (bf16[64,512]{1,0:T(8,128)(2,1)S(1)}, bf16[64,512]{1,0:T(8,128)(2,1)S(1)}, u32[]{:S(2)}, u32[]{:S(2)}) collective-permute-start(bf16[64,512]{1,0:T(8,128)(2,1)S(1)} %copy-done.12), channel_id=1, source_target_pairs={{0,64},{16,80},{32,96},{48,112},{64,128},{80,144},{96,160},{112,17... | collective-permute-start | bytes 196616 | tf_op jit(solution)/shard_map/ppermute | solution.py:406
  143.7 18.4 %collective-permute-start.9 = (bf16[64,512]{1,0:T(8,128)(2,1)S(1)}, bf16[64,512]{1,0:T(8,128)(2,1)}, u32[]{:S(2)}, u32[]{:S(2)}) collective-permute-start(bf16[64,512]{1,0:T(8,128)(2,1)S(1)} %copy-done.11), channel_id=1, source_target_pairs={{0,128},{16,144},{32,160},{48,176},{64,192},{80,208},{96,224},{112... | collective-permute-start | bytes 196616 | tf_op jit(solution)/shard_map/ppermute | solution.py:406
  163.0 10.5 %collective-permute-start.11 = (f32[32,512]{1,0:T(8,128)S(1)}, f32[32,512]{1,0:T(8,128)S(1)}, u32[]{:S(2)}, u32[]{:S(2)}) collective-permute-start(f32[32,512]{1,0:T(8,128)S(1)} %dynamic-slice_bitcast_fusion), channel_id=1, source_target_pairs={{0,8},{1,9},{2,10},{3,11},{4,12},{5,13},{6,14},{7,15},{8,0},{9,1},... | collective-permute-start | bytes 196616 | tf_op jit(solution)/shard_map/ppermute | solution.py:438
  173.5 5.0 %collective-permute-start.12 = (f32[16,512]{1,0:T(8,128)S(1)}, f32[16,512]{1,0:T(8,128)S(1)}, u32[]{:S(2)}, u32[]{:S(2)}) collective-permute-start(f32[16,512]{1,0:T(8,128)S(1)} %dynamic-slice_bitcast_fusion.1), channel_id=1, source_target_pairs={{0,4},{1,5},{2,6},{3,7},{4,0},{5,1},{6,2},{7,3},{8,12},{9,13},{10,... | collective-permute-start | bytes 98312 | tf_op jit(solution)/shard_map/ppermute | solution.py:438
  178.6 3.8 %collective-permute-start.13 = (f32[8,512]{1,0:T(8,128)S(1)}, f32[8,512]{1,0:T(8,128)S(1)}, u32[]{:S(2)}, u32[]{:S(2)}) collective-permute-start(f32[8,512]{1,0:T(8,128)S(1)} %dynamic-slice_bitcast_fusion.2), channel_id=1, source_target_pairs={{0,2},{1,3},{2,0},{3,1},{4,6},{5,7},{6,4},{7,5},{8,10},{9,11},{10,... | collective-permute-start | bytes 49160 | tf_op jit(solution)/shard_map/ppermute | solution.py:438
  182.5 1.3 collective-permute-start.14
  (2 other events, 1.5 us)

commit v9 on v8

--- a/solution.py
+++ b/solution.py
@@ -14,7 +14,7 @@
 MIB = 1 << 20
 DENSE_MIB = 56
 OWN_MIB = 60
-WEIGHT_MIB = 60
+WEIGHT_MIB = 8
 FINAL_MIB = 50
 SCATTER_MIB = 56
 CHUNK = 512
@@ -201,10 +201,10 @@
 
 
 def dense_kernel(chunk, *refs):
-    half_ref, sources, targets, held = refs[0], refs[1:9], refs[9:15], refs[15:23]
-    (agg_hbm, hidden_hbm, dpre_hbm, dagg_hbm, second_hbm, sent_hbm) = targets
+    core_ref, sources, targets, held = refs[0], refs[1:9], refs[9:16], refs[16:24]
+    (agg_hbm, hidden_hbm, dpre_hbm, dagg_hbm, second_hbm, sent_hbm, kept_hbm) = targets
     (tiles, turned, x_ref, picked, w_neigh, pre_ref, cot_ref, w_back) = held
-    (agg, hidden, dpre, dagg, second, sent, in_sems, out_sems) = refs[23:]
+    (agg, hidden, dpre, dagg, second, sent, kept, in_sems, out_sems) = refs[24:]
     size = w_neigh.shape[0]
     pair = tiles.shape[-1]
     part = [slice(i, i + chunk) for i in range(0, size, chunk)]
@@ -248,15 +248,17 @@
         store(3, dagg, dagg_hbm, i)
         store(4, second, second_hbm, i)
     width = sent.shape[1]
-    half = agg.at[pl.ds(pl.multiple_of(half_ref[0] * width, width), width)]
-    for i in range(len(part)):
-        sent[part[i], :] = dot(dpre[part[i], :], half[...], NT).astype(BF16)
-        store(5, sent, sent_hbm, i)
+    core = core_ref[0]
+    for k, owner, out, target in ((5, 1 - core, sent, sent_hbm), (6, core, kept, kept_hbm)):
+        half = agg.at[pl.ds(pl.multiple_of(owner * width, width), width)]
+        for i in range(len(part)):
+            out[part[i], :] = dot(dpre[part[i], :], half[...], NT).astype(BF16)
+            store(k, out, target, i)
     for copy in stores:
         copy.wait()
 
 
-def dense(half, tiles, turned, x_rows, picked, w_neigh, pre_self, cot, w_back):
+def dense(core, tiles, turned, x_rows, picked, w_neigh, pre_self, cot, w_back):
     size, width = picked.shape
     chunk = CHUNK
     out = jax.ShapeDtypeStruct((size, width), BF16)
@@ -264,17 +266,17 @@
     return pl.pallas_call(
         functools.partial(dense_kernel, chunk),
         in_specs=[SMEM] + [ANYWHERE] * len(args),
-        out_specs=[ANYWHERE] * 6,
-        out_shape=[out] * 5 + [jax.ShapeDtypeStruct((size, size // CORES), BF16)],
+        out_specs=[ANYWHERE] * 7,
+        out_shape=[out] * 5 + [jax.ShapeDtypeStruct((size, size // CORES), BF16)] * 2,
         scratch_shapes=[pltpu.VMEM(arg.shape, arg.dtype) for arg in args]
         + [pltpu.VMEM((size, width), BF16)] * 5
-        + [pltpu.VMEM((size, size // CORES), BF16)]
-        + [pltpu.SemaphoreType.DMA((len(args),)), pltpu.SemaphoreType.DMA((6, size // chunk))],
+        + [pltpu.VMEM((size, size // CORES), BF16)] * 2
+        + [pltpu.SemaphoreType.DMA((len(args),)), pltpu.SemaphoreType.DMA((7, size // chunk))],
         compiler_params=whole_params(DENSE_MIB),
         cost_estimate=pl.CostEstimate(
             flops=4 * size * size * width, bytes_accessed=16 * MIB, transcendentals=size * width
         ),
-    )(half, *args)
+    )(core, *args)
 
 
 def own_kernel(chunk, w_back, dpre, dagg_ref, turned, own):
@@ -304,36 +306,29 @@
     )(w_back, dpre, dagg, turned)
 
 
-def weight_kernel(core_ref, me_ref, dpre, agg_ref, other_ref, *outs):
-    core, me = core_ref[0], me_ref[0]
-    rows, width = outs[0].shape
-    half = agg_ref.at[pl.ds(pl.multiple_of(core * width, width), width)]
+def weight_kernel(me_ref, kept_ref, other_ref, *outs):
+    rows = outs[0].shape[0]
     each = rows // SIDE
-
-    def picked(ref, there):
-        first = lax.rem(me + there, SIDE) * each
-        places = [pl.multiple_of(i * rows + first, each) for i in range(SIDE)]
-        return jnp.concatenate([ref[pl.ds(place, each), :] for place in places], axis=0)
-
     for step, out in enumerate(outs):
-        total = dot(picked(dpre, step), half[...], NT) + picked(other_ref, step).astype(F32)
-        out[...] = total.astype(out.dtype)
-
-
-def weight_pieces(core, me, dpre, agg_rows, other):
-    size, width = dpre.shape
-    shape = (size // SIDE, size // CORES)
+        first = lax.rem(me_ref[0] + step, SIDE) * each
+        for i in range(SIDE):
+            there = pl.ds(pl.multiple_of(i * rows + first, each), each)
+            total = kept_ref[there, :].astype(F32) + other_ref[there, :].astype(F32)
+            out[i * each : (i + 1) * each, :] = total.astype(out.dtype)
+
+
+def weight_pieces(me, kept, other):
+    size, width = kept.shape
+    shape = (size // SIDE, width)
     return pl.pallas_call(
         weight_kernel,
-        in_specs=[SMEM] * 2 + [VMEM] * 3,
+        in_specs=[SMEM] + [VMEM] * 2,
         out_specs=[VMEM] * SIDE,
         out_shape=[jax.ShapeDtypeStruct(shape, F32)]
         + [jax.ShapeDtypeStruct(shape, BF16)] * (SIDE - 1),
         compiler_params=whole_params(WEIGHT_MIB),
-        cost_estimate=pl.CostEstimate(
-            flops=size * size * width, bytes_accessed=4 * MIB, transcendentals=0
-        ),
-    )(core[None], me[None], dpre, agg_rows, other)
+        cost_estimate=pl.CostEstimate(flops=0, bytes_accessed=4 * MIB, transcendentals=0),
+    )(me[None], kept, other)
 
 
 def add_kernel(index_ref, *refs):
@@ -408,22 +403,22 @@
     ]
 
 
-def weight_pieces_along_x(sent, dpre, agg_rows, groups, own_rows):
-    feat, node = lax.axis_index("feat"), lax.axis_index("node")
+def weight_terms(sent, kept, groups, own_rows):
+    node = lax.axis_index("node")
     other = lax.ppermute(sent, "feat", [(i, i ^ 1) for i in range(groups)])
-    pieces = weight_pieces(lax.rem(feat, CORES), lax.rem(node, SIDE), dpre, agg_rows, other)
+    pieces = weight_pieces(lax.rem(node, SIDE), kept, other)
     parts = sent_round(pieces, "node", lambda i, s: i // SIDE * SIDE + (i + s) % SIDE)
     parts, own_rows = lax.optimization_barrier((parts, own_rows))
-    return added_pieces(lax.div(node, SIDE), parts)
+    pieces = added_pieces(lax.div(node, SIDE), parts)
+    return sent_round(pieces, "node", lambda i, s: (i + s * SIDE) % (SIDE * SIDE))
 
 
 def piece_at(pieces, index):
     return lax.dynamic_index_in_dim(pieces, index, 0, keepdims=False)
 
 
-def weight_total(pieces, groups, halo):
+def weight_total(parts, groups, halo):
     feat = lax.axis_index("feat")
-    parts = sent_round(pieces, "node", lambda i, s: (i + s * SIDE) % (SIDE * SIDE))
     value = parts[0]
     for part in parts[1:]:
         value = value + part.astype(F32)
@@ -479,19 +474,19 @@
     )
     pre_self = self_product(w_self, x_rows)
     core = lax.rem(feat, CORES)
-    agg_rows, hidden, dpre, dagg, second, sent = dense(
-        1 - core[None], straight, turned, x_rows, picked, w_neigh, pre_self, cotangent, neigh_back
+    _, hidden, dpre, dagg, second, sent, kept = dense(
+        core[None], straight, turned, x_rows, picked, w_neigh, pre_self, cotangent, neigh_back
     )
     second_cols = exchange(second.reshape(groups, feat_dev, -1), "feat")
     own_rows = own_part(self_back, dpre, dagg, turned, groups)
-    pieces = weight_pieces_along_x(sent, dpre, agg_rows, groups, own_rows)
-    _, second_cols, own_rows = lax.optimization_barrier((pieces, second_cols, own_rows))
+    terms = weight_terms(sent, kept, groups, own_rows)
+    terms, second_cols, own_rows = lax.optimization_barrier((terms, second_cols, own_rows))
+    to_before, spread, to_after = scatter(col, second_cols)
     own_cols = exchange(own_rows, "feat")
-    to_before, spread, to_after = scatter(col, second_cols)
     from_after = shifted(to_before, "node", -1)
     from_before = shifted(to_after, "node", 1)
-    pieces, _ = lax.optimization_barrier((pieces, spread))
-    grad_w_neigh = weight_total(pieces, groups, (from_after, from_before))
+    terms, _ = lax.optimization_barrier((terms, spread))
+    grad_w_neigh = weight_total(terms, groups, (from_after, from_before))
     grad_features = finish(spread, from_before, from_after, own_cols)
     return (hidden, grad_features, grad_w_neigh)
 

time: 190 us -> 188 us (0.989)
  Pallas kernels: 36 us -> 31.6 us
  waiting for transfers between devices: 76.9 us -> 80.8 us
  local copies, waits for them, and re-layouts: 12.9 us -> 10.2 us
    ppermute x3, waiting for transfers between devices: 14.4 us -> 31.3 us  [weight_total(): lax.ppermute(piece_at(pieces, 1 - bit), 'feat', flip)]
    ppermute x6, waiting for transfers between devices: 24.6 us -> 11.5 us  [sent_round(): lax.ppermute(piece, axis, [(i, partner(i, step + 1)) for i in range(count)])]
    pallas_call x1, Pallas kernels: 3.38 us -> 0.23 us  [weight_pieces(): pl.pallas_call(weight_kernel, in_specs=[SMEM] + [VMEM] * 2, out_specs=[VM...]
    ppermute x3, starting transfers between devices: 4.97 us -> 7.85 us  [weight_total(): lax.ppermute(piece_at(pieces, 1 - bit), 'feat', flip)]
    unnamed x34 -> x22, local copies, waits for them, and re-layouts: 10.5 us -> 7.79 us
    ppermute x4, starting transfers between devices: 15.9 us -> 13.8 us  [shifted(): lax.ppermute(value, axis, [(source, source + steps) for source in range(f...]
    pallas_call x1, Pallas kernels: 2.05 us -> 0.11 us  [added_pieces(): pl.pallas_call(add_kernel, in_specs=[SMEM] + [VMEM] * SIDE, out_specs=[VM...]
  transfers between devices with their start and end apart: 19 -> 19, of which waited for: 12 -> 13; matrix products, arithmetic and copies ran while one was open for 6% -> 6% of each run, Pallas kernels for 9% -> 7%
where the time goes in v9:
time: 188 us; the launch traced here: 186 us
  waiting for transfers between devices  80.8 us (43%)
  starting transfers between devices  59.7 us (32%)
  Pallas kernels  31.6 us (17%)
  local copies, waits for them, and re-layouts  10.2 us (5%)
  other arithmetic  2.58 us (1%)
    ppermute x3, waiting for transfers between devices, weight_total(): lax.ppermute(piece_at(pieces, 1 - bit), 'feat', flip)  31.3 us
    all_to_all x4, starting transfers between devices, exchange(): return lax.all_to_all(value, axis, split_axis=0, concat_axis=0, tiled=True)  27 us
    ppermute x4, waiting for transfers between devices, shifted(): lax.ppermute(value, axis, [(source, source + steps) for source in range(f...  22.6 us
    ppermute x4, starting transfers between devices, shifted(): lax.ppermute(value, axis, [(source, source + steps) for source in range(f...  13.8 us
    all_to_all x4, waiting for transfers between devices, exchange(): return lax.all_to_all(value, axis, split_axis=0, concat_axis=0, tiled=True)  11.9 us
    ppermute x6, waiting for transfers between devices, sent_round(): lax.ppermute(piece, axis, [(i, partner(i, step + 1)) for i in range(count)])  11.5 us
    ppermute x6, starting transfers between devices, sent_round(): lax.ppermute(piece, axis, [(i, partner(i, step + 1)) for i in range(count)])  9.79 us
    pallas_call x1, Pallas kernels, dense(): pl.pallas_call(functools.partial(dense_kernel, chunk), in_specs=[SMEM] +...  8.78 us
  transfers between devices with their start and end apart: 19, of which 13 were waited for; matrix products, arithmetic and copies ran while one was open for 6% of the time, Pallas kernels for 7%

profile of v9, /device:TPU:2, one launch (start us, length us, event | category | flops | bytes accessed | tf_op | source)
XLA Modules:
  0.0 185.8 jit_solution(18400897099999647342)
XLA Ops:
  0.6 2.2 %shard_map.94 = bf16[16,64,512]{2,1,0:T(8,128)(2,1)} custom-call(bf16[64,8192]{1,0:T(8,128)(2,1)} %own.1), custom_call_target="tpu_custom_call" | custom-call | tf_op jit(solution)/shard_map/pallas_call | solution.py:61
  2.9 8.6 %all-to-all-start = ((bf16[16,64,512]{2,1,0:T(8,128)(2,1)}), bf16[16,64,512]{2,1,0:T(8,128)(2,1)}, u32[]{:S(2)}, u32[]{:S(2)}) async-start(bf16[16,64,512]{2,1,0:T(8,128)(2,1)} %shard_map.94), calls=%async_computation | async-start | bytes 2097152 | tf_op jit(solution)/shard_map/all_to_all | solution.py:391
  11.5 3.5 %collective-permute-start = (bf16[64,8192]{1,0:T(8,128)(2,1)S(1)}, bf16[64,8192]{1,0:T(8,128)(2,1)S(1)}, u32[]{:S(2)}, u32[]{:S(2)}) collective-permute-start(bf16[64,8192]{1,0:T(8,128)(2,1)S(1)} %copy-done), channel_id=1, source_target_pairs={{0,16},{16,32},{32,48},{48,64},{64,80},{80,96},{96,112},{112,128},... | collective-permute-start | bytes 3145736 | tf_op jit(solution)/shard_map/ppermute | solution.py:387
  15.0 4.5 %collective-permute-start.1 = (bf16[64,8192]{1,0:T(8,128)(2,1)S(1)}, bf16[64,8192]{1,0:T(8,128)(2,1)S(1)}, u32[]{:S(2)}, u32[]{:S(2)}) collective-permute-start(bf16[64,8192]{1,0:T(8,128)(2,1)S(1)} %copy-done), channel_id=1, source_target_pairs={{16,0},{32,16},{48,32},{64,48},{80,64},{96,80},{112,96},{128,112},... | collective-permute-start | bytes 3145736 | tf_op jit(solution)/shard_map/ppermute | solution.py:387
  19.6 21.4 %collective-permute-done.before = bf16[64,8192]{1,0:T(8,128)(2,1)S(1)} collective-permute-done((bf16[64,8192]{1,0:T(8,128)(2,1)S(1)}, bf16[64,8192]{1,0:T(8,128)(2,1)S(1)}, u32[]{:S(2)}, u32[]{:S(2)}) %collective-permute-start) | collective-permute-done | bytes 1048608 | tf_op jit(solution)/shard_map/ppermute | solution.py:387
  42.2 2.9 %shard_map.95 = bf16[16,64,512]{2,1,0:T(8,128)(2,1)} custom-call(s32[64]{0:T(128)S(1)} %subtract_bitcast_fusion.col_ref, bf16[64,8192]{1,0:T(8,128)(2,1)S(1)} %collective-permute-done.before, bf16[64,8192]{1,0:T(8,128)(2,1)S(1)} %copy-done, bf16[64,8192]{1,0:T(8,128)(2,1)S(1)} %collective-permute-done.1.after), custom_call_target="tpu_custom_call" | custom-call | bytes 8388608 | tf_op jit(solution)/shard_map/pallas_call | solution.py:105
  45.1 7.1 %all-to-all-start.1 = ((bf16[16,64,512]{2,1,0:T(8,128)(2,1)}), bf16[16,64,512]{2,1,0:T(8,128)(2,1)S(1)}, u32[]{:S(2)}, u32[]{:S(2)}) async-start(bf16[16,64,512]{2,1,0:T(8,128)(2,1)} %shard_map.95), calls=%async_computation.1 | async-start | bytes 2097152 | tf_op jit(solution)/shard_map/all_to_all | solution.py:391
  53.9 2.6 %copy.14 = bf16[1024,1024]{0,1:T(8,128)(2,1)} copy(bf16[1024,1024]{1,0:T(8,128)(2,1)S(1)} %copy-done.3) | data formatting | bytes 4194304 | tf_op args[4]
  56.5 3.9 %copy.15 = bf16[1024,1024]{0,1:T(8,128)(2,1)} copy(bf16[1024,1024]{1,0:T(8,128)(2,1)} %refs_5_.1) | data formatting | bytes 4194304 | tf_op args[5]
  62.4 4.5 %shard_map.96.refs_6_ = f32[1024,512]{1,0:T(8,128)} custom-call(bf16[1024,1024]{1,0:T(8,128)(2,1)} %w_self.1, bf16[1024,512]{1,0:T(8,128)(2,1)} %bitcast.1.x_ref.refs_3_), custom_call_target="tpu_custom_call" | custom-call | flops 1073741824 | bytes 5242880 | tf_op jit(solution)/shard_map/pallas_call | solution.py:191
  66.9 11.9 %all-to-all-done.1 = bf16[16,64,512]{2,1,0:T(8,128)(2,1)S(1)} async-done(((bf16[16,64,512]{2,1,0:T(8,128)(2,1)}), bf16[16,64,512]{2,1,0:T(8,128)(2,1)S(1)}, u32[]{:S(2)}, u32[]{:S(2)}) %all-to-all-start.1) | async-done | bytes 1048608 | tf_op jit(solution)/shard_map/all_to_all | solution.py:391
  79.8 8.8 %shard_map.97 = (bf16[1024,512]{1,0:T(8,128)(2,1)}, bf16[1024,512]{1,0:T(8,128)(2,1)}, bf16[1024,512]{1,0:T(8,128)(2,1)}, bf16[1024,512]{1,0:T(8,128)(2,1)}, bf1...) custom-call(s32[1]{0:T(128)} %bitcast.refs_0_, ...), custom_call_target="tpu_custom_call" | custom-call | flops 2147483648 | bytes 16777216 | tf_op jit(solution)/shard_map/pallas_call | solution.py:266
  88.6 5.0 %all-to-all-start.2 = ((bf16[16,64,512]{2,1,0:T(8,128)(2,1)}), bf16[16,64,512]{2,1,0:T(8,128)(2,1)}, u32[]{:S(2)}, u32[]{:S(2)}) async-start(bf16[16,64,512]{2,1,0:T(8,128)(2,1)} %bitcast.54), calls=%async_computation.2 | async-start | bytes 2097152 | tf_op jit(solution)/shard_map/all_to_all | solution.py:391
  94.8 2.3 %collective-permute-done.2.other_ref = bf16[1024,512]{1,0:T(8,128)(2,1)S(1)} collective-permute-done((bf16[1024,512]{1,0:T(8,128)(2,1)S(1)}, bf16[1024,512]{1,0:T(8,128)(2,1)S(1)}, u32[]{:S(2)}, u32[]{:S(2)}) %collective-permute-start.2) | collective-permute-done | bytes 1048608 | tf_op jit(solution)/shard_map/ppermute | solution.py:408
  97.3 1.6 collective-permute-start.3
  98.9 4.6 %collective-permute-start.4 = (bf16[256,512]{1,0:T(8,128)(2,1)S(1)}, bf16[256,512]{1,0:T(8,128)(2,1)S(1)}, u32[]{:S(2)}, u32[]{:S(2)}) collective-permute-start(bf16[256,512]{1,0:T(8,128)(2,1)S(1)} %get-tuple-element.49), channel_id=1, source_target_pairs={{0,32},{16,48},{32,0},{48,16},{64,96},{80,112},{96,64},{112,80},{1... | collective-permute-start | bytes 786440 | tf_op jit(solution)/shard_map/ppermute | solution.py:401
  103.5 4.8 %shard_map.99 = bf16[16,64,512]{2,1,0:T(8,128)(2,1)} custom-call(bf16[1024,1024]{1,0:T(8,128)(2,1)} %bitcast.51, bf16[1024,512]{1,0:T(8,128)(2,1)} %get-tuple-element.52.dpre, bf16[1024,512]{1,0:T(8,128)(2,1)} %get-tuple-element.53.dagg_ref, bf16[2,2,256,256]{3,2,1,0:T(8,128)(2,1)} %get-tuple-element.41.refs_2_.turned), custom_call_target="tpu_custom_call" | custom-call | flops 1073741824 | bytes 5242880 | tf_op jit(solution)/shard_map/pallas_call | solution.py:297
  108.8 6.8 %collective-permute-done.4.refs_2_ = bf16[256,512]{1,0:T(8,128)(2,1)S(1)} collective-permute-done((bf16[256,512]{1,0:T(8,128)(2,1)S(1)}, bf16[256,512]{1,0:T(8,128)(2,1)S(1)}, u32[]{:S(2)}, u32[]{:S(2)}) %collective-permute-start.4) | collective-permute-done | bytes 262176 | tf_op jit(solution)/shard_map/ppermute | solution.py:401
  115.8 1.5 collective-permute-start.6
  117.2 1.4 collective-permute-start.7
  119.4 1.5 collective-permute-done.6
  120.9 2.2 %collective-permute-done.7 = bf16[64,512]{1,0:T(8,128)(2,1)S(1)} collective-permute-done((bf16[64,512]{1,0:T(8,128)(2,1)S(1)}, bf16[64,512]{1,0:T(8,128)(2,1)S(1)}, u32[]{:S(2)}, u32[]{:S(2)}) %collective-permute-start.7) | collective-permute-done | bytes 65568 | tf_op jit(solution)/shard_map/ppermute | solution.py:401
  123.6 4.3 %shard_map.101 = (bf16[64,64,128]{2,1,0:T(8,128)(2,1)}, f32[64,64,128]{2,1,0:T(8,128)}, bf16[64,64,128]{2,1,0:T(8,128)(2,1)}) custom-call(s32[64]{0:T(128)} %copy-done.2, bf16[16,64,512]{2,1,0:T(8,128)(2,1)} %all-to-all-done.2.parts_hbm), custom_call_target="tpu_custom_call" | custom-call | bytes 8388608 | tf_op jit(solution)/shard_map/pallas_call | solution.py:161
  127.9 3.9 %collective-permute-start.10 = (bf16[64,64,128]{2,1,0:T(8,128)(2,1)}, bf16[64,64,128]{2,1,0:T(8,128)(2,1)S(1)}, u32[]{:S(2)}, u32[]{:S(2)}) collective-permute-start(bf16[64,64,128]{2,1,0:T(8,128)(2,1)} %get-tuple-element.66), channel_id=1, source_target_pairs={{16,0},{32,16},{48,32},{64,48},{80,64},{96,80},{112,96},{128,112},... | collective-permute-start | bytes 3145736 | tf_op jit(solution)/shard_map/ppermute | solution.py:387
  131.7 2.0 %collective-permute-start.9 = (bf16[64,64,128]{2,1,0:T(8,128)(2,1)}, bf16[64,64,128]{2,1,0:T(8,128)(2,1)S(1)}, u32[]{:S(2)}, u32[]{:S(2)}) collective-permute-start(bf16[64,64,128]{2,1,0:T(8,128)(2,1)} %get-tuple-element.65), channel_id=1, source_target_pairs={{0,16},{16,32},{32,48},{48,64},{64,80},{80,96},{96,112},{112,128},... | collective-permute-start | bytes 3145736 | tf_op jit(solution)/shard_map/ppermute | solution.py:387
  133.7 6.3 %all-to-all-start.3 = ((bf16[16,64,512]{2,1,0:T(8,128)(2,1)}), bf16[16,64,512]{2,1,0:T(8,128)(2,1)S(1)}, u32[]{:S(2)}, u32[]{:S(2)}) async-start(bf16[16,64,512]{2,1,0:T(8,128)(2,1)} %shard_map.99), calls=%async_computation.3 | async-start | bytes 2097152 | tf_op jit(solution)/shard_map/all_to_all | solution.py:391
  140.9 5.9 %collective-permute-start.11 = (f32[32,512]{1,0:T(8,128)S(1)}, f32[32,512]{1,0:T(8,128)S(1)}, u32[]{:S(2)}, u32[]{:S(2)}) collective-permute-start(f32[32,512]{1,0:T(8,128)S(1)} %dynamic-slice_bitcast_fusion), channel_id=1, source_target_pairs={{0,8},{1,9},{2,10},{3,11},{4,12},{5,13},{6,14},{7,15},{8,0},{9,1},... | collective-permute-start | bytes 196616 | tf_op jit(solution)/shard_map/ppermute | solution.py:433
  146.8 24.5 %collective-permute-done.11 = f32[32,512]{1,0:T(8,128)S(1)} collective-permute-done((f32[32,512]{1,0:T(8,128)S(1)}, f32[32,512]{1,0:T(8,128)S(1)}, u32[]{:S(2)}, u32[]{:S(2)}) %collective-permute-start.11) | collective-permute-done | bytes 65568 | tf_op jit(solution)/shard_map/ppermute | solution.py:433
  171.6 4.6 %collective-permute-done.12 = f32[16,512]{1,0:T(8,128)S(1)} collective-permute-done((f32[16,512]{1,0:T(8,128)S(1)}, f32[16,512]{1,0:T(8,128)S(1)}, u32[]{:S(2)}, u32[]{:S(2)}) %collective-permute-start.12) | collective-permute-done | bytes 32800 | tf_op jit(solution)/shard_map/ppermute | solution.py:433
  176.3 1.7 collective-permute-start.13
  178.0 2.1 %collective-permute-done.13 = f32[8,512]{1,0:T(8,128)S(1)} collective-permute-done((f32[8,512]{1,0:T(8,128)S(1)}, f32[8,512]{1,0:T(8,128)S(1)}, u32[]{:S(2)}, u32[]{:S(2)}) %collective-permute-start.13) | collective-permute-done | bytes 16416 | tf_op jit(solution)/shard_map/ppermute | solution.py:433
  182.0 3.8 %shard_map.102 = bf16[64,8192]{1,0:T(8,128)(2,1)} custom-call(f32[64,64,128]{2,1,0:T(8,128)} %get-tuple-element.64.own_ref, bf16[64,64,128]{2,1,0:T(8,128)(2,1)S(1)} %collective-permute-done.9.before_ref, bf16[64,64,128]{2,1,0:T(8,128)(2,1)S(1)} %collective-permute-done.10.after_ref, bf16[16,64,512]{2,1,0:T(8,128)(2,1)S(1)} %all-to-all-done.3.dself_ref), custom_call_target="tpu_custom_call" | custom-call | tf_op jit(solution)/shard_map/pallas_call | solution.py:373
  (60 shorter events, 12.2 us)
Async XLA Ops:
  0.6 10.9 %copy-start = (bf16[64,8192]{1,0:T(8,128)(2,1)S(1)}, bf16[64,8192]{1,0:T(8,128)(2,1)}, u32[]{:S(2)}) copy-start(bf16[64,8192]{1,0:T(8,128)(2,1)} %own.1) | copy-start | bytes 3145732
  0.6 18.9 %copy-start.7 = (s32[64,2]{0,1:T(2,128)S(1)}, s32[64,2]{0,1:T(2,128)}, u32[]{:S(2)}) copy-start(s32[64,2]{0,1:T(2,128)} %param.9) | copy-start | bytes 1540
  2.9 42.2 %all-to-all-start = ((bf16[16,64,512]{2,1,0:T(8,128)(2,1)}), bf16[16,64,512]{2,1,0:T(8,128)(2,1)}, u32[]{:S(2)}, u32[]{:S(2)}) async-start(bf16[16,64,512]{2,1,0:T(8,128)(2,1)} %shard_map.94), calls=%async_computation | async-start | bytes 2097152 | tf_op jit(solution)/shard_map/all_to_all | solution.py:391
  11.5 29.4 %collective-permute-start = (bf16[64,8192]{1,0:T(8,128)(2,1)S(1)}, bf16[64,8192]{1,0:T(8,128)(2,1)S(1)}, u32[]{:S(2)}, u32[]{:S(2)}) collective-permute-start(bf16[64,8192]{1,0:T(8,128)(2,1)S(1)} %copy-done), channel_id=1, source_target_pairs={{0,16},{16,32},{32,48},{48,64},{64,80},{80,96},{96,112},{112,128},... | collective-permute-start | bytes 3145736 | tf_op jit(solution)/shard_map/ppermute | solution.py:387
  15.0 27.1 %collective-permute-start.1 = (bf16[64,8192]{1,0:T(8,128)(2,1)S(1)}, bf16[64,8192]{1,0:T(8,128)(2,1)S(1)}, u32[]{:S(2)}, u32[]{:S(2)}) collective-permute-start(bf16[64,8192]{1,0:T(8,128)(2,1)S(1)} %copy-done), channel_id=1, source_target_pairs={{16,0},{32,16},{48,32},{64,48},{80,64},{96,80},{112,96},{128,112},... | collective-permute-start | bytes 3145736 | tf_op jit(solution)/shard_map/ppermute | solution.py:387
  19.5 25.5 %copy-start.2 = (s32[64]{0:T(128)}, s32[64]{0:T(128)S(1)}, u32[]{:S(2)}) copy-start(s32[64]{0:T(128)S(1)} %subtract_bitcast_fusion.col_ref) | copy-start | bytes 772
  45.0 8.3 %copy-start.8 = (s32[64]{0:T(128)S(1)}, s32[64]{0:T(128)}, u32[]{:S(2)}) copy-start(s32[64]{0:T(128)} %param.10) | copy-start | bytes 772
  45.0 8.8 %copy-start.3 = (bf16[1024,1024]{1,0:T(8,128)(2,1)S(1)}, bf16[1024,1024]{1,0:T(8,128)(2,1)}, u32[]{:S(2)}) copy-start(bf16[1024,1024]{1,0:T(8,128)(2,1)} %w_self.1) | copy-start | bytes 6291460
  45.1 33.8 %all-to-all-start.1 = ((bf16[16,64,512]{2,1,0:T(8,128)(2,1)}), bf16[16,64,512]{2,1,0:T(8,128)(2,1)S(1)}, u32[]{:S(2)}, u32[]{:S(2)}) async-start(bf16[16,64,512]{2,1,0:T(8,128)(2,1)} %shard_map.95), calls=%async_computation.1 | async-start | bytes 2097152 | tf_op jit(solution)/shard_map/all_to_all | solution.py:391
  78.8 1.0 copy-start.4
  88.6 5.0 %copy-start.6 = (bf16[1024,512]{1,0:T(8,128)(2,1)S(1)}, bf16[1024,512]{1,0:T(8,128)(2,1)}, u32[]{:S(2)}) copy-start(bf16[1024,512]{1,0:T(8,128)(2,1)} %get-tuple-element.46) | copy-start | bytes 3145732
  88.6 8.5 %copy-start.1 = (bf16[1024,512]{1,0:T(8,128)(2,1)S(1)}, bf16[1024,512]{1,0:T(8,128)(2,1)}, u32[]{:S(2)}) copy-start(bf16[1024,512]{1,0:T(8,128)(2,1)} %get-tuple-element.45.kept_ref) | copy-start | bytes 3145732
  88.6 35.0 %all-to-all-start.2 = ((bf16[16,64,512]{2,1,0:T(8,128)(2,1)}), bf16[16,64,512]{2,1,0:T(8,128)(2,1)}, u32[]{:S(2)}, u32[]{:S(2)}) async-start(bf16[16,64,512]{2,1,0:T(8,128)(2,1)} %bitcast.54), calls=%async_computation.2 | async-start | bytes 2097152 | tf_op jit(solution)/shard_map/all_to_all | solution.py:391
  93.6 3.4 %collective-permute-start.2 = (bf16[1024,512]{1,0:T(8,128)(2,1)S(1)}, bf16[1024,512]{1,0:T(8,128)(2,1)S(1)}, u32[]{:S(2)}, u32[]{:S(2)}) collective-permute-start(bf16[1024,512]{1,0:T(8,128)(2,1)S(1)} %copy-done.6), channel_id=1, source_target_pairs={{0,1},{1,0},{2,3},{3,2},{4,5},{5,4},{6,7},{7,6},{8,9},{9,8},{10,11... | collective-permute-start | bytes 3145736 | tf_op jit(solution)/shard_map/ppermute | solution.py:408
  97.3 11.5 %collective-permute-start.3 = (bf16[256,512]{1,0:T(8,128)(2,1)S(1)}, bf16[256,512]{1,0:T(8,128)(2,1)S(1)}, u32[]{:S(2)}, u32[]{:S(2)}) collective-permute-start(bf16[256,512]{1,0:T(8,128)(2,1)S(1)} %get-tuple-element.48), channel_id=1, source_target_pairs={{0,16},{16,32},{32,48},{48,0},{64,80},{80,96},{96,112},{112,64},{1... | collective-permute-start | bytes 786440 | tf_op jit(solution)/shard_map/ppermute | solution.py:401
  98.9 16.7 %collective-permute-start.4 = (bf16[256,512]{1,0:T(8,128)(2,1)S(1)}, bf16[256,512]{1,0:T(8,128)(2,1)S(1)}, u32[]{:S(2)}, u32[]{:S(2)}) collective-permute-start(bf16[256,512]{1,0:T(8,128)(2,1)S(1)} %get-tuple-element.49), channel_id=1, source_target_pairs={{0,32},{16,48},{32,0},{48,16},{64,96},{80,112},{96,64},{112,80},{1... | collective-permute-start | bytes 786440 | tf_op jit(solution)/shard_map/ppermute | solution.py:401
  103.5 12.2 %collective-permute-start.5 = (bf16[256,512]{1,0:T(8,128)(2,1)S(1)}, bf16[256,512]{1,0:T(8,128)(2,1)S(1)}, u32[]{:S(2)}, u32[]{:S(2)}) collective-permute-start(bf16[256,512]{1,0:T(8,128)(2,1)S(1)} %get-tuple-element.50), channel_id=1, source_target_pairs={{0,48},{16,0},{32,16},{48,32},{64,112},{80,64},{96,80},{112,96},{1... | collective-permute-start | bytes 786440 | tf_op jit(solution)/shard_map/ppermute | solution.py:401
  115.8 5.1 %collective-permute-start.6 = (bf16[64,512]{1,0:T(8,128)(2,1)S(1)}, bf16[64,512]{1,0:T(8,128)(2,1)S(1)}, u32[]{:S(2)}, u32[]{:S(2)}) collective-permute-start(bf16[64,512]{1,0:T(8,128)(2,1)S(1)} %get-tuple-element.59), channel_id=1, source_target_pairs={{0,64},{16,80},{32,96},{48,112},{64,128},{80,144},{96,160},{112,17... | collective-permute-start | bytes 196616 | tf_op jit(solution)/shard_map/ppermute | solution.py:401
  117.2 5.9 %collective-permute-start.7 = (bf16[64,512]{1,0:T(8,128)(2,1)S(1)}, bf16[64,512]{1,0:T(8,128)(2,1)S(1)}, u32[]{:S(2)}, u32[]{:S(2)}) collective-permute-start(bf16[64,512]{1,0:T(8,128)(2,1)S(1)} %get-tuple-element.60), channel_id=1, source_target_pairs={{0,128},{16,144},{32,160},{48,176},{64,192},{80,208},{96,224},{112... | collective-permute-start | bytes 196616 | tf_op jit(solution)/shard_map/ppermute | solution.py:401
  118.6 5.0 %collective-permute-start.8 = (bf16[64,512]{1,0:T(8,128)(2,1)S(1)}, bf16[64,512]{1,0:T(8,128)(2,1)S(1)}, u32[]{:S(2)}, u32[]{:S(2)}) collective-permute-start(bf16[64,512]{1,0:T(8,128)(2,1)S(1)} %get-tuple-element.61), channel_id=1, source_target_pairs={{0,192},{16,208},{32,224},{48,240},{64,0},{80,16},{96,32},{112,48}... | collective-permute-start | bytes 196616 | tf_op jit(solution)/shard_map/ppermute | solution.py:401
  123.6 16.4 %copy-start.5 = (bf16[64,512]{1,0:T(8,128)(2,1)}, bf16[64,512]{1,0:T(8,128)(2,1)S(1)}, u32[]{:S(2)}) copy-start(bf16[64,512]{1,0:T(8,128)(2,1)S(1)} %collective-permute-done.8) | copy-start | bytes 196612
  127.9 43.5 %collective-permute-start.10 = (bf16[64,64,128]{2,1,0:T(8,128)(2,1)}, bf16[64,64,128]{2,1,0:T(8,128)(2,1)S(1)}, u32[]{:S(2)}, u32[]{:S(2)}) collective-permute-start(bf16[64,64,128]{2,1,0:T(8,128)(2,1)} %get-tuple-element.66), channel_id=1, source_target_pairs={{16,0},{32,16},{48,32},{64,48},{80,64},{96,80},{112,96},{128,112},... | collective-permute-start | bytes 3145736 | tf_op jit(solution)/shard_map/ppermute | solution.py:387
  131.7 39.6 %collective-permute-start.9 = (bf16[64,64,128]{2,1,0:T(8,128)(2,1)}, bf16[64,64,128]{2,1,0:T(8,128)(2,1)S(1)}, u32[]{:S(2)}, u32[]{:S(2)}) collective-permute-start(bf16[64,64,128]{2,1,0:T(8,128)(2,1)} %get-tuple-element.65), channel_id=1, source_target_pairs={{0,16},{16,32},{32,48},{48,64},{64,80},{80,96},{96,112},{112,128},... | collective-permute-start | bytes 3145736 | tf_op jit(solution)/shard_map/ppermute | solution.py:387
  133.7 48.3 %all-to-all-start.3 = ((bf16[16,64,512]{2,1,0:T(8,128)(2,1)}), bf16[16,64,512]{2,1,0:T(8,128)(2,1)S(1)}, u32[]{:S(2)}, u32[]{:S(2)}) async-start(bf16[16,64,512]{2,1,0:T(8,128)(2,1)} %shard_map.99), calls=%async_computation.3 | async-start | bytes 2097152 | tf_op jit(solution)/shard_map/all_to_all | solution.py:391
  140.9 30.4 %collective-permute-start.11 = (f32[32,512]{1,0:T(8,128)S(1)}, f32[32,512]{1,0:T(8,128)S(1)}, u32[]{:S(2)}, u32[]{:S(2)}) collective-permute-start(f32[32,512]{1,0:T(8,128)S(1)} %dynamic-slice_bitcast_fusion), channel_id=1, source_target_pairs={{0,8},{1,9},{2,10},{3,11},{4,12},{5,13},{6,14},{7,15},{8,0},{9,1},... | collective-permute-start | bytes 196616 | tf_op jit(solution)/shard_map/ppermute | solution.py:433
  171.4 4.9 %collective-permute-start.12 = (f32[16,512]{1,0:T(8,128)S(1)}, f32[16,512]{1,0:T(8,128)S(1)}, u32[]{:S(2)}, u32[]{:S(2)}) collective-permute-start(f32[16,512]{1,0:T(8,128)S(1)} %dynamic-slice_bitcast_fusion.1), channel_id=1, source_target_pairs={{0,4},{1,5},{2,6},{3,7},{4,0},{5,1},{6,2},{7,3},{8,12},{9,13},{10,... | collective-permute-start | bytes 98312 | tf_op jit(solution)/shard_map/ppermute | solution.py:433
  176.3 3.8 %collective-permute-start.13 = (f32[8,512]{1,0:T(8,128)S(1)}, f32[8,512]{1,0:T(8,128)S(1)}, u32[]{:S(2)}, u32[]{:S(2)}) collective-permute-start(f32[8,512]{1,0:T(8,128)S(1)} %dynamic-slice_bitcast_fusion.2), channel_id=1, source_target_pairs={{0,2},{1,3},{2,0},{3,1},{4,6},{5,7},{6,4},{7,5},{8,10},{9,11},{10,... | collective-permute-start | bytes 49160 | tf_op jit(solution)/shard_map/ppermute | solution.py:433
  180.1 1.3 collective-permute-start.14

commit v10 on v9

--- a/solution.py
+++ b/solution.py
@@ -279,9 +279,12 @@
     )(core, *args)
 
 
+EXTRA = 8
+
+
 def own_kernel(chunk, w_back, dpre, dagg_ref, turned, own):
     pair = turned.shape[-1]
-    each = own.shape[1]
+    each = own.shape[1] - EXTRA
     for i in range(0, dpre.shape[0], chunk):
         rows = slice(i, i + chunk)
         dself = dot(w_back[rows, :], dpre[...])
@@ -289,7 +292,7 @@
             here = slice(p * pair, (p + 1) * pair)
             total = dself[:, here] + dot(dagg_ref[rows, here], turned[0, p])
             for g in range(chunk // each):
-                own[i // each + g, :, here] = total[g * each : (g + 1) * each].astype(BF16)
+                own[i // each + g, :each, here] = total[g * each : (g + 1) * each].astype(BF16)
 
 
 def own_part(w_back, dpre, dagg, turned, groups):
@@ -298,7 +301,7 @@
         functools.partial(own_kernel, 256),
         in_specs=[VMEM] * 4,
         out_specs=VMEM,
-        out_shape=jax.ShapeDtypeStruct((groups, size // groups, width), BF16),
+        out_shape=jax.ShapeDtypeStruct((groups, size // groups + EXTRA, width), BF16),
         compiler_params=whole_params(OWN_MIB),
         cost_estimate=pl.CostEstimate(
             flops=2 * size * size * width, bytes_accessed=5 * MIB, transcendentals=0
@@ -403,42 +406,29 @@
     ]
 
 
-def weight_terms(sent, kept, groups, own_rows):
+def weight_rows(sent, kept, groups, own_rows):
     node = lax.axis_index("node")
     other = lax.ppermute(sent, "feat", [(i, i ^ 1) for i in range(groups)])
     pieces = weight_pieces(lax.rem(node, SIDE), kept, other)
     parts = sent_round(pieces, "node", lambda i, s: i // SIDE * SIDE + (i + s) % SIDE)
     parts, own_rows = lax.optimization_barrier((parts, own_rows))
     pieces = added_pieces(lax.div(node, SIDE), parts)
-    return sent_round(pieces, "node", lambda i, s: (i + s * SIDE) % (SIDE * SIDE))
-
-
-def piece_at(pieces, index):
-    return lax.dynamic_index_in_dim(pieces, index, 0, keepdims=False)
-
-
-def weight_total(parts, groups, halo):
-    feat = lax.axis_index("feat")
-    value = parts[0]
+    parts = sent_round(pieces, "node", lambda i, s: (i + s * SIDE) % (SIDE * SIDE))
+    total = parts[0]
     for part in parts[1:]:
-        value = value + part.astype(F32)
-    width = value.shape[1]
-    half = groups // 2
-    while half >= CORES:
-        if half == 2 * CORES:
-            value, _ = lax.optimization_barrier((value, halo))
-        bit = lax.rem(lax.div(feat, half), 2)
-        pieces = value.reshape(2, -1, width)
-        flip = [(i, i ^ half) for i in range(groups)]
-        value = piece_at(pieces, bit) + lax.ppermute(piece_at(pieces, 1 - bit), "feat", flip)
-        half //= 2
-    core = lax.rem(feat, CORES)
-    pieces = value.reshape(CORES, -1, width)
-    flip = [(i, i ^ 1) for i in range(groups)]
-    other = lax.ppermute(piece_at(pieces, 1 - core), "feat", flip)
-    kept = piece_at(pieces, core)
-    first, second = jnp.where(core == 0, kept, other), jnp.where(core == 0, other, kept)
-    return jnp.concatenate([first, second], axis=1)
+        total = total + part.astype(F32)
+    total = total.reshape(groups, EXTRA // 2, -1)
+    high = total.astype(BF16)
+    low = (total - high.astype(F32)).astype(BF16)
+    rows = jnp.concatenate([high, low], axis=1)
+    return lax.dynamic_update_slice(own_rows, rows, (0, own_rows.shape[1] - EXTRA, 0))
+
+
+def weight_total(rows):
+    groups, count, width = rows.shape
+    rows = rows.astype(F32).reshape(groups // CORES, CORES, 2, count // 2, width)
+    total = jnp.sum(rows, axis=(0, 2))
+    return jnp.concatenate([total[i] for i in range(CORES)], axis=1)
 
 
 def paired(tiles):
@@ -479,14 +469,11 @@
     )
     second_cols = exchange(second.reshape(groups, feat_dev, -1), "feat")
     own_rows = own_part(self_back, dpre, dagg, turned, groups)
-    terms = weight_terms(sent, kept, groups, own_rows)
-    terms, second_cols, own_rows = lax.optimization_barrier((terms, second_cols, own_rows))
+    own_cols = exchange(weight_rows(sent, kept, groups, own_rows), "feat")
     to_before, spread, to_after = scatter(col, second_cols)
-    own_cols = exchange(own_rows, "feat")
     from_after = shifted(to_before, "node", -1)
     from_before = shifted(to_after, "node", 1)
-    terms, _ = lax.optimization_barrier((terms, spread))
-    grad_w_neigh = weight_total(terms, groups, (from_after, from_before))
+    grad_w_neigh = weight_total(own_cols[:, feat_dev:])
     grad_features = finish(spread, from_before, from_after, own_cols)
     return (hidden, grad_features, grad_w_neigh)
 

time: 188 us -> 172 us (0.915)
  waiting for transfers between devices: 80.8 us -> 69.5 us
  starting transfers between devices: 59.7 us -> 53.5 us
    ppermute x5 -> x1, waiting for transfers between devices: 34.7 us -> 2.5 us  [weight_rows(): other = lax.ppermute(sent, 'feat', [(i, i ^ 1) for i in range(groups)])]
    all_to_all x4, waiting for transfers between devices: 11.9 us -> 29.1 us  [exchange(): return lax.all_to_all(value, axis, split_axis=0, concat_axis=0, tiled=True)]
    ppermute x5 -> x1, starting transfers between devices: 9.1 us -> 1.17 us  [weight_rows(): other = lax.ppermute(sent, 'feat', [(i, i ^ 1) for i in range(groups)])]
    ppermute x4, waiting for transfers between devices: 22.6 us -> 26 us  [shifted(): lax.ppermute(value, axis, [(source, source + steps) for source in range(f...]
    ppermute x4, starting transfers between devices: 13.8 us -> 15.9 us  [shifted(): lax.ppermute(value, axis, [(source, source + steps) for source in range(f...]
    unnamed x22 -> x18, local copies, waits for them, and re-layouts: 7.79 us -> 7.75 us
  transfers between devices with their start and end apart: 19 -> 15, of which waited for: 13 -> 12; matrix products, arithmetic and copies ran while one was open for 6% -> 8% of each run, Pallas kernels for 7% -> 10%
where the time goes in v10:
time: 172 us; the launch traced here: 170 us
  waiting for transfers between devices  69.5 us (40%)
  starting transfers between devices  53.5 us (31%)
  Pallas kernels  31.6 us (18%)
  local copies, waits for them, and re-layouts  11.2 us (7%)
  other arithmetic  3.26 us (2%)
    all_to_all x4, waiting for transfers between devices, exchange(): return lax.all_to_all(value, axis, split_axis=0, concat_axis=0, tiled=True)  29.1 us
    all_to_all x4, starting transfers between devices, exchange(): return lax.all_to_all(value, axis, split_axis=0, concat_axis=0, tiled=True)  26.9 us
    ppermute x4, waiting for transfers between devices, shifted(): lax.ppermute(value, axis, [(source, source + steps) for source in range(f...  26 us
    ppermute x4, starting transfers between devices, shifted(): lax.ppermute(value, axis, [(source, source + steps) for source in range(f...  15.9 us
    ppermute x6, waiting for transfers between devices, sent_round(): lax.ppermute(piece, axis, [(i, partner(i, step + 1)) for i in range(count)])  11.9 us
    ppermute x6, starting transfers between devices, sent_round(): lax.ppermute(piece, axis, [(i, partner(i, step + 1)) for i in range(count)])  9.57 us
    pallas_call x1, Pallas kernels, dense(): pl.pallas_call(functools.partial(dense_kernel, chunk), in_specs=[SMEM] +...  8.78 us
    unnamed x18, local copies, waits for them, and re-layouts  7.75 us
  transfers between devices with their start and end apart: 15, of which 12 were waited for; matrix products, arithmetic and copies ran while one was open for 8% of the time, Pallas kernels for 10%

profile of v10, /device:TPU:2, one launch (start us, length us, event | category | flops | bytes accessed | tf_op | source)
XLA Modules:
  0.0 170.1 jit_solution(724121473728659121)
XLA Ops:
  0.6 2.2 %shard_map.94 = bf16[16,64,512]{2,1,0:T(8,128)(2,1)} custom-call(bf16[64,8192]{1,0:T(8,128)(2,1)} %own.1), custom_call_target="tpu_custom_call" | custom-call | tf_op jit(solution)/shard_map/pallas_call | solution.py:61
  2.9 8.6 %all-to-all-start = ((bf16[16,64,512]{2,1,0:T(8,128)(2,1)}), bf16[16,64,512]{2,1,0:T(8,128)(2,1)}, u32[]{:S(2)}, u32[]{:S(2)}) async-start(bf16[16,64,512]{2,1,0:T(8,128)(2,1)} %shard_map.94), calls=%async_computation | async-start | bytes 2097152 | tf_op jit(solution)/shard_map/all_to_all | solution.py:394
  11.5 3.5 %collective-permute-start = (bf16[64,8192]{1,0:T(8,128)(2,1)S(1)}, bf16[64,8192]{1,0:T(8,128)(2,1)S(1)}, u32[]{:S(2)}, u32[]{:S(2)}) collective-permute-start(bf16[64,8192]{1,0:T(8,128)(2,1)S(1)} %copy-done), channel_id=1, source_target_pairs={{0,16},{16,32},{32,48},{48,64},{64,80},{80,96},{96,112},{112,128},... | collective-permute-start | bytes 3145736 | tf_op jit(solution)/shard_map/ppermute | solution.py:390
  15.0 4.5 %collective-permute-start.1 = (bf16[64,8192]{1,0:T(8,128)(2,1)S(1)}, bf16[64,8192]{1,0:T(8,128)(2,1)S(1)}, u32[]{:S(2)}, u32[]{:S(2)}) collective-permute-start(bf16[64,8192]{1,0:T(8,128)(2,1)S(1)} %copy-done), channel_id=1, source_target_pairs={{16,0},{32,16},{48,32},{64,48},{80,64},{96,80},{112,96},{128,112},... | collective-permute-start | bytes 3145736 | tf_op jit(solution)/shard_map/ppermute | solution.py:390
  19.6 21.4 %collective-permute-done.before = bf16[64,8192]{1,0:T(8,128)(2,1)S(1)} collective-permute-done((bf16[64,8192]{1,0:T(8,128)(2,1)S(1)}, bf16[64,8192]{1,0:T(8,128)(2,1)S(1)}, u32[]{:S(2)}, u32[]{:S(2)}) %collective-permute-start) | collective-permute-done | bytes 1048608 | tf_op jit(solution)/shard_map/ppermute | solution.py:390
  41.0 1.2 collective-permute-done.1.after
  42.2 2.9 %shard_map.95 = bf16[16,64,512]{2,1,0:T(8,128)(2,1)} custom-call(s32[64]{0:T(128)S(1)} %subtract_bitcast_fusion.col_ref, bf16[64,8192]{1,0:T(8,128)(2,1)S(1)} %collective-permute-done.before, bf16[64,8192]{1,0:T(8,128)(2,1)S(1)} %copy-done, bf16[64,8192]{1,0:T(8,128)(2,1)S(1)} %collective-permute-done.1.after), custom_call_target="tpu_custom_call" | custom-call | bytes 8388608 | tf_op jit(solution)/shard_map/pallas_call | solution.py:105
  45.1 7.1 %all-to-all-start.1 = ((bf16[16,64,512]{2,1,0:T(8,128)(2,1)}), bf16[16,64,512]{2,1,0:T(8,128)(2,1)S(1)}, u32[]{:S(2)}, u32[]{:S(2)}) async-start(bf16[16,64,512]{2,1,0:T(8,128)(2,1)} %shard_map.95), calls=%async_computation.1 | async-start | bytes 2097152 | tf_op jit(solution)/shard_map/all_to_all | solution.py:394
  53.9 2.6 %copy.14 = bf16[1024,1024]{0,1:T(8,128)(2,1)} copy(bf16[1024,1024]{1,0:T(8,128)(2,1)S(1)} %copy-done.3) | data formatting | bytes 4194304 | tf_op args[4]
  56.5 3.9 %copy.15 = bf16[1024,1024]{0,1:T(8,128)(2,1)} copy(bf16[1024,1024]{1,0:T(8,128)(2,1)} %refs_5_.1) | data formatting | bytes 4194304 | tf_op args[5]
  62.4 4.5 %shard_map.96.refs_6_ = f32[1024,512]{1,0:T(8,128)} custom-call(bf16[1024,1024]{1,0:T(8,128)(2,1)} %w_self.1, bf16[1024,512]{1,0:T(8,128)(2,1)} %bitcast.1.x_ref.refs_3_), custom_call_target="tpu_custom_call" | custom-call | flops 1073741824 | bytes 5242880 | tf_op jit(solution)/shard_map/pallas_call | solution.py:191
  66.9 11.9 %all-to-all-done.1 = bf16[16,64,512]{2,1,0:T(8,128)(2,1)S(1)} async-done(((bf16[16,64,512]{2,1,0:T(8,128)(2,1)}), bf16[16,64,512]{2,1,0:T(8,128)(2,1)S(1)}, u32[]{:S(2)}, u32[]{:S(2)}) %all-to-all-start.1) | async-done | bytes 1048608 | tf_op jit(solution)/shard_map/all_to_all | solution.py:394
  79.8 8.8 %shard_map.97 = (bf16[1024,512]{1,0:T(8,128)(2,1)}, bf16[1024,512]{1,0:T(8,128)(2,1)}, bf16[1024,512]{1,0:T(8,128)(2,1)}, bf16[1024,512]{1,0:T(8,128)(2,1)}, bf1...) custom-call(s32[1]{0:T(128)} %bitcast.refs_0_, ...), custom_call_target="tpu_custom_call" | custom-call | flops 2147483648 | bytes 16777216 | tf_op jit(solution)/shard_map/pallas_call | solution.py:266
  88.6 5.0 %all-to-all-start.2 = ((bf16[16,64,512]{2,1,0:T(8,128)(2,1)}), bf16[16,64,512]{2,1,0:T(8,128)(2,1)}, u32[]{:S(2)}, u32[]{:S(2)}) async-start(bf16[16,64,512]{2,1,0:T(8,128)(2,1)} %bitcast.35), calls=%async_computation.2 | async-start | bytes 2097152 | tf_op jit(solution)/shard_map/all_to_all | solution.py:394
  93.6 1.2 collective-permute-start.4
  94.8 2.5 %collective-permute-done.4.other_ref = bf16[1024,512]{1,0:T(8,128)(2,1)S(1)} collective-permute-done((bf16[1024,512]{1,0:T(8,128)(2,1)}, bf16[1024,512]{1,0:T(8,128)(2,1)S(1)}, u32[]{:S(2)}, u32[]{:S(2)}) %collective-permute-start.4) | collective-permute-done | bytes 1048608 | tf_op jit(solution)/shard_map/ppermute | solution.py:411
  97.5 1.6 collective-permute-start.5
  99.1 4.6 %collective-permute-start.6 = (bf16[256,512]{1,0:T(8,128)(2,1)S(1)}, bf16[256,512]{1,0:T(8,128)(2,1)S(1)}, u32[]{:S(2)}, u32[]{:S(2)}) collective-permute-start(bf16[256,512]{1,0:T(8,128)(2,1)S(1)} %get-tuple-element.43), channel_id=1, source_target_pairs={{0,32},{16,48},{32,0},{48,16},{64,96},{80,112},{96,64},{112,80},{1... | collective-permute-start | bytes 786440 | tf_op jit(solution)/shard_map/ppermute | solution.py:404
  103.7 4.9 %shard_map.100 = bf16[16,72,512]{2,1,0:T(8,128)(2,1)} custom-call(bf16[1024,1024]{1,0:T(8,128)(2,1)} %bitcast.32, bf16[1024,512]{1,0:T(8,128)(2,1)} %get-tuple-element.46.dpre, bf16[1024,512]{1,0:T(8,128)(2,1)} %get-tuple-element.47.dagg_ref, bf16[2,2,256,256]{3,2,1,0:T(8,128)(2,1)} %get-tuple-element.31.refs_2_.turned), custom_call_target="tpu_custom_call" | custom-call | flops 1073741824 | bytes 5242880 | tf_op jit(solution)/shard_map/pallas_call | solution.py:300
  109.0 6.8 %collective-permute-done.6.refs_2_ = bf16[256,512]{1,0:T(8,128)(2,1)S(1)} collective-permute-done((bf16[256,512]{1,0:T(8,128)(2,1)S(1)}, bf16[256,512]{1,0:T(8,128)(2,1)S(1)}, u32[]{:S(2)}, u32[]{:S(2)}) %collective-permute-start.6) | collective-permute-done | bytes 262176 | tf_op jit(solution)/shard_map/ppermute | solution.py:404
  116.7 1.5 collective-permute-start.8
  118.2 1.1 collective-permute-start.9
  119.3 1.1 collective-permute-done.10
  121.0 3.0 %collective-permute-done.9 = bf16[64,512]{1,0:T(8,128)(2,1)S(1)} collective-permute-done((bf16[64,512]{1,0:T(8,128)(2,1)S(1)}, bf16[64,512]{1,0:T(8,128)(2,1)S(1)}, u32[]{:S(2)}, u32[]{:S(2)}) %collective-permute-start.9) | collective-permute-done | bytes 65568 | tf_op jit(solution)/shard_map/ppermute | solution.py:404
  124.9 6.2 %all-to-all-start.3 = ((bf16[16,72,512]{2,1,0:T(8,128)(2,1)}), bf16[16,72,512]{2,1,0:T(8,128)(2,1)S(1)}, u32[]{:S(2)}, u32[]{:S(2)}) async-start(bf16[16,72,512]{2,1,0:T(8,128)(2,1)} %maximum_dynamic-update-slice_fusion), calls=%async_computation.3 | async-start | bytes 2359296 | tf_op jit(solution)/shard_map/all_to_all | solution.py:394
  131.0 4.3 %shard_map.98 = (bf16[64,64,128]{2,1,0:T(8,128)(2,1)}, f32[64,64,128]{2,1,0:T(8,128)}, bf16[64,64,128]{2,1,0:T(8,128)(2,1)}) custom-call(s32[64]{0:T(128)} %copy-done.2, bf16[16,64,512]{2,1,0:T(8,128)(2,1)} %all-to-all-done.2.parts_hbm), custom_call_target="tpu_custom_call" | custom-call | bytes 8388608 | tf_op jit(solution)/shard_map/pallas_call | solution.py:161
  135.3 1.9 %collective-permute-start.2 = (bf16[64,64,128]{2,1,0:T(8,128)(2,1)}, bf16[64,64,128]{2,1,0:T(8,128)(2,1)S(1)}, u32[]{:S(2)}, u32[]{:S(2)}) collective-permute-start(bf16[64,64,128]{2,1,0:T(8,128)(2,1)} %get-tuple-element.37), channel_id=1, source_target_pairs={{0,16},{16,32},{32,48},{48,64},{64,80},{80,96},{96,112},{112,128},... | collective-permute-start | bytes 3145736 | tf_op jit(solution)/shard_map/ppermute | solution.py:390
  137.2 6.0 %collective-permute-start.3 = (bf16[64,64,128]{2,1,0:T(8,128)(2,1)}, bf16[64,64,128]{2,1,0:T(8,128)(2,1)S(1)}, u32[]{:S(2)}, u32[]{:S(2)}) collective-permute-start(bf16[64,64,128]{2,1,0:T(8,128)(2,1)} %get-tuple-element.38), channel_id=1, source_target_pairs={{16,0},{32,16},{48,32},{64,48},{80,64},{96,80},{112,96},{128,112},... | collective-permute-start | bytes 3145736 | tf_op jit(solution)/shard_map/ppermute | solution.py:390
  143.3 17.2 %all-to-all-done.3.dself_ref = bf16[16,72,512]{2,1,0:T(8,128)(2,1)S(1)} async-done(((bf16[16,72,512]{2,1,0:T(8,128)(2,1)}), bf16[16,72,512]{2,1,0:T(8,128)(2,1)S(1)}, u32[]{:S(2)}, u32[]{:S(2)}) %all-to-all-start.3) | async-done | bytes 1179680 | tf_op jit(solution)/shard_map/all_to_all | solution.py:394
  162.9 2.1 %collective-permute-done.2.before_ref = bf16[64,64,128]{2,1,0:T(8,128)(2,1)S(1)} collective-permute-done((bf16[64,64,128]{2,1,0:T(8,128)(2,1)}, bf16[64,64,128]{2,1,0:T(8,128)(2,1)S(1)}, u32[]{:S(2)}, u32[]{:S(2)}) %collective-permute-start.2) | collective-permute-done | bytes 1048608 | tf_op jit(solution)/shard_map/ppermute | solution.py:390
  165.0 1.3 collective-permute-done.3.after_ref
  166.3 3.8 %shard_map.102 = bf16[64,8192]{1,0:T(8,128)(2,1)} custom-call(f32[64,64,128]{2,1,0:T(8,128)} %get-tuple-element.36.own_ref, bf16[64,64,128]{2,1,0:T(8,128)(2,1)S(1)} %collective-permute-done.2.before_ref, bf16[64,64,128]{2,1,0:T(8,128)(2,1)S(1)} %collective-permute-done.3.after_ref, bf16[16,72,512]{2,1,0:T(8,128)(2,1)S(1)} %all-to-all-done.3.dself_ref), custom_call_target="tpu_custom_call" | custom-call | tf_op jit(solution)/shard_map/pallas_call | solution.py:376
  (46 shorter events, 10.1 us)
Async XLA Ops:
  0.6 10.9 %copy-start = (bf16[64,8192]{1,0:T(8,128)(2,1)S(1)}, bf16[64,8192]{1,0:T(8,128)(2,1)}, u32[]{:S(2)}) copy-start(bf16[64,8192]{1,0:T(8,128)(2,1)} %own.1) | copy-start | bytes 3145732
  0.6 18.9 %copy-start.5 = (s32[64,2]{0,1:T(2,128)S(1)}, s32[64,2]{0,1:T(2,128)}, u32[]{:S(2)}) copy-start(s32[64,2]{0,1:T(2,128)} %param.9) | copy-start | bytes 1540
  2.9 42.2 %all-to-all-start = ((bf16[16,64,512]{2,1,0:T(8,128)(2,1)}), bf16[16,64,512]{2,1,0:T(8,128)(2,1)}, u32[]{:S(2)}, u32[]{:S(2)}) async-start(bf16[16,64,512]{2,1,0:T(8,128)(2,1)} %shard_map.94), calls=%async_computation | async-start | bytes 2097152 | tf_op jit(solution)/shard_map/all_to_all | solution.py:394
  11.5 29.4 %collective-permute-start = (bf16[64,8192]{1,0:T(8,128)(2,1)S(1)}, bf16[64,8192]{1,0:T(8,128)(2,1)S(1)}, u32[]{:S(2)}, u32[]{:S(2)}) collective-permute-start(bf16[64,8192]{1,0:T(8,128)(2,1)S(1)} %copy-done), channel_id=1, source_target_pairs={{0,16},{16,32},{32,48},{48,64},{64,80},{80,96},{96,112},{112,128},... | collective-permute-start | bytes 3145736 | tf_op jit(solution)/shard_map/ppermute | solution.py:390
  15.0 27.1 %collective-permute-start.1 = (bf16[64,8192]{1,0:T(8,128)(2,1)S(1)}, bf16[64,8192]{1,0:T(8,128)(2,1)S(1)}, u32[]{:S(2)}, u32[]{:S(2)}) collective-permute-start(bf16[64,8192]{1,0:T(8,128)(2,1)S(1)} %copy-done), channel_id=1, source_target_pairs={{16,0},{32,16},{48,32},{64,48},{80,64},{96,80},{112,96},{128,112},... | collective-permute-start | bytes 3145736 | tf_op jit(solution)/shard_map/ppermute | solution.py:390
  19.5 25.5 %copy-start.2 = (s32[64]{0:T(128)}, s32[64]{0:T(128)S(1)}, u32[]{:S(2)}) copy-start(s32[64]{0:T(128)S(1)} %subtract_bitcast_fusion.col_ref) | copy-start | bytes 772
  45.0 8.3 %copy-start.6 = (s32[64]{0:T(128)S(1)}, s32[64]{0:T(128)}, u32[]{:S(2)}) copy-start(s32[64]{0:T(128)} %param.10) | copy-start | bytes 772
  45.0 8.8 %copy-start.3 = (bf16[1024,1024]{1,0:T(8,128)(2,1)S(1)}, bf16[1024,1024]{1,0:T(8,128)(2,1)}, u32[]{:S(2)}) copy-start(bf16[1024,1024]{1,0:T(8,128)(2,1)} %w_self.1) | copy-start | bytes 6291460
  45.1 33.8 %all-to-all-start.1 = ((bf16[16,64,512]{2,1,0:T(8,128)(2,1)}), bf16[16,64,512]{2,1,0:T(8,128)(2,1)S(1)}, u32[]{:S(2)}, u32[]{:S(2)}) async-start(bf16[16,64,512]{2,1,0:T(8,128)(2,1)} %shard_map.95), calls=%async_computation.1 | async-start | bytes 2097152 | tf_op jit(solution)/shard_map/all_to_all | solution.py:394
  78.8 1.0 copy-start.4
  88.6 8.7 %copy-start.1 = (bf16[1024,512]{1,0:T(8,128)(2,1)S(1)}, bf16[1024,512]{1,0:T(8,128)(2,1)}, u32[]{:S(2)}) copy-start(bf16[1024,512]{1,0:T(8,128)(2,1)} %get-tuple-element.39.kept_ref) | copy-start | bytes 3145732
  88.6 36.3 %all-to-all-start.2 = ((bf16[16,64,512]{2,1,0:T(8,128)(2,1)}), bf16[16,64,512]{2,1,0:T(8,128)(2,1)}, u32[]{:S(2)}, u32[]{:S(2)}) async-start(bf16[16,64,512]{2,1,0:T(8,128)(2,1)} %bitcast.35), calls=%async_computation.2 | async-start | bytes 2097152 | tf_op jit(solution)/shard_map/all_to_all | solution.py:394
  93.6 3.7 %collective-permute-start.4 = (bf16[1024,512]{1,0:T(8,128)(2,1)}, bf16[1024,512]{1,0:T(8,128)(2,1)S(1)}, u32[]{:S(2)}, u32[]{:S(2)}) collective-permute-start(bf16[1024,512]{1,0:T(8,128)(2,1)} %get-tuple-element.40), channel_id=1, source_target_pairs={{0,1},{1,0},{2,3},{3,2},{4,5},{5,4},{6,7},{7,6},{8,9},{9,8},{10,11... | collective-permute-start | bytes 3145736 | tf_op jit(solution)/shard_map/ppermute | solution.py:411
  97.5 11.5 %collective-permute-start.5 = (bf16[256,512]{1,0:T(8,128)(2,1)S(1)}, bf16[256,512]{1,0:T(8,128)(2,1)S(1)}, u32[]{:S(2)}, u32[]{:S(2)}) collective-permute-start(bf16[256,512]{1,0:T(8,128)(2,1)S(1)} %get-tuple-element.42), channel_id=1, source_target_pairs={{0,16},{16,32},{32,48},{48,0},{64,80},{80,96},{96,112},{112,64},{1... | collective-permute-start | bytes 786440 | tf_op jit(solution)/shard_map/ppermute | solution.py:404
  99.1 16.7 %collective-permute-start.6 = (bf16[256,512]{1,0:T(8,128)(2,1)S(1)}, bf16[256,512]{1,0:T(8,128)(2,1)S(1)}, u32[]{:S(2)}, u32[]{:S(2)}) collective-permute-start(bf16[256,512]{1,0:T(8,128)(2,1)S(1)} %get-tuple-element.43), channel_id=1, source_target_pairs={{0,32},{16,48},{32,0},{48,16},{64,96},{80,112},{96,64},{112,80},{1... | collective-permute-start | bytes 786440 | tf_op jit(solution)/shard_map/ppermute | solution.py:404
  103.7 12.2 %collective-permute-start.7 = (bf16[256,512]{1,0:T(8,128)(2,1)S(1)}, bf16[256,512]{1,0:T(8,128)(2,1)S(1)}, u32[]{:S(2)}, u32[]{:S(2)}) collective-permute-start(bf16[256,512]{1,0:T(8,128)(2,1)S(1)} %get-tuple-element.44), channel_id=1, source_target_pairs={{0,48},{16,0},{32,16},{48,32},{64,112},{80,64},{96,80},{112,96},{1... | collective-permute-start | bytes 786440 | tf_op jit(solution)/shard_map/ppermute | solution.py:404
  115.9 4.5 %collective-permute-start.10 = (bf16[64,512]{1,0:T(8,128)(2,1)S(1)}, bf16[64,512]{1,0:T(8,128)(2,1)S(1)}, u32[]{:S(2)}, u32[]{:S(2)}) collective-permute-start(bf16[64,512]{1,0:T(8,128)(2,1)S(1)} %get-tuple-element.56), channel_id=1, source_target_pairs={{0,192},{16,208},{32,224},{48,240},{64,0},{80,16},{96,32},{112,48}... | collective-permute-start | bytes 196616 | tf_op jit(solution)/shard_map/ppermute | solution.py:404
  116.7 4.3 %collective-permute-start.8 = (bf16[64,512]{1,0:T(8,128)(2,1)S(1)}, bf16[64,512]{1,0:T(8,128)(2,1)S(1)}, u32[]{:S(2)}, u32[]{:S(2)}) collective-permute-start(bf16[64,512]{1,0:T(8,128)(2,1)S(1)} %get-tuple-element.54), channel_id=1, source_target_pairs={{0,64},{16,80},{32,96},{48,112},{64,128},{80,144},{96,160},{112,17... | collective-permute-start | bytes 196616 | tf_op jit(solution)/shard_map/ppermute | solution.py:404
  118.2 5.8 %collective-permute-start.9 = (bf16[64,512]{1,0:T(8,128)(2,1)S(1)}, bf16[64,512]{1,0:T(8,128)(2,1)S(1)}, u32[]{:S(2)}, u32[]{:S(2)}) collective-permute-start(bf16[64,512]{1,0:T(8,128)(2,1)S(1)} %get-tuple-element.55), channel_id=1, source_target_pairs={{0,128},{16,144},{32,160},{48,176},{64,192},{80,208},{96,224},{112... | collective-permute-start | bytes 196616 | tf_op jit(solution)/shard_map/ppermute | solution.py:404
  124.9 35.6 %all-to-all-start.3 = ((bf16[16,72,512]{2,1,0:T(8,128)(2,1)}), bf16[16,72,512]{2,1,0:T(8,128)(2,1)S(1)}, u32[]{:S(2)}, u32[]{:S(2)}) async-start(bf16[16,72,512]{2,1,0:T(8,128)(2,1)} %maximum_dynamic-update-slice_fusion), calls=%async_computation.3 | async-start | bytes 2359296 | tf_op jit(solution)/shard_map/all_to_all | solution.py:394
  135.3 29.7 %collective-permute-start.2 = (bf16[64,64,128]{2,1,0:T(8,128)(2,1)}, bf16[64,64,128]{2,1,0:T(8,128)(2,1)S(1)}, u32[]{:S(2)}, u32[]{:S(2)}) collective-permute-start(bf16[64,64,128]{2,1,0:T(8,128)(2,1)} %get-tuple-element.37), channel_id=1, source_target_pairs={{0,16},{16,32},{32,48},{48,64},{64,80},{80,96},{96,112},{112,128},... | collective-permute-start | bytes 3145736 | tf_op jit(solution)/shard_map/ppermute | solution.py:390
  137.2 29.1 %collective-permute-start.3 = (bf16[64,64,128]{2,1,0:T(8,128)(2,1)}, bf16[64,64,128]{2,1,0:T(8,128)(2,1)S(1)}, u32[]{:S(2)}, u32[]{:S(2)}) collective-permute-start(bf16[64,64,128]{2,1,0:T(8,128)(2,1)} %get-tuple-element.38), channel_id=1, source_target_pairs={{16,0},{32,16},{48,32},{64,48},{80,64},{96,80},{112,96},{128,112},... | collective-permute-start | bytes 3145736 | tf_op jit(solution)/shard_map/ppermute | solution.py:390

commit v11 on v10

--- a/solution.py
+++ b/solution.py
@@ -15,7 +15,7 @@
 DENSE_MIB = 56
 OWN_MIB = 60
 WEIGHT_MIB = 8
-FINAL_MIB = 50
+FINAL_MIB = 16
 SCATTER_MIB = 56
 CHUNK = 512
 
@@ -359,29 +359,48 @@
     )(me[None], *parts)
 
 
-def final_kernel(own_ref, before_ref, after_ref, dself_ref, out_ref):
-    tile = own_ref.shape[2]
-    per = dself_ref.shape[2] // tile
-    for b in range(own_ref.shape[0]):
-        grad = dself_ref[b // per, : own_ref.shape[1], (b % per) * tile : (b % per + 1) * tile]
-        total = own_ref[b] + before_ref[b].astype(F32) + after_ref[b].astype(F32)
-        out_ref[:, b * tile : (b + 1) * tile] = (grad.astype(F32) + total).astype(BF16)
-
-
-def finish(own, before, after, dself):
-    groups, high, width = dself.shape
-    blocks, rows, tile = own.shape
+def base_kernel(spread_ref, own_ref, out_ref):
+    rows, tile = spread_ref.shape[1:]
+    per = own_ref.shape[2] // tile
+    for b in range(spread_ref.shape[0]):
+        part = own_ref[b // per, :rows, (b % per) * tile : (b % per + 1) * tile]
+        out_ref[b] = spread_ref[b] + part.astype(F32)
+
+
+def based(spread, own):
+    groups, high, width = own.shape
+    blocks, rows, tile = spread.shape
     steps = 4
     part = pl.BlockSpec((blocks // steps, rows, tile), lambda g: (g, 0, 0))
     return pl.pallas_call(
+        base_kernel,
+        grid=(steps,),
+        in_specs=[part, pl.BlockSpec((groups // steps, high, width), lambda g: (g, 0, 0))],
+        out_specs=part,
+        out_shape=jax.ShapeDtypeStruct(spread.shape, F32),
+        compiler_params=params(FINAL_MIB),
+    )(spread, own)
+
+
+def final_kernel(base_ref, before_ref, after_ref, out_ref):
+    tile = base_ref.shape[2]
+    for b in range(base_ref.shape[0]):
+        total = base_ref[b] + before_ref[b].astype(F32) + after_ref[b].astype(F32)
+        out_ref[:, b * tile : (b + 1) * tile] = total.astype(BF16)
+
+
+def finish(base, before, after):
+    blocks, rows, tile = base.shape
+    steps = 4
+    part = pl.BlockSpec((blocks // steps, rows, tile), lambda g: (g, 0, 0))
+    return pl.pallas_call(
         final_kernel,
         grid=(steps,),
-        in_specs=[part, part, part]
-        + [pl.BlockSpec((groups // steps, high, width), lambda g: (g, 0, 0))],
-        out_specs=pl.BlockSpec((rows, groups * width // steps), lambda g: (0, g)),
-        out_shape=jax.ShapeDtypeStruct((rows, groups * width), BF16),
+        in_specs=[part, part, part],
+        out_specs=pl.BlockSpec((rows, blocks * tile // steps), lambda g: (0, g)),
+        out_shape=jax.ShapeDtypeStruct((rows, blocks * tile), BF16),
         compiler_params=params(FINAL_MIB),
-    )(own, before, after, dself)
+    )(base, before, after)
 
 
 def shifted(value, axis, steps):
@@ -406,7 +425,7 @@
     ]
 
 
-def weight_rows(sent, kept, groups, own_rows):
+def weight_rows(sent, kept, groups, own_rows, spread):
     node = lax.axis_index("node")
     other = lax.ppermute(sent, "feat", [(i, i ^ 1) for i in range(groups)])
     pieces = weight_pieces(lax.rem(node, SIDE), kept, other)
@@ -414,6 +433,7 @@
     parts, own_rows = lax.optimization_barrier((parts, own_rows))
     pieces = added_pieces(lax.div(node, SIDE), parts)
     parts = sent_round(pieces, "node", lambda i, s: (i + s * SIDE) % (SIDE * SIDE))
+    parts, _ = lax.optimization_barrier((parts, spread))
     total = parts[0]
     for part in parts[1:]:
         total = total + part.astype(F32)
@@ -469,12 +489,12 @@
     )
     second_cols = exchange(second.reshape(groups, feat_dev, -1), "feat")
     own_rows = own_part(self_back, dpre, dagg, turned, groups)
-    own_cols = exchange(weight_rows(sent, kept, groups, own_rows), "feat")
     to_before, spread, to_after = scatter(col, second_cols)
+    own_cols = exchange(weight_rows(sent, kept, groups, own_rows, spread), "feat")
     from_after = shifted(to_before, "node", -1)
     from_before = shifted(to_after, "node", 1)
     grad_w_neigh = weight_total(own_cols[:, feat_dev:])
-    grad_features = finish(spread, from_before, from_after, own_cols)
+    grad_features = finish(based(spread, own_cols), from_before, from_after)
     return (hidden, grad_features, grad_w_neigh)
 
 

time: 172 us -> 172 us (level)
    all_to_all x4, waiting for transfers between devices: 29.1 us -> 34.1 us  [exchange(): return lax.all_to_all(value, axis, split_axis=0, concat_axis=0, tiled=True)]
    ppermute x6, waiting for transfers between devices: 11.9 us -> 7.3 us  [sent_round(): lax.ppermute(piece, axis, [(i, partner(i, step + 1)) for i in range(count)])]
    pallas_call x1 -> x2, Pallas kernels: 3.77 us -> 3.92 us  [the longest x1 3.68 us: finish(): pl.pallas_call(final_kernel, grid=(steps,), in_specs=[part, part, part],...]
    unnamed x18 -> x20, local copies, waits for them, and re-layouts: 7.75 us -> 7.77 us
  transfers between devices with their start and end apart: 15 -> 15, of which waited for: 12 -> 9; matrix products, arithmetic and copies ran while one was open for 8% -> 7% of each run, Pallas kernels for 10% -> 10%
where the time goes in v11:
time: 172 us; the launch traced here: 170 us
  waiting for transfers between devices  69.9 us (41%)
  starting transfers between devices  53 us (31%)
  Pallas kernels  31.7 us (18%)
  local copies, waits for them, and re-layouts  11.2 us (7%)
  other arithmetic  3.27 us (2%)
    all_to_all x4, waiting for transfers between devices, exchange(): return lax.all_to_all(value, axis, split_axis=0, concat_axis=0, tiled=True)  34.1 us
    all_to_all x4, starting transfers between devices, exchange(): return lax.all_to_all(value, axis, split_axis=0, concat_axis=0, tiled=True)  26.2 us
    ppermute x4, waiting for transfers between devices, shifted(): lax.ppermute(value, axis, [(source, source + steps) for source in range(f...  26 us
    ppermute x4, starting transfers between devices, shifted(): lax.ppermute(value, axis, [(source, source + steps) for source in range(f...  15.9 us
    ppermute x6, starting transfers between devices, sent_round(): lax.ppermute(piece, axis, [(i, partner(i, step + 1)) for i in range(count)])  9.79 us
    pallas_call x1, Pallas kernels, dense(): pl.pallas_call(functools.partial(dense_kernel, chunk), in_specs=[SMEM] +...  8.78 us
    unnamed x20, local copies, waits for them, and re-layouts  7.77 us
    ppermute x6, waiting for transfers between devices, sent_round(): lax.ppermute(piece, axis, [(i, partner(i, step + 1)) for i in range(count)])  7.3 us
  transfers between devices with their start and end apart: 15, of which 9 were waited for; matrix products, arithmetic and copies ran while one was open for 7% of the time, Pallas kernels for 10%

profile of v11, /device:TPU:2, one launch (start us, length us, event | category | flops | bytes accessed | tf_op | source)
XLA Modules:
  0.0 170.2 jit_solution(12444031160514416882)
XLA Ops:
  0.6 2.2 %shard_map.94 = bf16[16,64,512]{2,1,0:T(8,128)(2,1)} custom-call(bf16[64,8192]{1,0:T(8,128)(2,1)} %own.1), custom_call_target="tpu_custom_call" | custom-call | tf_op jit(solution)/shard_map/pallas_call | solution.py:61
  2.9 8.6 %all-to-all-start = ((bf16[16,64,512]{2,1,0:T(8,128)(2,1)}), bf16[16,64,512]{2,1,0:T(8,128)(2,1)}, u32[]{:S(2)}, u32[]{:S(2)}) async-start(bf16[16,64,512]{2,1,0:T(8,128)(2,1)} %shard_map.94), calls=%async_computation | async-start | bytes 2097152 | tf_op jit(solution)/shard_map/all_to_all | solution.py:413
  11.5 3.5 %collective-permute-start = (bf16[64,8192]{1,0:T(8,128)(2,1)S(1)}, bf16[64,8192]{1,0:T(8,128)(2,1)S(1)}, u32[]{:S(2)}, u32[]{:S(2)}) collective-permute-start(bf16[64,8192]{1,0:T(8,128)(2,1)S(1)} %copy-done), channel_id=1, source_target_pairs={{0,16},{16,32},{32,48},{48,64},{64,80},{80,96},{96,112},{112,128},... | collective-permute-start | bytes 3145736 | tf_op jit(solution)/shard_map/ppermute | solution.py:409
  15.0 4.5 %collective-permute-start.1 = (bf16[64,8192]{1,0:T(8,128)(2,1)S(1)}, bf16[64,8192]{1,0:T(8,128)(2,1)S(1)}, u32[]{:S(2)}, u32[]{:S(2)}) collective-permute-start(bf16[64,8192]{1,0:T(8,128)(2,1)S(1)} %copy-done), channel_id=1, source_target_pairs={{16,0},{32,16},{48,32},{64,48},{80,64},{96,80},{112,96},{128,112},... | collective-permute-start | bytes 3145736 | tf_op jit(solution)/shard_map/ppermute | solution.py:409
  19.6 21.4 %collective-permute-done.before = bf16[64,8192]{1,0:T(8,128)(2,1)S(1)} collective-permute-done((bf16[64,8192]{1,0:T(8,128)(2,1)S(1)}, bf16[64,8192]{1,0:T(8,128)(2,1)S(1)}, u32[]{:S(2)}, u32[]{:S(2)}) %collective-permute-start) | collective-permute-done | bytes 1048608 | tf_op jit(solution)/shard_map/ppermute | solution.py:409
  41.0 1.2 collective-permute-done.1.after
  42.2 2.9 %shard_map.95 = bf16[16,64,512]{2,1,0:T(8,128)(2,1)} custom-call(s32[64]{0:T(128)S(1)} %subtract_bitcast_fusion.col_ref, bf16[64,8192]{1,0:T(8,128)(2,1)S(1)} %collective-permute-done.before, bf16[64,8192]{1,0:T(8,128)(2,1)S(1)} %copy-done, bf16[64,8192]{1,0:T(8,128)(2,1)S(1)} %collective-permute-done.1.after), custom_call_target="tpu_custom_call" | custom-call | bytes 8388608 | tf_op jit(solution)/shard_map/pallas_call | solution.py:105
  45.1 7.1 %all-to-all-start.1 = ((bf16[16,64,512]{2,1,0:T(8,128)(2,1)}), bf16[16,64,512]{2,1,0:T(8,128)(2,1)S(1)}, u32[]{:S(2)}, u32[]{:S(2)}) async-start(bf16[16,64,512]{2,1,0:T(8,128)(2,1)} %shard_map.95), calls=%async_computation.1 | async-start | bytes 2097152 | tf_op jit(solution)/shard_map/all_to_all | solution.py:413
  52.2 1.0 constant_dynamic-slice_fusion
  53.9 2.6 %copy.14 = bf16[1024,1024]{0,1:T(8,128)(2,1)} copy(bf16[1024,1024]{1,0:T(8,128)(2,1)S(1)} %copy-done.4) | data formatting | bytes 4194304 | tf_op args[4]
  56.5 3.9 %copy.15 = bf16[1024,1024]{0,1:T(8,128)(2,1)} copy(bf16[1024,1024]{1,0:T(8,128)(2,1)} %refs_5_.1) | data formatting | bytes 4194304 | tf_op args[5]
  61.4 1.0 copy.21.refs_1_
  62.4 4.5 %shard_map.96.refs_6_ = f32[1024,512]{1,0:T(8,128)} custom-call(bf16[1024,1024]{1,0:T(8,128)(2,1)} %w_self.1, bf16[1024,512]{1,0:T(8,128)(2,1)} %bitcast.1.x_ref.refs_3_), custom_call_target="tpu_custom_call" | custom-call | flops 1073741824 | bytes 5242880 | tf_op jit(solution)/shard_map/pallas_call | solution.py:191
  66.9 11.9 %all-to-all-done.1 = bf16[16,64,512]{2,1,0:T(8,128)(2,1)S(1)} async-done(((bf16[16,64,512]{2,1,0:T(8,128)(2,1)}), bf16[16,64,512]{2,1,0:T(8,128)(2,1)S(1)}, u32[]{:S(2)}, u32[]{:S(2)}) %all-to-all-start.1) | async-done | bytes 1048608 | tf_op jit(solution)/shard_map/all_to_all | solution.py:413
  79.8 8.8 %shard_map.97 = (bf16[1024,512]{1,0:T(8,128)(2,1)}, bf16[1024,512]{1,0:T(8,128)(2,1)}, bf16[1024,512]{1,0:T(8,128)(2,1)}, bf16[1024,512]{1,0:T(8,128)(2,1)}, bf1...) custom-call(s32[1]{0:T(128)} %bitcast.refs_0_, ...), custom_call_target="tpu_custom_call" | custom-call | flops 2147483648 | bytes 16777216 | tf_op jit(solution)/shard_map/pallas_call | solution.py:266
  88.6 5.0 %all-to-all-start.2 = ((bf16[16,64,512]{2,1,0:T(8,128)(2,1)}), bf16[16,64,512]{2,1,0:T(8,128)(2,1)}, u32[]{:S(2)}, u32[]{:S(2)}) async-start(bf16[16,64,512]{2,1,0:T(8,128)(2,1)} %bitcast.35), calls=%async_computation.2 | async-start | bytes 2097152 | tf_op jit(solution)/shard_map/all_to_all | solution.py:413
  93.6 1.2 collective-permute-start.2
  94.7 2.5 %collective-permute-done.2.other_ref = bf16[1024,512]{1,0:T(8,128)(2,1)S(1)} collective-permute-done((bf16[1024,512]{1,0:T(8,128)(2,1)}, bf16[1024,512]{1,0:T(8,128)(2,1)S(1)}, u32[]{:S(2)}, u32[]{:S(2)}) %collective-permute-start.2) | collective-permute-done | bytes 1048608 | tf_op jit(solution)/shard_map/ppermute | solution.py:430
  97.5 1.6 collective-permute-start.3
  99.1 4.6 %collective-permute-start.4 = (bf16[256,512]{1,0:T(8,128)(2,1)S(1)}, bf16[256,512]{1,0:T(8,128)(2,1)S(1)}, u32[]{:S(2)}, u32[]{:S(2)}) collective-permute-start(bf16[256,512]{1,0:T(8,128)(2,1)S(1)} %get-tuple-element.45), channel_id=1, source_target_pairs={{0,32},{16,48},{32,0},{48,16},{64,96},{80,112},{96,64},{112,80},{1... | collective-permute-start | bytes 786440 | tf_op jit(solution)/shard_map/ppermute | solution.py:423
  103.7 4.9 %shard_map.100 = bf16[16,72,512]{2,1,0:T(8,128)(2,1)} custom-call(bf16[1024,1024]{1,0:T(8,128)(2,1)} %bitcast.32, bf16[1024,512]{1,0:T(8,128)(2,1)} %get-tuple-element.48.dpre, bf16[1024,512]{1,0:T(8,128)(2,1)} %get-tuple-element.49.dagg_ref, bf16[2,2,256,256]{3,2,1,0:T(8,128)(2,1)} %get-tuple-element.35.refs_2_.turned), custom_call_target="tpu_custom_call" | custom-call | flops 1073741824 | bytes 5242880 | tf_op jit(solution)/shard_map/pallas_call | solution.py:300
  109.0 6.8 %collective-permute-done.4.refs_2_ = bf16[256,512]{1,0:T(8,128)(2,1)S(1)} collective-permute-done((bf16[256,512]{1,0:T(8,128)(2,1)S(1)}, bf16[256,512]{1,0:T(8,128)(2,1)S(1)}, u32[]{:S(2)}, u32[]{:S(2)}) %collective-permute-start.4) | collective-permute-done | bytes 262176 | tf_op jit(solution)/shard_map/ppermute | solution.py:423
  115.9 1.4 collective-permute-start.6
  117.4 1.4 collective-permute-start.7
  120.3 4.2 %shard_map.98 = (bf16[64,64,128]{2,1,0:T(8,128)(2,1)}, f32[64,64,128]{2,1,0:T(8,128)}, bf16[64,64,128]{2,1,0:T(8,128)(2,1)}) custom-call(s32[64]{0:T(128)} %copy-done.3, bf16[16,64,512]{2,1,0:T(8,128)(2,1)} %all-to-all-done.2.parts_hbm), custom_call_target="tpu_custom_call" | custom-call | bytes 8388608 | tf_op jit(solution)/shard_map/pallas_call | solution.py:161
  125.5 5.4 %all-to-all-start.3 = ((bf16[16,72,512]{2,1,0:T(8,128)(2,1)}), bf16[16,72,512]{2,1,0:T(8,128)(2,1)S(1)}, u32[]{:S(2)}, u32[]{:S(2)}) async-start(bf16[16,72,512]{2,1,0:T(8,128)(2,1)} %maximum_dynamic-update-slice_fusion), calls=%async_computation.3 | async-start | bytes 2359296 | tf_op jit(solution)/shard_map/all_to_all | solution.py:413
  130.9 6.0 %collective-permute-start.10 = (bf16[64,64,128]{2,1,0:T(8,128)(2,1)}, bf16[64,64,128]{2,1,0:T(8,128)(2,1)}, u32[]{:S(2)}, u32[]{:S(2)}) collective-permute-start(bf16[64,64,128]{2,1,0:T(8,128)(2,1)} %get-tuple-element.64), channel_id=1, source_target_pairs={{16,0},{32,16},{48,32},{64,48},{80,64},{96,80},{112,96},{128,112},... | collective-permute-start | bytes 3145736 | tf_op jit(solution)/shard_map/ppermute | solution.py:409
  137.0 1.9 %collective-permute-start.9 = (bf16[64,64,128]{2,1,0:T(8,128)(2,1)}, bf16[64,64,128]{2,1,0:T(8,128)(2,1)}, u32[]{:S(2)}, u32[]{:S(2)}) collective-permute-start(bf16[64,64,128]{2,1,0:T(8,128)(2,1)} %get-tuple-element.63), channel_id=1, source_target_pairs={{0,16},{16,32},{32,48},{48,64},{64,80},{80,96},{96,112},{112,128},... | collective-permute-start | bytes 3145736 | tf_op jit(solution)/shard_map/ppermute | solution.py:409
  138.9 21.5 %all-to-all-done.3.own_ref = bf16[16,72,512]{2,1,0:T(8,128)(2,1)S(1)} async-done(((bf16[16,72,512]{2,1,0:T(8,128)(2,1)}), bf16[16,72,512]{2,1,0:T(8,128)(2,1)S(1)}, u32[]{:S(2)}, u32[]{:S(2)}) %all-to-all-start.3) | async-done | bytes 1179680 | tf_op jit(solution)/shard_map/all_to_all | solution.py:413
  161.1 1.0 reshape.38
  163.0 3.4 %collective-permute-done.9.before_ref = bf16[64,64,128]{2,1,0:T(8,128)(2,1)} collective-permute-done((bf16[64,64,128]{2,1,0:T(8,128)(2,1)}, bf16[64,64,128]{2,1,0:T(8,128)(2,1)}, u32[]{:S(2)}, u32[]{:S(2)}) %collective-permute-start.9) | collective-permute-done | bytes 1048608 | tf_op jit(solution)/shard_map/ppermute | solution.py:409
  166.5 3.7 %shard_map.103 = bf16[64,8192]{1,0:T(8,128)(2,1)} custom-call(f32[64,64,128]{2,1,0:T(8,128)S(1)} %shard_map.102.base_ref, bf16[64,64,128]{2,1,0:T(8,128)(2,1)} %collective-permute-done.9.before_ref, bf16[64,64,128]{2,1,0:T(8,128)(2,1)} %collective-permute-done.10.after_ref), custom_call_target="tpu_custom_call" | custom-call | tf_op jit(solution)/shard_map/pallas_call | solution.py:396
  (49 shorter events, 7.5 us)
Async XLA Ops:
  0.6 10.9 %copy-start = (bf16[64,8192]{1,0:T(8,128)(2,1)S(1)}, bf16[64,8192]{1,0:T(8,128)(2,1)}, u32[]{:S(2)}) copy-start(bf16[64,8192]{1,0:T(8,128)(2,1)} %own.1) | copy-start | bytes 3145732
  0.6 18.9 %copy-start.6 = (s32[64,2]{0,1:T(2,128)S(1)}, s32[64,2]{0,1:T(2,128)}, u32[]{:S(2)}) copy-start(s32[64,2]{0,1:T(2,128)} %param.9) | copy-start | bytes 1540
  2.9 42.2 %all-to-all-start = ((bf16[16,64,512]{2,1,0:T(8,128)(2,1)}), bf16[16,64,512]{2,1,0:T(8,128)(2,1)}, u32[]{:S(2)}, u32[]{:S(2)}) async-start(bf16[16,64,512]{2,1,0:T(8,128)(2,1)} %shard_map.94), calls=%async_computation | async-start | bytes 2097152 | tf_op jit(solution)/shard_map/all_to_all | solution.py:413
  11.5 29.4 %collective-permute-start = (bf16[64,8192]{1,0:T(8,128)(2,1)S(1)}, bf16[64,8192]{1,0:T(8,128)(2,1)S(1)}, u32[]{:S(2)}, u32[]{:S(2)}) collective-permute-start(bf16[64,8192]{1,0:T(8,128)(2,1)S(1)} %copy-done), channel_id=1, source_target_pairs={{0,16},{16,32},{32,48},{48,64},{64,80},{80,96},{96,112},{112,128},... | collective-permute-start | bytes 3145736 | tf_op jit(solution)/shard_map/ppermute | solution.py:409
  15.0 27.1 %collective-permute-start.1 = (bf16[64,8192]{1,0:T(8,128)(2,1)S(1)}, bf16[64,8192]{1,0:T(8,128)(2,1)S(1)}, u32[]{:S(2)}, u32[]{:S(2)}) collective-permute-start(bf16[64,8192]{1,0:T(8,128)(2,1)S(1)} %copy-done), channel_id=1, source_target_pairs={{16,0},{32,16},{48,32},{64,48},{80,64},{96,80},{112,96},{128,112},... | collective-permute-start | bytes 3145736 | tf_op jit(solution)/shard_map/ppermute | solution.py:409
  19.5 25.5 %copy-start.3 = (s32[64]{0:T(128)}, s32[64]{0:T(128)S(1)}, u32[]{:S(2)}) copy-start(s32[64]{0:T(128)S(1)} %subtract_bitcast_fusion.col_ref) | copy-start | bytes 772
  45.0 8.3 %copy-start.7 = (s32[64]{0:T(128)S(1)}, s32[64]{0:T(128)}, u32[]{:S(2)}) copy-start(s32[64]{0:T(128)} %param.10) | copy-start | bytes 772
  45.0 8.8 %copy-start.4 = (bf16[1024,1024]{1,0:T(8,128)(2,1)S(1)}, bf16[1024,1024]{1,0:T(8,128)(2,1)}, u32[]{:S(2)}) copy-start(bf16[1024,1024]{1,0:T(8,128)(2,1)} %w_self.1) | copy-start | bytes 6291460
  45.1 33.8 %all-to-all-start.1 = ((bf16[16,64,512]{2,1,0:T(8,128)(2,1)}), bf16[16,64,512]{2,1,0:T(8,128)(2,1)S(1)}, u32[]{:S(2)}, u32[]{:S(2)}) async-start(bf16[16,64,512]{2,1,0:T(8,128)(2,1)} %shard_map.95), calls=%async_computation.1 | async-start | bytes 2097152 | tf_op jit(solution)/shard_map/all_to_all | solution.py:413
  78.8 1.0 copy-start.5
  88.6 8.7 %copy-start.2 = (bf16[1024,512]{1,0:T(8,128)(2,1)S(1)}, bf16[1024,512]{1,0:T(8,128)(2,1)}, u32[]{:S(2)}) copy-start(bf16[1024,512]{1,0:T(8,128)(2,1)} %get-tuple-element.41.kept_ref) | copy-start | bytes 3145732
  88.6 31.7 %all-to-all-start.2 = ((bf16[16,64,512]{2,1,0:T(8,128)(2,1)}), bf16[16,64,512]{2,1,0:T(8,128)(2,1)}, u32[]{:S(2)}, u32[]{:S(2)}) async-start(bf16[16,64,512]{2,1,0:T(8,128)(2,1)} %bitcast.35), calls=%async_computation.2 | async-start | bytes 2097152 | tf_op jit(solution)/shard_map/all_to_all | solution.py:413
  93.6 3.7 %collective-permute-start.2 = (bf16[1024,512]{1,0:T(8,128)(2,1)}, bf16[1024,512]{1,0:T(8,128)(2,1)S(1)}, u32[]{:S(2)}, u32[]{:S(2)}) collective-permute-start(bf16[1024,512]{1,0:T(8,128)(2,1)} %get-tuple-element.42), channel_id=1, source_target_pairs={{0,1},{1,0},{2,3},{3,2},{4,5},{5,4},{6,7},{7,6},{8,9},{9,8},{10,11... | collective-permute-start | bytes 3145736 | tf_op jit(solution)/shard_map/ppermute | solution.py:430
  97.5 11.5 %collective-permute-start.3 = (bf16[256,512]{1,0:T(8,128)(2,1)S(1)}, bf16[256,512]{1,0:T(8,128)(2,1)S(1)}, u32[]{:S(2)}, u32[]{:S(2)}) collective-permute-start(bf16[256,512]{1,0:T(8,128)(2,1)S(1)} %get-tuple-element.44), channel_id=1, source_target_pairs={{0,16},{16,32},{32,48},{48,0},{64,80},{80,96},{96,112},{112,64},{1... | collective-permute-start | bytes 786440 | tf_op jit(solution)/shard_map/ppermute | solution.py:423
  99.1 16.7 %collective-permute-start.4 = (bf16[256,512]{1,0:T(8,128)(2,1)S(1)}, bf16[256,512]{1,0:T(8,128)(2,1)S(1)}, u32[]{:S(2)}, u32[]{:S(2)}) collective-permute-start(bf16[256,512]{1,0:T(8,128)(2,1)S(1)} %get-tuple-element.45), channel_id=1, source_target_pairs={{0,32},{16,48},{32,0},{48,16},{64,96},{80,112},{96,64},{112,80},{1... | collective-permute-start | bytes 786440 | tf_op jit(solution)/shard_map/ppermute | solution.py:423
  103.7 12.2 %collective-permute-start.5 = (bf16[256,512]{1,0:T(8,128)(2,1)S(1)}, bf16[256,512]{1,0:T(8,128)(2,1)S(1)}, u32[]{:S(2)}, u32[]{:S(2)}) collective-permute-start(bf16[256,512]{1,0:T(8,128)(2,1)S(1)} %get-tuple-element.46), channel_id=1, source_target_pairs={{0,48},{16,0},{32,16},{48,32},{64,112},{80,64},{96,80},{112,96},{1... | collective-permute-start | bytes 786440 | tf_op jit(solution)/shard_map/ppermute | solution.py:423
  115.9 8.6 %collective-permute-start.6 = (bf16[64,512]{1,0:T(8,128)(2,1)S(1)}, bf16[64,512]{1,0:T(8,128)(2,1)S(1)}, u32[]{:S(2)}, u32[]{:S(2)}) collective-permute-start(bf16[64,512]{1,0:T(8,128)(2,1)S(1)} %get-tuple-element.56), channel_id=1, source_target_pairs={{0,64},{16,80},{32,96},{48,112},{64,128},{80,144},{96,160},{112,17... | collective-permute-start | bytes 196616 | tf_op jit(solution)/shard_map/ppermute | solution.py:423
  117.4 7.2 %collective-permute-start.7 = (bf16[64,512]{1,0:T(8,128)(2,1)S(1)}, bf16[64,512]{1,0:T(8,128)(2,1)S(1)}, u32[]{:S(2)}, u32[]{:S(2)}) collective-permute-start(bf16[64,512]{1,0:T(8,128)(2,1)S(1)} %get-tuple-element.57), channel_id=1, source_target_pairs={{0,128},{16,144},{32,160},{48,176},{64,192},{80,208},{96,224},{112... | collective-permute-start | bytes 196616 | tf_op jit(solution)/shard_map/ppermute | solution.py:423
  118.8 5.8 %collective-permute-start.8 = (bf16[64,512]{1,0:T(8,128)(2,1)S(1)}, bf16[64,512]{1,0:T(8,128)(2,1)S(1)}, u32[]{:S(2)}, u32[]{:S(2)}) collective-permute-start(bf16[64,512]{1,0:T(8,128)(2,1)S(1)} %get-tuple-element.58), channel_id=1, source_target_pairs={{0,192},{16,208},{32,224},{48,240},{64,0},{80,16},{96,32},{112,48}... | collective-permute-start | bytes 196616 | tf_op jit(solution)/shard_map/ppermute | solution.py:423
  124.7 37.5 %copy-start.1 = (f32[64,64,128]{2,1,0:T(8,128)S(1)}, f32[64,64,128]{2,1,0:T(8,128)}, u32[]{:S(2)}) copy-start(f32[64,64,128]{2,1,0:T(8,128)} %get-tuple-element.40.spread_ref) | copy-start | bytes 6291460
  125.5 34.9 %all-to-all-start.3 = ((bf16[16,72,512]{2,1,0:T(8,128)(2,1)}), bf16[16,72,512]{2,1,0:T(8,128)(2,1)S(1)}, u32[]{:S(2)}, u32[]{:S(2)}) async-start(bf16[16,72,512]{2,1,0:T(8,128)(2,1)} %maximum_dynamic-update-slice_fusion), calls=%async_computation.3 | async-start | bytes 2359296 | tf_op jit(solution)/shard_map/all_to_all | solution.py:413
  130.9 32.1 %collective-permute-start.10 = (bf16[64,64,128]{2,1,0:T(8,128)(2,1)}, bf16[64,64,128]{2,1,0:T(8,128)(2,1)}, u32[]{:S(2)}, u32[]{:S(2)}) collective-permute-start(bf16[64,64,128]{2,1,0:T(8,128)(2,1)} %get-tuple-element.64), channel_id=1, source_target_pairs={{16,0},{32,16},{48,32},{64,48},{80,64},{96,80},{112,96},{128,112},... | collective-permute-start | bytes 3145736 | tf_op jit(solution)/shard_map/ppermute | solution.py:409
  137.0 29.5 %collective-permute-start.9 = (bf16[64,64,128]{2,1,0:T(8,128)(2,1)}, bf16[64,64,128]{2,1,0:T(8,128)(2,1)}, u32[]{:S(2)}, u32[]{:S(2)}) collective-permute-start(bf16[64,64,128]{2,1,0:T(8,128)(2,1)} %get-tuple-element.63), channel_id=1, source_target_pairs={{0,16},{16,32},{32,48},{48,64},{64,80},{80,96},{96,112},{112,128},... | collective-permute-start | bytes 3145736 | tf_op jit(solution)/shard_map/ppermute | solution.py:409

commit v12 on v11

--- a/solution.py
+++ b/solution.py
@@ -359,12 +359,24 @@
     )(me[None], *parts)
 
 
-def base_kernel(spread_ref, own_ref, out_ref):
+def base_kernel(spread_ref, own_ref, out_ref, weight_ref):
     rows, tile = spread_ref.shape[1:]
-    per = own_ref.shape[2] // tile
+    width = own_ref.shape[2]
+    per = width // tile
+    count = weight_ref.shape[0]
     for b in range(spread_ref.shape[0]):
         part = own_ref[b // per, :rows, (b % per) * tile : (b % per + 1) * tile]
         out_ref[b] = spread_ref[b] + part.astype(F32)
+
+    @pl.when(pl.program_id(0) == 0)
+    def _():
+        weight_ref[...] = jnp.zeros_like(weight_ref)
+
+    for core in range(CORES):
+        here = slice(core * width, (core + 1) * width)
+        for group in range(core, own_ref.shape[0], CORES):
+            terms = own_ref[group, rows:, :].astype(F32)
+            weight_ref[:, here] += terms[:count] + terms[count:]
 
 
 def based(spread, own):
@@ -372,34 +384,68 @@
     blocks, rows, tile = spread.shape
     steps = 4
     part = pl.BlockSpec((blocks // steps, rows, tile), lambda g: (g, 0, 0))
+    weight = ((high - rows) // 2, CORES * width)
     return pl.pallas_call(
         base_kernel,
         grid=(steps,),
         in_specs=[part, pl.BlockSpec((groups // steps, high, width), lambda g: (g, 0, 0))],
-        out_specs=part,
-        out_shape=jax.ShapeDtypeStruct(spread.shape, F32),
+        out_specs=[part, pl.BlockSpec(weight, lambda g: (0, 0))],
+        out_shape=[
+            jax.ShapeDtypeStruct(spread.shape, F32),
+            jax.ShapeDtypeStruct(weight, F32),
+        ],
         compiler_params=params(FINAL_MIB),
     )(spread, own)
 
 
-def final_kernel(base_ref, before_ref, after_ref, out_ref):
-    tile = base_ref.shape[2]
-    for b in range(base_ref.shape[0]):
-        total = base_ref[b] + before_ref[b].astype(F32) + after_ref[b].astype(F32)
-        out_ref[:, b * tile : (b + 1) * tile] = total.astype(BF16)
+def final_kernel(
+    base_ref, before_hbm, after_hbm, out_hbm, before_ref, after_ref, out_ref, in_sems, out_sems
+):
+    blocks, _, tile = base_ref.shape
+    steps = out_sems.shape[0]
+    each = blocks // steps
+    loads, stores = [], []
+    for i in range(steps):
+        part = slice(i * each, (i + 1) * each)
+        columns = slice(i * each * tile, (i + 1) * each * tile)
+        loads.append(
+            [
+                pltpu.make_async_copy(before_hbm.at[part], before_ref.at[part], in_sems.at[0, i]),
+                pltpu.make_async_copy(after_hbm.at[part], after_ref.at[part], in_sems.at[1, i]),
+            ]
+        )
+        stores.append(
+            pltpu.make_async_copy(out_ref.at[:, columns], out_hbm.at[:, columns], out_sems.at[i])
+        )
+        for copy in loads[i]:
+            copy.start()
+    for i in range(steps):
+        for copy in loads[i]:
+            copy.wait()
+        for b in range(i * each, (i + 1) * each):
+            total = base_ref[b] + before_ref[b].astype(F32) + after_ref[b].astype(F32)
+            out_ref[:, b * tile : (b + 1) * tile] = total.astype(BF16)
+        stores[i].start()
+    for copy in stores:
+        copy.wait()
 
 
 def finish(base, before, after):
     blocks, rows, tile = base.shape
     steps = 4
-    part = pl.BlockSpec((blocks // steps, rows, tile), lambda g: (g, 0, 0))
     return pl.pallas_call(
         final_kernel,
-        grid=(steps,),
-        in_specs=[part, part, part],
-        out_specs=pl.BlockSpec((rows, blocks * tile // steps), lambda g: (0, g)),
+        in_specs=[VMEM, ANYWHERE, ANYWHERE],
+        out_specs=ANYWHERE,
         out_shape=jax.ShapeDtypeStruct((rows, blocks * tile), BF16),
-        compiler_params=params(FINAL_MIB),
+        scratch_shapes=[
+            pltpu.VMEM(before.shape, BF16),
+            pltpu.VMEM(after.shape, BF16),
+            pltpu.VMEM((rows, blocks * tile), BF16),
+            pltpu.SemaphoreType.DMA((2, steps)),
+            pltpu.SemaphoreType.DMA((steps,)),
+        ],
+        compiler_params=whole_params(FINAL_MIB),
     )(base, before, after)
 
 
@@ -442,13 +488,6 @@
     low = (total - high.astype(F32)).astype(BF16)
     rows = jnp.concatenate([high, low], axis=1)
     return lax.dynamic_update_slice(own_rows, rows, (0, own_rows.shape[1] - EXTRA, 0))
-
-
-def weight_total(rows):
-    groups, count, width = rows.shape
-    rows = rows.astype(F32).reshape(groups // CORES, CORES, 2, count // 2, width)
-    total = jnp.sum(rows, axis=(0, 2))
-    return jnp.concatenate([total[i] for i in range(CORES)], axis=1)
 
 
 def paired(tiles):
@@ -493,8 +532,8 @@
     own_cols = exchange(weight_rows(sent, kept, groups, own_rows, spread), "feat")
     from_after = shifted(to_before, "node", -1)
     from_before = shifted(to_after, "node", 1)
-    grad_w_neigh = weight_total(own_cols[:, feat_dev:])
-    grad_features = finish(based(spread, own_cols), from_before, from_after)
+    base, grad_w_neigh = based(spread, own_cols)
+    grad_features = finish(base, from_before, from_after)
     return (hidden, grad_features, grad_w_neigh)
 
 

time: 172 us -> 170 us (0.988)
  waiting for transfers between devices: 69.9 us -> 71.8 us
    ppermute x4, waiting for transfers between devices: 26 us -> 27.9 us  [shifted(): lax.ppermute(value, axis, [(source, source + steps) for source in range(f...]
  transfers between devices with their start and end apart: 15 -> 15, of which waited for: 9 -> 9; matrix products, arithmetic and copies ran while one was open for 7% -> 6% of each run, Pallas kernels for 10% -> 10%
where the time goes in v12:
time: 170 us; the launch traced here: 169 us
  waiting for transfers between devices  71.8 us (42%)
  starting transfers between devices  53 us (31%)
  Pallas kernels  31.1 us (18%)
  local copies, waits for them, and re-layouts  10.2 us (6%)
  other arithmetic  1.91 us (1%)
    all_to_all x4, waiting for transfers between devices, exchange(): return lax.all_to_all(value, axis, split_axis=0, concat_axis=0, tiled=True)  34.1 us
    ppermute x4, waiting for transfers between devices, shifted(): lax.ppermute(value, axis, [(source, source + steps) for source in range(f...  27.9 us
    all_to_all x4, starting transfers between devices, exchange(): return lax.all_to_all(value, axis, split_axis=0, concat_axis=0, tiled=True)  26.2 us
    ppermute x4, starting transfers between devices, shifted(): lax.ppermute(value, axis, [(source, source + steps) for source in range(f...  15.9 us
    ppermute x6, starting transfers between devices, sent_round(): lax.ppermute(piece, axis, [(i, partner(i, step + 1)) for i in range(count)])  9.81 us
    pallas_call x1, Pallas kernels, dense(): pl.pallas_call(functools.partial(dense_kernel, chunk), in_specs=[SMEM] +...  8.78 us
    unnamed x20, local copies, waits for them, and re-layouts  7.76 us
    ppermute x6, waiting for transfers between devices, sent_round(): lax.ppermute(piece, axis, [(i, partner(i, step + 1)) for i in range(count)])  7.29 us
  transfers between devices with their start and end apart: 15, of which 9 were waited for; matrix products, arithmetic and copies ran while one was open for 6% of the time, Pallas kernels for 10%

profile of v12, /device:TPU:2, one launch (start us, length us, event | category | flops | bytes accessed | tf_op | source)
XLA Modules:
  0.0 169.1 jit_solution(7359207516222496243)
XLA Ops:
  0.6 2.2 %shard_map.94 = bf16[16,64,512]{2,1,0:T(8,128)(2,1)} custom-call(bf16[64,8192]{1,0:T(8,128)(2,1)} %own.1), custom_call_target="tpu_custom_call" | custom-call | tf_op jit(solution)/shard_map/pallas_call | solution.py:61
  2.9 8.6 %all-to-all-start = ((bf16[16,64,512]{2,1,0:T(8,128)(2,1)}), bf16[16,64,512]{2,1,0:T(8,128)(2,1)}, u32[]{:S(2)}, u32[]{:S(2)}) async-start(bf16[16,64,512]{2,1,0:T(8,128)(2,1)} %shard_map.94), calls=%async_computation | async-start | bytes 2097152 | tf_op jit(solution)/shard_map/all_to_all | solution.py:459
  11.5 3.5 %collective-permute-start = (bf16[64,8192]{1,0:T(8,128)(2,1)S(1)}, bf16[64,8192]{1,0:T(8,128)(2,1)S(1)}, u32[]{:S(2)}, u32[]{:S(2)}) collective-permute-start(bf16[64,8192]{1,0:T(8,128)(2,1)S(1)} %copy-done), channel_id=1, source_target_pairs={{0,16},{16,32},{32,48},{48,64},{64,80},{80,96},{96,112},{112,128},... | collective-permute-start | bytes 3145736 | tf_op jit(solution)/shard_map/ppermute | solution.py:455
  15.0 4.5 %collective-permute-start.1 = (bf16[64,8192]{1,0:T(8,128)(2,1)S(1)}, bf16[64,8192]{1,0:T(8,128)(2,1)S(1)}, u32[]{:S(2)}, u32[]{:S(2)}) collective-permute-start(bf16[64,8192]{1,0:T(8,128)(2,1)S(1)} %copy-done), channel_id=1, source_target_pairs={{16,0},{32,16},{48,32},{64,48},{80,64},{96,80},{112,96},{128,112},... | collective-permute-start | bytes 3145736 | tf_op jit(solution)/shard_map/ppermute | solution.py:455
  19.6 21.4 %collective-permute-done.before = bf16[64,8192]{1,0:T(8,128)(2,1)S(1)} collective-permute-done((bf16[64,8192]{1,0:T(8,128)(2,1)S(1)}, bf16[64,8192]{1,0:T(8,128)(2,1)S(1)}, u32[]{:S(2)}, u32[]{:S(2)}) %collective-permute-start) | collective-permute-done | bytes 1048608 | tf_op jit(solution)/shard_map/ppermute | solution.py:455
  41.0 1.2 collective-permute-done.1.after
  42.2 2.9 %shard_map.95 = bf16[16,64,512]{2,1,0:T(8,128)(2,1)} custom-call(s32[64]{0:T(128)S(1)} %subtract_bitcast_fusion.col_ref, bf16[64,8192]{1,0:T(8,128)(2,1)S(1)} %collective-permute-done.before, bf16[64,8192]{1,0:T(8,128)(2,1)S(1)} %copy-done, bf16[64,8192]{1,0:T(8,128)(2,1)S(1)} %collective-permute-done.1.after), custom_call_target="tpu_custom_call" | custom-call | bytes 8388608 | tf_op jit(solution)/shard_map/pallas_call | solution.py:105
  45.1 7.1 %all-to-all-start.1 = ((bf16[16,64,512]{2,1,0:T(8,128)(2,1)}), bf16[16,64,512]{2,1,0:T(8,128)(2,1)S(1)}, u32[]{:S(2)}, u32[]{:S(2)}) async-start(bf16[16,64,512]{2,1,0:T(8,128)(2,1)} %shard_map.95), calls=%async_computation.1 | async-start | bytes 2097152 | tf_op jit(solution)/shard_map/all_to_all | solution.py:459
  52.2 1.0 constant_dynamic-slice_fusion
  53.9 2.6 %copy.14 = bf16[1024,1024]{0,1:T(8,128)(2,1)} copy(bf16[1024,1024]{1,0:T(8,128)(2,1)S(1)} %copy-done.4) | data formatting | bytes 4194304 | tf_op args[4]
  56.4 3.9 %copy.15 = bf16[1024,1024]{0,1:T(8,128)(2,1)} copy(bf16[1024,1024]{1,0:T(8,128)(2,1)} %refs_5_.1) | data formatting | bytes 4194304 | tf_op args[5]
  61.4 1.0 copy.21.refs_1_
  62.4 4.5 %shard_map.96.refs_6_ = f32[1024,512]{1,0:T(8,128)} custom-call(bf16[1024,1024]{1,0:T(8,128)(2,1)} %w_self.1, bf16[1024,512]{1,0:T(8,128)(2,1)} %bitcast.1.x_ref.refs_3_), custom_call_target="tpu_custom_call" | custom-call | flops 1073741824 | bytes 5242880 | tf_op jit(solution)/shard_map/pallas_call | solution.py:191
  66.9 11.9 %all-to-all-done.1 = bf16[16,64,512]{2,1,0:T(8,128)(2,1)S(1)} async-done(((bf16[16,64,512]{2,1,0:T(8,128)(2,1)}), bf16[16,64,512]{2,1,0:T(8,128)(2,1)S(1)}, u32[]{:S(2)}, u32[]{:S(2)}) %all-to-all-start.1) | async-done | bytes 1048608 | tf_op jit(solution)/shard_map/all_to_all | solution.py:459
  78.8 1.0 copy-done.5
  79.8 8.8 %shard_map.97 = (bf16[1024,512]{1,0:T(8,128)(2,1)}, bf16[1024,512]{1,0:T(8,128)(2,1)}, bf16[1024,512]{1,0:T(8,128)(2,1)}, bf16[1024,512]{1,0:T(8,128)(2,1)}, bf1...) custom-call(s32[1]{0:T(128)} %bitcast.refs_0_, ...), custom_call_target="tpu_custom_call" | custom-call | flops 2147483648 | bytes 16777216 | tf_op jit(solution)/shard_map/pallas_call | solution.py:266
  88.6 5.0 %all-to-all-start.2 = ((bf16[16,64,512]{2,1,0:T(8,128)(2,1)}), bf16[16,64,512]{2,1,0:T(8,128)(2,1)}, u32[]{:S(2)}, u32[]{:S(2)}) async-start(bf16[16,64,512]{2,1,0:T(8,128)(2,1)} %bitcast.31), calls=%async_computation.2 | async-start | bytes 2097152 | tf_op jit(solution)/shard_map/all_to_all | solution.py:459
  93.6 1.2 collective-permute-start.2
  94.7 2.5 %collective-permute-done.2.other_ref = bf16[1024,512]{1,0:T(8,128)(2,1)S(1)} collective-permute-done((bf16[1024,512]{1,0:T(8,128)(2,1)}, bf16[1024,512]{1,0:T(8,128)(2,1)S(1)}, u32[]{:S(2)}, u32[]{:S(2)}) %collective-permute-start.2) | collective-permute-done | bytes 1048608 | tf_op jit(solution)/shard_map/ppermute | solution.py:476
  97.5 1.6 collective-permute-start.3
  99.1 4.6 %collective-permute-start.4 = (bf16[256,512]{1,0:T(8,128)(2,1)S(1)}, bf16[256,512]{1,0:T(8,128)(2,1)S(1)}, u32[]{:S(2)}, u32[]{:S(2)}) collective-permute-start(bf16[256,512]{1,0:T(8,128)(2,1)S(1)} %get-tuple-element.47), channel_id=1, source_target_pairs={{0,32},{16,48},{32,0},{48,16},{64,96},{80,112},{96,64},{112,80},{1... | collective-permute-start | bytes 786440 | tf_op jit(solution)/shard_map/ppermute | solution.py:469
  103.7 4.9 %shard_map.100 = bf16[16,72,512]{2,1,0:T(8,128)(2,1)} custom-call(bf16[1024,1024]{1,0:T(8,128)(2,1)} %bitcast.28, bf16[1024,512]{1,0:T(8,128)(2,1)} %get-tuple-element.50.dpre, bf16[1024,512]{1,0:T(8,128)(2,1)} %get-tuple-element.51.dagg_ref, bf16[2,2,256,256]{3,2,1,0:T(8,128)(2,1)} %get-tuple-element.37.refs_2_.turned), custom_call_target="tpu_custom_call" | custom-call | flops 1073741824 | bytes 5242880 | tf_op jit(solution)/shard_map/pallas_call | solution.py:300
  109.0 6.8 %collective-permute-done.4.refs_2_ = bf16[256,512]{1,0:T(8,128)(2,1)S(1)} collective-permute-done((bf16[256,512]{1,0:T(8,128)(2,1)S(1)}, bf16[256,512]{1,0:T(8,128)(2,1)S(1)}, u32[]{:S(2)}, u32[]{:S(2)}) %collective-permute-start.4) | collective-permute-done | bytes 262176 | tf_op jit(solution)/shard_map/ppermute | solution.py:469
  115.9 1.5 collective-permute-start.6
  117.4 1.4 collective-permute-start.7
  120.3 4.2 %shard_map.98 = (bf16[64,64,128]{2,1,0:T(8,128)(2,1)}, f32[64,64,128]{2,1,0:T(8,128)}, bf16[64,64,128]{2,1,0:T(8,128)(2,1)}) custom-call(s32[64]{0:T(128)} %copy-done.3, bf16[16,64,512]{2,1,0:T(8,128)(2,1)} %all-to-all-done.2.parts_hbm), custom_call_target="tpu_custom_call" | custom-call | bytes 8388608 | tf_op jit(solution)/shard_map/pallas_call | solution.py:161
  125.5 5.4 %all-to-all-start.3 = ((bf16[16,72,512]{2,1,0:T(8,128)(2,1)}), bf16[16,72,512]{2,1,0:T(8,128)(2,1)S(1)}, u32[]{:S(2)}, u32[]{:S(2)}) async-start(bf16[16,72,512]{2,1,0:T(8,128)(2,1)} %maximum_dynamic-update-slice_fusion), calls=%async_computation.3 | async-start | bytes 2359296 | tf_op jit(solution)/shard_map/all_to_all | solution.py:459
  130.9 6.0 %collective-permute-start.10 = (bf16[64,64,128]{2,1,0:T(8,128)(2,1)}, bf16[64,64,128]{2,1,0:T(8,128)(2,1)}, u32[]{:S(2)}, u32[]{:S(2)}) collective-permute-start(bf16[64,64,128]{2,1,0:T(8,128)(2,1)} %get-tuple-element.67), channel_id=1, source_target_pairs={{16,0},{32,16},{48,32},{64,48},{80,64},{96,80},{112,96},{128,112},... | collective-permute-start | bytes 3145736 | tf_op jit(solution)/shard_map/ppermute | solution.py:455
  137.0 1.9 %collective-permute-start.9 = (bf16[64,64,128]{2,1,0:T(8,128)(2,1)}, bf16[64,64,128]{2,1,0:T(8,128)(2,1)}, u32[]{:S(2)}, u32[]{:S(2)}) collective-permute-start(bf16[64,64,128]{2,1,0:T(8,128)(2,1)} %get-tuple-element.66), channel_id=1, source_target_pairs={{0,16},{16,32},{32,48},{48,64},{64,80},{80,96},{96,112},{112,128},... | collective-permute-start | bytes 3145736 | tf_op jit(solution)/shard_map/ppermute | solution.py:455
  138.9 21.5 %all-to-all-done.3.own_ref = bf16[16,72,512]{2,1,0:T(8,128)(2,1)S(1)} async-done(((bf16[16,72,512]{2,1,0:T(8,128)(2,1)}), bf16[16,72,512]{2,1,0:T(8,128)(2,1)S(1)}, u32[]{:S(2)}, u32[]{:S(2)}) %all-to-all-start.3) | async-done | bytes 1179680 | tf_op jit(solution)/shard_map/all_to_all | solution.py:459
  161.2 5.3 %collective-permute-done.9.before_hbm = bf16[64,64,128]{2,1,0:T(8,128)(2,1)} collective-permute-done((bf16[64,64,128]{2,1,0:T(8,128)(2,1)}, bf16[64,64,128]{2,1,0:T(8,128)(2,1)}, u32[]{:S(2)}, u32[]{:S(2)}) %collective-permute-start.9) | collective-permute-done | bytes 1048608 | tf_op jit(solution)/shard_map/ppermute | solution.py:455
  166.5 2.4 %shard_map.103 = bf16[64,8192]{1,0:T(8,128)(2,1)} custom-call(f32[64,64,128]{2,1,0:T(8,128)S(1)} %get-tuple-element.65.base_ref, bf16[64,64,128]{2,1,0:T(8,128)(2,1)} %collective-permute-done.9.before_hbm, bf16[64,64,128]{2,1,0:T(8,128)(2,1)} %collective-permute-done.10.after_hbm), custom_call_target="tpu_custom_call" | custom-call | tf_op jit(solution)/shard_map/pallas_call | solution.py:436
  (44 shorter events, 5.8 us)
Async XLA Ops:
  0.6 10.9 %copy-start = (bf16[64,8192]{1,0:T(8,128)(2,1)S(1)}, bf16[64,8192]{1,0:T(8,128)(2,1)}, u32[]{:S(2)}) copy-start(bf16[64,8192]{1,0:T(8,128)(2,1)} %own.1) | copy-start | bytes 3145732
  0.6 18.9 %copy-start.6 = (s32[64,2]{0,1:T(2,128)S(1)}, s32[64,2]{0,1:T(2,128)}, u32[]{:S(2)}) copy-start(s32[64,2]{0,1:T(2,128)} %param.9) | copy-start | bytes 1540
  2.9 42.1 %all-to-all-start = ((bf16[16,64,512]{2,1,0:T(8,128)(2,1)}), bf16[16,64,512]{2,1,0:T(8,128)(2,1)}, u32[]{:S(2)}, u32[]{:S(2)}) async-start(bf16[16,64,512]{2,1,0:T(8,128)(2,1)} %shard_map.94), calls=%async_computation | async-start | bytes 2097152 | tf_op jit(solution)/shard_map/all_to_all | solution.py:459
  11.5 29.4 %collective-permute-start = (bf16[64,8192]{1,0:T(8,128)(2,1)S(1)}, bf16[64,8192]{1,0:T(8,128)(2,1)S(1)}, u32[]{:S(2)}, u32[]{:S(2)}) collective-permute-start(bf16[64,8192]{1,0:T(8,128)(2,1)S(1)} %copy-done), channel_id=1, source_target_pairs={{0,16},{16,32},{32,48},{48,64},{64,80},{80,96},{96,112},{112,128},... | collective-permute-start | bytes 3145736 | tf_op jit(solution)/shard_map/ppermute | solution.py:455
  15.0 27.1 %collective-permute-start.1 = (bf16[64,8192]{1,0:T(8,128)(2,1)S(1)}, bf16[64,8192]{1,0:T(8,128)(2,1)S(1)}, u32[]{:S(2)}, u32[]{:S(2)}) collective-permute-start(bf16[64,8192]{1,0:T(8,128)(2,1)S(1)} %copy-done), channel_id=1, source_target_pairs={{16,0},{32,16},{48,32},{64,48},{80,64},{96,80},{112,96},{128,112},... | collective-permute-start | bytes 3145736 | tf_op jit(solution)/shard_map/ppermute | solution.py:455
  19.5 25.5 %copy-start.3 = (s32[64]{0:T(128)}, s32[64]{0:T(128)S(1)}, u32[]{:S(2)}) copy-start(s32[64]{0:T(128)S(1)} %subtract_bitcast_fusion.col_ref) | copy-start | bytes 772
  45.0 8.3 %copy-start.7 = (s32[64]{0:T(128)S(1)}, s32[64]{0:T(128)}, u32[]{:S(2)}) copy-start(s32[64]{0:T(128)} %param.10) | copy-start | bytes 772
  45.0 8.8 %copy-start.4 = (bf16[1024,1024]{1,0:T(8,128)(2,1)S(1)}, bf16[1024,1024]{1,0:T(8,128)(2,1)}, u32[]{:S(2)}) copy-start(bf16[1024,1024]{1,0:T(8,128)(2,1)} %w_self.1) | copy-start | bytes 6291460
  45.1 33.8 %all-to-all-start.1 = ((bf16[16,64,512]{2,1,0:T(8,128)(2,1)}), bf16[16,64,512]{2,1,0:T(8,128)(2,1)S(1)}, u32[]{:S(2)}, u32[]{:S(2)}) async-start(bf16[16,64,512]{2,1,0:T(8,128)(2,1)} %shard_map.95), calls=%async_computation.1 | async-start | bytes 2097152 | tf_op jit(solution)/shard_map/all_to_all | solution.py:459
  78.8 1.0 copy-start.5
  88.6 8.7 %copy-start.2 = (bf16[1024,512]{1,0:T(8,128)(2,1)S(1)}, bf16[1024,512]{1,0:T(8,128)(2,1)}, u32[]{:S(2)}) copy-start(bf16[1024,512]{1,0:T(8,128)(2,1)} %get-tuple-element.43.kept_ref) | copy-start | bytes 3145732
  88.6 31.7 %all-to-all-start.2 = ((bf16[16,64,512]{2,1,0:T(8,128)(2,1)}), bf16[16,64,512]{2,1,0:T(8,128)(2,1)}, u32[]{:S(2)}, u32[]{:S(2)}) async-start(bf16[16,64,512]{2,1,0:T(8,128)(2,1)} %bitcast.31), calls=%async_computation.2 | async-start | bytes 2097152 | tf_op jit(solution)/shard_map/all_to_all | solution.py:459
  93.6 3.7 %collective-permute-start.2 = (bf16[1024,512]{1,0:T(8,128)(2,1)}, bf16[1024,512]{1,0:T(8,128)(2,1)S(1)}, u32[]{:S(2)}, u32[]{:S(2)}) collective-permute-start(bf16[1024,512]{1,0:T(8,128)(2,1)} %get-tuple-element.44), channel_id=1, source_target_pairs={{0,1},{1,0},{2,3},{3,2},{4,5},{5,4},{6,7},{7,6},{8,9},{9,8},{10,11... | collective-permute-start | bytes 3145736 | tf_op jit(solution)/shard_map/ppermute | solution.py:476
  97.5 11.5 %collective-permute-start.3 = (bf16[256,512]{1,0:T(8,128)(2,1)S(1)}, bf16[256,512]{1,0:T(8,128)(2,1)S(1)}, u32[]{:S(2)}, u32[]{:S(2)}) collective-permute-start(bf16[256,512]{1,0:T(8,128)(2,1)S(1)} %get-tuple-element.46), channel_id=1, source_target_pairs={{0,16},{16,32},{32,48},{48,0},{64,80},{80,96},{96,112},{112,64},{1... | collective-permute-start | bytes 786440 | tf_op jit(solution)/shard_map/ppermute | solution.py:469
  99.1 16.8 %collective-permute-start.4 = (bf16[256,512]{1,0:T(8,128)(2,1)S(1)}, bf16[256,512]{1,0:T(8,128)(2,1)S(1)}, u32[]{:S(2)}, u32[]{:S(2)}) collective-permute-start(bf16[256,512]{1,0:T(8,128)(2,1)S(1)} %get-tuple-element.47), channel_id=1, source_target_pairs={{0,32},{16,48},{32,0},{48,16},{64,96},{80,112},{96,64},{112,80},{1... | collective-permute-start | bytes 786440 | tf_op jit(solution)/shard_map/ppermute | solution.py:469
  103.7 12.2 %collective-permute-start.5 = (bf16[256,512]{1,0:T(8,128)(2,1)S(1)}, bf16[256,512]{1,0:T(8,128)(2,1)S(1)}, u32[]{:S(2)}, u32[]{:S(2)}) collective-permute-start(bf16[256,512]{1,0:T(8,128)(2,1)S(1)} %get-tuple-element.48), channel_id=1, source_target_pairs={{0,48},{16,0},{32,16},{48,32},{64,112},{80,64},{96,80},{112,96},{1... | collective-permute-start | bytes 786440 | tf_op jit(solution)/shard_map/ppermute | solution.py:469
  115.9 8.6 %collective-permute-start.6 = (bf16[64,512]{1,0:T(8,128)(2,1)S(1)}, bf16[64,512]{1,0:T(8,128)(2,1)S(1)}, u32[]{:S(2)}, u32[]{:S(2)}) collective-permute-start(bf16[64,512]{1,0:T(8,128)(2,1)S(1)} %get-tuple-element.58), channel_id=1, source_target_pairs={{0,64},{16,80},{32,96},{48,112},{64,128},{80,144},{96,160},{112,17... | collective-permute-start | bytes 196616 | tf_op jit(solution)/shard_map/ppermute | solution.py:469
  117.4 7.2 %collective-permute-start.7 = (bf16[64,512]{1,0:T(8,128)(2,1)S(1)}, bf16[64,512]{1,0:T(8,128)(2,1)S(1)}, u32[]{:S(2)}, u32[]{:S(2)}) collective-permute-start(bf16[64,512]{1,0:T(8,128)(2,1)S(1)} %get-tuple-element.59), channel_id=1, source_target_pairs={{0,128},{16,144},{32,160},{48,176},{64,192},{80,208},{96,224},{112... | collective-permute-start | bytes 196616 | tf_op jit(solution)/shard_map/ppermute | solution.py:469
  118.8 5.8 %collective-permute-start.8 = (bf16[64,512]{1,0:T(8,128)(2,1)S(1)}, bf16[64,512]{1,0:T(8,128)(2,1)S(1)}, u32[]{:S(2)}, u32[]{:S(2)}) collective-permute-start(bf16[64,512]{1,0:T(8,128)(2,1)S(1)} %get-tuple-element.60), channel_id=1, source_target_pairs={{0,192},{16,208},{32,224},{48,240},{64,0},{80,16},{96,32},{112,48}... | collective-permute-start | bytes 196616 | tf_op jit(solution)/shard_map/ppermute | solution.py:469
  124.5 35.8 %copy-start.1 = (f32[64,64,128]{2,1,0:T(8,128)S(1)}, f32[64,64,128]{2,1,0:T(8,128)}, u32[]{:S(2)}) copy-start(f32[64,64,128]{2,1,0:T(8,128)} %get-tuple-element.42.spread_ref) | copy-start | bytes 6291460
  125.5 34.9 %all-to-all-start.3 = ((bf16[16,72,512]{2,1,0:T(8,128)(2,1)}), bf16[16,72,512]{2,1,0:T(8,128)(2,1)S(1)}, u32[]{:S(2)}, u32[]{:S(2)}) async-start(bf16[16,72,512]{2,1,0:T(8,128)(2,1)} %maximum_dynamic-update-slice_fusion), calls=%async_computation.3 | async-start | bytes 2359296 | tf_op jit(solution)/shard_map/all_to_all | solution.py:459
  130.9 30.3 %collective-permute-start.10 = (bf16[64,64,128]{2,1,0:T(8,128)(2,1)}, bf16[64,64,128]{2,1,0:T(8,128)(2,1)}, u32[]{:S(2)}, u32[]{:S(2)}) collective-permute-start(bf16[64,64,128]{2,1,0:T(8,128)(2,1)} %get-tuple-element.67), channel_id=1, source_target_pairs={{16,0},{32,16},{48,32},{64,48},{80,64},{96,80},{112,96},{128,112},... | collective-permute-start | bytes 3145736 | tf_op jit(solution)/shard_map/ppermute | solution.py:455
  137.0 29.5 %collective-permute-start.9 = (bf16[64,64,128]{2,1,0:T(8,128)(2,1)}, bf16[64,64,128]{2,1,0:T(8,128)(2,1)}, u32[]{:S(2)}, u32[]{:S(2)}) collective-permute-start(bf16[64,64,128]{2,1,0:T(8,128)(2,1)} %get-tuple-element.66), channel_id=1, source_target_pairs={{0,16},{16,32},{32,48},{48,64},{64,80},{80,96},{96,112},{112,128},... | collective-permute-start | bytes 3145736 | tf_op jit(solution)/shard_map/ppermute | solution.py:455

commit v13 on v12

--- a/solution.py
+++ b/solution.py
@@ -201,10 +201,10 @@
 
 
 def dense_kernel(chunk, *refs):
-    core_ref, sources, targets, held = refs[0], refs[1:9], refs[9:16], refs[16:24]
-    (agg_hbm, hidden_hbm, dpre_hbm, dagg_hbm, second_hbm, sent_hbm, kept_hbm) = targets
+    core_ref, sources, targets, held = refs[0], refs[1:9], refs[9:15], refs[15:23]
+    (hidden_hbm, dpre_hbm, dagg_hbm, second_hbm, sent_hbm, kept_hbm) = targets
     (tiles, turned, x_ref, picked, w_neigh, pre_ref, cot_ref, w_back) = held
-    (agg, hidden, dpre, dagg, second, sent, kept, in_sems, out_sems) = refs[24:]
+    (agg, hidden, dpre, dagg, second, sent, kept, in_sems, out_sems) = refs[23:]
     size = w_neigh.shape[0]
     pair = tiles.shape[-1]
     part = [slice(i, i + chunk) for i in range(0, size, chunk)]
@@ -212,7 +212,7 @@
     loads = [
         pltpu.make_async_copy(sources[k], held[k], in_sems.at[k]) for k in (0, 2, 3, 4, 5, 6, 7, 1)
     ]
-    for copy in loads:
+    for copy in loads[:6]:
         copy.start()
     stores = []
 
@@ -223,6 +223,8 @@
 
     for copy in loads[:3]:
         copy.wait()
+    for copy in loads[6:]:
+        copy.start()
     for i in range(len(part)):
         for p in range(len(here)):
             total = dot(x_ref[part[i], here[p]], tiles[0, p])
@@ -231,7 +233,6 @@
     for copy in loads[3:6]:
         copy.wait()
     for i in range(len(part)):
-        store(0, agg, agg_hbm, i)
         pre = pre_ref[part[i], :] + dot(w_neigh[part[i], :], agg[...])
         sig = 0.5 + 0.5 * jnp.tanh(0.5 * pre)
         hidden[part[i], :] = (pre * sig).astype(BF16)
@@ -266,8 +267,8 @@
     return pl.pallas_call(
         functools.partial(dense_kernel, chunk),
         in_specs=[SMEM] + [ANYWHERE] * len(args),
-        out_specs=[ANYWHERE] * 7,
-        out_shape=[out] * 5 + [jax.ShapeDtypeStruct((size, size // CORES), BF16)] * 2,
+        out_specs=[ANYWHERE] * 6,
+        out_shape=[out] * 4 + [jax.ShapeDtypeStruct((size, size // CORES), BF16)] * 2,
         scratch_shapes=[pltpu.VMEM(arg.shape, arg.dtype) for arg in args]
         + [pltpu.VMEM((size, width), BF16)] * 5
         + [pltpu.VMEM((size, size // CORES), BF16)] * 2
@@ -523,7 +524,7 @@
     )
     pre_self = self_product(w_self, x_rows)
     core = lax.rem(feat, CORES)
-    _, hidden, dpre, dagg, second, sent, kept = dense(
+    hidden, dpre, dagg, second, sent, kept = dense(
         core[None], straight, turned, x_rows, picked, w_neigh, pre_self, cotangent, neigh_back
     )
     second_cols = exchange(second.reshape(groups, feat_dev, -1), "feat")

time: 170 us -> 170 us (level)
  no operation moved by 1% of the time
where the time goes in v13:
time: 170 us; the launch traced here: 169 us
  waiting for transfers between devices  71.8 us (42%)
  starting transfers between devices  53 us (31%)
  Pallas kernels  31.1 us (18%)
  local copies, waits for them, and re-layouts  10.1 us (6%)
  other arithmetic  1.94 us (1%)
    all_to_all x4, waiting for transfers between devices, exchange(): return lax.all_to_all(value, axis, split_axis=0, concat_axis=0, tiled=True)  34.1 us
    ppermute x4, waiting for transfers between devices, shifted(): lax.ppermute(value, axis, [(source, source + steps) for source in range(f...  27.9 us
    all_to_all x4, starting transfers between devices, exchange(): return lax.all_to_all(value, axis, split_axis=0, concat_axis=0, tiled=True)  26.2 us
    ppermute x4, starting transfers between devices, shifted(): lax.ppermute(value, axis, [(source, source + steps) for source in range(f...  15.9 us
    ppermute x6, starting transfers between devices, sent_round(): lax.ppermute(piece, axis, [(i, partner(i, step + 1)) for i in range(count)])  9.79 us
    pallas_call x1, Pallas kernels, dense(): pl.pallas_call(functools.partial(dense_kernel, chunk), in_specs=[SMEM] +...  8.78 us
    unnamed x20, local copies, waits for them, and re-layouts  7.76 us
    ppermute x6, waiting for transfers between devices, sent_round(): lax.ppermute(piece, axis, [(i, partner(i, step + 1)) for i in range(count)])  7.29 us
  transfers between devices with their start and end apart: 15, of which 9 were waited for; matrix products, arithmetic and copies ran while one was open for 6% of the time, Pallas kernels for 10%

profile of v13, /device:TPU:2, one launch (start us, length us, event | category | flops | bytes accessed | tf_op | source)
XLA Modules:
  0.0 169.1 jit_solution(12319548953151338810)
XLA Ops:
  0.6 2.2 %shard_map.94 = bf16[16,64,512]{2,1,0:T(8,128)(2,1)} custom-call(bf16[64,8192]{1,0:T(8,128)(2,1)} %own.1), custom_call_target="tpu_custom_call" | custom-call | tf_op jit(solution)/shard_map/pallas_call | solution.py:61
  2.9 8.6 %all-to-all-start = ((bf16[16,64,512]{2,1,0:T(8,128)(2,1)}), bf16[16,64,512]{2,1,0:T(8,128)(2,1)}, u32[]{:S(2)}, u32[]{:S(2)}) async-start(bf16[16,64,512]{2,1,0:T(8,128)(2,1)} %shard_map.94), calls=%async_computation | async-start | bytes 2097152 | tf_op jit(solution)/shard_map/all_to_all | solution.py:460
  11.5 3.5 %collective-permute-start = (bf16[64,8192]{1,0:T(8,128)(2,1)S(1)}, bf16[64,8192]{1,0:T(8,128)(2,1)S(1)}, u32[]{:S(2)}, u32[]{:S(2)}) collective-permute-start(bf16[64,8192]{1,0:T(8,128)(2,1)S(1)} %copy-done), channel_id=1, source_target_pairs={{0,16},{16,32},{32,48},{48,64},{64,80},{80,96},{96,112},{112,128},... | collective-permute-start | bytes 3145736 | tf_op jit(solution)/shard_map/ppermute | solution.py:456
  15.0 4.5 %collective-permute-start.1 = (bf16[64,8192]{1,0:T(8,128)(2,1)S(1)}, bf16[64,8192]{1,0:T(8,128)(2,1)S(1)}, u32[]{:S(2)}, u32[]{:S(2)}) collective-permute-start(bf16[64,8192]{1,0:T(8,128)(2,1)S(1)} %copy-done), channel_id=1, source_target_pairs={{16,0},{32,16},{48,32},{64,48},{80,64},{96,80},{112,96},{128,112},... | collective-permute-start | bytes 3145736 | tf_op jit(solution)/shard_map/ppermute | solution.py:456
  19.6 21.4 %collective-permute-done.before = bf16[64,8192]{1,0:T(8,128)(2,1)S(1)} collective-permute-done((bf16[64,8192]{1,0:T(8,128)(2,1)S(1)}, bf16[64,8192]{1,0:T(8,128)(2,1)S(1)}, u32[]{:S(2)}, u32[]{:S(2)}) %collective-permute-start) | collective-permute-done | bytes 1048608 | tf_op jit(solution)/shard_map/ppermute | solution.py:456
  41.0 1.2 collective-permute-done.1.after
  42.2 2.9 %shard_map.95 = bf16[16,64,512]{2,1,0:T(8,128)(2,1)} custom-call(s32[64]{0:T(128)S(1)} %subtract_bitcast_fusion.col_ref, bf16[64,8192]{1,0:T(8,128)(2,1)S(1)} %collective-permute-done.before, bf16[64,8192]{1,0:T(8,128)(2,1)S(1)} %copy-done, bf16[64,8192]{1,0:T(8,128)(2,1)S(1)} %collective-permute-done.1.after), custom_call_target="tpu_custom_call" | custom-call | bytes 8388608 | tf_op jit(solution)/shard_map/pallas_call | solution.py:105
  45.1 7.1 %all-to-all-start.1 = ((bf16[16,64,512]{2,1,0:T(8,128)(2,1)}), bf16[16,64,512]{2,1,0:T(8,128)(2,1)S(1)}, u32[]{:S(2)}, u32[]{:S(2)}) async-start(bf16[16,64,512]{2,1,0:T(8,128)(2,1)} %shard_map.95), calls=%async_computation.1 | async-start | bytes 2097152 | tf_op jit(solution)/shard_map/all_to_all | solution.py:460
  52.2 1.0 constant_dynamic-slice_fusion
  53.9 2.6 %copy.14 = bf16[1024,1024]{0,1:T(8,128)(2,1)} copy(bf16[1024,1024]{1,0:T(8,128)(2,1)S(1)} %copy-done.4) | data formatting | bytes 4194304 | tf_op args[4]
  56.4 3.9 %copy.15 = bf16[1024,1024]{0,1:T(8,128)(2,1)} copy(bf16[1024,1024]{1,0:T(8,128)(2,1)} %refs_5_.1) | data formatting | bytes 4194304 | tf_op args[5]
  61.4 1.0 copy.21.refs_1_
  62.4 4.5 %shard_map.96.refs_6_ = f32[1024,512]{1,0:T(8,128)} custom-call(bf16[1024,1024]{1,0:T(8,128)(2,1)} %w_self.1, bf16[1024,512]{1,0:T(8,128)(2,1)} %bitcast.1.x_ref.refs_3_), custom_call_target="tpu_custom_call" | custom-call | flops 1073741824 | bytes 5242880 | tf_op jit(solution)/shard_map/pallas_call | solution.py:191
  66.9 11.9 %all-to-all-done.1 = bf16[16,64,512]{2,1,0:T(8,128)(2,1)S(1)} async-done(((bf16[16,64,512]{2,1,0:T(8,128)(2,1)}), bf16[16,64,512]{2,1,0:T(8,128)(2,1)S(1)}, u32[]{:S(2)}, u32[]{:S(2)}) %all-to-all-start.1) | async-done | bytes 1048608 | tf_op jit(solution)/shard_map/all_to_all | solution.py:460
  78.8 1.0 copy-done.5
  79.8 8.8 %shard_map.97 = (bf16[1024,512]{1,0:T(8,128)(2,1)}, bf16[1024,512]{1,0:T(8,128)(2,1)}, bf16[1024,512]{1,0:T(8,128)(2,1)}, bf16[1024,512]{1,0:T(8,128)(2,1)}, bf1...) custom-call(s32[1]{0:T(128)} %bitcast.refs_0_, bf16[2,2,256,256]{3,2,1,0:T(8,128)(2,1)} %copy.21.refs_1_, ...), custom_call_target="tpu_custom_call" | custom-call | flops 2147483648 | bytes 16777216 | tf_op jit(solution)/shard_map/pallas_call | solution.py:267
  88.6 5.0 %all-to-all-start.2 = ((bf16[16,64,512]{2,1,0:T(8,128)(2,1)}), bf16[16,64,512]{2,1,0:T(8,128)(2,1)}, u32[]{:S(2)}, u32[]{:S(2)}) async-start(bf16[16,64,512]{2,1,0:T(8,128)(2,1)} %bitcast.31), calls=%async_computation.2 | async-start | bytes 2097152 | tf_op jit(solution)/shard_map/all_to_all | solution.py:460
  93.6 1.2 collective-permute-start.2
  94.7 2.5 %collective-permute-done.2.other_ref = bf16[1024,512]{1,0:T(8,128)(2,1)S(1)} collective-permute-done((bf16[1024,512]{1,0:T(8,128)(2,1)}, bf16[1024,512]{1,0:T(8,128)(2,1)S(1)}, u32[]{:S(2)}, u32[]{:S(2)}) %collective-permute-start.2) | collective-permute-done | bytes 1048608 | tf_op jit(solution)/shard_map/ppermute | solution.py:477
  97.5 1.6 collective-permute-start.3
  99.1 4.6 %collective-permute-start.4 = (bf16[256,512]{1,0:T(8,128)(2,1)S(1)}, bf16[256,512]{1,0:T(8,128)(2,1)S(1)}, u32[]{:S(2)}, u32[]{:S(2)}) collective-permute-start(bf16[256,512]{1,0:T(8,128)(2,1)S(1)} %get-tuple-element.47), channel_id=1, source_target_pairs={{0,32},{16,48},{32,0},{48,16},{64,96},{80,112},{96,64},{112,80},{1... | collective-permute-start | bytes 786440 | tf_op jit(solution)/shard_map/ppermute | solution.py:470
  103.7 4.9 %shard_map.100 = bf16[16,72,512]{2,1,0:T(8,128)(2,1)} custom-call(bf16[1024,1024]{1,0:T(8,128)(2,1)} %bitcast.28, bf16[1024,512]{1,0:T(8,128)(2,1)} %get-tuple-element.50.dpre, bf16[1024,512]{1,0:T(8,128)(2,1)} %get-tuple-element.51.dagg_ref, bf16[2,2,256,256]{3,2,1,0:T(8,128)(2,1)} %get-tuple-element.37.refs_2_.turned), custom_call_target="tpu_custom_call" | custom-call | flops 1073741824 | bytes 5242880 | tf_op jit(solution)/shard_map/pallas_call | solution.py:301
  109.0 6.8 %collective-permute-done.4.refs_2_ = bf16[256,512]{1,0:T(8,128)(2,1)S(1)} collective-permute-done((bf16[256,512]{1,0:T(8,128)(2,1)S(1)}, bf16[256,512]{1,0:T(8,128)(2,1)S(1)}, u32[]{:S(2)}, u32[]{:S(2)}) %collective-permute-start.4) | collective-permute-done | bytes 262176 | tf_op jit(solution)/shard_map/ppermute | solution.py:470
  115.9 1.5 collective-permute-start.6
  117.4 1.4 collective-permute-start.7
  120.3 4.2 %shard_map.98 = (bf16[64,64,128]{2,1,0:T(8,128)(2,1)}, f32[64,64,128]{2,1,0:T(8,128)}, bf16[64,64,128]{2,1,0:T(8,128)(2,1)}) custom-call(s32[64]{0:T(128)} %copy-done.3, bf16[16,64,512]{2,1,0:T(8,128)(2,1)} %all-to-all-done.2.parts_hbm), custom_call_target="tpu_custom_call" | custom-call | bytes 8388608 | tf_op jit(solution)/shard_map/pallas_call | solution.py:161
  125.5 5.4 %all-to-all-start.3 = ((bf16[16,72,512]{2,1,0:T(8,128)(2,1)}), bf16[16,72,512]{2,1,0:T(8,128)(2,1)S(1)}, u32[]{:S(2)}, u32[]{:S(2)}) async-start(bf16[16,72,512]{2,1,0:T(8,128)(2,1)} %maximum_dynamic-update-slice_fusion), calls=%async_computation.3 | async-start | bytes 2359296 | tf_op jit(solution)/shard_map/all_to_all | solution.py:460
  130.9 6.0 %collective-permute-start.10 = (bf16[64,64,128]{2,1,0:T(8,128)(2,1)}, bf16[64,64,128]{2,1,0:T(8,128)(2,1)}, u32[]{:S(2)}, u32[]{:S(2)}) collective-permute-start(bf16[64,64,128]{2,1,0:T(8,128)(2,1)} %get-tuple-element.67), channel_id=1, source_target_pairs={{16,0},{32,16},{48,32},{64,48},{80,64},{96,80},{112,96},{128,112},... | collective-permute-start | bytes 3145736 | tf_op jit(solution)/shard_map/ppermute | solution.py:456
  137.0 1.9 %collective-permute-start.9 = (bf16[64,64,128]{2,1,0:T(8,128)(2,1)}, bf16[64,64,128]{2,1,0:T(8,128)(2,1)}, u32[]{:S(2)}, u32[]{:S(2)}) collective-permute-start(bf16[64,64,128]{2,1,0:T(8,128)(2,1)} %get-tuple-element.66), channel_id=1, source_target_pairs={{0,16},{16,32},{32,48},{48,64},{64,80},{80,96},{96,112},{112,128},... | collective-permute-start | bytes 3145736 | tf_op jit(solution)/shard_map/ppermute | solution.py:456
  138.9 21.5 %all-to-all-done.3.own_ref = bf16[16,72,512]{2,1,0:T(8,128)(2,1)S(1)} async-done(((bf16[16,72,512]{2,1,0:T(8,128)(2,1)}), bf16[16,72,512]{2,1,0:T(8,128)(2,1)S(1)}, u32[]{:S(2)}, u32[]{:S(2)}) %all-to-all-start.3) | async-done | bytes 1179680 | tf_op jit(solution)/shard_map/all_to_all | solution.py:460
  161.2 5.3 %collective-permute-done.9.before_hbm = bf16[64,64,128]{2,1,0:T(8,128)(2,1)} collective-permute-done((bf16[64,64,128]{2,1,0:T(8,128)(2,1)}, bf16[64,64,128]{2,1,0:T(8,128)(2,1)}, u32[]{:S(2)}, u32[]{:S(2)}) %collective-permute-start.9) | collective-permute-done | bytes 1048608 | tf_op jit(solution)/shard_map/ppermute | solution.py:456
  166.5 2.4 %shard_map.103 = bf16[64,8192]{1,0:T(8,128)(2,1)} custom-call(f32[64,64,128]{2,1,0:T(8,128)S(1)} %get-tuple-element.65.base_ref, bf16[64,64,128]{2,1,0:T(8,128)(2,1)} %collective-permute-done.9.before_hbm, bf16[64,64,128]{2,1,0:T(8,128)(2,1)} %collective-permute-done.10.after_hbm), custom_call_target="tpu_custom_call" | custom-call | tf_op jit(solution)/shard_map/pallas_call | solution.py:437
  (44 shorter events, 5.8 us)
Async XLA Ops:
  0.6 10.9 %copy-start = (bf16[64,8192]{1,0:T(8,128)(2,1)S(1)}, bf16[64,8192]{1,0:T(8,128)(2,1)}, u32[]{:S(2)}) copy-start(bf16[64,8192]{1,0:T(8,128)(2,1)} %own.1) | copy-start | bytes 3145732
  0.6 18.9 %copy-start.6 = (s32[64,2]{0,1:T(2,128)S(1)}, s32[64,2]{0,1:T(2,128)}, u32[]{:S(2)}) copy-start(s32[64,2]{0,1:T(2,128)} %param.9) | copy-start | bytes 1540
  2.9 42.2 %all-to-all-start = ((bf16[16,64,512]{2,1,0:T(8,128)(2,1)}), bf16[16,64,512]{2,1,0:T(8,128)(2,1)}, u32[]{:S(2)}, u32[]{:S(2)}) async-start(bf16[16,64,512]{2,1,0:T(8,128)(2,1)} %shard_map.94), calls=%async_computation | async-start | bytes 2097152 | tf_op jit(solution)/shard_map/all_to_all | solution.py:460
  11.5 29.4 %collective-permute-start = (bf16[64,8192]{1,0:T(8,128)(2,1)S(1)}, bf16[64,8192]{1,0:T(8,128)(2,1)S(1)}, u32[]{:S(2)}, u32[]{:S(2)}) collective-permute-start(bf16[64,8192]{1,0:T(8,128)(2,1)S(1)} %copy-done), channel_id=1, source_target_pairs={{0,16},{16,32},{32,48},{48,64},{64,80},{80,96},{96,112},{112,128},... | collective-permute-start | bytes 3145736 | tf_op jit(solution)/shard_map/ppermute | solution.py:456
  15.0 27.1 %collective-permute-start.1 = (bf16[64,8192]{1,0:T(8,128)(2,1)S(1)}, bf16[64,8192]{1,0:T(8,128)(2,1)S(1)}, u32[]{:S(2)}, u32[]{:S(2)}) collective-permute-start(bf16[64,8192]{1,0:T(8,128)(2,1)S(1)} %copy-done), channel_id=1, source_target_pairs={{16,0},{32,16},{48,32},{64,48},{80,64},{96,80},{112,96},{128,112},... | collective-permute-start | bytes 3145736 | tf_op jit(solution)/shard_map/ppermute | solution.py:456
  19.5 25.5 %copy-start.3 = (s32[64]{0:T(128)}, s32[64]{0:T(128)S(1)}, u32[]{:S(2)}) copy-start(s32[64]{0:T(128)S(1)} %subtract_bitcast_fusion.col_ref) | copy-start | bytes 772
  45.0 8.3 %copy-start.7 = (s32[64]{0:T(128)S(1)}, s32[64]{0:T(128)}, u32[]{:S(2)}) copy-start(s32[64]{0:T(128)} %param.10) | copy-start | bytes 772
  45.0 8.8 %copy-start.4 = (bf16[1024,1024]{1,0:T(8,128)(2,1)S(1)}, bf16[1024,1024]{1,0:T(8,128)(2,1)}, u32[]{:S(2)}) copy-start(bf16[1024,1024]{1,0:T(8,128)(2,1)} %w_self.1) | copy-start | bytes 6291460
  45.1 33.8 %all-to-all-start.1 = ((bf16[16,64,512]{2,1,0:T(8,128)(2,1)}), bf16[16,64,512]{2,1,0:T(8,128)(2,1)S(1)}, u32[]{:S(2)}, u32[]{:S(2)}) async-start(bf16[16,64,512]{2,1,0:T(8,128)(2,1)} %shard_map.95), calls=%async_computation.1 | async-start | bytes 2097152 | tf_op jit(solution)/shard_map/all_to_all | solution.py:460
  78.8 1.0 copy-start.5
  88.6 8.7 %copy-start.2 = (bf16[1024,512]{1,0:T(8,128)(2,1)S(1)}, bf16[1024,512]{1,0:T(8,128)(2,1)}, u32[]{:S(2)}) copy-start(bf16[1024,512]{1,0:T(8,128)(2,1)} %get-tuple-element.43.kept_ref) | copy-start | bytes 3145732
  88.6 31.7 %all-to-all-start.2 = ((bf16[16,64,512]{2,1,0:T(8,128)(2,1)}), bf16[16,64,512]{2,1,0:T(8,128)(2,1)}, u32[]{:S(2)}, u32[]{:S(2)}) async-start(bf16[16,64,512]{2,1,0:T(8,128)(2,1)} %bitcast.31), calls=%async_computation.2 | async-start | bytes 2097152 | tf_op jit(solution)/shard_map/all_to_all | solution.py:460
  93.6 3.7 %collective-permute-start.2 = (bf16[1024,512]{1,0:T(8,128)(2,1)}, bf16[1024,512]{1,0:T(8,128)(2,1)S(1)}, u32[]{:S(2)}, u32[]{:S(2)}) collective-permute-start(bf16[1024,512]{1,0:T(8,128)(2,1)} %get-tuple-element.44), channel_id=1, source_target_pairs={{0,1},{1,0},{2,3},{3,2},{4,5},{5,4},{6,7},{7,6},{8,9},{9,8},{10,11... | collective-permute-start | bytes 3145736 | tf_op jit(solution)/shard_map/ppermute | solution.py:477
  97.5 11.5 %collective-permute-start.3 = (bf16[256,512]{1,0:T(8,128)(2,1)S(1)}, bf16[256,512]{1,0:T(8,128)(2,1)S(1)}, u32[]{:S(2)}, u32[]{:S(2)}) collective-permute-start(bf16[256,512]{1,0:T(8,128)(2,1)S(1)} %get-tuple-element.46), channel_id=1, source_target_pairs={{0,16},{16,32},{32,48},{48,0},{64,80},{80,96},{96,112},{112,64},{1... | collective-permute-start | bytes 786440 | tf_op jit(solution)/shard_map/ppermute | solution.py:470
  99.1 16.7 %collective-permute-start.4 = (bf16[256,512]{1,0:T(8,128)(2,1)S(1)}, bf16[256,512]{1,0:T(8,128)(2,1)S(1)}, u32[]{:S(2)}, u32[]{:S(2)}) collective-permute-start(bf16[256,512]{1,0:T(8,128)(2,1)S(1)} %get-tuple-element.47), channel_id=1, source_target_pairs={{0,32},{16,48},{32,0},{48,16},{64,96},{80,112},{96,64},{112,80},{1... | collective-permute-start | bytes 786440 | tf_op jit(solution)/shard_map/ppermute | solution.py:470
  103.7 12.2 %collective-permute-start.5 = (bf16[256,512]{1,0:T(8,128)(2,1)S(1)}, bf16[256,512]{1,0:T(8,128)(2,1)S(1)}, u32[]{:S(2)}, u32[]{:S(2)}) collective-permute-start(bf16[256,512]{1,0:T(8,128)(2,1)S(1)} %get-tuple-element.48), channel_id=1, source_target_pairs={{0,48},{16,0},{32,16},{48,32},{64,112},{80,64},{96,80},{112,96},{1... | collective-permute-start | bytes 786440 | tf_op jit(solution)/shard_map/ppermute | solution.py:470
  115.9 8.6 %collective-permute-start.6 = (bf16[64,512]{1,0:T(8,128)(2,1)S(1)}, bf16[64,512]{1,0:T(8,128)(2,1)S(1)}, u32[]{:S(2)}, u32[]{:S(2)}) collective-permute-start(bf16[64,512]{1,0:T(8,128)(2,1)S(1)} %get-tuple-element.58), channel_id=1, source_target_pairs={{0,64},{16,80},{32,96},{48,112},{64,128},{80,144},{96,160},{112,17... | collective-permute-start | bytes 196616 | tf_op jit(solution)/shard_map/ppermute | solution.py:470
  117.4 7.2 %collective-permute-start.7 = (bf16[64,512]{1,0:T(8,128)(2,1)S(1)}, bf16[64,512]{1,0:T(8,128)(2,1)S(1)}, u32[]{:S(2)}, u32[]{:S(2)}) collective-permute-start(bf16[64,512]{1,0:T(8,128)(2,1)S(1)} %get-tuple-element.59), channel_id=1, source_target_pairs={{0,128},{16,144},{32,160},{48,176},{64,192},{80,208},{96,224},{112... | collective-permute-start | bytes 196616 | tf_op jit(solution)/shard_map/ppermute | solution.py:470
  118.8 5.8 %collective-permute-start.8 = (bf16[64,512]{1,0:T(8,128)(2,1)S(1)}, bf16[64,512]{1,0:T(8,128)(2,1)S(1)}, u32[]{:S(2)}, u32[]{:S(2)}) collective-permute-start(bf16[64,512]{1,0:T(8,128)(2,1)S(1)} %get-tuple-element.60), channel_id=1, source_target_pairs={{0,192},{16,208},{32,224},{48,240},{64,0},{80,16},{96,32},{112,48}... | collective-permute-start | bytes 196616 | tf_op jit(solution)/shard_map/ppermute | solution.py:470
  124.5 35.8 %copy-start.1 = (f32[64,64,128]{2,1,0:T(8,128)S(1)}, f32[64,64,128]{2,1,0:T(8,128)}, u32[]{:S(2)}) copy-start(f32[64,64,128]{2,1,0:T(8,128)} %get-tuple-element.42.spread_ref) | copy-start | bytes 6291460
  125.5 34.9 %all-to-all-start.3 = ((bf16[16,72,512]{2,1,0:T(8,128)(2,1)}), bf16[16,72,512]{2,1,0:T(8,128)(2,1)S(1)}, u32[]{:S(2)}, u32[]{:S(2)}) async-start(bf16[16,72,512]{2,1,0:T(8,128)(2,1)} %maximum_dynamic-update-slice_fusion), calls=%async_computation.3 | async-start | bytes 2359296 | tf_op jit(solution)/shard_map/all_to_all | solution.py:460
  130.9 30.3 %collective-permute-start.10 = (bf16[64,64,128]{2,1,0:T(8,128)(2,1)}, bf16[64,64,128]{2,1,0:T(8,128)(2,1)}, u32[]{:S(2)}, u32[]{:S(2)}) collective-permute-start(bf16[64,64,128]{2,1,0:T(8,128)(2,1)} %get-tuple-element.67), channel_id=1, source_target_pairs={{16,0},{32,16},{48,32},{64,48},{80,64},{96,80},{112,96},{128,112},... | collective-permute-start | bytes 3145736 | tf_op jit(solution)/shard_map/ppermute | solution.py:456
  137.0 29.5 %collective-permute-start.9 = (bf16[64,64,128]{2,1,0:T(8,128)(2,1)}, bf16[64,64,128]{2,1,0:T(8,128)(2,1)}, u32[]{:S(2)}, u32[]{:S(2)}) collective-permute-start(bf16[64,64,128]{2,1,0:T(8,128)(2,1)} %get-tuple-element.66), channel_id=1, source_target_pairs={{0,16},{16,32},{32,48},{48,64},{64,80},{80,96},{96,112},{112,128},... | collective-permute-start | bytes 3145736 | tf_op jit(solution)/shard_map/ppermute | solution.py:456
